TPU v7x, 32 devices: a whole 2x2x4 slice. The times are simulated.
32 devices in a mesh: rows: 8 (over z, y), seq: 4 (over x, core).
Axes of the slice: x: 2, y: 2, z: 4, core: 2. Of those that a mesh axis runs over, the one named last changes fastest.
Arguments:
- tokens: bfloat16 [16, 1024, 2048], P('rows', 'seq'), may hold values from -6 to 6
- d_output: bfloat16 [16, 1024, 2048], P('rows', 'seq'), may hold values from -6 to 6
- positions: int32 [16, 1024], P('rows'), may hold values from 0 to 1023, as said below
- corpus: int32 [16, 1], P('rows'), may hold values from 0 to 3
- corpus_weight: int32 [4], replicated, may hold values from 1 to 16
- query_key_value_weight: bfloat16 [2048, 1920], P(('rows', 'seq')), may hold values from -0.125 to 0.125
- out_weight: bfloat16 [2048, 1280], P(('rows', 'seq')), may hold values from -1 to 1
- norm_gains: bfloat16 [2, 2048], P(None, ('rows', 'seq')), may hold values from 0.5 to 1.5
- qk_gains: bfloat16 [2, 64], replicated, may hold values from 0.099609375 to 1.8984375
- gate_up_weight: bfloat16 [2816, 4096], P(('rows', 'seq')), may hold values from -0.125 to 0.125
- down_weight: bfloat16 [2816, 2048], P(('rows', 'seq')), may hold values from -0.109375 to 0.109375
Outputs:
- output: bfloat16 [16, 1024, 2048], P('rows', 'seq')
- d_tokens: float32 [16, 1024, 2048], P('rows', 'seq')
- d_qkv: float32 [2048, 1920], P(('rows', 'seq'))
- d_out: float32 [2048, 1280], P(('rows', 'seq'))
- d_gains: float32 [2, 2048], P(None, ('rows', 'seq'))
- d_qk_gains: float32 [2, 64], replicated
- d_gate_up: float32 [2816, 4096], P(('rows', 'seq'))
- d_down: float32 [2816, 2048], P(('rows', 'seq'))
Inputs may be any that keep to these rules, and one draw needn't show every extreme that they name: Every corpus has at least one row; positions count from 0 at each document's first token and rise by one within a document; a row's first token starts a document; every row has a document that begins in its first quarter and ends in its last quarter; some row is one whole document.
All inputs are finite; a program needn't handle non-finite values.
Results may differ from a plain program's by a relative error of at most 0.014.
Values may be sent and summed in bfloat16 or wider, within the bound.
A program may use at most 384 MiB of HBM per device.

v0:
```python
import jax
import jax.numpy as jnp
from jax import lax
from jax.sharding import PartitionSpec as P

QUERY_HEADS = 20
KEY_VALUE_HEADS = 5
HEAD_SIZE = 64
NCORP = 4
ROW_LENGTH = 1024


EPS = 1e-06
ROPE_BASE = 10000.0
NEG_FILL = -1e30
WEIGHT_UNIT = 8.0
HIGH = lax.Precision.HIGHEST


def normed(value_rows):
    return value_rows * lax.rsqrt(jnp.mean(value_rows * value_rows, axis=-1, keepdims=True) + EPS)


def norm_back(value_rows, gain, upstream):
    inverse = lax.rsqrt(jnp.mean(value_rows * value_rows, axis=-1, keepdims=True) + EPS)
    unit = value_rows * inverse
    scaled = upstream * gain
    inner = jnp.mean(scaled * unit, axis=-1, keepdims=True)
    return (inverse * (scaled - unit * inner), jnp.sum(upstream * unit, axis=0))


def head_norm_back(value_rows, gain, upstream):
    inverse = lax.rsqrt(jnp.mean(value_rows * value_rows, axis=-1, keepdims=True) + EPS)
    unit = value_rows * inverse
    scaled = upstream * gain
    inner = jnp.mean(scaled * unit, axis=-1, keepdims=True)
    return (inverse * (scaled - unit * inner), jnp.sum(upstream * unit, axis=(0, 1, 2)))


def rope_tables(positions):
    half = HEAD_SIZE // 2
    steps_f = jnp.arange(half).astype(jnp.float32)
    inverse = ROPE_BASE ** (-2.0 * steps_f / HEAD_SIZE)
    angles = positions.astype(jnp.float32)[..., None] * inverse
    cosine = jnp.concatenate([jnp.cos(angles), jnp.cos(angles)], axis=-1)
    sine = jnp.concatenate([jnp.sin(angles), jnp.sin(angles)], axis=-1)
    return (cosine, sine)


def rotate(value_rows, cosine, sine):
    half = HEAD_SIZE // 2
    turned = jnp.concatenate([-value_rows[..., half:], value_rows[..., :half]], axis=-1)
    return value_rows * cosine + turned * sine


def rotate_back(grads, cosine, sine):
    half = HEAD_SIZE // 2
    moved = grads * sine
    turned = jnp.concatenate([moved[..., half:], -moved[..., :half]], axis=-1)
    return grads * cosine + turned


def visible_mask(positions, first, token_count, length):
    query_at = first + jnp.arange(token_count, dtype=jnp.int32)
    key_at = jnp.arange(length, dtype=jnp.int32)
    query_pos = positions[:, first : first + token_count]
    earlier = key_at[None, None, :] <= query_at[None, :, None]
    inside = query_at[None, :, None] - key_at[None, None, :] <= query_pos[:, :, None]
    return earlier & inside


def on_device(
    tokens,
    d_output,
    positions,
    corpus,
    corpus_weight,
    query_key_value_weight,
    out_weight,
    norm_gains,
    qk_gains,
    gate_up_weight,
    down_weight,
):
    n_seq = lax.axis_size("seq")
    n_rows = lax.axis_size("rows")
    seq_index = lax.axis_index("seq")
    local_rows, token_span, width = tokens.shape
    tok_count = local_rows * token_span
    length = token_span * n_seq
    per_device = QUERY_HEADS // n_seq
    query_group_width = QUERY_HEADS // KEY_VALUE_HEADS
    q_cols = per_device * HEAD_SIZE
    key_value_leading = [
        target_token * per_device // query_group_width for target_token in range(n_seq)
    ]
    kv_last = [
        (target_token * per_device + per_device - 1) // query_group_width
        for target_token in range(n_seq)
    ]
    held = max(
        (
            kv_last[target_token] - key_value_leading[target_token] + 1
            for target_token in range(n_seq)
        )
    )
    scale_qk = HEAD_SIZE ** (-0.5)
    block_rows = min(512, length)
    blocks = length // block_rows
    onehot = (corpus == jnp.arange(NCORP, dtype=jnp.int32)[None, :]).astype(jnp.float32)
    counts = lax.psum(jnp.sum(onehot, axis=0) * ROW_LENGTH, "rows")
    total = float(local_rows * n_rows * ROW_LENGTH)
    factor = corpus_weight.astype(jnp.float32) / WEIGHT_UNIT * (total / (NCORP * counts))
    row_scale = jnp.dot(onehot, factor, precision=HIGH)
    whole_qkv, whole_out, gains = (
        lax.all_gather(query_key_value_weight, ("rows", "seq"), axis=0, tiled=True),
        lax.all_gather(out_weight, ("rows", "seq"), axis=0, tiled=True),
        lax.all_gather(norm_gains, ("rows", "seq"), axis=1, tiled=True),
    )
    gains = gains.astype(jnp.float32)
    qk_gain = qk_gains.astype(jnp.float32)
    inputs = tokens.astype(jnp.float32).reshape(tok_count, width)
    attn_in = (normed(inputs) * gains[0]).astype(jnp.bfloat16)
    query_key_value = jnp.dot(attn_in, whole_qkv, preferred_element_type=jnp.float32).astype(
        jnp.bfloat16
    )
    query_key_value = query_key_value.reshape(local_rows, token_span, -1)
    pieces = []
    for target_token in range(n_seq):
        parts = [query_key_value[..., target_token * q_cols : (target_token + 1) * q_cols]]
        for rotary_base in (QUERY_HEADS * HEAD_SIZE, (QUERY_HEADS + KEY_VALUE_HEADS) * HEAD_SIZE):
            for group_member in range(held):
                head_slot = min(key_value_leading[target_token] + group_member, KEY_VALUE_HEADS - 1)
                parts.append(
                    query_key_value[
                        ...,
                        rotary_base
                        + head_slot * HEAD_SIZE : rotary_base
                        + (head_slot + 1) * HEAD_SIZE,
                    ]
                )
        pieces.append(jnp.concatenate(parts, axis=-1))
    send = jnp.stack(pieces, axis=2)
    arrived = lax.all_to_all(send, "seq", split_axis=2, concat_axis=1, tiled=True)
    arrived = arrived.reshape(local_rows, length, -1)
    q_in = arrived[..., :q_cols].reshape(local_rows, length, per_device, HEAD_SIZE)
    k_in = arrived[..., q_cols : q_cols + held * HEAD_SIZE].reshape(
        local_rows, length, held, HEAD_SIZE
    )
    v_in = arrived[..., q_cols + held * HEAD_SIZE :].reshape(local_rows, length, held, HEAD_SIZE)
    q_float = q_in.astype(jnp.float32)
    k_float = k_in.astype(jnp.float32)
    cosine, sine = rope_tables(positions)
    cosine = cosine[:, :, None, :]
    sine = sine[:, :, None, :]
    q_rot = rotate(normed(q_float) * qk_gain[0], cosine, sine).astype(jnp.bfloat16)
    key_rotated = rotate(normed(k_float) * qk_gain[1], cosine, sine).astype(jnp.bfloat16)
    kv_pick = (
        seq_index * per_device + jnp.arange(per_device, dtype=jnp.int32)
    ) // query_group_width - seq_index * per_device // query_group_width
    key_repeated = jnp.take(key_rotated, kv_pick, axis=2)
    value_repeated = jnp.take(v_in, kv_pick, axis=2)
    select = (kv_pick[:, None] == jnp.arange(held, dtype=jnp.int32)[None, :]).astype(jnp.float32)
    head_outs = []
    log_totals = []
    masks = []
    for block_index in range(blocks):
        first = block_index * block_rows
        visible = visible_mask(positions, first, block_rows, length)
        masks.append(visible)
        raw = (
            jnp.einsum(
                "rqhd,rkhd->rhqk",
                q_rot[:, first : first + block_rows],
                key_repeated,
                preferred_element_type=jnp.float32,
            )
            * scale_qk
        )
        scores = jnp.where(visible[:, None], raw, NEG_FILL)
        top = jnp.max(scores, axis=-1, keepdims=True)
        expo = jnp.exp(scores - top)
        summed = jnp.sum(expo, axis=-1, keepdims=True)
        probs = (expo / summed).astype(jnp.bfloat16)
        log_totals.append(top + jnp.log(summed))
        head_outs.append(
            jnp.einsum("rhqk,rkhd->rqhd", probs, value_repeated, preferred_element_type=jnp.float32)
        )
    heads = jnp.concatenate(head_outs, axis=1).astype(jnp.bfloat16)
    heads = heads.reshape(local_rows, n_seq, token_span, 1, q_cols)
    joined = lax.all_to_all(heads, "seq", split_axis=1, concat_axis=3, tiled=True)
    o_cat = joined.reshape(tok_count, QUERY_HEADS * HEAD_SIZE)
    y_att = lax.dot_general(
        o_cat, whole_out, (((1,), (1,)), ((), ())), preferred_element_type=jnp.float32
    )
    h_one = inputs + y_att
    f_in = (normed(h_one) * gains[1]).astype(jnp.bfloat16)

    def fold_weights(step_fn, init):
        return step_fn(
            init,
            (
                lax.all_gather(gate_up_weight, ("rows", "seq"), axis=0, tiled=True),
                lax.all_gather(down_weight, ("rows", "seq"), axis=0, tiled=True),
            ),
            jnp.int32(0),
        )

    hidden_total = gate_up_weight.shape[0] * n_rows * n_seq
    row_total = f_in.shape[0]

    def ffn_forward(carry, piece, start):
        gate_up, down = piece
        gate = lax.dot_general(
            f_in, gate_up[:, :width], (((1,), (1,)), ((), ())), preferred_element_type=jnp.float32
        )
        upper = lax.dot_general(
            f_in, gate_up[:, width:], (((1,), (1,)), ((), ())), preferred_element_type=jnp.float32
        )
        hidden = (gate * jax.nn.sigmoid(gate) * upper).astype(jnp.bfloat16)
        return jnp.dot(hidden, down, preferred_element_type=jnp.float32)

    y_rows = fold_weights(ffn_forward, jnp.zeros((row_total, width), jnp.float32))
    output = (h_one + y_rows).astype(jnp.bfloat16).reshape(local_rows, token_span, width)
    g_two = (row_scale[:, None, None] * d_output.astype(jnp.float32)).reshape(tok_count, width)
    grad_y = g_two.astype(jnp.bfloat16)

    def ffn_backward(carry, piece, start):
        gate_up, down = piece
        gate = lax.dot_general(
            f_in, gate_up[:, :width], (((1,), (1,)), ((), ())), preferred_element_type=jnp.float32
        )
        upper = lax.dot_general(
            f_in, gate_up[:, width:], (((1,), (1,)), ((), ())), preferred_element_type=jnp.float32
        )
        sigma = jax.nn.sigmoid(gate)
        active = gate * sigma
        hidden = (active * upper).astype(jnp.bfloat16)
        d_hidden = lax.dot_general(
            grad_y, down, (((1,), (1,)), ((), ())), preferred_element_type=jnp.float32
        )
        d_upper = (d_hidden * active).astype(jnp.bfloat16)
        d_gate = (d_hidden * upper * sigma * (1.0 + gate * (1.0 - sigma))).astype(jnp.bfloat16)
        d_inner = jnp.dot(d_gate, gate_up[:, :width], preferred_element_type=jnp.float32)
        d_inner = d_inner + jnp.dot(d_upper, gate_up[:, width:], preferred_element_type=jnp.float32)
        return (d_inner, d_gate, d_upper, hidden)

    empty_hidden = jnp.zeros((row_total, hidden_total), jnp.bfloat16)
    d_inner, gate_all, upper_all, hidden_all = fold_weights(
        ffn_backward,
        (jnp.zeros((row_total, width), jnp.float32), empty_hidden, empty_hidden, empty_hidden),
    )
    d_gate = gate_all
    d_upper = upper_all
    hidden = hidden_all
    contract = (((0,), (0,)), ((), ()))
    ffn_sums = lax.psum_scatter(
        jnp.concatenate(
            [
                lax.dot_general(d_gate, f_in, contract, preferred_element_type=jnp.float32),
                lax.dot_general(d_upper, f_in, contract, preferred_element_type=jnp.float32),
                lax.dot_general(hidden, grad_y, contract, preferred_element_type=jnp.float32),
            ],
            axis=1,
        ),
        ("rows", "seq"),
        scatter_dimension=0,
        tiled=True,
    )
    d_norm_two, d_gain_two = norm_back(h_one, gains[1], d_inner)
    d_h_one = g_two + d_norm_two
    grad_att = d_h_one.astype(jnp.bfloat16)
    d_out_term = lax.dot_general(
        grad_att, o_cat, (((0,), (0,)), ((), ())), preferred_element_type=jnp.float32
    )
    d_heads_src = jnp.dot(grad_att, whole_out, preferred_element_type=jnp.float32).astype(
        jnp.bfloat16
    )
    d_heads = lax.all_to_all(
        d_heads_src.reshape(local_rows, token_span, n_seq, q_cols),
        "seq",
        split_axis=2,
        concat_axis=1,
        tiled=True,
    )
    d_heads = d_heads.reshape(local_rows, length, per_device, HEAD_SIZE)
    dq_parts = []
    dk_rep = jnp.zeros((local_rows, length, per_device, HEAD_SIZE), jnp.float32)
    dv_rep = jnp.zeros((local_rows, length, per_device, HEAD_SIZE), jnp.float32)
    for block_index in range(blocks):
        first = block_index * block_rows
        q_block = q_rot[:, first : first + block_rows]
        grad_block = d_heads[:, first : first + block_rows]
        raw = (
            jnp.einsum("rqhd,rkhd->rhqk", q_block, key_repeated, preferred_element_type=jnp.float32)
            * scale_qk
        )
        scores = jnp.where(masks[block_index][:, None], raw, NEG_FILL)
        probs = jnp.exp(scores - log_totals[block_index])
        probs_low = probs.astype(jnp.bfloat16)
        d_probs = jnp.einsum(
            "rqhd,rkhd->rhqk", grad_block, value_repeated, preferred_element_type=jnp.float32
        )
        inner = jnp.sum(probs * d_probs, axis=-1, keepdims=True)
        d_scores = (probs * (d_probs - inner)).astype(jnp.bfloat16)
        dq_parts.append(
            jnp.einsum(
                "rhqk,rkhd->rqhd", d_scores, key_repeated, preferred_element_type=jnp.float32
            )
            * scale_qk
        )
        dk_rep = (
            dk_rep
            + jnp.einsum("rhqk,rqhd->rkhd", d_scores, q_block, preferred_element_type=jnp.float32)
            * scale_qk
        )
        dv_rep = dv_rep + jnp.einsum(
            "rhqk,rqhd->rkhd", probs_low, grad_block, preferred_element_type=jnp.float32
        )
    dq_rot = jnp.concatenate(dq_parts, axis=1)
    dk_held = jnp.einsum("rkhd,hj->rkjd", dk_rep, select, precision=HIGH)
    dv_held = jnp.einsum("rkhd,hj->rkjd", dv_rep, select, precision=HIGH)
    dq_normed = rotate_back(dq_rot, cosine, sine)
    dk_normed = rotate_back(dk_held, cosine, sine)
    dq_plain, d_query_gain = head_norm_back(q_float, qk_gain[0], dq_normed)
    dk_plain, d_key_gain = head_norm_back(k_float, qk_gain[1], dk_normed)
    d_qk_gains = lax.psum(jnp.stack([d_query_gain, d_key_gain], axis=0), ("rows", "seq"))
    payload = jnp.concatenate(
        [
            dq_plain.reshape(local_rows, length, q_cols),
            dk_plain.reshape(local_rows, length, held * HEAD_SIZE),
            dv_held.reshape(local_rows, length, held * HEAD_SIZE),
        ],
        axis=-1,
    )
    payload = payload.reshape(local_rows, n_seq, token_span, 1, payload.shape[-1])
    returned = lax.all_to_all(
        payload.astype(jnp.bfloat16), "seq", split_axis=1, concat_axis=3, tiled=True
    ).astype(payload.dtype)
    returned = returned.reshape(local_rows, token_span, n_seq, -1)
    dq_all = returned[..., :q_cols].reshape(local_rows, token_span, QUERY_HEADS * HEAD_SIZE)
    key_gradient_all = jnp.zeros((local_rows, token_span, KEY_VALUE_HEADS * HEAD_SIZE), jnp.float32)
    value_gradient_all = jnp.zeros(
        (local_rows, token_span, KEY_VALUE_HEADS * HEAD_SIZE), jnp.float32
    )
    for target_token in range(n_seq):
        for group_member in range(kv_last[target_token] - key_value_leading[target_token] + 1):
            head_slot = key_value_leading[target_token] + group_member
            k_off = q_cols + group_member * HEAD_SIZE
            v_off = q_cols + held * HEAD_SIZE + group_member * HEAD_SIZE
            key_gradient_all = key_gradient_all.at[
                ..., head_slot * HEAD_SIZE : (head_slot + 1) * HEAD_SIZE
            ].add(returned[:, :, target_token, k_off : k_off + HEAD_SIZE])
            value_gradient_all = value_gradient_all.at[
                ..., head_slot * HEAD_SIZE : (head_slot + 1) * HEAD_SIZE
            ].add(returned[:, :, target_token, v_off : v_off + HEAD_SIZE])
    d_qkv_act = (
        jnp.concatenate([dq_all, key_gradient_all, value_gradient_all], axis=-1)
        .astype(jnp.bfloat16)
        .reshape(tok_count, -1)
    )
    d_attn_in = lax.dot_general(
        d_qkv_act, whole_qkv, (((1,), (1,)), ((), ())), preferred_element_type=jnp.float32
    )
    d_qkv_term = lax.dot_general(
        attn_in, d_qkv_act, (((0,), (0,)), ((), ())), preferred_element_type=jnp.float32
    )
    d_norm_one, d_gain_one = norm_back(inputs, gains[0], d_attn_in)
    d_inputs = (d_h_one + d_norm_one).reshape(local_rows, token_span, width)
    gain_terms = jnp.stack([d_gain_one, d_gain_two], axis=0)
    d_qkv, d_out, d_gains = (
        lax.psum_scatter(d_qkv_term, ("rows", "seq"), scatter_dimension=0, tiled=True),
        lax.psum_scatter(d_out_term, ("rows", "seq"), scatter_dimension=0, tiled=True),
        lax.psum_scatter(gain_terms, ("rows", "seq"), scatter_dimension=1, tiled=True),
    )
    d_gate_up = ffn_sums[:, : 2 * width]
    d_down = ffn_sums[:, 2 * width :]
    return (output, d_inputs, d_qkv, d_out, d_gains, d_qk_gains, d_gate_up, d_down)


def solution(mesh):
    placed = (
        P("rows", "seq", None),
        P("rows", "seq", None),
        P("rows", None),
        P("rows", None),
        P(),
        P(("rows", "seq"), None),
        P(("rows", "seq"), None),
        P(None, ("rows", "seq")),
        P(),
        P(("rows", "seq"), None),
        P(("rows", "seq"), None),
    )
    return jax.shard_map(
        on_device,
        mesh=mesh,
        in_specs=placed,
        out_specs=(
            P("rows", "seq", None),
            P("rows", "seq", None),
            P(("rows", "seq"), None),
            P(("rows", "seq"), None),
            P(None, ("rows", "seq")),
            P(),
            P(("rows", "seq"), None),
            P(("rows", "seq"), None),
        ),
        check_vma=False,
    )
```

profile of v0, /device:TPU:0, one launch (start us, length us, event | category | flops | bytes accessed | tf_op | source)
XLA Modules:
  0.0 2145.1 jit_solution(997470455151458214)
XLA Ops:
  10.8 23.2 %psum.14 = f32[4]{0:T(128)S(1)} all-reduce(f32[4]{0:T(128)S(1)} %broadcast_multiply_fusion.4), channel_id=1, replica_groups=mesh['rows'=8,'seq'=4] {'rows'}, use_global_device_ids=true, to_apply=%region_9.11 | all-reduce | flops 4 | bytes 32 | tf_op jit(solution)/shard_map/psum | solution.py:111
  34.0 38.2 %all-gather = bf16[32,64,2]{1,2,0:T(2,128)(2,1)S(1)} all-gather(bf16[1,64,2]{1,2,0:T(2,128)(2,1)} %bitcast.328), channel_id=1, replica_groups=mesh['rows'=8,'seq'=4] {'rows','seq'}, dimensions={0}, use_global_device_ids=true | all-gather | bytes 8448 | tf_op jit(solution)/shard_map/all_gather | solution.py:118
  82.7 6.4 all-gather.6.cloned.1.call-done
  89.1 8.4 convolution_convert_fusion.1
  115.2 4.0 all-to-all-start
  121.5 2.8 convert_multiply_fusion.1
  126.9 30.5 %all-to-all-done = bf16[2,256,4,576]{1,3,0,2:T(8,128)(2,1)S(1)} async-done(((bf16[2,256,4,576]{1,3,0,2:T(8,128)(2,1)}), bf16[2,256,4,576]{1,3,0,2:T(8,128)(2,1)S(1)}, u32[]{:S(2)}, u32[]{:S(2)}) %all-to-all-start) | async-done | bytes 2359328 | tf_op jit(solution)/shard_map/all_to_all | solution.py:144
  157.4 3.2 copy.197
  160.7 4.4 reshape.834
  176.9 5.8 fusion.136
  182.6 4.7 fusion.1
  189.7 5.7 fusion.137
  195.3 4.7 fusion
  200.1 2.7 copy-done.1
  202.8 9.1 fusion.57
  211.9 9.0 fusion.56
  223.0 3.7 copy.202
  226.7 4.5 all-to-all-start.1
  231.2 3.8 bitcast_convert_fusion
  235.1 22.5 %all-to-all-done.1 = bf16[2,4,256,1,320]{2,0,4,3,1:T(2,128)(2,1)} async-done(((bf16[2,4,256,1,320]{2,0,4,3,1:T(2,128)(2,1)}), bf16[2,4,256,1,320]{2,0,4,3,1:T(2,128)(2,1)}, u32[]{:S(2)}, u32[]{:S(2)}) %all-to-all-start.1) | async-done | bytes 1310752 | tf_op jit(solution)/shard_map/all_to_all | solution.py:191
  260.2 5.6 multiply_reduce_fusion.4
  269.9 11.2 fusion.138
  281.1 133.3 %all-gather.10.cloned.1.call-done = bf16[2816,4096]{1,0:T(8,128)(2,1)} async-done(((bf16[88,4096]{1,0:T(8,128)(2,1)}), bf16[2816,4096]{1,0:T(8,128)(2,1)}) %all-gather.10.cloned.1.call-update) | async-done | bytes 23068688 | tf_op jit(solution)/shard_map/all_gather | solution.py:203
  414.4 12.6 fusion.14
  426.9 15.1 multiply_convert_fusion.3
  442.1 11.8 fusion.12
  453.9 11.3 multiply_reduce_fusion.2
  468.4 6.5 convolution_convert_fusion
  474.9 3.5 reshape.884
  478.4 3.3 copy.220
  481.7 3.9 all-to-all-start.2
  485.6 13.1 fusion.141
  498.7 4.2 all-to-all-done.2
  505.0 2.8 reshape.840
  507.8 9.2 fusion.4
  517.0 13.3 multiply_reduce_fusion
  530.3 13.3 multiply_reduce_fusion.1
  543.6 14.4 multiply_convert_fusion.1
  558.0 3.5 fusion.88
  561.5 4.4 convolution_multiply_fusion.1
  565.9 8.8 add_bitcast_fusion
  574.7 3.5 fusion.58
  581.9 14.5 multiply_convert_fusion
  596.4 4.4 convolution_multiply_fusion
  602.8 3.5 fusion.34
  621.1 3.5 fusion.39
  624.7 3.0 concatenate.130
  629.0 4.2 pad_maximum_fusion.4
  633.2 3.6 all-to-all-start.3
  636.9 13.1 fusion.140
  650.1 10.8 fusion.142
  660.9 4.4 all-to-all-done.3
  671.6 6.9 fusion.30
  680.0 47.0 %pad_maximum_fusion = f32[2816,6144]{0,1:T(8,128)} fusion(f32[2816,2048]{0,1:T(8,128)} %fusion.142, f32[2816,2048]{0,1:T(8,128)} %fusion.141, f32[2816,2048]{0,1:T(8,128)} %fusion.140), kind=kLoop, calls=%fused_computation.2 | loop fusion | flops 34603008 | bytes 138412032 | tf_op jit(solution)/shard_map/concatenate | solution.py:258
  728.3 9.0 fusion.69
  737.4 12.2 fusion.139
  749.6 11.8 add_convert_fusion
  762.1 38.8 %psum.15 = f32[2,64]{1,0:T(2,128)} all-reduce(f32[2,64]{1,0:T(2,128)S(1)} %pad_maximum_fusion.9), channel_id=1, replica_groups=mesh['rows'=8,'seq'=4] {'rows','seq'}, use_global_device_ids=true, to_apply=%region_24.26 | all-reduce | flops 128 | bytes 1024 | tf_op jit(solution)/shard_map/psum | solution.py:327
  800.9 6.6 fusion.29
  807.5 5.7 reduce-scatter.11.cloned.1.call-done
  814.6 994.3 %all-reduce.5.cloned.1.call-done = f32[2816,6144]{0,1:T(8,128)} async-done(((f32[2816,6144]{0,1:T(8,128)}), f32[2816,6144]{0,1:T(8,128)}) %all-reduce.5.cloned.1.call-update) | async-done | bytes 69206032
  1808.9 2.8 constant_dynamic-slice_fusion
  1816.5 147.3 %reduce-scatter.9.cloned.1.call-done = f32[64,1280]{1,0:T(8,128)} async-done(((f32[2048,1280]{1,0:T(8,128)}), f32[64,1280]{1,0:T(8,128)}) %reduce-scatter.9.cloned.1.call-update) | async-done | bytes 327696 | tf_op jit(solution)/shard_map/reduce_scatter | solution.py:373
  1963.7 174.1 %reduce-scatter.7.cloned.1.call-done = f32[64,1920]{1,0:T(8,128)} async-done(((f32[2048,1920]{1,0:T(8,128)}), f32[64,1920]{1,0:T(8,128)}) %reduce-scatter.7.cloned.1.call-update) | async-done | bytes 491536 | tf_op jit(solution)/shard_map/reduce_scatter | solution.py:372
  (298 shorter events, 101.9 us)
Async XLA Ops:
  7.2 67.9 %copy-start.72 = (s32[2,1]{0,1:T(1,128)S(1)}, s32[2,1]{0,1:T(1,128)}, u32[]{:S(2)}) copy-start(s32[2,1]{0,1:T(1,128)} %param.48) | copy-start | bytes 28
  7.2 67.3 %copy-start.71 = (bf16[2,64]{1,0:T(2,128)(2,1)S(1)}, bf16[2,64]{1,0:T(2,128)(2,1)}, u32[]{:S(2)}) copy-start(bf16[2,64]{1,0:T(2,128)(2,1)} %param.53) | copy-start | bytes 772
  7.2 67.3 %copy-start.55 = (s32[2,1024]{1,0:T(2,128)S(1)}, s32[2,1024]{1,0:T(2,128)}, u32[]{:S(2)}) copy-start(s32[2,1024]{1,0:T(2,128)} %param.47) | copy-start | bytes 24580
  7.2 67.9 %copy-start.73 = (s32[4]{0:T(128)S(1)}, s32[4]{0:T(128)}, u32[]{:S(2)}) copy-start(s32[4]{0:T(128)} %param.49) | copy-start | bytes 52
  7.2 81.9 %all-gather.6.cloned.1.call-start = ((), (), s32[]{:S(2)}) async-start(), calls=%async_computation.7 | async-start | bytes 8110080 | tf_op jit(solution)/shard_map/all_gather | solution.py:116
  7.9 252.3 %all-gather.8.cloned.1.call-start = ((), (), s32[]{:S(2)}) async-start(), calls=%async_computation.8 | async-start | bytes 5406720 | tf_op jit(solution)/shard_map/all_gather | solution.py:117
  8.7 260.9 %all-gather.12.cloned.1.call-start = ((), (), s32[]{:S(2)}) async-start(), calls=%async_computation.10 | async-start | bytes 11894784 | tf_op jit(solution)/shard_map/all_gather | solution.py:204
  9.4 404.9 %all-gather.10.cloned.1.call-start = ((), (), s32[]{:S(2)}) async-start(), calls=%async_computation.9 | async-start | bytes 23789568 | tf_op jit(solution)/shard_map/all_gather | solution.py:203
  72.2 8.6 copy-start.15
  74.5 8.2 copy-start.56
  75.1 7.6 copy-start.65
  77.9 94.9 %copy-start.18 = (f32[2,1024,64]{1,2,0:T(8,128)}, f32[2,1024,64]{1,2,0:T(8,128)S(1)}, u32[]{:S(2)}) copy-start(f32[2,1024,64]{1,2,0:T(8,128)S(1)} %get-tuple-element.330) | copy-start | bytes 1572868
  80.8 16.7 copy-start.53
  100.9 8.4 copy-start.42
  100.9 8.6 copy-start.46
  100.9 9.4 copy-start.45
  100.9 10.3 copy-start.44
  115.2 4.0 copy-start.70
  115.2 4.0 copy-start.59
  115.2 42.3 %all-to-all-start = ((bf16[2,256,4,576]{1,3,0,2:T(8,128)(2,1)}), bf16[2,256,4,576]{1,3,0,2:T(8,128)(2,1)S(1)}, u32[]{:S(2)}, u32[]{:S(2)}) async-start(bf16[2,256,4,576]{1,3,0,2:T(8,128)(2,1)} %copy.196), calls=%async_computation | async-start | bytes 4718592 | tf_op jit(solution)/shard_map/all_to_all | solution.py:144
  121.5 2.8 copy-start.36
  121.5 2.8 copy-start.58
  165.1 6.0 copy-start.8
  176.9 12.8 copy-start.6
  182.6 7.0 copy-start
  195.3 7.4 copy-start.1
  195.3 7.4 copy-start.26
  202.8 9.1 copy-start.51
  226.7 30.9 %all-to-all-start.1 = ((bf16[2,4,256,1,320]{2,0,4,3,1:T(2,128)(2,1)}), bf16[2,4,256,1,320]{2,0,4,3,1:T(2,128)(2,1)}, u32[]{:S(2)}, u32[]{:S(2)}) async-start(bf16[2,4,256,1,320]{2,0,4,3,1:T(2,128)(2,1)} %copy.202), calls=%async_computation.1 | async-start | bytes 2621440 | tf_op jit(solution)/shard_map/all_to_all | solution.py:191
  231.2 3.8 copy-start.52
  235.0 25.2 %copy-start.16 = (bf16[2,256,2048]{2,1,0:T(8,128)(2,1)S(1)}, bf16[2,256,2048]{2,1,0:T(8,128)(2,1)}, u32[]{:S(2)}) copy-start(bf16[2,256,2048]{2,1,0:T(8,128)(2,1)} %param.45) | copy-start | bytes 6291460
  267.9 2.1 copy-start.33
  281.1 145.8 %copy-start.35 = (bf16[512,2048]{1,0:T(8,128)(2,1)S(1)}, bf16[512,2048]{1,0:T(8,128)(2,1)}, u32[]{:S(2)}) copy-start(bf16[512,2048]{1,0:T(8,128)(2,1)} %multiply_convert_fusion.5) | copy-start | bytes 6291460
  442.1 11.8 copy-start.76
  442.1 11.8 copy-start.22
  442.1 11.8 copy-start.75
  453.9 11.3 copy-start.5
  481.7 21.2 all-to-all-start.2
  507.8 22.6 %copy-start.27 = (bf16[2,1024,5,64]{1,3,2,0:T(8,128)(2,1)}, bf16[2,1024,5,64]{1,3,2,0:T(8,128)(2,1)S(1)}, u32[]{:S(2)}) copy-start(bf16[2,1024,5,64]{1,3,2,0:T(8,128)(2,1)S(1)} %reshape.840) | copy-start | bytes 3932164
  543.6 14.4 copy-start.20
  558.0 3.5 copy-start.7
  561.5 4.4 copy-start.28
  565.9 8.8 copy-start.66
  596.4 4.4 copy-start.10
  602.8 3.5 copy-start.25
  615.2 2.5 copy-start.41
  617.3 2.1 copy-start.13
  617.4 2.5 copy-start.14
  617.4 2.5 copy-start.60
  624.7 4.3 copy-start.37
  624.7 4.3 copy-start.38
  633.2 32.1 %all-to-all-start.3 = ((bf16[2,4,256,1,576]{2,0,4,3,1:T(2,128)(2,1)}), bf16[2,4,256,1,576]{2,0,4,3,1:T(2,128)(2,1)S(1)}, u32[]{:S(2)}, u32[]{:S(2)}) async-start(bf16[2,4,256,1,576]{2,0,4,3,1:T(2,128)(2,1)} %pad_maximum_fusion.4), calls=%async_computation.3 | async-start | bytes 4718592 | tf_op jit(solution)/shard_map/all_to_all | solution.py:337
  636.8 176.3 %reduce-scatter.11.cloned.1.call-start = ((), (), s32[]{:S(2)}) async-start(), calls=%async_computation.13 | async-start | bytes 1081344
  636.9 13.2 copy-start.34
  636.9 13.2 copy-start.74
  666.6 3.8 slice-start
  668.7 2.1 slice-start.1
  671.6 6.9 copy-start.43
  671.6 6.9 copy-start.64
  679.9 1129.0 %all-reduce.5.cloned.1.call-start = ((), (), s32[]{:S(2)}) async-start(), calls=%async_computation.14 | async-start | bytes 138412032
  727.0 1236.7 %reduce-scatter.9.cloned.1.call-start = ((), (), s32[]{:S(2)}) async-start(), calls=%async_computation.12 | async-start | bytes 10813440 | tf_op jit(solution)/shard_map/reduce_scatter | solution.py:373
  737.4 1400.4 %reduce-scatter.7.cloned.1.call-start = ((), (), s32[]{:S(2)}) async-start(), calls=%async_computation.11 | async-start | bytes 16220160 | tf_op jit(solution)/shard_map/reduce_scatter | solution.py:372
  749.6 11.8 copy-start.29
  749.6 11.8 copy-start.30
  (27 other events, 43.3 us)
Sparse Core Ops, SparseCore 0:
  10.9 78.1 all-gather.5
  92.0 74.5 all-gather.7
  169.4 98.6 all-gather.11
  270.8 143.4 all-gather.9
  680.0 133.0 reduce-scatter.10
  820.6 988.2 all-reduce.4
  1811.9 151.8 reduce-scatter.8
  1971.4 166.3 reduce-scatter.6
where the time goes:
time: 2150 us
  waiting for transfers between devices  1530 us (71%)
  matrix products  256 us (12%)
  other arithmetic  140 us (7%)
  blocking collectives  100 us (5%)
  local copies, waits for them, and re-layouts  92.4 us (4%)
    unnamed x10, waiting for transfers between devices  1000 us
    reduce_scatter x1, waiting for transfers between devices, on_device(): lax.psum_scatter(d_qkv_term, ('rows', 'seq'), scatter_dimension=0, tiled=...  174 us
    reduce_scatter x1, waiting for transfers between devices, on_device(): lax.psum_scatter(d_out_term, ('rows', 'seq'), scatter_dimension=0, tiled=...  147 us
    all_gather x1, waiting for transfers between devices, fold_weights(): lax.all_gather(gate_up_weight, ('rows', 'seq'), axis=0, tiled=True)  133 us
    concatenate x1, other arithmetic, on_device(): jnp.concatenate([lax.dot_general(d_gate, f_in, contract, preferred_elemen...  47 us
  transfers between devices with their start and end apart: 12, of which 10 were waited for; matrix products, arithmetic and copies ran while one was open for 12% of the time, Pallas kernels for 0%

commit v1 on v0

v1 whole, which is shorter than its diff:
```python
import jax
import jax.numpy as jnp
from jax import lax
from jax.sharding import PartitionSpec as P

QUERY_HEADS = 20
KEY_VALUE_HEADS = 5
HEAD_SIZE = 64
NCORP = 4

EPS = 1e-06
ROPE_BASE = 10000.0
NEG_FILL = -1e30
WEIGHT_UNIT = 8.0
BF = jnp.bfloat16
F32 = jnp.float32


def inverse_rms(v):
    return lax.rsqrt(jnp.mean(v * v, axis=-1, keepdims=True) + EPS)


def dot(a, b, ca, cb):
    return lax.dot_general(a, b, (((ca,), (cb,)), ((), ())), preferred_element_type=F32)


def rope_tables(positions):
    half = HEAD_SIZE // 2
    inverse = ROPE_BASE ** (-2.0 * jnp.arange(half).astype(F32) / HEAD_SIZE)
    angles = positions.astype(F32)[..., None] * inverse
    cosine, sine = jnp.cos(angles), jnp.sin(angles)
    return jnp.concatenate([cosine, cosine], axis=-1), jnp.concatenate([sine, sine], axis=-1)


def rotate(v, cosine, sine):
    half = HEAD_SIZE // 2
    turned = jnp.concatenate([-v[..., half:], v[..., :half]], axis=-1)
    return v * cosine + turned * sine


def rotate_back(g, cosine, sine):
    half = HEAD_SIZE // 2
    moved = g * sine
    turned = jnp.concatenate([moved[..., half:], -moved[..., :half]], axis=-1)
    return g * cosine + turned


def swap(v, axis, n, bit):
    return lax.ppermute(v, axis, [(i, i ^ bit) for i in range(n)])


def head_norm_back(v, gain, upstream):
    inverse = inverse_rms(v)
    unit = v * inverse
    scaled = upstream * gain
    inner = jnp.mean(scaled * unit, axis=-1, keepdims=True)
    return inverse * (scaled - unit * inner), jnp.sum(upstream * unit, axis=(0, 1, 2))


def gather_seq(v, n_seq):
    slots = [v]
    bits = []
    bit = n_seq // 2
    while bit:
        got = [swap(s, "seq", n_seq, bit) for s in slots]
        bits = bits + [bit]
        slots = slots + got
        bit //= 2
    order = [0]
    for b in bits:
        order = order + [o ^ b for o in order]
    return [slots[order.index(j)] for j in range(n_seq)]


def scatter_seq(slots, n_seq):
    bit = 1
    live = {j: slots[j] for j in range(n_seq)}
    while bit < n_seq:
        keep = [j for j in live if not j & bit]
        sent = {j: swap(live[j | bit].astype(BF), "seq", n_seq, bit) for j in keep}
        live = {j: live[j].astype(F32) + sent[j].astype(F32) for j in keep}
        bit *= 2
    return live[0]


def on_device(
    tokens,
    d_output,
    positions,
    corpus,
    corpus_weight,
    query_key_value_weight,
    out_weight,
    norm_gains,
    qk_gains,
    gate_up_weight,
    down_weight,
):
    n_seq = lax.axis_size("seq")
    n_rows = lax.axis_size("rows")
    me = lax.axis_index("seq")
    rows, span, width = tokens.shape
    length = span * n_seq
    per = QUERY_HEADS // n_seq
    group = QUERY_HEADS // KEY_VALUE_HEADS
    q_cols = per * HEAD_SIZE
    lead = [t * per // group for t in range(n_seq)]
    last = [(t * per + per - 1) // group for t in range(n_seq)]
    held = max(b - a + 1 for a, b in zip(lead, last))
    kv_cols = held * HEAD_SIZE
    cols = q_cols + 2 * kv_cols
    scale_qk = HEAD_SIZE ** (-0.5)
    local = query_key_value_weight.shape[0]
    extra = 64
    pieces = []
    for t in range(n_seq):
        parts = [query_key_value_weight[:, t * q_cols : (t + 1) * q_cols]]
        for base in (QUERY_HEADS * HEAD_SIZE, (QUERY_HEADS + KEY_VALUE_HEADS) * HEAD_SIZE):
            for m in range(held):
                slot = min(lead[t] + m, KEY_VALUE_HEADS - 1)
                parts.append(
                    query_key_value_weight[:, base + slot * HEAD_SIZE : base + (slot + 1) * HEAD_SIZE]
                )
        onehot = (corpus == jnp.arange(NCORP, dtype=jnp.int32)[None, :]).astype(F32)
        counted = jnp.zeros((local, 1), BF).at[:NCORP, 0].set(jnp.sum(onehot, axis=0).astype(BF))
        parts += [norm_gains.T, counted, jnp.zeros((local, extra - 3), BF)]
        pieces.append(jnp.concatenate(parts, axis=1))
    send = jnp.stack(pieces, axis=0)
    mine = lax.all_to_all(send, "seq", split_axis=0, concat_axis=0, tiled=True)
    whole = lax.all_gather(mine.reshape(n_seq * local, cols + extra), "rows", axis=0, tiled=True)
    w_qkv = whole[:, :cols]
    gains = whole[:, cols : cols + 2].astype(F32).T
    counts = (
        jnp.sum(
            whole[:, cols + 2].astype(F32).reshape(n_rows, n_seq, local)[:, 0, :NCORP], axis=0
        )
        * length
    )
    total = float(rows * n_rows * length)
    factor = corpus_weight.astype(F32) / WEIGHT_UNIT * (total / (NCORP * counts))
    row_scale = jnp.sum(onehot * factor[None, :], axis=1)
    qk_gain = qk_gains.astype(F32)

    x_slots = gather_seq(tokens, n_seq)
    x_all = jnp.stack(x_slots, axis=1).reshape(rows * length, width).astype(F32)
    dy_all = jnp.stack(gather_seq(d_output, n_seq), axis=1)
    rel = me ^ jnp.arange(n_seq, dtype=jnp.int32)
    at = (rel[:, None] * span + jnp.arange(span, dtype=jnp.int32)[None, :]).reshape(length)
    pos = jnp.take(positions.reshape(rows, n_seq, span), rel, axis=1).reshape(rows, length)

    unit_one = x_all * inverse_rms(x_all)
    a_in = (unit_one * gains[0]).astype(BF)
    qkv = dot(a_in, w_qkv, 1, 0).astype(BF).reshape(rows, length, cols)
    q_f = qkv[..., :q_cols].reshape(rows, length, per, HEAD_SIZE).astype(F32)
    k_f = qkv[..., q_cols : q_cols + kv_cols].reshape(rows, length, held, HEAD_SIZE).astype(F32)
    v_h = qkv[..., q_cols + kv_cols :].reshape(rows, length, held, HEAD_SIZE)
    cosine, sine = rope_tables(pos)
    cosine, sine = cosine[:, :, None, :], sine[:, :, None, :]
    q_rot = rotate(q_f * inverse_rms(q_f) * qk_gain[0], cosine, sine).astype(BF)
    k_rot = rotate(k_f * inverse_rms(k_f) * qk_gain[1], cosine, sine).astype(BF)
    pick = (me * per + jnp.arange(per, dtype=jnp.int32)) // group - me * per // group
    k_rep = jnp.take(k_rot, pick, axis=2)
    v_rep = jnp.take(v_h, pick, axis=2)
    select = (pick[:, None] == jnp.arange(held, dtype=jnp.int32)[None, :]).astype(F32)
    visible = (at[None, :] <= at[:, None])[None] & (
        (at[:, None] - at[None, :])[None] <= pos[:, :, None]
    )
    raw = jnp.einsum("rqhd,rkhd->rhqk", q_rot, k_rep, preferred_element_type=F32) * scale_qk
    scores = jnp.where(visible[:, None], raw, NEG_FILL)
    top = jnp.max(scores, axis=-1, keepdims=True)
    expo = jnp.exp(scores - top)
    summed = jnp.sum(expo, axis=-1, keepdims=True)
    log_total = top + jnp.log(summed)
    o_mine = jnp.einsum(
        "rhqk,rkhd->rqhd", (expo / summed).astype(BF), v_rep, preferred_element_type=F32
    ).astype(BF)
    o_mine = o_mine.reshape(rows, n_seq, span, q_cols)

    o_got = gather_seq(o_mine, n_seq)
    o_cols = []
    for m in range(n_seq):
        o_cols.append(jnp.stack([o_got[m][:, m ^ j] for j in range(n_seq)], axis=1))
    o_all = jnp.concatenate(o_cols, axis=-1).reshape(rows * length, QUERY_HEADS * HEAD_SIZE)
    w_out = lax.all_gather(out_weight, ("rows", "seq"), axis=0, tiled=True)
    w_out = jnp.take(w_out.reshape(width, n_seq, q_cols), rel, axis=1).reshape(width, -1)
    h_all = x_all + dot(o_all, w_out, 1, 1)
    unit_two = h_all * inverse_rms(h_all)
    f_in = (unit_two * gains[1]).astype(BF)

    w_gu = lax.all_gather(gate_up_weight, "rows", axis=0, tiled=True)
    w_dn = lax.all_gather(down_weight, "rows", axis=0, tiled=True)
    w_g, w_u = w_gu[:, :width], w_gu[:, width:]
    gy = (
        (row_scale[:, None, None, None] * dy_all.astype(F32))
        .astype(BF)
        .reshape(rows * length, width)
    )
    gate = dot(f_in, w_g, 1, 1)
    upper = dot(f_in, w_u, 1, 1)
    sigma = jax.nn.sigmoid(gate)
    active = gate * sigma
    hidden = (active * upper).astype(BF)
    d_hidden = dot(gy, w_dn, 1, 1)
    d_upper = (d_hidden * active).astype(BF)
    d_gate = (d_hidden * upper * sigma * (1.0 + gate * (1.0 - sigma))).astype(BF)
    df_part = dot(d_gate, w_g, 1, 0) + dot(d_upper, w_u, 1, 0)
    d_gain_two = jnp.sum(df_part * unit_two, axis=0)
    df_slots = df_part.reshape(rows, n_seq, span, width)
    df = scatter_seq([df_slots[:, j] for j in range(n_seq)], n_seq).reshape(rows * span, width)
    y_slots = dot(hidden, w_dn, 1, 0).reshape(rows, n_seq, span, width)
    y = scatter_seq([y_slots[:, j] for j in range(n_seq)], n_seq)
    h_own = h_all.reshape(rows, n_seq, span, width)[:, 0]
    output = (h_own + y).astype(BF)
    ffn_grads = jnp.concatenate(
        [dot(d_gate, f_in, 0, 0), dot(d_upper, f_in, 0, 0), dot(hidden, gy, 0, 0)], axis=1
    ).astype(BF)
    ffn_sums = lax.psum_scatter(ffn_grads, "rows", scatter_dimension=0, tiled=True).astype(F32)

    h_one = h_own.reshape(rows * span, width)
    inverse = inverse_rms(h_one)
    unit = h_one * inverse
    scaled = df * gains[1]
    g_two = (row_scale[:, None, None] * d_output.astype(F32)).reshape(rows * span, width)
    d_h = g_two + inverse * (scaled - unit * jnp.mean(scaled * unit, axis=-1, keepdims=True))
    grad_att = d_h.astype(BF)
    o_own = o_all.reshape(rows, n_seq, span, -1)[:, 0].reshape(rows * span, -1)
    d_out_term = dot(grad_att, o_own, 0, 0).reshape(width, n_seq, q_cols)
    d_out_term = jnp.take(d_out_term, rel, axis=1).reshape(width, -1).astype(BF)
    d_out = lax.psum_scatter(
        d_out_term, ("rows", "seq"), scatter_dimension=0, tiled=True
    ).astype(F32)
    do_src = dot(grad_att, w_out, 1, 0).astype(BF).reshape(rows, span, n_seq, q_cols)
    do_slots = [do_src[:, :, 0]] + [
        swap(do_src[:, :, m], "seq", n_seq, m) for m in range(1, n_seq)
    ]
    d_o = jnp.stack(do_slots, axis=1).reshape(rows, length, per, HEAD_SIZE)

    probs = jnp.exp(scores - log_total)
    d_probs = jnp.einsum("rqhd,rkhd->rhqk", d_o, v_rep, preferred_element_type=F32)
    inner = jnp.sum(probs * d_probs, axis=-1, keepdims=True)
    d_scores = (probs * (d_probs - inner)).astype(BF)
    dq_rot = jnp.einsum("rhqk,rkhd->rqhd", d_scores, k_rep, preferred_element_type=F32) * scale_qk
    dk_rep = jnp.einsum("rhqk,rqhd->rkhd", d_scores, q_rot, preferred_element_type=F32) * scale_qk
    dv_rep = jnp.einsum("rhqk,rqhd->rkhd", probs.astype(BF), d_o, preferred_element_type=F32)
    high = lax.Precision.HIGHEST
    dk_held = jnp.einsum("rkhd,hj->rkjd", dk_rep, select, precision=high)
    dv_held = jnp.einsum("rkhd,hj->rkjd", dv_rep, select, precision=high)
    dq, d_query_gain = head_norm_back(q_f, qk_gain[0], rotate_back(dq_rot, cosine, sine))
    dk, d_key_gain = head_norm_back(k_f, qk_gain[1], rotate_back(dk_held, cosine, sine))
    d_qkv_act = jnp.concatenate(
        [
            dq.reshape(rows * length, q_cols),
            dk.reshape(rows * length, kv_cols),
            dv_held.reshape(rows * length, kv_cols),
        ],
        axis=-1,
    ).astype(BF)
    da_part = dot(d_qkv_act, w_qkv, 1, 1)
    d_gain_one = jnp.sum(da_part * unit_one, axis=0)
    da_slots = da_part.reshape(rows, n_seq, span, width)
    da = scatter_seq([da_slots[:, j] for j in range(n_seq)], n_seq).reshape(rows * span, width)
    x_own = tokens.astype(F32).reshape(rows * span, width)
    inverse = inverse_rms(x_own)
    unit = x_own * inverse
    scaled = da * gains[0]
    d_tokens = d_h + inverse * (scaled - unit * jnp.mean(scaled * unit, axis=-1, keepdims=True))
    d_tokens = d_tokens.reshape(rows, span, width)

    spread = 2 * HEAD_SIZE // local
    small = jnp.concatenate([d_query_gain, d_key_gain]).reshape(local, spread)
    tail = jnp.concatenate(
        [d_gain_one[:, None], d_gain_two[:, None], jnp.tile(small, (width // local, 1))], axis=1
    )
    d_w = jnp.concatenate(
        [dot(a_in, d_qkv_act, 0, 0), tail, jnp.zeros((width, extra - 2 - spread), F32)], axis=1
    ).astype(BF)
    d_w = lax.psum_scatter(d_w, "rows", scatter_dimension=0, tiled=True)
    d_w = lax.all_to_all(
        d_w.reshape(n_seq, local, cols + extra), "seq", split_axis=0, concat_axis=0, tiled=True
    ).astype(F32)
    k_sum = [jnp.zeros((local, HEAD_SIZE), F32) for _ in range(KEY_VALUE_HEADS)]
    v_sum = [jnp.zeros((local, HEAD_SIZE), F32) for _ in range(KEY_VALUE_HEADS)]
    for t in range(n_seq):
        for m in range(last[t] - lead[t] + 1):
            a = q_cols + m * HEAD_SIZE
            k_sum[lead[t] + m] += d_w[t, :, a : a + HEAD_SIZE]
            v_sum[lead[t] + m] += d_w[t, :, a + kv_cols : a + kv_cols + HEAD_SIZE]
    d_qkv = jnp.concatenate([d_w[t, :, :q_cols] for t in range(n_seq)] + k_sum + v_sum, axis=1)
    ends = jnp.sum(d_w[:, :, cols : cols + 2 + spread], axis=0)
    d_gains = ends[:, :2].T
    d_qk_gains = ends[:, 2:].reshape(2, HEAD_SIZE)
    return (
        output,
        d_tokens,
        d_qkv,
        d_out,
        d_gains,
        d_qk_gains,
        ffn_sums[:, : 2 * width],
        ffn_sums[:, 2 * width :],
    )


def solution(mesh):
    both = ("rows", "seq")
    acts = P("rows", "seq", None)
    return jax.shard_map(
        on_device,
        mesh=mesh,
        in_specs=(
            acts,
            acts,
            P("rows", None),
            P("rows", None),
            P(),
            P(both, None),
            P(both, None),
            P(None, both),
            P(),
            P(both, None),
            P(both, None),
        ),
        out_specs=(
            acts,
            acts,
            P(both, None),
            P(both, None),
            P(None, both),
            P(),
            P(both, None),
            P(both, None),
        ),
        check_vma=False,
    )
```

time: 2150 us -> 1130 us (0.53)
  waiting for transfers between devices: 1530 us -> 466 us
  blocking collectives: 100 us -> 10.7 us
  local copies, waits for them, and re-layouts: 92.4 us -> 174 us
  other arithmetic: 140 us -> 172 us
    unnamed x10 -> x8, waiting for transfers between devices: 1000 us -> 31.9 us
    ppermute x0 -> x21, waiting for transfers between devices: none -> 280 us  [swap(): return lax.ppermute(v, axis, [(i, i ^ bit) for i in range(n)])]
    reduce_scatter x2, waiting for transfers between devices: 321 us -> 151 us  [the longest x1 151 us: on_device(): lax.psum_scatter(ffn_grads, 'rows', scatter_dimension=0, tiled=True)]
    all_gather x4, waiting for transfers between devices: 140 us -> 0.03 us  [the longest x1 0.02 us: on_device(): lax.all_gather(mine.reshape(n_seq * local, cols + extra), 'rows', axis=0,...]
    psum x2 -> x0, blocking collectives: 62 us -> none  [the longest x1 38.8 us: on_device(): lax.psum(jnp.stack([d_query_gain, d_key_gain], axis=0), ('rows', 'seq'))]
    all_to_all x4 -> x1, waiting for transfers between devices: 61.6 us -> 2.77 us  [on_device(): lax.all_to_all(d_w.reshape(n_seq, local, cols + extra), 'seq', split_axis...]
    concatenate x5 -> x1, other arithmetic: 53.6 us -> 3.88 us  [on_device(): jnp.concatenate([dot(d_gate, f_in, 0, 0), dot(d_upper, f_in, 0, 0), dot(h...]
    convert_element_type x12 -> x15, other arithmetic: 40.7 us -> 89.2 us  [the longest x1 33.8 us: on_device(): d_scores = (probs * (d_probs - inner)).astype(BF)]
  transfers between devices with their start and end apart: 12 -> 29, of which waited for: 10 -> 12; matrix products, arithmetic and copies ran while one was open for 12% -> 32% of each run, Pallas kernels for 0% -> 0%
where the time goes in v1:
time: 1130 us; the launch traced here: 1120 us
  waiting for transfers between devices  466 us (41%)
  matrix products  272 us (24%)
  local copies, waits for them, and re-layouts  174 us (15%)
  other arithmetic  172 us (15%)
  between operations  16.2 us (1%)
  starting transfers between devices  13 us (1%)
    ppermute x21, waiting for transfers between devices, swap(): return lax.ppermute(v, axis, [(i, i ^ bit) for i in range(n)])  280 us
    dot_general x15, matrix products, dot(): lax.dot_general(a, b, (((ca,), (cb,)), ((), ())), preferred_element_type=...  163 us
    reduce_scatter x1, waiting for transfers between devices, on_device(): lax.psum_scatter(ffn_grads, 'rows', scatter_dimension=0, tiled=True)  151 us
    unnamed x216, local copies, waits for them, and re-layouts  40.5 us
    convert_element_type x1, other arithmetic, on_device(): d_scores = (probs * (d_probs - inner)).astype(BF)  33.8 us
    unnamed x8, waiting for transfers between devices  31.9 us
    dot_general x1, matrix products, on_device(): jnp.einsum('rqhd,rkhd->rhqk', d_o, v_rep, preferred_element_type=F32)  27.4 us
  transfers between devices with their start and end apart: 29, of which 12 were waited for; matrix products, arithmetic and copies ran while one was open for 32% of the time, Pallas kernels for 0%

profile of v1, /device:TPU:0, one launch (start us, length us, event | category | flops | bytes accessed | tf_op | source)
XLA Modules:
  0.0 1123.1 jit_solution(13181702221858504857)
XLA Ops:
  11.6 10.7 all_to_all.10
  28.1 45.4 %collective-permute-done.1 = bf16[2,256,2048]{2,1,0:T(8,128)(2,1)} collective-permute-done((bf16[2,256,2048]{2,1,0:T(8,128)(2,1)S(1)}, bf16[2,256,2048]{2,1,0:T(8,128)(2,1)}, u32[]{:S(2)}, u32[]{:S(2)}) %collective-permute-start.1) | collective-permute-done | bytes 2097184 | tf_op jit(solution)/shard_map/ppermute | solution.py:49
  80.1 42.9 %collective-permute-done.10 = bf16[2,256,2048]{2,1,0:T(8,128)(2,1)} collective-permute-done((bf16[2,256,2048]{2,1,0:T(8,128)(2,1)}, bf16[2,256,2048]{2,1,0:T(8,128)(2,1)}, u32[]{:S(2)}, u32[]{:S(2)}) %collective-permute-start.10) | collective-permute-done | bytes 2097184 | tf_op jit(solution)/shard_map/ppermute | solution.py:49
  123.1 4.1 maximum_convert_fusion
  127.1 4.8 multiply_reduce_fusion.4
  131.9 6.1 copy.371
  140.1 7.3 multiply_convert_fusion.2
  150.7 6.3 convolution_convert_fusion.4
  157.1 5.9 reshape.617
  175.5 19.4 %fusion.117 = (f32[2,5,1024]{2,1,0:T(8,128)S(1)}, f32[2,5,1024,1024]{2,3,1,0:T(8,128)}) fusion(bf16[2,1024,5,64]{1,3,2,0:T(8,128)(2,1)S(1)} %fusion.55, bf16[2,1024,5,64]{1,3,0,2:T(8,128)(2,1)} %get-tuple-element.178, pred[2,1024,1024]{1,2,0:T(8,128)(4,1)} %compare_and_fusion), kind=kOutput, calls=%fused_computation.261 | convolution fusion | flops 1373624320 | bytes 46702592 | tf_op jit(solution)/shard_map/rqhd,rkhd->rhqk/dot_general | solution.py:168
  194.9 16.5 %fusion = f32[2,5,1024]{2,1,0:T(8,128)S(1)} fusion(f32[2,5,1024,1024]{2,3,1,0:T(8,128)} %get-tuple-element.180, f32[2,5,1024]{2,1,0:T(8,128)S(1)} %get-tuple-element.179), kind=kLoop, calls=%fused_computation.11 | loop fusion | flops 20961280 | bytes 42024960 | tf_op jit(solution)/shard_map/reduce_sum | solution.py:172
  212.0 16.8 %fusion.70 = bf16[2,1024,5,64]{1,3,2,0:T(8,128)(2,1)} fusion(f32[2,5,1024,1024]{2,3,1,0:T(8,128)} %get-tuple-element.180, f32[2,5,1024]{2,1,0:T(8,128)S(1)} %fusion, f32[2,5,1024]{2,1,0:T(8,128)S(1)} %get-tuple-element.179, bf16[2,1024,5,64]{1,3,0,2:T(8,128)(2,1)S(1)} %copy-done.32), kind=kOutput, calls=%fused_computation.135 | convolution fusion | flops 1374289920 | bytes 44646400 | tf_op jit(solution)/shard_map/rhqk,rkhd->rqhd/dot_general | solution.py:174
  233.2 6.6 pad_maximum_fusion.1
  242.2 22.6 %collective-permute-done.4 = bf16[2,4,256,320]{2,3,1,0:T(8,128)(2,1)} collective-permute-done((bf16[2,4,256,320]{2,3,1,0:T(8,128)(2,1)}, bf16[2,4,256,320]{2,3,1,0:T(8,128)(2,1)}, u32[]{:S(2)}, u32[]{:S(2)}) %collective-permute-start.4) | collective-permute-done | bytes 1310752 | tf_op jit(solution)/shard_map/ppermute | solution.py:49
  264.9 8.2 fusion.6
  295.1 7.9 copy.404
  303.1 5.8 gather_fusion.1
  308.8 5.5 bitcast_select_fusion.1
  314.4 20.4 %multiply_reduce_fusion.3 = (f32[2048]{0:T(1024)S(1)}, f32[2048,2048]{1,0:T(8,128)}) fusion(bf16[2048,1280]{0,1:T(8,128)(2,1)} %bitcast_select_fusion.1, bf16[2048,320]{0,1:T(8,128)(2,1)} %concatenate.87, bf16[2048,320]{0,1:T(8,128)(2,1)} %concatenate.86, bf16[2048,320]{0,1:T(8,128)(2,1)S(1)} %copy-done.46, bf16[2048,320]{0,1:T(8,128)(2,1)S(1)} %bitcast.356, ...), kind=kOutput, calls=%fused_computation.23 | convolution fusion | flops 10770970624 | bytes 44048384 | tf_op jit(solution)/shard_map/dot_general | solution.py:24
  334.9 9.5 multiply_convert_fusion.1
  344.3 12.2 %fusion.57 = f32[2048,704]{0,1:T(8,128)} fusion(bf16[2048,2048]{1,0:T(8,128)(2,1)} %multiply_convert_fusion.1, bf16[704,4096]{1,0:T(8,128)(2,1)} %all-gather.9.cloned.1.call-done), kind=kOutput, calls=%fused_computation.113 | convolution fusion | flops 5905580032 | bytes 17039360 | tf_op jit(solution)/shard_map/dot_general | solution.py:24
  356.5 8.1 fusion.61
  364.6 15.2 %multiply_convert_fusion.3 = (bf16[2048,704]{0,1:T(8,128)(2,1)S(1)}, bf16[2048,704]{0,1:T(8,128)(2,1)S(1)}, bf16[2048,704]{0,1:T(8,128)(2,1)}) fusion(f32[2048,704]{0,1:T(8,128)} %fusion.61, f32[2048,704]{0,1:T(8,128)} %fusion.57, bf16[2048,2048]{1,0:T(8,128)(2,1)} %fusion.6, bf16[704,2048]{1,0:T(8,128)(2,1)} %all-gather.11.cloned.1.call-done), kind=kOutput, calls=%fused_computation.33 | convolution fusion | flops 5927206912 | bytes 31457280 | tf_op jit(solution)/shard_map/dot_general | solution.py:24
  379.8 14.1 %fusion.59 = f32[2048,2048]{1,0:T(8,128)} fusion(bf16[2048,704]{0,1:T(8,128)(2,1)S(1)} %get-tuple-element.107, bf16[704,4096]{1,0:T(8,128)(2,1)} %all-gather.9.cloned.1.call-done), kind=kOutput, calls=%fused_computation.115 | convolution fusion | flops 5905580032 | bytes 22544384 | tf_op jit(solution)/shard_map/dot_general | solution.py:24
  393.9 18.8 %multiply_reduce_fusion.1 = (bf16[2048]{0:T(1024)(128)(2,1)S(1)}, f32[2048,2048]{1,0:T(8,128)}) fusion(f32[2048,2048]{1,0:T(8,128)} %get-tuple-element.182, f32[2048]{0:T(1024)S(1)} %add_rsqrt_fusion.2, f32[2048,2048]{1,0:T(8,128)} %fusion.59, bf16[2048,704]{0,1:T(8,128)(2,1)S(1)} %get-tuple-element.106, bf16[704,4096]{1,0:T(8,128)(2,1)} %all-gather.9.cloned.1.call-done), kind=kOutput, calls=%fused_computation.20 | convolution fusion | flops 5922355200 | bytes 56111104 | tf_op jit(solution)/shard_map/dot_general | solution.py:24
  412.7 5.6 slice_bitcast_fusion.9
  418.8 10.8 fusion.118
  429.5 6.3 slice_bitcast_fusion.11
  436.4 3.7 fusion.29
  440.4 4.3 fusion.34
  451.8 37.1 %collective-permute-done.14 = bf16[2,256,2048]{2,1,0:T(8,128)(2,1)} collective-permute-done((bf16[2,256,2048]{2,1,0:T(8,128)(2,1)}, bf16[2,256,2048]{2,1,0:T(8,128)(2,1)}, u32[]{:S(2)}, u32[]{:S(2)}) %collective-permute-start.14) | collective-permute-done | bytes 2097184 | tf_op jit(solution)/shard_map/ppermute | solution.py:49
  488.8 3.6 multiply_reduce_fusion.5
  492.5 40.4 %collective-permute-done.8 = bf16[2,256,2048]{2,1,0:T(8,128)(2,1)} collective-permute-done((bf16[2,256,2048]{2,1,0:T(8,128)(2,1)}, bf16[2,256,2048]{2,1,0:T(8,128)(2,1)}, u32[]{:S(2)}, u32[]{:S(2)}) %collective-permute-start.8) | collective-permute-done | bytes 2097184 | tf_op jit(solution)/shard_map/ppermute | solution.py:49
  532.9 8.5 fusion.103
  542.7 6.5 convolution_convert_fusion.5
  572.2 6.2 collective-permute-done.17
  579.2 3.7 pad_maximum_fusion.5
  587.8 27.4 %multiply_reduce_fusion = (f32[2,5,1024]{2,1,0:T(8,128)S(1)}, f32[2,5,1024,1024]{2,3,1,0:T(8,128)}) fusion(f32[2,5,1024,1024]{2,3,1,0:T(8,128)} %get-tuple-element.180, f32[2,5,1024]{2,1,0:T(8,128)S(1)} %log_add_fusion, bf16[2,1024,5,64]{1,3,2,0:T(8,128)(2,1)S(1)} %reshape.626, bf16[2,1024,5,64]{1,3,0,2:T(8,128)(2,1)} %get-tuple-element.177), kind=kOutput, calls=%fused_computation.6 | convolution fusion | flops 1373624320 | bytes 86589440 | tf_op jit(solution)/shard_map/rqhd,rkhd->rhqk/dot_general | solution.py:239
  615.1 16.5 %fusion.66 = f32[2,1024,5,64]{1,3,2,0:T(8,128)} fusion(bf16[2,1024,5,64]{1,3,2,0:T(8,128)(2,1)S(1)} %reshape.626, f32[2,5,1024,1024]{2,3,1,0:T(8,128)} %get-tuple-element.180, f32[2,5,1024]{2,1,0:T(8,128)S(1)} %log_add_fusion), kind=kOutput, calls=%fused_computation.130 | convolution fusion | flops 1363148800 | bytes 45916160 | tf_op jit(solution)/shard_map/rhqk,rqhd->rkhd/dot_general | solution.py:244
  631.6 33.8 %multiply_convert_fusion = bf16[2,5,1024,1024]{2,3,1,0:T(8,128)(2,1)} fusion(f32[2,5,1024,1024]{2,3,1,0:T(8,128)} %get-tuple-element.184, f32[2,5,1024,1024]{2,3,1,0:T(8,128)} %get-tuple-element.180, f32[2,5,1024]{2,1,0:T(8,128)S(1)} %get-tuple-element.183, f32[2,5,1024]{2,1,0:T(8,128)S(1)} %log_add_fusion), kind=kLoop, calls=%fused_computation.5 | loop fusion | flops 41943040 | bytes 104939520 | tf_op jit(solution)/shard_map/convert_element_type | solution.py:241
  665.4 10.6 multiply_bitcast_fusion
  682.3 9.2 bitcast_multiply_fusion.3
  696.4 5.2 fusion.74
  707.2 6.4 convolution_convert_fusion.3
  713.6 14.3 %multiply_reduce_fusion.2 = (bf16[2048]{0:T(1024)(128)(2,1)S(1)}, f32[2048,2048]{1,0:T(8,128)}) fusion(f32[2,4,256,2048]{3,2,1,0:T(8,128)} %copy.371, f32[2048]{0:T(1024)S(1)} %bitcast.370, bf16[2048,576]{0,1:T(8,128)(2,1)S(1)} %constant_dynamic-update-slice_fusion, bf16[2048,640]{0,1:T(8,128)(2,1)S(1)} %copy-done.38), kind=kOutput, calls=%fused_computation.21 | convolution fusion | flops 4844419072 | bytes 38285312 | tf_op jit(solution)/shard_map/dot_general | solution.py:24
  727.9 13.5 %concatenate.95 = bf16[2048,640]{0,1:T(8,128)(2,1)} concatenate(bf16[2048,576]{0,1:T(8,128)(2,1)} %convolution_convert_fusion.3, bf16[2048,1]{0,1:T(2,128)(2,1)S(1)} %broadcast_in_dim.117, bf16[2048,1]{0,1:T(2,128)(2,1)S(1)} %broadcast_in_dim.118, bf16[2048,2]{0,1:T(2,128)(2,1)S(1)} %tile.10, bf16[2048,60]{0,1:T(8,128)(2,1)S(1)} %broadcast_in_dim.119), dimensions={1} | concatenate | bytes 5242880 | tf_op jit(solution)/shard_map/concatenate | solution.py:274
  741.5 3.7 copy.435
  745.2 9.7 concatenate.97
  757.9 5.9 fusion.119
  763.8 5.9 gather_fusion.2
  769.7 5.7 fusion.7
  775.5 7.9 copy.446
  785.3 9.0 convolution_convert_fusion.1
  794.3 8.7 convolution_convert_fusion.2
  803.1 6.4 convolution_convert_fusion
  809.4 3.9 pad_maximum_fusion
  813.3 4.1 slice_bitcast_fusion.7
  818.0 3.6 collective-permute-done.19
  825.6 79.8 %collective-permute-done.20 = bf16[2,256,2048]{2,1,0:T(8,128)(2,1)S(1)} collective-permute-done((bf16[2,256,2048]{2,1,0:T(8,128)(2,1)S(1)}, bf16[2,256,2048]{2,1,0:T(8,128)(2,1)S(1)}, u32[]{:S(2)}, u32[]{:S(2)}) %collective-permute-start.20) | collective-permute-done | bytes 2097184 | tf_op jit(solution)/shard_map/ppermute | solution.py:49
  905.4 4.4 fusion.18
  911.8 3.7 all-to-all-start.1
  915.5 7.1 fusion.21
  928.0 30.4 %reduce-scatter.10.cloned.1.call-done = bf16[64,1280]{1,0:T(8,128)(2,1)} async-done(((bf16[2048,1280]{1,0:T(8,128)(2,1)}), bf16[64,1280]{1,0:T(8,128)(2,1)}) %reduce-scatter.10.cloned.1.call-update) | async-done | bytes 163856
  960.5 151.1 %reduce-scatter.8.cloned.1.call-done = bf16[88,6144]{1,0:T(8,128)(2,1)} async-done(((bf16[704,6144]{1,0:T(8,128)(2,1)}), bf16[88,6144]{1,0:T(8,128)(2,1)}) %reduce-scatter.8.cloned.1.call-update) | async-done | bytes 1081360 | tf_op jit(solution)/shard_map/reduce_scatter | solution.py:217
  (397 shorter events, 141.3 us)
Async XLA Ops:
  7.2 20.2 %copy-start = (s32[2,1024]{1,0:T(2,128)S(1)}, s32[2,1024]{1,0:T(2,128)}, u32[]{:S(2)}) copy-start(s32[2,1024]{1,0:T(2,128)} %param.23) | copy-start | bytes 24580
  7.2 17.6 %copy-start.2 = (bf16[2,256,2048]{2,1,0:T(8,128)(2,1)S(1)}, bf16[2,256,2048]{2,1,0:T(8,128)(2,1)}, u32[]{:S(2)}) copy-start(bf16[2,256,2048]{2,1,0:T(8,128)(2,1)} %param.21) | copy-start | bytes 6291460
  7.2 66.3 %copy-start.76 = (bf16[2,64]{1,0:T(2,128)(2,1)S(1)}, bf16[2,64]{1,0:T(2,128)(2,1)}, u32[]{:S(2)}) copy-start(bf16[2,64]{1,0:T(2,128)(2,1)} %param.29) | copy-start | bytes 772
  7.2 130.9 %all-gather.5.cloned.1.call-start = ((), (), s32[]{:S(2)}) async-start(), calls=%async_computation.5 | async-start | bytes 2949120 | tf_op jit(solution)/shard_map/all_gather | solution.py:130
  23.3 271.9 %all-gather.7.cloned.1.call-start = ((), (), s32[]{:S(2)}) async-start(), calls=%async_computation.6 | async-start | bytes 5406720 | tf_op jit(solution)/shard_map/all_gather | solution.py:184
  24.0 320.3 %all-gather.9.cloned.1.call-start = ((), (), s32[]{:S(2)}) async-start(), calls=%async_computation.7 | async-start | bytes 6488064 | tf_op jit(solution)/shard_map/all_gather | solution.py:190
  24.7 339.8 %all-gather.11.cloned.1.call-start = ((), (), s32[]{:S(2)}) async-start(), calls=%async_computation.8 | async-start | bytes 3244032 | tf_op jit(solution)/shard_map/all_gather | solution.py:191
  24.8 48.7 %collective-permute-start.1 = (bf16[2,256,2048]{2,1,0:T(8,128)(2,1)S(1)}, bf16[2,256,2048]{2,1,0:T(8,128)(2,1)}, u32[]{:S(2)}, u32[]{:S(2)}) collective-permute-start(bf16[2,256,2048]{2,1,0:T(8,128)(2,1)S(1)} %copy-done.2), channel_id=1, source_target_pairs={{0,2},{1,3},{2,0},{3,1},{4,6},{5,7},{6,4},{7,5},{8,10},{9,11},{10,... | collective-permute-start | bytes 6291464 | tf_op jit(solution)/shard_map/ppermute | solution.py:49
  25.2 97.8 %collective-permute-start = (bf16[2,256,2048]{2,1,0:T(8,128)(2,1)S(1)}, bf16[2,256,2048]{2,1,0:T(8,128)(2,1)}, u32[]{:S(2)}, u32[]{:S(2)}) collective-permute-start(bf16[2,256,2048]{2,1,0:T(8,128)(2,1)S(1)} %copy-done.2), channel_id=1, source_target_pairs={{0,1},{1,0},{2,3},{3,2},{4,5},{5,4},{6,7},{7,6},{8,9},{9,8},{10,11... | collective-permute-start | bytes 6291464 | tf_op jit(solution)/shard_map/ppermute | solution.py:49
  25.2 97.8 %collective-permute-start.10 = (bf16[2,256,2048]{2,1,0:T(8,128)(2,1)}, bf16[2,256,2048]{2,1,0:T(8,128)(2,1)}, u32[]{:S(2)}, u32[]{:S(2)}) collective-permute-start(bf16[2,256,2048]{2,1,0:T(8,128)(2,1)} %param.22), channel_id=1, source_target_pairs={{0,2},{1,3},{2,0},{3,1},{4,6},{5,7},{6,4},{7,5},{8,10},{9,11},{10,... | collective-permute-start | bytes 6291464 | tf_op jit(solution)/shard_map/ppermute | solution.py:49
  26.9 206.3 %collective-permute-start.9 = (bf16[2,256,2048]{2,1,0:T(8,128)(2,1)}, bf16[2,256,2048]{2,1,0:T(8,128)(2,1)}, u32[]{:S(2)}, u32[]{:S(2)}) collective-permute-start(bf16[2,256,2048]{2,1,0:T(8,128)(2,1)} %param.22), channel_id=1, source_target_pairs={{0,1},{1,0},{2,3},{3,2},{4,5},{5,4},{6,7},{7,6},{8,9},{9,8},{10,11... | collective-permute-start | bytes 6291464 | tf_op jit(solution)/shard_map/ppermute | solution.py:49
  27.1 882.8 %reduce-scatter.6.cloned.1.call-start = ((), (), s32[]{:S(2)}) async-start(), calls=%async_computation.9 | async-start | bytes 2949120 | tf_op jit(solution)/shard_map/reduce_scatter | solution.py:277
  27.2 48.0 %copy-start.73 = (pred[4]{0:T(512)(128)(4,1)}, pred[4]{0:T(512)(128)(4,1)S(1)}, u32[]{:S(2)}) copy-start(pred[4]{0:T(512)(128)(4,1)S(1)} %compare_and_fusion.2) | copy-start | bytes 16
  27.3 46.9 %copy-start.68 = (s32[1024]{0:T(1024)}, s32[1024]{0:T(1024)S(1)}, u32[]{:S(2)}) copy-start(s32[1024]{0:T(1024)S(1)} %pad_clamp_fusion) | copy-start | bytes 12292
  28.0 45.5 %copy-start.69 = (s32[5]{0:T(128)}, s32[5]{0:T(128)S(1)}, u32[]{:S(2)}) copy-start(s32[5]{0:T(128)S(1)} %get-tuple-element.102) | copy-start | bytes 64
  73.5 49.6 %collective-permute-start.2 = (bf16[2,256,2048]{2,1,0:T(8,128)(2,1)}, bf16[2,256,2048]{2,1,0:T(8,128)(2,1)}, u32[]{:S(2)}, u32[]{:S(2)}) collective-permute-start(bf16[2,256,2048]{2,1,0:T(8,128)(2,1)} %collective-permute-done.1), channel_id=1, source_target_pairs={{0,1},{1,0},{2,3},{3,2},{4,5},{5,4},{6,7},{7,6},{8,9},{9,8},{10,11... | collective-permute-start | bytes 6291464 | tf_op jit(solution)/shard_map/ppermute | solution.py:49
  76.6 95.7 %copy-start.19 = (f32[2,1024,64]{1,2,0:T(8,128)}, f32[2,1024,64]{1,2,0:T(8,128)S(1)}, u32[]{:S(2)}) copy-start(f32[2,1024,64]{1,2,0:T(8,128)S(1)} %get-tuple-element.191) | copy-start | bytes 1572868
  76.6 89.9 %copy-start.66 = (f32[64]{0:T(128)}, f32[64]{0:T(128)S(1)}, u32[]{:S(2)}) copy-start(f32[64]{0:T(128)S(1)} %get-tuple-element.175) | copy-start | bytes 772
  76.6 95.7 %copy-start.64 = (f32[64]{0:T(128)}, f32[64]{0:T(128)S(1)}, u32[]{:S(2)}) copy-start(f32[64]{0:T(128)S(1)} %get-tuple-element.176) | copy-start | bytes 772
  123.0 110.1 %collective-permute-start.11 = (bf16[2,256,2048]{2,1,0:T(8,128)(2,1)}, bf16[2,256,2048]{2,1,0:T(8,128)(2,1)}, u32[]{:S(2)}, u32[]{:S(2)}) collective-permute-start(bf16[2,256,2048]{2,1,0:T(8,128)(2,1)} %collective-permute-done.10), channel_id=1, source_target_pairs={{0,1},{1,0},{2,3},{3,2},{4,5},{5,4},{6,7},{7,6},{8,9},{9,8},{10,11... | collective-permute-start | bytes 6291464 | tf_op jit(solution)/shard_map/ppermute | solution.py:49
  173.6 21.3 %copy-start.8 = (bf16[2,1024,5,64]{1,3,2,0:T(8,128)(2,1)}, bf16[2,1024,5,64]{1,3,2,0:T(8,128)(2,1)S(1)}, u32[]{:S(2)}) copy-start(bf16[2,1024,5,64]{1,3,2,0:T(8,128)(2,1)S(1)} %fusion.55) | copy-start | bytes 3932164
  194.9 16.5 %copy-start.47 = (f32[2,5,1024]{2,1,0:T(8,128)}, f32[2,5,1024]{2,1,0:T(8,128)S(1)}, u32[]{:S(2)}) copy-start(f32[2,5,1024]{2,1,0:T(8,128)S(1)} %get-tuple-element.179) | copy-start | bytes 122884
  194.9 17.1 %copy-start.32 = (bf16[2,1024,5,64]{1,3,0,2:T(8,128)(2,1)S(1)}, bf16[2,1024,5,64]{1,3,0,2:T(8,128)(2,1)}, u32[]{:S(2)}) copy-start(bf16[2,1024,5,64]{1,3,0,2:T(8,128)(2,1)} %get-tuple-element.177) | copy-start | bytes 3932164
  233.2 31.7 %collective-permute-start.4 = (bf16[2,4,256,320]{2,3,1,0:T(8,128)(2,1)}, bf16[2,4,256,320]{2,3,1,0:T(8,128)(2,1)}, u32[]{:S(2)}, u32[]{:S(2)}) collective-permute-start(bf16[2,4,256,320]{2,3,1,0:T(8,128)(2,1)} %copy.389), channel_id=1, source_target_pairs={{0,2},{1,3},{2,0},{3,1},{4,6},{5,7},{6,4},{7,5},{8,10},{9,11},{10,... | collective-permute-start | bytes 3932168 | tf_op jit(solution)/shard_map/ppermute | solution.py:49
  239.9 36.0 %collective-permute-start.3 = (bf16[2,4,256,320]{2,3,1,0:T(8,128)(2,1)}, bf16[2,4,256,320]{2,3,1,0:T(8,128)(2,1)S(1)}, u32[]{:S(2)}, u32[]{:S(2)}) collective-permute-start(bf16[2,4,256,320]{2,3,1,0:T(8,128)(2,1)} %copy.389), channel_id=1, source_target_pairs={{0,1},{1,0},{2,3},{3,2},{4,5},{5,4},{6,7},{7,6},{8,9},{9,8},{10,11... | collective-permute-start | bytes 3932168 | tf_op jit(solution)/shard_map/ppermute | solution.py:49
  264.9 24.0 %collective-permute-start.5 = (bf16[2,4,256,320]{2,3,1,0:T(8,128)(2,1)}, bf16[2,4,256,320]{2,3,1,0:T(8,128)(2,1)}, u32[]{:S(2)}, u32[]{:S(2)}) collective-permute-start(bf16[2,4,256,320]{2,3,1,0:T(8,128)(2,1)} %collective-permute-done.4), channel_id=1, source_target_pairs={{0,1},{1,0},{2,3},{3,2},{4,5},{5,4},{6,7},{7,6},{8,9},{9,8},{10,11... | collective-permute-start | bytes 3932168 | tf_op jit(solution)/shard_map/ppermute | solution.py:49
  291.5 11.6 %copy-start.16 = (bf16[2,4,256,320]{3,2,0,1:T(8,128)(2,1)}, bf16[2,4,256,320]{3,2,0,1:T(8,128)(2,1)S(1)}, u32[]{:S(2)}) copy-start(bf16[2,4,256,320]{3,2,0,1:T(8,128)(2,1)S(1)} %pad_maximum_fusion.4) | copy-start | bytes 3932164
  314.4 20.5 %copy-start.59 = (f32[1,2048]{1,0:T(1,128)S(1)}, f32[1,2048]{1,0:T(1,128)}, u32[]{:S(2)}) copy-start(f32[1,2048]{1,0:T(1,128)} %get-tuple-element.171) | copy-start | bytes 24580
  344.3 12.2 %copy-start.27 = (bf16[2048,2048]{1,0:T(8,128)(2,1)S(1)}, bf16[2048,2048]{1,0:T(8,128)(2,1)}, u32[]{:S(2)}) copy-start(bf16[2048,2048]{1,0:T(8,128)(2,1)} %multiply_convert_fusion.1) | copy-start | bytes 25165828
  344.3 12.2 %copy-start.44 = (bf16[704,4096]{1,0:T(8,128)(2,1)S(1)}, bf16[704,4096]{1,0:T(8,128)(2,1)}, u32[]{:S(2)}) copy-start(bf16[704,4096]{1,0:T(8,128)(2,1)} %all-gather.9.cloned.1.call-done) | copy-start | bytes 17301508
  379.8 14.1 %copy-start.81 = (bf16[2048,704]{0,1:T(8,128)(2,1)}, bf16[2048,704]{0,1:T(8,128)(2,1)S(1)}, u32[]{:S(2)}) copy-start(bf16[2048,704]{0,1:T(8,128)(2,1)S(1)} %get-tuple-element.107) | copy-start | bytes 8650756
  379.8 14.1 %copy-start.30 = (bf16[2048,704]{0,1:T(8,128)(2,1)}, bf16[2048,704]{0,1:T(8,128)(2,1)S(1)}, u32[]{:S(2)}) copy-start(bf16[2048,704]{0,1:T(8,128)(2,1)S(1)} %get-tuple-element.106) | copy-start | bytes 8650756
  418.2 18.1 %collective-permute-start.13 = (bf16[2,256,2048]{2,1,0:T(8,128)(2,1)S(1)}, bf16[2,256,2048]{2,1,0:T(8,128)(2,1)}, u32[]{:S(2)}, u32[]{:S(2)}) collective-permute-start(bf16[2,256,2048]{2,1,0:T(8,128)(2,1)S(1)} %get-tuple-element.112), channel_id=1, source_target_pairs={{0,1},{1,0},{2,3},{3,2},{4,5},{5,4},{6,7},{7,6},{8,9},{9,8},{10,11... | collective-permute-start | bytes 6291464 | tf_op jit(solution)/shard_map/ppermute | solution.py:49
  418.7 17.6 %slice-start = ((s8[16777216]{0:T(1024)(128)(4,1)}), s8[4194304]{0:T(1024)(128)(4,1)S(1)}, s32[]{:S(2)}) async-start(s8[16777216]{0:T(1024)(128)(4,1)} %bitcast.318), calls=%async_computation.12 | async-start | bytes 8388608
  418.7 17.6 %slice-start.1 = ((s8[16777216]{0:T(1024)(128)(4,1)}), s8[4194304]{0:T(1024)(128)(4,1)S(1)}, s32[]{:S(2)}) async-start(s8[16777216]{0:T(1024)(128)(4,1)} %bitcast.318), calls=%async_computation.13 | async-start | bytes 8388608
  418.7 17.6 %slice-start.2 = ((s8[16777216]{0:T(1024)(128)(4,1)}), s8[4194304]{0:T(1024)(128)(4,1)S(1)}, s32[]{:S(2)}) async-start(s8[16777216]{0:T(1024)(128)(4,1)} %bitcast.318), calls=%async_computation.14 | async-start | bytes 8388608
  418.7 17.6 %slice-start.3 = ((s8[16777216]{0:T(1024)(128)(4,1)}), s8[4194304]{0:T(1024)(128)(4,1)S(1)}, s32[]{:S(2)}) async-start(s8[16777216]{0:T(1024)(128)(4,1)} %bitcast.318), calls=%async_computation.15 | async-start | bytes 8388608
  429.5 19.4 %slice-start.4 = ((s8[5242880]{0:T(1024)(128)(4,1)}), s8[4194304]{0:T(1024)(128)(4,1)S(1)}, s32[]{:S(2)}) async-start(s8[5242880]{0:T(1024)(128)(4,1)} %bitcast.325), calls=%async_computation.16 | async-start | bytes 8388608
  435.8 4.6 collective-permute-start.7
  435.8 13.1 %slice-start.5 = ((s8[5242880]{0:T(1024)(128)(4,1)}), s8[1048576]{0:T(1024)(128)(4,1)S(1)}, s32[]{:S(2)}) async-start(s8[5242880]{0:T(1024)(128)(4,1)} %bitcast.325), calls=%async_computation.17 | async-start | bytes 2097152
  435.8 15.9 %collective-permute-start.12 = (bf16[2,256,2048]{2,1,0:T(8,128)(2,1)}, bf16[2,256,2048]{2,1,0:T(8,128)(2,1)S(1)}, u32[]{:S(2)}, u32[]{:S(2)}) collective-permute-start(bf16[2,256,2048]{2,1,0:T(8,128)(2,1)} %get-tuple-element.111), channel_id=1, source_target_pairs={{0,1},{1,0},{2,3},{3,2},{4,5},{5,4},{6,7},{7,6},{8,9},{9,8},{10,11... | collective-permute-start | bytes 6291464 | tf_op jit(solution)/shard_map/ppermute | solution.py:49
  440.0 48.8 %collective-permute-start.14 = (bf16[2,256,2048]{2,1,0:T(8,128)(2,1)}, bf16[2,256,2048]{2,1,0:T(8,128)(2,1)}, u32[]{:S(2)}, u32[]{:S(2)}) collective-permute-start(bf16[2,256,2048]{2,1,0:T(8,128)(2,1)} %fusion.29), channel_id=1, source_target_pairs={{0,2},{1,3},{2,0},{3,1},{4,6},{5,7},{6,4},{7,5},{8,10},{9,11},{10,... | collective-permute-start | bytes 6291464 | tf_op jit(solution)/shard_map/ppermute | solution.py:49
  440.4 52.1 %collective-permute-start.6 = (bf16[2,256,2048]{2,1,0:T(8,128)(2,1)}, bf16[2,256,2048]{2,1,0:T(8,128)(2,1)}, u32[]{:S(2)}, u32[]{:S(2)}) collective-permute-start(bf16[2,256,2048]{2,1,0:T(8,128)(2,1)} %get-tuple-element.113), channel_id=1, source_target_pairs={{0,1},{1,0},{2,3},{3,2},{4,5},{5,4},{6,7},{7,6},{8,9},{9,8},{10,11... | collective-permute-start | bytes 6291464 | tf_op jit(solution)/shard_map/ppermute | solution.py:49
  444.7 88.3 %collective-permute-start.8 = (bf16[2,256,2048]{2,1,0:T(8,128)(2,1)}, bf16[2,256,2048]{2,1,0:T(8,128)(2,1)}, u32[]{:S(2)}, u32[]{:S(2)}) collective-permute-start(bf16[2,256,2048]{2,1,0:T(8,128)(2,1)} %fusion.34), channel_id=1, source_target_pairs={{0,2},{1,3},{2,0},{3,1},{4,6},{5,7},{6,4},{7,5},{8,10},{9,11},{10,... | collective-permute-start | bytes 6291464 | tf_op jit(solution)/shard_map/ppermute | solution.py:49
  488.8 44.1 %copy-start.29 = (bf16[2,256,2048]{2,1,0:T(8,128)(2,1)S(1)}, bf16[2,256,2048]{2,1,0:T(8,128)(2,1)}, u32[]{:S(2)}) copy-start(bf16[2,256,2048]{2,1,0:T(8,128)(2,1)} %param.22) | copy-start | bytes 6291460
  488.8 44.1 %copy-start.72 = (f32[2]{0:T(128)S(1)}, f32[2]{0:T(128)}, u32[]{:S(2)}) copy-start(f32[2]{0:T(128)} %copy-done.71) | copy-start | bytes 28
  552.7 13.6 %copy-start.5 = (f32[2,1024,128]{1,0,2:T(2,128)S(1)}, f32[2,1024,128]{1,0,2:T(2,128)}, u32[]{:S(2)}) copy-start(f32[2,1024,128]{1,0,2:T(2,128)} %copy-done.4) | copy-start | bytes 3145732
  556.1 11.5 %copy-start.55 = (f32[2,5,1024]{2,1,0:T(8,128)S(1)}, f32[2,5,1024]{2,1,0:T(8,128)}, u32[]{:S(2)}) copy-start(f32[2,5,1024]{2,1,0:T(8,128)} %copy-done.54) | copy-start | bytes 122884
  558.5 11.5 %collective-permute-start.15 = (bf16[2,256,320]{1,0,2:T(2,128)(2,1)S(1)}, bf16[2,256,320]{1,0,2:T(2,128)(2,1)S(1)}, u32[]{:S(2)}, u32[]{:S(2)}) collective-permute-start(bf16[2,256,320]{1,0,2:T(2,128)(2,1)S(1)} %bitcast.367), channel_id=1, source_target_pairs={{0,1},{1,0},{2,3},{3,2},{4,5},{5,4},{6,7},{7,6},{8,9},{9,8},{10,11... | collective-permute-start | bytes 983048 | tf_op jit(solution)/shard_map/ppermute | solution.py:49
  561.5 10.7 collective-permute-start.16
  564.9 13.6 %collective-permute-start.17 = (bf16[2,256,320]{1,0,2:T(2,128)(2,1)}, bf16[2,256,320]{1,0,2:T(2,128)(2,1)S(1)}, u32[]{:S(2)}, u32[]{:S(2)}) collective-permute-start(bf16[2,256,320]{1,0,2:T(2,128)(2,1)} %bitcast.368), channel_id=1, source_target_pairs={{0,3},{1,2},{2,1},{3,0},{4,7},{5,6},{6,5},{7,4},{8,11},{9,10},{10,... | collective-permute-start | bytes 983048 | tf_op jit(solution)/shard_map/ppermute | solution.py:49
  631.6 33.8 %copy-start.9 = (bf16[2,1024,5,64]{1,3,2,0:T(8,128)(2,1)S(1)}, bf16[2,1024,5,64]{1,3,2,0:T(8,128)(2,1)}, u32[]{:S(2)}) copy-start(bf16[2,1024,5,64]{1,3,2,0:T(8,128)(2,1)} %copy-done.8) | copy-start | bytes 3932164
  727.9 17.3 %copy-start.13 = (bf16[2,4,256,320]{3,2,0,1:T(8,128)(2,1)S(1)}, bf16[2,4,256,320]{3,2,0,1:T(8,128)(2,1)}, u32[]{:S(2)}) copy-start(bf16[2,4,256,320]{3,2,0,1:T(8,128)(2,1)} %copy-done.12) | copy-start | bytes 3932164
  727.9 17.3 %copy-start.15 = (bf16[2,4,256,320]{3,2,0,1:T(8,128)(2,1)S(1)}, bf16[2,4,256,320]{3,2,0,1:T(8,128)(2,1)}, u32[]{:S(2)}) copy-start(bf16[2,4,256,320]{3,2,0,1:T(8,128)(2,1)} %copy-done.14) | copy-start | bytes 3932164
  741.4 217.0 %reduce-scatter.10.cloned.1.call-start = ((), (), s32[]{:S(2)}) async-start(), calls=%async_computation.11 | async-start | bytes 5406720
  783.4 328.1 %reduce-scatter.8.cloned.1.call-start = ((), (), s32[]{:S(2)}) async-start(), calls=%async_computation.10 | async-start | bytes 9732096 | tf_op jit(solution)/shard_map/reduce_scatter | solution.py:217
  785.3 17.8 %slice-start.6 = ((s8[8388608]{0:T(1024)(128)(4,1)}), s8[4194304]{0:T(1024)(128)(4,1)S(1)}, s32[]{:S(2)}) async-start(s8[8388608]{0:T(1024)(128)(4,1)} %bitcast.339), calls=%async_computation.18 | async-start | bytes 8388608
  817.5 4.2 collective-permute-start.19
  817.6 87.9 %copy-start.61 = (f32[1,2048]{1,0:T(1,128)S(1)}, f32[1,2048]{1,0:T(1,128)}, u32[]{:S(2)}) copy-start(f32[1,2048]{1,0:T(1,128)} %copy-done.60) | copy-start | bytes 24580
  817.6 8.0 collective-permute-start.18
  824.6 80.8 %collective-permute-start.20 = (bf16[2,256,2048]{2,1,0:T(8,128)(2,1)S(1)}, bf16[2,256,2048]{2,1,0:T(8,128)(2,1)S(1)}, u32[]{:S(2)}, u32[]{:S(2)}) collective-permute-start(bf16[2,256,2048]{2,1,0:T(8,128)(2,1)S(1)} %fusion.24), channel_id=1, source_target_pairs={{0,2},{1,3},{2,0},{3,1},{4,6},{5,7},{6,4},{7,5},{8,10},{9,11},{10,... | collective-permute-start | bytes 6291464 | tf_op jit(solution)/shard_map/ppermute | solution.py:49
  825.6 84.3 %copy-start.24 = (bf16[2,256,2048]{2,1,0:T(8,128)(2,1)}, bf16[2,256,2048]{2,1,0:T(8,128)(2,1)S(1)}, u32[]{:S(2)}) copy-start(bf16[2,256,2048]{2,1,0:T(8,128)(2,1)S(1)} %collective-permute-done.18) | copy-start | bytes 6291460
  911.8 13.6 %all-to-all-start.1 = ((bf16[4,64,640]{2,1,0:T(8,128)(2,1)}), bf16[4,64,640]{2,1,0:T(8,128)(2,1)S(1)}, u32[]{:S(2)}, u32[]{:S(2)}) async-start(bf16[4,64,640]{2,1,0:T(8,128)(2,1)} %bitcast.73), calls=%async_computation.2 | async-start | bytes 655360 | tf_op jit(solution)/shard_map/all_to_all | solution.py:278
  926.2 189.5 %copy-start.1 = (s32[2,1024]{1,0:T(2,128)S(1)}, s32[2,1024]{1,0:T(2,128)}, u32[]{:S(2)}) copy-start(s32[2,1024]{1,0:T(2,128)} %param.23) | copy-start | bytes 24580
  (58 other events, 264.0 us)
Sparse Core Ops, SparseCore 0:
  23.4 57.1 all-gather.4
  83.5 68.1 all-gather.6
  153.8 91.1 all-gather.8
  247.0 55.8 all-gather.10
  741.5 71.7 reduce-scatter.5
  815.5 142.9 reduce-scatter.9
  962.1 149.4 reduce-scatter.7

commit v2 on v1

v2 whole, which is shorter than its diff:
```python
import functools

import jax
import jax.numpy as jnp
from jax import lax
from jax.experimental import pallas as pl
from jax.experimental.pallas import tpu as pltpu
from jax.sharding import PartitionSpec as P

QUERY_HEADS = 20
KEY_VALUE_HEADS = 5
HEAD_SIZE = 64
NCORP = 4

EPS = 1e-06
ROPE_BASE = 10000.0
WEIGHT_UNIT = 8.0
BF = jnp.bfloat16
F32 = jnp.float32


def inverse_rms(v):
    return lax.rsqrt(jnp.mean(v * v, axis=-1, keepdims=True) + EPS)


def dot(a, b, ca, cb):
    return lax.dot_general(a, b, (((ca,), (cb,)), ((), ())), preferred_element_type=F32)


def swap(v, axis, n, bit):
    return lax.ppermute(v, axis, [(i, i ^ bit) for i in range(n)])


def after(v, *marks):
    return lax.optimization_barrier((v,) + marks)[0]


def gather_seq(v, n_seq):
    slots, order = [v], [0]
    bit = n_seq // 2
    while bit:
        slots = slots + [swap(s, "seq", n_seq, bit) for s in slots]
        order = order + [o ^ bit for o in order]
        bit //= 2
    return [slots[order.index(j)] for j in range(n_seq)]


def scatter_seq(slots, n_seq):
    bit = 1
    live = dict(enumerate(slots))
    while bit < n_seq:
        keep = [j for j in live if not j & bit]
        sent = {j: swap(live[j | bit].astype(BF), "seq", n_seq, bit) for j in keep}
        live = {j: live[j].astype(F32) + sent[j].astype(F32) for j in keep}
        bit *= 2
    return live[0]


def ring(v, n_rows):
    return lax.ppermute(v, "rows", [(r, (r + 2) % n_rows) for r in range(n_rows)])


def gather_rows(v, n_rows):
    slots, held = [], v
    for i in range(n_rows // 2):
        if i:
            held = ring(held, n_rows)
        slots += [held, swap(held, "rows", n_rows, 1)]
    return slots


def scatter_rows(slots, n_rows):
    count = n_rows // 2
    total = None
    for i in list(range(1, count)) + [0]:
        part = slots[2 * i].astype(F32) + swap(slots[2 * i + 1], "rows", n_rows, 1).astype(F32)
        if total is not None:
            part = part + total.astype(F32)
        total = ring(part.astype(BF), n_rows) if i else part
    return total


def head_unit(v):
    inverse = lax.rsqrt(jnp.mean(v * v, axis=0, keepdims=True) + EPS)
    return v * inverse, inverse


def turn(v, cosine, sine):
    half = HEAD_SIZE // 2
    a, b = v[:half], v[half:]
    return jnp.concatenate([a * cosine - b * sine, b * cosine + a * sine], axis=0)


def turn_back(v, cosine, sine):
    half = HEAD_SIZE // 2
    a, b = v[:half], v[half:]
    return jnp.concatenate([a * cosine + b * sine, b * cosine - a * sine], axis=0)


def mm(a, b):
    return jnp.dot(a, b, preferred_element_type=F32)


def flip(v):
    return v.astype(F32).T.astype(BF)


def seen(kk, qq, first, span):
    key_at = kk * span + lax.broadcasted_iota(jnp.int32, (span, span), 0)
    mask = key_at >= first
    if kk == qq:
        lanes = qq * span + lax.broadcasted_iota(jnp.int32, (span, span), 1)
        mask = mask & (key_at <= lanes)
    return mask


def forward_heads(plan, me_ref, x_ref, cos_ref, sin_ref, first_ref, gain_ref, o_ref, inv_ref, k_nat, q_tr):
    n, span, per, group, q_cols, kv_cols = plan
    me, h = me_ref[0], pl.program_id(0)
    pick = lax.div(me * per + h, group) - lax.div(me * per, group)
    cosine, sine = cos_ref[...], sin_ref[...]
    k, _ = head_unit(x_ref[pl.ds(pl.multiple_of(q_cols + pick * HEAD_SIZE, HEAD_SIZE), HEAD_SIZE), :].astype(F32))
    k_nat[...] = flip(turn(k * gain_ref[:, 1:2], cosine, sine))
    q, _ = head_unit(x_ref[pl.ds(pl.multiple_of(h * HEAD_SIZE, HEAD_SIZE), HEAD_SIZE), :].astype(F32))
    q_tr[...] = (turn(q * gain_ref[:, 0:1], cosine, sine) * HEAD_SIZE**-0.5).astype(BF)
    v_rows = pl.ds(pl.multiple_of(q_cols + kv_cols + pick * HEAD_SIZE, HEAD_SIZE), HEAD_SIZE)
    for qq in range(n):
        q_at = pl.ds(pl.multiple_of((me ^ qq) * span, span), span)
        q_block, first = q_tr[:, q_at], first_ref[:, q_at]
        out = jnp.zeros((HEAD_SIZE, span), F32)
        summed = jnp.zeros((1, span), F32)
        for kk in range(qq + 1):
            k_at = pl.ds(pl.multiple_of((me ^ kk) * span, span), span)
            expo = jnp.exp(mm(k_nat[k_at, :], q_block))
            expo = jnp.where(seen(kk, qq, first, span), expo, 0.0)
            summed += jnp.sum(expo, axis=0, keepdims=True)
            out += mm(x_ref[v_rows, k_at], expo.astype(BF))
        inverse = 1.0 / summed
        o_ref[:, q_at] = (out * inverse).astype(BF)
        inv_ref[:, q_at] = inverse


def backward_heads(
    plan, me_ref, x_ref, cos_ref, sin_ref, first_ref, gain_ref, o_ref, inv_ref, do_ref,
    dx_ref, sum_ref, k_tr, k_nat, v_nat, q_tr, q_nat, do_nat, dq_tr, dk_acc, dv_acc,
):
    n, span, per, group, q_cols, kv_cols = plan
    me, h = me_ref[0], pl.program_id(0)
    pick = lax.div(me * per + h, group) - lax.div(me * per, group)
    scale = HEAD_SIZE**-0.5
    cosine, sine = cos_ref[...], sin_ref[...]

    @pl.when(h == 0)
    def _():
        dk_acc[...] = jnp.zeros_like(dk_acc)
        dv_acc[...] = jnp.zeros_like(dv_acc)
        sum_ref[...] = jnp.zeros_like(sum_ref)

    def add_gain(which, product):
        lanes = product[:, :128]
        for c in range(1, product.shape[1] // 128):
            lanes = lanes + product[:, c * 128 : (c + 1) * 128]
        sum_ref[which] += lanes

    k, _ = head_unit(x_ref[pl.ds(pl.multiple_of(q_cols + pick * HEAD_SIZE, HEAD_SIZE), HEAD_SIZE), :].astype(F32))
    k = turn(k * gain_ref[:, 1:2], cosine, sine)
    k_tr[...] = k.astype(BF)
    k_nat[...] = flip(k)
    h_rows = pl.ds(pl.multiple_of(h * HEAD_SIZE, HEAD_SIZE), HEAD_SIZE)
    q_unit, q_inverse = head_unit(x_ref[h_rows, :].astype(F32))
    q = turn(q_unit * gain_ref[:, 0:1], cosine, sine) * scale
    q_tr[...] = q.astype(BF)
    q_nat[...] = flip(q)
    v_nat[...] = flip(x_ref[pl.ds(pl.multiple_of(q_cols + kv_cols + pick * HEAD_SIZE, HEAD_SIZE), HEAD_SIZE), :])
    do_nat[...] = flip(do_ref[...])
    for qq in range(n):
        q_at = pl.ds(pl.multiple_of((me ^ qq) * span, span), span)
        q_block, first, inverse = q_tr[:, q_at], first_ref[:, q_at], inv_ref[:, q_at]
        do_block = do_ref[:, q_at]
        inner = jnp.sum(o_ref[:, q_at].astype(F32) * do_block.astype(F32), axis=0, keepdims=True)
        dq = jnp.zeros((HEAD_SIZE, span), F32)
        for kk in range(qq + 1):
            k_at = pl.ds(pl.multiple_of((me ^ kk) * span, span), span)
            probs = jnp.exp(mm(k_nat[k_at, :], q_block)) * inverse
            probs = jnp.where(seen(kk, qq, first, span), probs, 0.0)
            d_probs = mm(v_nat[k_at, :], do_block)
            d_scores = (probs * (d_probs - inner)).astype(BF)
            dv_acc[pick, k_at, :] += mm(probs.astype(BF), do_nat[q_at, :])
            dk_acc[pick, k_at, :] += mm(d_scores, q_nat[q_at, :])
            dq += mm(k_tr[:, k_at], d_scores)
        dq_tr[:, q_at] = dq * scale
    dq = turn_back(dq_tr[...], cosine, sine)
    add_gain(0, dq * q_unit)
    scaled = dq * gain_ref[:, 0:1]
    inner = jnp.mean(scaled * q_unit, axis=0, keepdims=True)
    dx_ref[h_rows, :] = (q_inverse * (scaled - q_unit * inner)).astype(BF)

    @pl.when(h == per - 1)
    def _():
        for m in range(kv_cols // HEAD_SIZE):
            k_rows = slice(q_cols + m * HEAD_SIZE, q_cols + (m + 1) * HEAD_SIZE)
            unit, inv = head_unit(x_ref[k_rows, :].astype(F32))
            dk = turn_back(dk_acc[m].T, cosine, sine)
            add_gain(1, dk * unit)
            scl = dk * gain_ref[:, 1:2]
            mid = jnp.mean(scl * unit, axis=0, keepdims=True)
            dx_ref[k_rows, :] = (inv * (scl - unit * mid)).astype(BF)
            v_rows = slice(q_cols + kv_cols + m * HEAD_SIZE, q_cols + kv_cols + (m + 1) * HEAD_SIZE)
            dx_ref[v_rows, :] = dv_acc[m].T.astype(BF)


def whole_block(shape):
    return pl.BlockSpec(shape, lambda h, me: (0,) * len(shape))


def attention_forward(plan, me, x, cosine, sine, first, gain):
    n, span, per, _, q_cols, _ = plan
    length = n * span
    return pl.pallas_call(
        functools.partial(forward_heads, plan),
        out_shape=(
            jax.ShapeDtypeStruct((q_cols, length), BF),
            jax.ShapeDtypeStruct((per, 1, length), F32),
        ),
        grid_spec=pltpu.PrefetchScalarGridSpec(
            num_scalar_prefetch=1,
            grid=(per,),
            in_specs=[whole_block(v.shape) for v in (x, cosine, sine, first, gain)],
            out_specs=(
                pl.BlockSpec((HEAD_SIZE, length), lambda h, me: (h, 0)),
                pl.BlockSpec((None, 1, length), lambda h, me: (h, 0, 0)),
            ),
            scratch_shapes=[pltpu.VMEM((length, HEAD_SIZE), BF), pltpu.VMEM((HEAD_SIZE, length), BF)],
        ),
        compiler_params=pltpu.CompilerParams(vmem_limit_bytes=40 << 20),
        cost_estimate=pl.CostEstimate(
            flops=4 * per * length * length * HEAD_SIZE, bytes_accessed=4 << 20, transcendentals=0
        ),
        name="attention_forward",
    )(me, x, cosine, sine, first, gain)


def attention_backward(plan, me, x, cosine, sine, first, gain, o, inv, d_o):
    n, span, per, _, q_cols, kv_cols = plan
    length = n * span
    held = kv_cols // HEAD_SIZE
    by_head = pl.BlockSpec((HEAD_SIZE, length), lambda h, me: (h, 0))
    tall, wide = pltpu.VMEM((length, HEAD_SIZE), BF), pltpu.VMEM((HEAD_SIZE, length), BF)
    return pl.pallas_call(
        functools.partial(backward_heads, plan),
        out_shape=(
            jax.ShapeDtypeStruct(x.shape, BF),
            jax.ShapeDtypeStruct((2, HEAD_SIZE, 128), F32),
        ),
        grid_spec=pltpu.PrefetchScalarGridSpec(
            num_scalar_prefetch=1,
            grid=(per,),
            in_specs=[whole_block(v.shape) for v in (x, cosine, sine, first, gain)]
            + [by_head, pl.BlockSpec((None, 1, length), lambda h, me: (h, 0, 0)), by_head],
            out_specs=(whole_block(x.shape), whole_block((2, HEAD_SIZE, 128))),
            scratch_shapes=[wide, tall, tall, wide, tall, tall]
            + [pltpu.VMEM((HEAD_SIZE, length), F32)]
            + [pltpu.VMEM((held, length, HEAD_SIZE), F32)] * 2,
        ),
        compiler_params=pltpu.CompilerParams(vmem_limit_bytes=48 << 20),
        cost_estimate=pl.CostEstimate(
            flops=10 * per * length * length * HEAD_SIZE, bytes_accessed=6 << 20, transcendentals=0
        ),
        name="attention_backward",
    )(me, x, cosine, sine, first, gain, o, inv, d_o)


def on_device(
    tokens,
    d_output,
    positions,
    corpus,
    corpus_weight,
    query_key_value_weight,
    out_weight,
    norm_gains,
    qk_gains,
    gate_up_weight,
    down_weight,
):
    n_seq = lax.axis_size("seq")
    n_rows = lax.axis_size("rows")
    me = lax.axis_index("seq")
    row_at = lax.axis_index("rows")
    rows, span, width = tokens.shape
    length = span * n_seq
    per = QUERY_HEADS // n_seq
    group = QUERY_HEADS // KEY_VALUE_HEADS
    q_cols = per * HEAD_SIZE
    lead = [t * per // group for t in range(n_seq)]
    last = [(t * per + per - 1) // group for t in range(n_seq)]
    held = max(b - a + 1 for a, b in zip(lead, last))
    kv_cols = held * HEAD_SIZE
    cols = q_cols + 2 * kv_cols
    local = query_key_value_weight.shape[0]
    extra = 64
    plan = (n_seq, span, per, group, q_cols, kv_cols)
    half = n_rows // 2
    near = jnp.arange(n_rows, dtype=jnp.int32)
    slot_of = 2 * ((row_at // 2 - near // 2) % half) + ((row_at % 2) ^ (near % 2))
    device_of = 2 * ((row_at // 2 - near // 2) % half) + ((row_at % 2) ^ (near % 2))

    onehot = (corpus == jnp.arange(NCORP, dtype=jnp.int32)[None, :]).astype(F32)
    counted = jnp.zeros((local, 1), BF).at[:NCORP, 0].set(jnp.sum(onehot, axis=0).astype(BF))
    pieces = []
    for t in range(n_seq):
        parts = [query_key_value_weight[:, t * q_cols : (t + 1) * q_cols]]
        for base in (QUERY_HEADS * HEAD_SIZE, (QUERY_HEADS + KEY_VALUE_HEADS) * HEAD_SIZE):
            for m in range(held):
                at = base + min(lead[t] + m, KEY_VALUE_HEADS - 1) * HEAD_SIZE
                parts.append(query_key_value_weight[:, at : at + HEAD_SIZE])
        parts += [norm_gains.T, counted, jnp.zeros((local, extra - 3), BF)]
        pieces.append(jnp.concatenate(parts, axis=1))
    mine = lax.all_to_all(jnp.stack(pieces), "seq", split_axis=0, concat_axis=0, tiled=True)
    whole = jnp.stack(gather_rows(mine.reshape(n_seq * local, cols + extra), n_rows))
    whole = jnp.take(whole, slot_of, axis=0).reshape(width, cols + extra)
    w_qkv = whole[:, :cols]
    gains = whole[:, cols : cols + 2].astype(F32).T
    counts = whole[:, cols + 2].astype(F32).reshape(n_rows, n_seq, local)[:, 0, :NCORP]
    counts = jnp.sum(counts, axis=0) * length
    total = float(rows * n_rows * length)
    factor = corpus_weight.astype(F32) / WEIGHT_UNIT * (total / (NCORP * counts))
    row_scale = jnp.sum(onehot * factor[None, :], axis=1)
    qk_gain = qk_gains.astype(F32).T

    x_rows = [jnp.concatenate(gather_seq(tokens[r], n_seq), axis=0) for r in range(rows)]
    rel = me ^ jnp.arange(n_seq, dtype=jnp.int32)
    at = (rel[:, None] * span + jnp.arange(span, dtype=jnp.int32)[None, :]).reshape(length)
    pos = jnp.take(positions.reshape(rows, n_seq, span), rel, axis=1).reshape(rows, length)
    first = at[None, :] - pos
    base = ROPE_BASE ** (-2.0 * jnp.arange(HEAD_SIZE // 2).astype(F32) / HEAD_SIZE)
    angles = pos.astype(F32)[:, None, :] * base[None, :, None]
    cosine, sine = jnp.cos(angles), jnp.sin(angles)
    me_one = me.astype(jnp.int32).reshape(1)

    kept = []
    o_rows = []
    for r in range(rows):
        x = x_rows[r].astype(F32)
        a_in = (x * inverse_rms(x) * gains[0]).astype(BF)
        qkv = dot(w_qkv, a_in, 0, 1).astype(BF)
        args = (plan, me_one, qkv, cosine[r], sine[r], first[r : r + 1], qk_gain)
        o, inv = attention_forward(*args)
        kept.append((a_in, args, o, inv))
        got = gather_seq(o, n_seq)
        got = [
            jnp.concatenate(
                [got[m][:, (m ^ j) * span : ((m ^ j) + 1) * span] for j in range(n_seq)], axis=1
            )
            for m in range(n_seq)
        ]
        o_rows.append(jnp.take(jnp.stack(got), rel, axis=0).reshape(n_seq * q_cols, length))
    o_all = jnp.concatenate(o_rows, axis=1)
    x_all = jnp.concatenate(x_rows, axis=0).astype(F32)

    out_weight = after(out_weight, w_qkv)
    w_out = lax.all_gather(out_weight, ("rows", "seq"), axis=0, tiled=True)
    h_all = x_all + dot(o_all, w_out, 0, 1)
    inverse_two = inverse_rms(h_all)
    f_in = (h_all * inverse_two * gains[1]).astype(BF)

    ff_local = jnp.concatenate([gate_up_weight, down_weight], axis=1)
    ff_slots = gather_rows(after(ff_local, w_qkv), n_rows)
    w_g = jnp.concatenate([w[:, :width] for w in ff_slots], axis=0)
    w_u = jnp.concatenate([w[:, width : 2 * width] for w in ff_slots], axis=0)
    w_dn = jnp.concatenate([w[:, 2 * width :] for w in ff_slots], axis=0)
    dy_own = after(d_output, x_rows[-1])
    dy_all = jnp.stack(gather_seq(dy_own, n_seq), axis=1).astype(F32)
    gy = (row_scale[:, None, None, None] * dy_all).astype(BF).reshape(rows * length, width)
    gate = dot(f_in, w_g, 1, 1)
    upper = dot(f_in, w_u, 1, 1)
    sigma = jax.nn.sigmoid(gate)
    active = gate * sigma
    hidden = (active * upper).astype(BF)
    d_hidden = dot(gy, w_dn, 1, 1)
    d_upper = (d_hidden * active).astype(BF)
    d_gate = (d_hidden * upper * sigma * (1.0 + gate * (1.0 - sigma))).astype(BF)
    df_part = dot(d_gate, w_g, 1, 0) + dot(d_upper, w_u, 1, 0)
    d_gain_two = jnp.sum(df_part * (h_all * inverse_two), axis=0)
    df_slots = df_part.astype(BF).reshape(rows, n_seq, span, width)
    df = scatter_seq([df_slots[:, j] for j in range(n_seq)], n_seq).reshape(rows * span, width)
    ffn_grads = jnp.concatenate(
        [dot(d_gate, f_in, 0, 0), dot(d_upper, f_in, 0, 0), dot(hidden, gy, 0, 0)], axis=1
    ).astype(BF)
    df, ffn_grads = lax.optimization_barrier((df, ffn_grads))
    ff_rows = gate_up_weight.shape[0]
    ffn_sums = scatter_rows(
        [ffn_grads[i * ff_rows : (i + 1) * ff_rows] for i in range(n_rows)], n_rows
    )
    y_slots = dot(after(hidden, df), w_dn, 1, 0).astype(BF).reshape(rows, n_seq, span, width)
    y = scatter_seq([y_slots[:, j] for j in range(n_seq)], n_seq)
    h_own = h_all.reshape(rows, n_seq, span, width)[:, 0]
    output = (h_own + y).astype(BF)

    h_one = h_own.reshape(rows * span, width)
    inverse = inverse_rms(h_one)
    unit = h_one * inverse
    scaled = df * gains[1]
    g_two = (row_scale[:, None, None] * d_output.astype(F32)).reshape(rows * span, width)
    d_h = g_two + inverse * (scaled - unit * jnp.mean(scaled * unit, axis=-1, keepdims=True))
    grad_att = d_h.astype(BF)
    o_own = jnp.concatenate([o[:, :span] for o in o_rows], axis=1)
    d_out = lax.psum_scatter(
        dot(grad_att, o_own, 0, 1).astype(BF), ("rows", "seq"), scatter_dimension=0, tiled=True
    ).astype(F32)
    do_src = dot(w_out, grad_att, 0, 1).astype(BF).reshape(n_seq, q_cols, rows * span)
    do_src = jnp.take(do_src, rel, axis=0)
    do_slots = [do_src[0]] + [swap(do_src[m], "seq", n_seq, m) for m in range(1, n_seq)]

    d_acts, d_parts, d_heads, d_gain_one = [], [], 0.0, 0.0
    for r in range(rows):
        a_in, args, o, inv = kept[r]
        d_o = jnp.concatenate([d[:, r * span : (r + 1) * span] for d in do_slots], axis=1)
        d_act, head_sums = attention_backward(*args, o, inv, d_o)
        d_heads = d_heads + jnp.sum(head_sums, axis=-1)
        part = dot(d_act, w_qkv, 0, 1)
        x = x_rows[r].astype(F32)
        d_gain_one = d_gain_one + jnp.sum(part * (x * inverse_rms(x)), axis=0)
        part = part.astype(BF)
        d_parts.append(
            scatter_seq([part[j * span : (j + 1) * span] for j in range(n_seq)], n_seq)
        )
        d_acts.append(d_act)
    d_a = jnp.concatenate(d_parts, axis=0)
    x_own = tokens.astype(F32).reshape(rows * span, width)
    inverse = inverse_rms(x_own)
    unit = x_own * inverse
    scaled = d_a * gains[0]
    d_tokens = d_h + inverse * (scaled - unit * jnp.mean(scaled * unit, axis=-1, keepdims=True))
    d_tokens = d_tokens.reshape(rows, span, width)

    spread = 2 * HEAD_SIZE // local
    tail = jnp.concatenate(
        [
            d_gain_one[:, None],
            d_gain_two[:, None],
            jnp.tile(d_heads.reshape(local, spread), (width // local, 1)),
            jnp.zeros((width, extra - 2 - spread), F32),
        ],
        axis=1,
    )
    d_w = sum(dot(kept[r][0], d_acts[r], 0, 1) for r in range(rows))
    d_w = jnp.concatenate([d_w.astype(BF), tail.astype(BF)], axis=1)
    d_w = jnp.take(d_w.reshape(n_rows, n_seq * local, cols + extra), device_of, axis=0)
    d_w = scatter_rows([d_w[i] for i in range(n_rows)], n_rows).astype(BF)
    d_w = lax.all_to_all(
        d_w.reshape(n_seq, local, cols + extra), "seq", split_axis=0, concat_axis=0, tiled=True
    ).astype(F32)
    k_sum = [jnp.zeros((local, HEAD_SIZE), F32) for _ in range(KEY_VALUE_HEADS)]
    v_sum = [jnp.zeros((local, HEAD_SIZE), F32) for _ in range(KEY_VALUE_HEADS)]
    for t in range(n_seq):
        for m in range(last[t] - lead[t] + 1):
            a = q_cols + m * HEAD_SIZE
            k_sum[lead[t] + m] += d_w[t, :, a : a + HEAD_SIZE]
            v_sum[lead[t] + m] += d_w[t, :, a + kv_cols : a + kv_cols + HEAD_SIZE]
    d_qkv = jnp.concatenate([d_w[t, :, :q_cols] for t in range(n_seq)] + k_sum + v_sum, axis=1)
    ends = jnp.sum(d_w[:, :, cols : cols + 2 + spread], axis=0)
    d_gains = ends[:, :2].T
    d_qk_gains = ends[:, 2:].reshape(2, HEAD_SIZE)
    return (
        output,
        d_tokens,
        d_qkv,
        d_out,
        d_gains,
        d_qk_gains,
        ffn_sums[:, : 2 * width],
        ffn_sums[:, 2 * width :],
    )


def solution(mesh):
    both = ("rows", "seq")
    acts = P("rows", "seq", None)
    return jax.shard_map(
        on_device,
        mesh=mesh,
        in_specs=(
            acts,
            acts,
            P("rows", None),
            P("rows", None),
            P(),
            P(both, None),
            P(both, None),
            P(None, both),
            P(),
            P(both, None),
            P(both, None),
        ),
        out_specs=(
            acts,
            acts,
            P(both, None),
            P(both, None),
            P(None, both),
            P(),
            P(both, None),
            P(both, None),
        ),
        check_vma=False,
    )
```

time: 1130 us -> 742 us (0.66)
  waiting for transfers between devices: 466 us -> 279 us
  matrix products: 272 us -> 160 us
  other arithmetic: 172 us -> 88.9 us
  local copies, waits for them, and re-layouts: 174 us -> 99.6 us
  Pallas kernels: 0 us -> 45.3 us
  starting transfers between devices: 13 us -> 47.2 us
    reduce_scatter x2 -> x1, waiting for transfers between devices: 151 us -> 0.01 us  [on_device(): lax.psum_scatter(dot(grad_att, o_own, 0, 1).astype(BF), ('rows', 'seq'),...]
    ppermute x21 -> x46, waiting for transfers between devices: 280 us -> 172 us  [swap(): return lax.ppermute(v, axis, [(i, i ^ bit) for i in range(n)])]
    dot_general x8 -> x0, matrix products: 109 us -> none  [the longest x1 27.4 us: on_device(): jnp.einsum('rqhd,rkhd->rhqk', d_o, v_rep, preferred_element_type=F32)]
    ppermute x0 -> x12, waiting for transfers between devices: none -> 89.2 us  [ring(): lax.ppermute(v, 'rows', [(r, (r + 2) % n_rows) for r in range(n_rows)])]
    convert_element_type x11, other arithmetic: 78.3 us -> 32 us  [the longest x6 8.37 us: scatter_rows(): total = ring(part.astype(BF), n_rows) if i else part]
    pallas_call x0 -> x4, Pallas kernels: none -> 45.3 us  [the longest x2 31.1 us: attention_backward(): pl.pallas_call(functools.partial(backward_heads, plan), out_shape=(jax.Sh...]
    unnamed x8 -> x2, waiting for transfers between devices: 31.9 us -> 0.05 us
    convert_element_type x6 -> x0, local copies, waits for them, and re-layouts: 24.7 us -> none  [the longest x3 16 us: scatter_seq(): sent = {j: swap(live[j | bit].astype(BF), 'seq', n_seq, bit) for j in keep}]
  transfers between devices with their start and end apart: 29 -> 62, of which waited for: 12 -> 30; matrix products, arithmetic and copies ran while one was open for 32% -> 30% of each run, Pallas kernels for 0% -> 6%
where the time goes in v2:
time: 742 us; the launch traced here: 735 us
  waiting for transfers between devices  279 us (38%)
  matrix products  160 us (22%)
  local copies, waits for them, and re-layouts  99.6 us (13%)
  other arithmetic  88.9 us (12%)
  starting transfers between devices  47.2 us (6%)
  Pallas kernels  45.3 us (6%)
  between operations  15.9 us (2%)
    ppermute x46, waiting for transfers between devices, swap(): return lax.ppermute(v, axis, [(i, i ^ bit) for i in range(n)])  172 us
    dot_general x18, matrix products, dot(): lax.dot_general(a, b, (((ca,), (cb,)), ((), ())), preferred_element_type=...  160 us
    ppermute x12, waiting for transfers between devices, ring(): lax.ppermute(v, 'rows', [(r, (r + 2) % n_rows) for r in range(n_rows)])  89.2 us
    unnamed x182, local copies, waits for them, and re-layouts  42.3 us
    ppermute x46, starting transfers between devices, swap(): return lax.ppermute(v, axis, [(i, i ^ bit) for i in range(n)])  33.2 us
    pallas_call x2, Pallas kernels, attention_backward(): pl.pallas_call(functools.partial(backward_heads, plan), out_shape=(jax.Sh...  31.1 us
  transfers between devices with their start and end apart: 62, of which 30 were waited for; matrix products, arithmetic and copies ran while one was open for 30% of the time, Pallas kernels for 6%

profile of v2, /device:TPU:0, one launch (start us, length us, event | category | flops | bytes accessed | tf_op | source)
XLA Modules:
  0.0 735.3 jit_solution(10932058897103573913)
XLA Ops:
  7.2 3.3 slice_bitcast_fusion.8
  10.5 2.9 collective-permute-start.1
  15.3 3.6 all-to-all-start
  27.8 13.3 %all-to-all-done = bf16[4,64,640]{2,1,0:T(8,128)(2,1)S(1)} async-done(((bf16[4,64,640]{2,1,0:T(8,128)(2,1)}), bf16[4,64,640]{2,1,0:T(8,128)(2,1)S(1)}, u32[]{:S(2)}, u32[]{:S(2)}) %all-to-all-start) | async-done | bytes 327712 | tf_op jit(solution)/shard_map/all_to_all | solution.py:319
  45.6 6.9 collective-permute-done.7
  54.5 5.1 collective-permute-done.8
  70.1 3.6 collective-permute-done.11
  76.6 4.2 collective-permute-done.12
  84.7 3.1 slice_dynamic-update-slice_fusion.21
  91.3 4.2 convert_multiply_fusion.5
  98.5 3.2 convolution_convert_fusion.6.x_ref
  101.7 7.1 attention_forward.3
  113.1 5.3 convolution_convert_fusion.7.x_ref
  118.5 7.1 attention_forward.2
  143.3 19.8 %collective-permute-done.14 = bf16[320,1024]{1,0:T(8,128)(2,1)S(1)} collective-permute-done((bf16[320,1024]{1,0:T(8,128)(2,1)S(1)}, bf16[320,1024]{1,0:T(8,128)(2,1)S(1)}, u32[]{:S(2)}, u32[]{:S(2)}) %collective-permute-start.14) | collective-permute-done | bytes 655392 | tf_op jit(solution)/shard_map/ppermute | solution.py:31
  167.0 16.9 %collective-permute-done.22 = bf16[88,6144]{1,0:T(8,128)(2,1)} collective-permute-done((bf16[88,6144]{1,0:T(8,128)(2,1)}, bf16[88,6144]{1,0:T(8,128)(2,1)}, u32[]{:S(2)}, u32[]{:S(2)}) %collective-permute-start.22) | collective-permute-done | bytes 1081376 | tf_op jit(solution)/shard_map/ppermute | solution.py:60
  188.0 4.1 gather_fusion.3
  198.0 9.7 %collective-permute-done.27 = bf16[2,256,2048]{2,1,0:T(8,128)(2,1)} collective-permute-done((bf16[2,256,2048]{2,1,0:T(8,128)(2,1)}, bf16[2,256,2048]{2,1,0:T(8,128)(2,1)}, u32[]{:S(2)}, u32[]{:S(2)}) %collective-permute-start.27) | collective-permute-done | bytes 2097184 | tf_op jit(solution)/shard_map/ppermute | solution.py:31
  214.8 4.2 collective-permute-done.23
  222.3 19.0 %collective-permute-done.25 = bf16[88,6144]{1,0:T(8,128)(2,1)S(1)} collective-permute-done((bf16[88,6144]{1,0:T(8,128)(2,1)}, bf16[88,6144]{1,0:T(8,128)(2,1)S(1)}, u32[]{:S(2)}, u32[]{:S(2)}) %collective-permute-start.25) | collective-permute-done | bytes 1081376 | tf_op jit(solution)/shard_map/ppermute | solution.py:31
  242.2 7.1 pad_maximum_fusion.1
  249.3 8.3 %fusion = bf16[2048,2048]{1,0:T(8,128)(2,1)} fusion(bf16[2,4,256,2048]{3,2,1,0:T(8,128)(2,1)} %pad_maximum_fusion.1, f32[2048]{0:T(1024)S(1)} %bitcast.323), kind=kLoop, calls=%fused_computation.7 | loop fusion | flops 12582912 | bytes 16785408 | tf_op jit(solution)/shard_map/convert_element_type | solution.py:374
  257.6 18.9 %multiply_reduce_fusion.1 = (f32[2048]{0:T(1024)S(1)}, f32[2048,2048]{1,0:T(8,128)}) fusion(bf16[2048,1280]{1,0:T(8,128)(2,1)} %all-gather.2.cloned.1.call-done, bf16[1280,1024]{1,0:T(8,128)(2,1)} %bitcast.303, bf16[1280,1024]{1,0:T(8,128)(2,1)S(1)} %bitcast.301, bf16[2048,2048]{1,0:T(8,128)(2,1)} %constant_dynamic-update-slice_fusion), kind=kOutput, calls=%fused_computation.10 | convolution fusion | flops 10764679168 | bytes 35659776 | tf_op jit(solution)/shard_map/dot_general | solution.py:27
  276.5 4.7 slice.666
  283.7 7.1 multiply_convert_fusion
  290.9 8.0 %fusion.89 = f32[2048,704]{0,1:T(8,128)} fusion(bf16[2048,2048]{1,0:T(8,128)(2,1)S(1)} %multiply_convert_fusion, bf16[704,2048]{1,0:T(8,128)(2,1)S(1)} %copy-done.49), kind=kOutput, calls=%fused_computation.281 | convolution fusion | flops 5905580032 | bytes 17039360 | tf_op jit(solution)/shard_map/dot_general | solution.py:27
  298.9 8.1 %fusion.88 = f32[2048,704]{0,1:T(8,128)} fusion(bf16[2048,2048]{1,0:T(8,128)(2,1)S(1)} %multiply_convert_fusion, bf16[704,2048]{1,0:T(8,128)(2,1)S(1)} %copy-done.50), kind=kOutput, calls=%fused_computation.280 | convolution fusion | flops 5905580032 | bytes 17039360 | tf_op jit(solution)/shard_map/dot_general | solution.py:27
  307.0 12.8 %multiply_convert_fusion.1 = (bf16[2048,704]{0,1:T(8,128)(2,1)}, bf16[2048,704]{0,1:T(8,128)(2,1)S(1)}, bf16[2048,704]{0,1:T(8,128)(2,1)}) fusion(f32[2048,704]{0,1:T(8,128)} %fusion.88, f32[2048,704]{0,1:T(8,128)} %fusion.89, bf16[2048,2048]{1,0:T(8,128)(2,1)S(1)} %bitcast.290, bf16[704,2048]{1,0:T(8,128)(2,1)S(1)} %copy-done.47), kind=kOutput, calls=%fused_computation.31 | convolution fusion | flops 5927206912 | bytes 31457280 | tf_op jit(solution)/shard_map/dot_general | solution.py:27
  319.9 9.6 %convolution_convert_fusion.4 = bf16[704,2048]{1,0:T(8,128)(2,1)S(1)} fusion(bf16[2048,704]{0,1:T(8,128)(2,1)S(1)} %get-tuple-element.73, bf16[2048,2048]{1,0:T(8,128)(2,1)} %copy-done.26), kind=kOutput, calls=%fused_computation.69 | convolution fusion | flops 5907021824 | bytes 14155776 | tf_op jit(solution)/shard_map/dot_general | solution.py:27
  329.6 10.4 %fusion.90 = f32[2048,2048]{1,0:T(8,128)} fusion(bf16[2048,704]{0,1:T(8,128)(2,1)S(1)} %copy-done.68, bf16[704,2048]{1,0:T(8,128)(2,1)S(1)} %copy-done.49), kind=kOutput, calls=%fused_computation.282 | convolution fusion | flops 5905580032 | bytes 22544384 | tf_op jit(solution)/shard_map/dot_general | solution.py:27
  339.9 19.9 %multiply_reduce_fusion = (bf16[2048]{0:T(1024)(128)(2,1)S(1)}, bf16[2048,2048]{1,0:T(8,128)(2,1)}) fusion(f32[2048,2048]{1,0:T(8,128)} %get-tuple-element.198, f32[2048]{0:T(1024)S(1)} %add_rsqrt_fusion, f32[2048,2048]{1,0:T(8,128)} %fusion.90, bf16[2048,704]{0,1:T(8,128)(2,1)} %copy-done.67, bf16[704,2048]{1,0:T(8,128)(2,1)} %get-tuple-element.103), kind=kOutput, calls=%fused_computation.8 | convolution fusion | flops 5926549504 | bytes 47722496 | tf_op jit(solution)/shard_map/dot_general | solution.py:27
  359.9 4.2 slice_bitcast_fusion.6
  364.7 9.6 %convolution_convert_fusion.3 = bf16[704,2048]{1,0:T(8,128)(2,1)S(1)} fusion(bf16[2048,704]{0,1:T(8,128)(2,1)} %get-tuple-element.72, bf16[2048,2048]{1,0:T(8,128)(2,1)} %copy-done.26), kind=kOutput, calls=%fused_computation.68 | convolution fusion | flops 5907021824 | bytes 14155776 | tf_op jit(solution)/shard_map/dot_general | solution.py:27
  377.4 6.4 convolution_convert_fusion.2
  385.0 39.5 %collective-permute-done.31 = bf16[2,256,2048]{2,1,0:T(8,128)(2,1)} collective-permute-done((bf16[2,256,2048]{2,1,0:T(8,128)(2,1)}, bf16[2,256,2048]{2,1,0:T(8,128)(2,1)}, u32[]{:S(2)}, u32[]{:S(2)}) %collective-permute-start.31) | collective-permute-done | bytes 2097184 | tf_op jit(solution)/shard_map/ppermute | solution.py:31
  424.5 3.4 fusion.23
  437.5 4.6 convolution_convert_fusion
  442.1 6.7 convolution_convert_fusion.5
  451.9 9.0 %convolution_convert_fusion.1 = bf16[2048,2048]{1,0:T(8,128)(2,1)S(1)} fusion(bf16[2048,704]{0,1:T(8,128)(2,1)} %get-tuple-element.42, bf16[704,2048]{1,0:T(8,128)(2,1)S(1)} %copy-done.48), kind=kOutput, calls=%fused_computation.29 | convolution fusion | flops 5909774336 | bytes 14155776 | tf_op jit(solution)/shard_map/dot_general | solution.py:27
  465.6 11.6 %collective-permute-done.37 = bf16[320,512]{1,0:T(8,128)(2,1)S(1)} collective-permute-done((bf16[320,512]{1,0:T(8,128)(2,1)S(1)}, bf16[320,512]{1,0:T(8,128)(2,1)S(1)}, u32[]{:S(2)}, u32[]{:S(2)}) %collective-permute-start.37) | collective-permute-done | bytes 327712 | tf_op jit(solution)/shard_map/ppermute | solution.py:31
  477.4 15.6 %attention_backward.3 = (bf16[576,1024]{1,0:T(8,128)(2,1)S(1)}, f32[2,64,128]{2,1,0:T(8,128)S(1)}) custom-call(s32[1]{0:T(128)} %bitcast.2.me_ref, bf16[576,1024]{1,0:T(8,128)(2,1)S(1)} %copy-done.15, f32[32,1024]{1,0:T(8,128)S(1)} %get-tuple-element.170.cos_ref, f32[32,1024]{1,0:T(8,128)S(1)} %get-tuple-element.168.sin_ref, s32[1,1024]{1,0:T(1,128)S(1)} %copy-done.11, ...), custom_call_target="tpu_custom_call" | custom-call | flops 3355443200 | bytes 6291456 | tf_op jit(solution)/shard_map/attention_backward/pallas_call | solution.py:249
  493.0 5.5 fusion.6
  498.5 4.5 fusion.33
  503.1 15.6 %attention_backward.2 = (bf16[576,1024]{1,0:T(8,128)(2,1)S(1)}, f32[2,64,128]{2,1,0:T(8,128)S(1)}) custom-call(s32[1]{0:T(128)} %bitcast.2.me_ref, bf16[576,1024]{1,0:T(8,128)(2,1)S(1)} %copy-done.13, f32[32,1024]{1,0:T(8,128)S(1)} %get-tuple-element.169.cos_ref, f32[32,1024]{1,0:T(8,128)S(1)} %get-tuple-element.167.sin_ref, s32[1,1024]{1,0:T(1,128)S(1)} %copy-done.9, ...), custom_call_target="tpu_custom_call" | custom-call | flops 3355443200 | bytes 6291456 | tf_op jit(solution)/shard_map/attention_backward/pallas_call | solution.py:249
  519.2 10.9 %fusion.8 = (f32[2048]{0:T(1024)S(1)}, bf16[1024,2048]{1,0:T(8,128)(2,1)}) fusion(f32[1024]{0:T(1024)S(1)} %copy-done.58, bf16[256,2048]{1,0:T(8,128)(2,1)} %collective-permute-done.2, bf16[256,2048]{1,0:T(8,128)(2,1)} %collective-permute-done.1, bf16[256,2048]{1,0:T(8,128)(2,1)} %collective-permute-done, bf16[256,2048]{1,0:T(8,128)(2,1)} %get-tuple-element.96, ...), kind=kOutput, calls=%fused_computation.24 | convolution fusion | flops 2441082880 | bytes 12201984 | tf_op jit(solution)/shard_map/dot_general | solution.py:27
  530.1 6.4 add_convert_fusion.1
  536.5 8.9 %concatenate.117 = bf16[2048,640]{0,1:T(8,128)(2,1)S(1)} concatenate(bf16[2048,576]{0,1:T(8,128)(2,1)} %add_convert_fusion.1, bf16[2048,1]{0,1:T(2,128)(2,1)S(1)} %add.320, bf16[2048,1]{0,1:T(2,128)(2,1)S(1)} %broadcast_in_dim.74, bf16[2048,2]{0,1:T(2,128)(2,1)S(1)} %tile.10, bf16[2048,60]{0,1:T(8,128)(2,1)S(1)} %broadcast_in_dim.75), dimensions={1} | concatenate | bytes 5242880 | tf_op jit(solution)/shard_map/concatenate | solution.py:448
  556.4 7.5 %collective-permute-done.47 = bf16[256,640]{1,0:T(8,128)(2,1)S(1)} collective-permute-done((bf16[256,640]{1,0:T(8,128)(2,1)S(1)}, bf16[256,640]{1,0:T(8,128)(2,1)S(1)}, u32[]{:S(2)}, u32[]{:S(2)}) %collective-permute-start.47) | collective-permute-done | bytes 327712 | tf_op jit(solution)/shard_map/ppermute | solution.py:31
  567.5 5.2 collective-permute-done.46
  572.6 3.8 collective-permute-done.48
  581.1 7.4 %collective-permute-done.49 = bf16[256,640]{1,0:T(8,128)(2,1)S(1)} collective-permute-done((bf16[256,640]{1,0:T(8,128)(2,1)S(1)}, bf16[256,640]{1,0:T(8,128)(2,1)S(1)}, u32[]{:S(2)}, u32[]{:S(2)}) %collective-permute-start.49) | collective-permute-done | bytes 327712 | tf_op jit(solution)/shard_map/ppermute | solution.py:60
  591.7 6.2 collective-permute-done.44
  601.9 3.5 all-to-all-start.1
  605.4 2.9 add_convert_fusion.5
  608.3 4.2 all-to-all-done.1
  617.8 16.0 %collective-permute-done.55 = bf16[88,6144]{1,0:T(8,128)(2,1)} collective-permute-done((bf16[88,6144]{1,0:T(8,128)(2,1)}, bf16[88,6144]{1,0:T(8,128)(2,1)}, u32[]{:S(2)}, u32[]{:S(2)}) %collective-permute-start.55) | collective-permute-done | bytes 1081376 | tf_op jit(solution)/shard_map/ppermute | solution.py:60
  638.5 5.2 collective-permute-done.40
  645.9 20.2 %collective-permute-done.43 = bf16[256,2048]{1,0:T(8,128)(2,1)S(1)} collective-permute-done((bf16[256,2048]{1,0:T(8,128)(2,1)S(1)}, bf16[256,2048]{1,0:T(8,128)(2,1)S(1)}, u32[]{:S(2)}, u32[]{:S(2)}) %collective-permute-start.43) | collective-permute-done | bytes 1048608 | tf_op jit(solution)/shard_map/ppermute | solution.py:31
  670.7 22.6 %collective-permute-done.56 = bf16[88,6144]{1,0:T(8,128)(2,1)S(1)} collective-permute-done((bf16[88,6144]{1,0:T(8,128)(2,1)S(1)}, bf16[88,6144]{1,0:T(8,128)(2,1)S(1)}, u32[]{:S(2)}, u32[]{:S(2)}) %collective-permute-start.56) | collective-permute-done | bytes 1081376 | tf_op jit(solution)/shard_map/ppermute | solution.py:60
  693.3 2.9 add_convert_fusion.2
  696.2 3.2 fusion.27
  699.4 11.3 %collective-permute-done.34 = bf16[2,256,2048]{2,1,0:T(8,128)(2,1)S(1)} collective-permute-done((bf16[2,256,2048]{2,1,0:T(8,128)(2,1)S(1)}, bf16[2,256,2048]{2,1,0:T(8,128)(2,1)S(1)}, u32[]{:S(2)}, u32[]{:S(2)}) %collective-permute-start.34) | collective-permute-done | bytes 2097184 | tf_op jit(solution)/shard_map/ppermute | solution.py:31
  710.7 5.7 fusion.18
  716.4 6.1 collective-permute-done.57
  (409 shorter events, 162.0 us)
Async XLA Ops:
  10.5 54.4 %collective-permute-start.1 = (bf16[256,2048]{1,0:T(8,128)(2,1)}, bf16[256,2048]{1,0:T(8,128)(2,1)}, u32[]{:S(2)}, u32[]{:S(2)}) collective-permute-start(bf16[256,2048]{1,0:T(8,128)(2,1)} %get-tuple-element.96), channel_id=1, source_target_pairs={{0,2},{1,3},{2,0},{3,1},{4,6},{5,7},{6,4},{7,5},{8,10},{9,11},{10,... | collective-permute-start | bytes 3145736 | tf_op jit(solution)/shard_map/ppermute | solution.py:31
  13.4 51.6 %collective-permute-start = (bf16[256,2048]{1,0:T(8,128)(2,1)}, bf16[256,2048]{1,0:T(8,128)(2,1)}, u32[]{:S(2)}, u32[]{:S(2)}) collective-permute-start(bf16[256,2048]{1,0:T(8,128)(2,1)} %get-tuple-element.96), channel_id=1, source_target_pairs={{0,1},{1,0},{2,3},{3,2},{4,5},{5,4},{6,7},{7,6},{8,9},{9,8},{10,11... | collective-permute-start | bytes 3145736 | tf_op jit(solution)/shard_map/ppermute | solution.py:31
  15.3 25.9 %all-to-all-start = ((bf16[4,64,640]{2,1,0:T(8,128)(2,1)}), bf16[4,64,640]{2,1,0:T(8,128)(2,1)S(1)}, u32[]{:S(2)}, u32[]{:S(2)}) async-start(bf16[4,64,640]{2,1,0:T(8,128)(2,1)} %pad_maximum_fusion.10), calls=%async_computation | async-start | bytes 655360 | tf_op jit(solution)/shard_map/all_to_all | solution.py:319
  18.8 238.8 %all-gather.2.cloned.1.call-start = ((), (), s32[]{:S(2)}) async-start(), calls=%async_computation.3 | async-start | bytes 5406720 | tf_op jit(solution)/shard_map/all_gather | solution.py:362
  18.9 46.0 %collective-permute-start.4 = (bf16[256,2048]{1,0:T(8,128)(2,1)}, bf16[256,2048]{1,0:T(8,128)(2,1)}, u32[]{:S(2)}, u32[]{:S(2)}) collective-permute-start(bf16[256,2048]{1,0:T(8,128)(2,1)} %get-tuple-element.95), channel_id=1, source_target_pairs={{0,2},{1,3},{2,0},{3,1},{4,6},{5,7},{6,4},{7,5},{8,10},{9,11},{10,... | collective-permute-start | bytes 3145736 | tf_op jit(solution)/shard_map/ppermute | solution.py:31
  20.8 172.3 %copy-start.61 = (pred[4]{0:T(512)(128)(4,1)}, pred[4]{0:T(512)(128)(4,1)S(1)}, u32[]{:S(2)}) copy-start(pred[4]{0:T(512)(128)(4,1)S(1)} %compare_and_fusion) | copy-start | bytes 16
  27.2 91.3 %copy-start.6 = (f32[2,64]{0,1:T(8,128)}, f32[2,64]{0,1:T(8,128)S(1)}, u32[]{:S(2)}) copy-start(f32[2,64]{0,1:T(8,128)S(1)} %copy.99) | copy-start | bytes 1540
  41.1 11.9 %collective-permute-start.6 = (bf16[256,640]{1,0:T(8,128)(2,1)S(1)}, bf16[256,640]{1,0:T(8,128)(2,1)S(1)}, u32[]{:S(2)}, u32[]{:S(2)}) collective-permute-start(bf16[256,640]{1,0:T(8,128)(2,1)S(1)} %bitcast.305), channel_id=1, source_target_pairs={{0,4},{4,0},{8,12},{12,8},{16,20},{20,16},{24,28},{28,24},{1,5},{5... | collective-permute-start | bytes 983048 | tf_op jit(solution)/shard_map/ppermute | solution.py:31
  43.2 9.3 %collective-permute-start.7 = (bf16[256,640]{1,0:T(8,128)(2,1)S(1)}, bf16[256,640]{1,0:T(8,128)(2,1)S(1)}, u32[]{:S(2)}, u32[]{:S(2)}) collective-permute-start(bf16[256,640]{1,0:T(8,128)(2,1)S(1)} %bitcast.306), channel_id=1, source_target_pairs={{0,8},{4,12},{8,16},{12,20},{16,24},{20,28},{24,0},{28,4},{1,9},{5... | collective-permute-start | bytes 983048 | tf_op jit(solution)/shard_map/ppermute | solution.py:60
  52.5 7.1 collective-permute-start.8
  53.0 8.9 %collective-permute-start.9 = (bf16[256,640]{1,0:T(8,128)(2,1)S(1)}, bf16[256,640]{1,0:T(8,128)(2,1)S(1)}, u32[]{:S(2)}, u32[]{:S(2)}) collective-permute-start(bf16[256,640]{1,0:T(8,128)(2,1)S(1)} %collective-permute-done.7), channel_id=1, source_target_pairs={{0,8},{4,12},{8,16},{12,20},{16,24},{20,28},{24,0},{28,4},{1,9},{5... | collective-permute-start | bytes 983048 | tf_op jit(solution)/shard_map/ppermute | solution.py:60
  59.6 36.0 %collective-permute-start.3 = (bf16[256,2048]{1,0:T(8,128)(2,1)}, bf16[256,2048]{1,0:T(8,128)(2,1)}, u32[]{:S(2)}, u32[]{:S(2)}) collective-permute-start(bf16[256,2048]{1,0:T(8,128)(2,1)} %get-tuple-element.95), channel_id=1, source_target_pairs={{0,1},{1,0},{2,3},{3,2},{4,5},{5,4},{6,7},{7,6},{8,9},{9,8},{10,11... | collective-permute-start | bytes 3145736 | tf_op jit(solution)/shard_map/ppermute | solution.py:31
  61.9 13.2 %collective-permute-start.10 = (bf16[256,640]{1,0:T(8,128)(2,1)S(1)}, bf16[256,640]{1,0:T(8,128)(2,1)S(1)}, u32[]{:S(2)}, u32[]{:S(2)}) collective-permute-start(bf16[256,640]{1,0:T(8,128)(2,1)S(1)} %collective-permute-done.9), channel_id=1, source_target_pairs={{0,4},{4,0},{8,12},{12,8},{16,20},{20,16},{24,28},{28,24},{1,5},{5... | collective-permute-start | bytes 983048 | tf_op jit(solution)/shard_map/ppermute | solution.py:31
  64.9 8.9 %collective-permute-start.11 = (bf16[256,640]{1,0:T(8,128)(2,1)S(1)}, bf16[256,640]{1,0:T(8,128)(2,1)S(1)}, u32[]{:S(2)}, u32[]{:S(2)}) collective-permute-start(bf16[256,640]{1,0:T(8,128)(2,1)S(1)} %collective-permute-done.9), channel_id=1, source_target_pairs={{0,8},{4,12},{8,16},{12,20},{16,24},{20,28},{24,0},{28,4},{1,9},{5... | collective-permute-start | bytes 983048 | tf_op jit(solution)/shard_map/ppermute | solution.py:60
  64.9 30.6 %collective-permute-start.5 = (bf16[256,2048]{1,0:T(8,128)(2,1)}, bf16[256,2048]{1,0:T(8,128)(2,1)}, u32[]{:S(2)}, u32[]{:S(2)}) collective-permute-start(bf16[256,2048]{1,0:T(8,128)(2,1)} %collective-permute-done.4), channel_id=1, source_target_pairs={{0,1},{1,0},{2,3},{3,2},{4,5},{5,4},{6,7},{7,6},{8,9},{9,8},{10,11... | collective-permute-start | bytes 3145736 | tf_op jit(solution)/shard_map/ppermute | solution.py:31
  65.0 45.5 %collective-permute-start.2 = (bf16[256,2048]{1,0:T(8,128)(2,1)}, bf16[256,2048]{1,0:T(8,128)(2,1)}, u32[]{:S(2)}, u32[]{:S(2)}) collective-permute-start(bf16[256,2048]{1,0:T(8,128)(2,1)} %collective-permute-done.1), channel_id=1, source_target_pairs={{0,1},{1,0},{2,3},{3,2},{4,5},{5,4},{6,7},{7,6},{8,9},{9,8},{10,11... | collective-permute-start | bytes 3145736 | tf_op jit(solution)/shard_map/ppermute | solution.py:31
  73.8 7.1 collective-permute-start.12
  87.8 48.5 %collective-permute-start.19 = (bf16[88,6144]{1,0:T(8,128)(2,1)}, bf16[88,6144]{1,0:T(8,128)(2,1)S(1)}, u32[]{:S(2)}, u32[]{:S(2)}) collective-permute-start(bf16[88,6144]{1,0:T(8,128)(2,1)} %pad_maximum_fusion.7), channel_id=1, source_target_pairs={{0,4},{4,0},{8,12},{12,8},{16,20},{20,16},{24,28},{28,24},{1,5},{5... | collective-permute-start | bytes 3244040 | tf_op jit(solution)/shard_map/ppermute | solution.py:31
  89.2 48.7 %collective-permute-start.20 = (bf16[88,6144]{1,0:T(8,128)(2,1)}, bf16[88,6144]{1,0:T(8,128)(2,1)}, u32[]{:S(2)}, u32[]{:S(2)}) collective-permute-start(bf16[88,6144]{1,0:T(8,128)(2,1)} %pad_maximum_fusion.7), channel_id=1, source_target_pairs={{0,8},{4,12},{8,16},{12,20},{16,24},{20,28},{24,0},{28,4},{1,9},{5... | collective-permute-start | bytes 3244040 | tf_op jit(solution)/shard_map/ppermute | solution.py:60
  90.6 635.9 %reduce-scatter.2.cloned.1.call-start = ((), (), s32[]{:S(2)}) async-start(), calls=%async_computation.4 | async-start | bytes 5406720 | tf_op jit(solution)/shard_map/reduce_scatter | solution.py:408
  108.8 32.8 %collective-permute-start.16 = (bf16[320,1024]{1,0:T(8,128)(2,1)S(1)}, bf16[320,1024]{1,0:T(8,128)(2,1)S(1)}, u32[]{:S(2)}, u32[]{:S(2)}) collective-permute-start(bf16[320,1024]{1,0:T(8,128)(2,1)S(1)} %get-tuple-element.37.o_ref), channel_id=1, source_target_pairs={{0,1},{1,0},{2,3},{3,2},{4,5},{5,4},{6,7},{7,6},{8,9},{9,8},{10,11... | collective-permute-start | bytes 1966088 | tf_op jit(solution)/shard_map/ppermute | solution.py:31
  108.9 32.8 %collective-permute-start.17 = (bf16[320,1024]{1,0:T(8,128)(2,1)S(1)}, bf16[320,1024]{1,0:T(8,128)(2,1)S(1)}, u32[]{:S(2)}, u32[]{:S(2)}) collective-permute-start(bf16[320,1024]{1,0:T(8,128)(2,1)S(1)} %get-tuple-element.37.o_ref), channel_id=1, source_target_pairs={{0,2},{1,3},{2,0},{3,1},{4,6},{5,7},{6,4},{7,5},{8,10},{9,11},{10,... | collective-permute-start | bytes 1966088 | tf_op jit(solution)/shard_map/ppermute | solution.py:31
  125.6 37.7 %collective-permute-start.13 = (bf16[320,1024]{1,0:T(8,128)(2,1)S(1)}, bf16[320,1024]{1,0:T(8,128)(2,1)S(1)}, u32[]{:S(2)}, u32[]{:S(2)}) collective-permute-start(bf16[320,1024]{1,0:T(8,128)(2,1)S(1)} %get-tuple-element.36.o_ref), channel_id=1, source_target_pairs={{0,1},{1,0},{2,3},{3,2},{4,5},{5,4},{6,7},{7,6},{8,9},{9,8},{10,11... | collective-permute-start | bytes 1966088 | tf_op jit(solution)/shard_map/ppermute | solution.py:31
  136.3 26.8 %collective-permute-start.14 = (bf16[320,1024]{1,0:T(8,128)(2,1)S(1)}, bf16[320,1024]{1,0:T(8,128)(2,1)S(1)}, u32[]{:S(2)}, u32[]{:S(2)}) collective-permute-start(bf16[320,1024]{1,0:T(8,128)(2,1)S(1)} %get-tuple-element.36.o_ref), channel_id=1, source_target_pairs={{0,2},{1,3},{2,0},{3,1},{4,6},{5,7},{6,4},{7,5},{8,10},{9,11},{10,... | collective-permute-start | bytes 1966088 | tf_op jit(solution)/shard_map/ppermute | solution.py:31
  137.9 69.8 %collective-permute-start.27 = (bf16[2,256,2048]{2,1,0:T(8,128)(2,1)}, bf16[2,256,2048]{2,1,0:T(8,128)(2,1)}, u32[]{:S(2)}, u32[]{:S(2)}) collective-permute-start(bf16[2,256,2048]{2,1,0:T(8,128)(2,1)} %param.18), channel_id=1, source_target_pairs={{0,2},{1,3},{2,0},{3,1},{4,6},{5,7},{6,4},{7,5},{8,10},{9,11},{10,... | collective-permute-start | bytes 6291464 | tf_op jit(solution)/shard_map/ppermute | solution.py:31
  141.6 100.6 %collective-permute-start.26 = (bf16[2,256,2048]{2,1,0:T(8,128)(2,1)}, bf16[2,256,2048]{2,1,0:T(8,128)(2,1)}, u32[]{:S(2)}, u32[]{:S(2)}) collective-permute-start(bf16[2,256,2048]{2,1,0:T(8,128)(2,1)} %param.18), channel_id=1, source_target_pairs={{0,1},{1,0},{2,3},{3,2},{4,5},{5,4},{6,7},{7,6},{8,9},{9,8},{10,11... | collective-permute-start | bytes 6291464 | tf_op jit(solution)/shard_map/ppermute | solution.py:31
  141.7 42.2 %collective-permute-start.22 = (bf16[88,6144]{1,0:T(8,128)(2,1)}, bf16[88,6144]{1,0:T(8,128)(2,1)}, u32[]{:S(2)}, u32[]{:S(2)}) collective-permute-start(bf16[88,6144]{1,0:T(8,128)(2,1)} %collective-permute-done.20), channel_id=1, source_target_pairs={{0,8},{4,12},{8,16},{12,20},{16,24},{20,28},{24,0},{28,4},{1,9},{5... | collective-permute-start | bytes 3244040 | tf_op jit(solution)/shard_map/ppermute | solution.py:60
  163.2 2.1 collective-permute-start.18
  163.3 3.2 collective-permute-start.15
  165.3 42.4 %collective-permute-start.21 = (bf16[88,6144]{1,0:T(8,128)(2,1)}, bf16[88,6144]{1,0:T(8,128)(2,1)}, u32[]{:S(2)}, u32[]{:S(2)}) collective-permute-start(bf16[88,6144]{1,0:T(8,128)(2,1)} %collective-permute-done.20), channel_id=1, source_target_pairs={{0,4},{4,0},{8,12},{12,8},{16,20},{20,16},{24,28},{28,24},{1,5},{5... | collective-permute-start | bytes 3244040 | tf_op jit(solution)/shard_map/ppermute | solution.py:31
  183.8 27.9 %collective-permute-start.24 = (bf16[88,6144]{1,0:T(8,128)(2,1)}, bf16[88,6144]{1,0:T(8,128)(2,1)}, u32[]{:S(2)}, u32[]{:S(2)}) collective-permute-start(bf16[88,6144]{1,0:T(8,128)(2,1)} %collective-permute-done.22), channel_id=1, source_target_pairs={{0,8},{4,12},{8,16},{12,20},{16,24},{20,28},{24,0},{28,4},{1,9},{5... | collective-permute-start | bytes 3244040 | tf_op jit(solution)/shard_map/ppermute | solution.py:60
  192.1 26.9 %collective-permute-start.23 = (bf16[88,6144]{1,0:T(8,128)(2,1)}, bf16[88,6144]{1,0:T(8,128)(2,1)S(1)}, u32[]{:S(2)}, u32[]{:S(2)}) collective-permute-start(bf16[88,6144]{1,0:T(8,128)(2,1)} %collective-permute-done.22), channel_id=1, source_target_pairs={{0,4},{4,0},{8,12},{12,8},{16,20},{20,16},{24,28},{28,24},{1,5},{5... | collective-permute-start | bytes 3244040 | tf_op jit(solution)/shard_map/ppermute | solution.py:31
  207.7 34.6 %collective-permute-start.28 = (bf16[2,256,2048]{2,1,0:T(8,128)(2,1)}, bf16[2,256,2048]{2,1,0:T(8,128)(2,1)S(1)}, u32[]{:S(2)}, u32[]{:S(2)}) collective-permute-start(bf16[2,256,2048]{2,1,0:T(8,128)(2,1)} %collective-permute-done.27), channel_id=1, source_target_pairs={{0,1},{1,0},{2,3},{3,2},{4,5},{5,4},{6,7},{7,6},{8,9},{9,8},{10,11... | collective-permute-start | bytes 6291464 | tf_op jit(solution)/shard_map/ppermute | solution.py:31
  211.7 29.5 %collective-permute-start.25 = (bf16[88,6144]{1,0:T(8,128)(2,1)}, bf16[88,6144]{1,0:T(8,128)(2,1)S(1)}, u32[]{:S(2)}, u32[]{:S(2)}) collective-permute-start(bf16[88,6144]{1,0:T(8,128)(2,1)} %collective-permute-done.24), channel_id=1, source_target_pairs={{0,4},{4,0},{8,12},{12,8},{16,20},{20,16},{24,28},{28,24},{1,5},{5... | collective-permute-start | bytes 3244040 | tf_op jit(solution)/shard_map/ppermute | solution.py:31
  364.1 10.1 %collective-permute-start.30 = (bf16[2,256,2048]{2,1,0:T(8,128)(2,1)S(1)}, bf16[2,256,2048]{2,1,0:T(8,128)(2,1)S(1)}, u32[]{:S(2)}, u32[]{:S(2)}) collective-permute-start(bf16[2,256,2048]{2,1,0:T(8,128)(2,1)S(1)} %get-tuple-element.86), channel_id=1, source_target_pairs={{0,1},{1,0},{2,3},{3,2},{4,5},{5,4},{6,7},{7,6},{8,9},{9,8},{10,11... | collective-permute-start | bytes 6291464 | tf_op jit(solution)/shard_map/ppermute | solution.py:31
  364.1 20.9 %collective-permute-start.29 = (bf16[2,256,2048]{2,1,0:T(8,128)(2,1)}, bf16[2,256,2048]{2,1,0:T(8,128)(2,1)}, u32[]{:S(2)}, u32[]{:S(2)}) collective-permute-start(bf16[2,256,2048]{2,1,0:T(8,128)(2,1)} %get-tuple-element.85), channel_id=1, source_target_pairs={{0,1},{1,0},{2,3},{3,2},{4,5},{5,4},{6,7},{7,6},{8,9},{9,8},{10,11... | collective-permute-start | bytes 6291464 | tf_op jit(solution)/shard_map/ppermute | solution.py:31
  376.6 47.9 %collective-permute-start.31 = (bf16[2,256,2048]{2,1,0:T(8,128)(2,1)}, bf16[2,256,2048]{2,1,0:T(8,128)(2,1)}, u32[]{:S(2)}, u32[]{:S(2)}) collective-permute-start(bf16[2,256,2048]{2,1,0:T(8,128)(2,1)} %fusion.22), channel_id=1, source_target_pairs={{0,2},{1,3},{2,0},{3,1},{4,6},{5,7},{6,4},{7,5},{8,10},{9,11},{10,... | collective-permute-start | bytes 6291464 | tf_op jit(solution)/shard_map/ppermute | solution.py:31
  430.1 146.4 %collective-permute-start.54 = (bf16[88,6144]{1,0:T(8,128)(2,1)}, bf16[88,6144]{1,0:T(8,128)(2,1)}, u32[]{:S(2)}, u32[]{:S(2)}) collective-permute-start(bf16[88,6144]{1,0:T(8,128)(2,1)} %get-tuple-element.76), channel_id=1, source_target_pairs={{0,4},{4,0},{8,12},{12,8},{16,20},{20,16},{24,28},{28,24},{1,5},{5... | collective-permute-start | bytes 3244040 | tf_op jit(solution)/shard_map/ppermute | solution.py:31
  430.9 186.8 %collective-permute-start.53 = (bf16[88,6144]{1,0:T(8,128)(2,1)}, bf16[88,6144]{1,0:T(8,128)(2,1)}, u32[]{:S(2)}, u32[]{:S(2)}) collective-permute-start(bf16[88,6144]{1,0:T(8,128)(2,1)} %get-tuple-element.77), channel_id=1, source_target_pairs={{0,4},{4,0},{8,12},{12,8},{16,20},{20,16},{24,28},{28,24},{1,5},{5... | collective-permute-start | bytes 3244040 | tf_op jit(solution)/shard_map/ppermute | solution.py:31
  449.9 15.6 %collective-permute-start.35 = (bf16[320,512]{1,0:T(8,128)(2,1)S(1)}, bf16[320,512]{1,0:T(8,128)(2,1)S(1)}, u32[]{:S(2)}, u32[]{:S(2)}) collective-permute-start(bf16[320,512]{1,0:T(8,128)(2,1)S(1)} %get-tuple-element.100), channel_id=1, source_target_pairs={{0,1},{1,0},{2,3},{3,2},{4,5},{5,4},{6,7},{7,6},{8,9},{9,8},{10,11... | collective-permute-start | bytes 983048 | tf_op jit(solution)/shard_map/ppermute | solution.py:31
  450.0 15.6 %collective-permute-start.36 = (bf16[320,512]{1,0:T(8,128)(2,1)S(1)}, bf16[320,512]{1,0:T(8,128)(2,1)S(1)}, u32[]{:S(2)}, u32[]{:S(2)}) collective-permute-start(bf16[320,512]{1,0:T(8,128)(2,1)S(1)} %get-tuple-element.99), channel_id=1, source_target_pairs={{0,2},{1,3},{2,0},{3,1},{4,6},{5,7},{6,4},{7,5},{8,10},{9,11},{10,... | collective-permute-start | bytes 983048 | tf_op jit(solution)/shard_map/ppermute | solution.py:31
  450.9 26.3 %collective-permute-start.37 = (bf16[320,512]{1,0:T(8,128)(2,1)S(1)}, bf16[320,512]{1,0:T(8,128)(2,1)S(1)}, u32[]{:S(2)}, u32[]{:S(2)}) collective-permute-start(bf16[320,512]{1,0:T(8,128)(2,1)S(1)} %get-tuple-element.98), channel_id=1, source_target_pairs={{0,3},{1,2},{2,1},{3,0},{4,7},{5,6},{6,5},{7,4},{8,11},{9,10},{10,... | collective-permute-start | bytes 983048 | tf_op jit(solution)/shard_map/ppermute | solution.py:31
  551.4 12.4 %collective-permute-start.47 = (bf16[256,640]{1,0:T(8,128)(2,1)S(1)}, bf16[256,640]{1,0:T(8,128)(2,1)S(1)}, u32[]{:S(2)}, u32[]{:S(2)}) collective-permute-start(bf16[256,640]{1,0:T(8,128)(2,1)S(1)} %get-tuple-element.92), channel_id=1, source_target_pairs={{0,4},{4,0},{8,12},{12,8},{16,20},{20,16},{24,28},{28,24},{1,5},{5... | collective-permute-start | bytes 983048 | tf_op jit(solution)/shard_map/ppermute | solution.py:31
  553.1 19.5 %collective-permute-start.46 = (bf16[256,640]{1,0:T(8,128)(2,1)S(1)}, bf16[256,640]{1,0:T(8,128)(2,1)S(1)}, u32[]{:S(2)}, u32[]{:S(2)}) collective-permute-start(bf16[256,640]{1,0:T(8,128)(2,1)S(1)} %get-tuple-element.93), channel_id=1, source_target_pairs={{0,4},{4,0},{8,12},{12,8},{16,20},{20,16},{24,28},{28,24},{1,5},{5... | collective-permute-start | bytes 983048 | tf_op jit(solution)/shard_map/ppermute | solution.py:31
  553.5 27.5 %collective-permute-start.45 = (bf16[256,640]{1,0:T(8,128)(2,1)S(1)}, bf16[256,640]{1,0:T(8,128)(2,1)S(1)}, u32[]{:S(2)}, u32[]{:S(2)}) collective-permute-start(bf16[256,640]{1,0:T(8,128)(2,1)S(1)} %get-tuple-element.94), channel_id=1, source_target_pairs={{0,4},{4,0},{8,12},{12,8},{16,20},{20,16},{24,28},{28,24},{1,5},{5... | collective-permute-start | bytes 983048 | tf_op jit(solution)/shard_map/ppermute | solution.py:31
  563.9 12.5 %collective-permute-start.48 = (bf16[256,640]{1,0:T(8,128)(2,1)S(1)}, bf16[256,640]{1,0:T(8,128)(2,1)S(1)}, u32[]{:S(2)}, u32[]{:S(2)}) collective-permute-start(bf16[256,640]{1,0:T(8,128)(2,1)S(1)} %fusion.38), channel_id=1, source_target_pairs={{0,8},{4,12},{8,16},{12,20},{16,24},{20,28},{24,0},{28,4},{1,9},{5... | collective-permute-start | bytes 983048 | tf_op jit(solution)/shard_map/ppermute | solution.py:60
  572.6 17.6 %collective-permute-start.39 = (bf16[256,2048]{1,0:T(8,128)(2,1)S(1)}, bf16[256,2048]{1,0:T(8,128)(2,1)S(1)}, u32[]{:S(2)}, u32[]{:S(2)}) collective-permute-start(bf16[256,2048]{1,0:T(8,128)(2,1)S(1)} %get-tuple-element.88), channel_id=1, source_target_pairs={{0,1},{1,0},{2,3},{3,2},{4,5},{5,4},{6,7},{7,6},{8,9},{9,8},{10,11... | collective-permute-start | bytes 3145736 | tf_op jit(solution)/shard_map/ppermute | solution.py:31
  576.4 28.9 %collective-permute-start.42 = (bf16[256,2048]{1,0:T(8,128)(2,1)}, bf16[256,2048]{1,0:T(8,128)(2,1)}, u32[]{:S(2)}, u32[]{:S(2)}) collective-permute-start(bf16[256,2048]{1,0:T(8,128)(2,1)} %get-tuple-element.90), channel_id=1, source_target_pairs={{0,1},{1,0},{2,3},{3,2},{4,5},{5,4},{6,7},{7,6},{8,9},{9,8},{10,11... | collective-permute-start | bytes 3145736 | tf_op jit(solution)/shard_map/ppermute | solution.py:31
  576.5 12.0 %collective-permute-start.49 = (bf16[256,640]{1,0:T(8,128)(2,1)S(1)}, bf16[256,640]{1,0:T(8,128)(2,1)S(1)}, u32[]{:S(2)}, u32[]{:S(2)}) collective-permute-start(bf16[256,640]{1,0:T(8,128)(2,1)S(1)} %fusion.40), channel_id=1, source_target_pairs={{0,8},{4,12},{8,16},{12,20},{16,24},{20,28},{24,0},{28,4},{1,9},{5... | collective-permute-start | bytes 983048 | tf_op jit(solution)/shard_map/ppermute | solution.py:60
  581.1 34.0 %collective-permute-start.33 = (bf16[2,256,2048]{2,1,0:T(8,128)(2,1)}, bf16[2,256,2048]{2,1,0:T(8,128)(2,1)S(1)}, u32[]{:S(2)}, u32[]{:S(2)}) collective-permute-start(bf16[2,256,2048]{2,1,0:T(8,128)(2,1)} %get-tuple-element.84), channel_id=1, source_target_pairs={{0,1},{1,0},{2,3},{3,2},{4,5},{5,4},{6,7},{7,6},{8,9},{9,8},{10,11... | collective-permute-start | bytes 6291464 | tf_op jit(solution)/shard_map/ppermute | solution.py:31
  588.5 9.3 %collective-permute-start.44 = (bf16[256,640]{1,0:T(8,128)(2,1)S(1)}, bf16[256,640]{1,0:T(8,128)(2,1)S(1)}, u32[]{:S(2)}, u32[]{:S(2)}) collective-permute-start(bf16[256,640]{1,0:T(8,128)(2,1)S(1)} %get-tuple-element.91), channel_id=1, source_target_pairs={{0,4},{4,0},{8,12},{12,8},{16,20},{20,16},{24,28},{28,24},{1,5},{5... | collective-permute-start | bytes 983048 | tf_op jit(solution)/shard_map/ppermute | solution.py:31
  590.2 10.8 %collective-permute-start.50 = (bf16[256,640]{1,0:T(8,128)(2,1)S(1)}, bf16[256,640]{1,0:T(8,128)(2,1)S(1)}, u32[]{:S(2)}, u32[]{:S(2)}) collective-permute-start(bf16[256,640]{1,0:T(8,128)(2,1)S(1)} %fusion.42), channel_id=1, source_target_pairs={{0,8},{4,12},{8,16},{12,20},{16,24},{20,28},{24,0},{28,4},{1,9},{5... | collective-permute-start | bytes 983048 | tf_op jit(solution)/shard_map/ppermute | solution.py:60
  597.8 72.8 %collective-permute-start.52 = (bf16[88,6144]{1,0:T(8,128)(2,1)}, bf16[88,6144]{1,0:T(8,128)(2,1)}, u32[]{:S(2)}, u32[]{:S(2)}) collective-permute-start(bf16[88,6144]{1,0:T(8,128)(2,1)} %get-tuple-element.78), channel_id=1, source_target_pairs={{0,4},{4,0},{8,12},{12,8},{16,20},{20,16},{24,28},{28,24},{1,5},{5... | collective-permute-start | bytes 3244040 | tf_op jit(solution)/shard_map/ppermute | solution.py:31
  601.0 37.1 %collective-permute-start.38 = (bf16[256,2048]{1,0:T(8,128)(2,1)}, bf16[256,2048]{1,0:T(8,128)(2,1)}, u32[]{:S(2)}, u32[]{:S(2)}) collective-permute-start(bf16[256,2048]{1,0:T(8,128)(2,1)} %get-tuple-element.87), channel_id=1, source_target_pairs={{0,1},{1,0},{2,3},{3,2},{4,5},{5,4},{6,7},{7,6},{8,9},{9,8},{10,11... | collective-permute-start | bytes 3145736 | tf_op jit(solution)/shard_map/ppermute | solution.py:31
  601.9 10.6 %all-to-all-start.1 = ((bf16[4,64,640]{2,1,0:T(8,128)(2,1)}), bf16[4,64,640]{2,1,0:T(8,128)(2,1)S(1)}, u32[]{:S(2)}, u32[]{:S(2)}) async-start(bf16[4,64,640]{2,1,0:T(8,128)(2,1)} %bitcast.80), calls=%async_computation.1 | async-start | bytes 655360 | tf_op jit(solution)/shard_map/all_to_all | solution.py:451
  605.3 28.4 %collective-permute-start.55 = (bf16[88,6144]{1,0:T(8,128)(2,1)}, bf16[88,6144]{1,0:T(8,128)(2,1)}, u32[]{:S(2)}, u32[]{:S(2)}) collective-permute-start(bf16[88,6144]{1,0:T(8,128)(2,1)} %add_convert_fusion.4), channel_id=1, source_target_pairs={{0,8},{4,12},{8,16},{12,20},{16,24},{20,28},{24,0},{28,4},{1,9},{5... | collective-permute-start | bytes 3244040 | tf_op jit(solution)/shard_map/ppermute | solution.py:60
  615.1 30.7 %collective-permute-start.41 = (bf16[256,2048]{1,0:T(8,128)(2,1)}, bf16[256,2048]{1,0:T(8,128)(2,1)S(1)}, u32[]{:S(2)}, u32[]{:S(2)}) collective-permute-start(bf16[256,2048]{1,0:T(8,128)(2,1)} %get-tuple-element.89), channel_id=1, source_target_pairs={{0,1},{1,0},{2,3},{3,2},{4,5},{5,4},{6,7},{7,6},{8,9},{9,8},{10,11... | collective-permute-start | bytes 3145736 | tf_op jit(solution)/shard_map/ppermute | solution.py:31
  617.7 26.0 %collective-permute-start.40 = (bf16[256,2048]{1,0:T(8,128)(2,1)S(1)}, bf16[256,2048]{1,0:T(8,128)(2,1)S(1)}, u32[]{:S(2)}, u32[]{:S(2)}) collective-permute-start(bf16[256,2048]{1,0:T(8,128)(2,1)S(1)} %copy-done.39), channel_id=1, source_target_pairs={{0,2},{1,3},{2,0},{3,1},{4,6},{5,7},{6,4},{7,5},{8,10},{9,11},{10,... | collective-permute-start | bytes 3145736 | tf_op jit(solution)/shard_map/ppermute | solution.py:31
  633.8 32.4 %collective-permute-start.43 = (bf16[256,2048]{1,0:T(8,128)(2,1)S(1)}, bf16[256,2048]{1,0:T(8,128)(2,1)S(1)}, u32[]{:S(2)}, u32[]{:S(2)}) collective-permute-start(bf16[256,2048]{1,0:T(8,128)(2,1)S(1)} %copy-done.40), channel_id=1, source_target_pairs={{0,2},{1,3},{2,0},{3,1},{4,6},{5,7},{6,4},{7,5},{8,10},{9,11},{10,... | collective-permute-start | bytes 3145736 | tf_op jit(solution)/shard_map/ppermute | solution.py:31
  638.1 78.2 %collective-permute-start.51 = (bf16[88,6144]{1,0:T(8,128)(2,1)S(1)}, bf16[88,6144]{1,0:T(8,128)(2,1)S(1)}, u32[]{:S(2)}, u32[]{:S(2)}) collective-permute-start(bf16[88,6144]{1,0:T(8,128)(2,1)S(1)} %copy-done.38), channel_id=1, source_target_pairs={{0,4},{4,0},{8,12},{12,8},{16,20},{20,16},{24,28},{28,24},{1,5},{5... | collective-permute-start | bytes 3244040 | tf_op jit(solution)/shard_map/ppermute | solution.py:31
  643.7 55.7 %collective-permute-start.32 = (bf16[2,256,2048]{2,1,0:T(8,128)(2,1)S(1)}, bf16[2,256,2048]{2,1,0:T(8,128)(2,1)S(1)}, u32[]{:S(2)}, u32[]{:S(2)}) collective-permute-start(bf16[2,256,2048]{2,1,0:T(8,128)(2,1)S(1)} %copy-done.37), channel_id=1, source_target_pairs={{0,1},{1,0},{2,3},{3,2},{4,5},{5,4},{6,7},{7,6},{8,9},{9,8},{10,11... | collective-permute-start | bytes 6291464 | tf_op jit(solution)/shard_map/ppermute | solution.py:31
  645.8 64.9 %collective-permute-start.34 = (bf16[2,256,2048]{2,1,0:T(8,128)(2,1)S(1)}, bf16[2,256,2048]{2,1,0:T(8,128)(2,1)S(1)}, u32[]{:S(2)}, u32[]{:S(2)}) collective-permute-start(bf16[2,256,2048]{2,1,0:T(8,128)(2,1)S(1)} %fusion.20), channel_id=1, source_target_pairs={{0,2},{1,3},{2,0},{3,1},{4,6},{5,7},{6,4},{7,5},{8,10},{9,11},{10,... | collective-permute-start | bytes 6291464 | tf_op jit(solution)/shard_map/ppermute | solution.py:31
  666.2 27.1 %collective-permute-start.56 = (bf16[88,6144]{1,0:T(8,128)(2,1)S(1)}, bf16[88,6144]{1,0:T(8,128)(2,1)S(1)}, u32[]{:S(2)}, u32[]{:S(2)}) collective-permute-start(bf16[88,6144]{1,0:T(8,128)(2,1)S(1)} %add_convert_fusion.3), channel_id=1, source_target_pairs={{0,8},{4,12},{8,16},{12,20},{16,24},{20,28},{24,0},{28,4},{1,9},{5... | collective-permute-start | bytes 3244040 | tf_op jit(solution)/shard_map/ppermute | solution.py:60
  696.2 26.3 %collective-permute-start.57 = (bf16[88,6144]{1,0:T(8,128)(2,1)}, bf16[88,6144]{1,0:T(8,128)(2,1)}, u32[]{:S(2)}, u32[]{:S(2)}) collective-permute-start(bf16[88,6144]{1,0:T(8,128)(2,1)} %add_convert_fusion.2), channel_id=1, source_target_pairs={{0,8},{4,12},{8,16},{12,20},{16,24},{20,28},{24,0},{28,4},{1,9},{5... | collective-permute-start | bytes 3244040 | tf_op jit(solution)/shard_map/ppermute | solution.py:60
  (74 other events, 1047.2 us)
Sparse Core Ops, SparseCore 0:
  90.8 88.7 all-gather.1
  442.3 146.0 reduce-scatter.1

commit v3 on v2

--- a/solution.py
+++ b/solution.py
@@ -15,6 +15,7 @@
 EPS = 1e-06
 ROPE_BASE = 10000.0
 WEIGHT_UNIT = 8.0
+MESH = pl.DeviceIdType.MESH
 BF = jnp.bfloat16
 F32 = jnp.float32
 
@@ -31,8 +32,7 @@
     return lax.ppermute(v, axis, [(i, i ^ bit) for i in range(n)])
 
 
-def after(v, *marks):
-    return lax.optimization_barrier((v,) + marks)[0]
+tie = lax.optimization_barrier
 
 
 def gather_seq(v, n_seq):
@@ -45,39 +45,421 @@
     return [slots[order.index(j)] for j in range(n_seq)]
 
 
-def scatter_seq(slots, n_seq):
+def fold_seq(slots, n_seq):
     bit = 1
     live = dict(enumerate(slots))
-    while bit < n_seq:
+    while bit < n_seq // 2:
         keep = [j for j in live if not j & bit]
         sent = {j: swap(live[j | bit].astype(BF), "seq", n_seq, bit) for j in keep}
         live = {j: live[j].astype(F32) + sent[j].astype(F32) for j in keep}
         bit *= 2
-    return live[0]
-
-
-def ring(v, n_rows):
-    return lax.ppermute(v, "rows", [(r, (r + 2) % n_rows) for r in range(n_rows)])
-
-
-def gather_rows(v, n_rows):
-    slots, held = [], v
-    for i in range(n_rows // 2):
-        if i:
-            held = ring(held, n_rows)
-        slots += [held, swap(held, "rows", n_rows, 1)]
-    return slots
-
-
-def scatter_rows(slots, n_rows):
-    count = n_rows // 2
-    total = None
-    for i in list(range(1, count)) + [0]:
-        part = slots[2 * i].astype(F32) + swap(slots[2 * i + 1], "rows", n_rows, 1).astype(F32)
-        if total is not None:
-            part = part + total.astype(F32)
-        total = ring(part.astype(BF), n_rows) if i else part
-    return total
+    return live[0], live[n_seq // 2].astype(BF)
+
+
+def cross_seq(v, n_seq):
+    return swap(v, "seq", n_seq, n_seq // 2)
+
+
+def flipped(v, bit):
+    return v + bit - 2 * bit * lax.rem(lax.div(v, bit), 2)
+
+
+def other(me, j, n_seq):
+    bit = 1
+    while bit < n_seq:
+        if j & bit:
+            me = flipped(me, bit)
+        bit *= 2
+    return me
+
+
+def greet(me, r, n_seq, n_rows):
+    a, b = lax.div(r, 2), lax.rem(r, 2)
+    half = n_rows // 2
+    up, down = 2 * lax.rem(a + 1, half) + b, 2 * lax.rem(a + half - 1, half) + b
+    beside = 2 * a + 1 - b
+    barrier = pltpu.get_barrier_semaphore()
+    for j in range(1, n_seq):
+        pl.semaphore_signal(
+            barrier, inc=1, device_id={"seq": other(me, j, n_seq)}, device_id_type=MESH
+        )
+    for peer in (up, down, beside):
+        pl.semaphore_signal(barrier, inc=1, device_id={"rows": peer}, device_id_type=MESH)
+    pl.semaphore_wait(barrier, n_seq + 2)
+    return up, beside
+
+
+def opening(
+    n_seq, n_rows, tokens, pieces, out_w, x_all, whole, wo,
+    kept_sem, swap_send, swap_recv, tok_send, tok_recv, ring_send, ring_recv, near_send, near_recv,
+):
+    me, r = lax.axis_index("seq"), lax.axis_index("rows")
+    a, b = lax.div(r, 2), lax.rem(r, 2)
+    half, top = n_rows // 2, n_seq // 2
+    rows, span, _ = tokens.shape
+    local = pieces.shape[1]
+    block = n_seq * local
+    up, beside = greet(me, r, n_seq, n_rows)
+    low, high = flipped(me, 1), flipped(me, top)
+    mine_low, mine_top = lax.rem(me, 2), lax.div(me, 2)
+
+    def send(src, dst, send_sem, recv_sem, **where):
+        copy = pltpu.make_async_remote_copy(
+            src_ref=src, dst_ref=dst, send_sem=send_sem, recv_sem=recv_sem,
+            device_id=where, device_id_type=MESH,
+        )
+        copy.start()
+        return copy
+
+    mine = whole.at[pl.ds(pl.multiple_of(r * block + me * local, local), local)]
+    kept = [
+        pltpu.make_async_copy(pieces.at[me], mine, kept_sem.at[0]),
+        pltpu.make_async_copy(out_w, wo.at[r, mine_low, mine_top], kept_sem.at[1]),
+        pltpu.make_async_copy(tokens, x_all.at[:, pl.ds(0, span)], kept_sem.at[2]),
+    ]
+    for copy in kept:
+        copy.start()
+    swaps = [
+        send(pieces.at[other(me, j, n_seq)], mine, swap_send.at[j], swap_recv.at[j], seq=other(me, j, n_seq))
+        for j in range(1, n_seq)
+    ]
+    swaps.append(send(out_w, wo.at[r, mine_low, mine_top], swap_send.at[0], swap_recv.at[0], seq=high))
+
+    def slot(j):
+        return pl.ds(j * span, span)
+
+    far = [
+        send(tokens.at[t], x_all.at[t, slot(top)], tok_send.at[t, top], tok_recv.at[t, top], seq=high)
+        for t in range(rows)
+    ]
+    near = [
+        send(tokens.at[t], x_all.at[t, slot(1)], tok_send.at[t, 1], tok_recv.at[t, 1], seq=low)
+        for t in range(rows)
+    ]
+    ring = {}
+    sides = []
+    out_near = []
+
+    def pass_on(i, kind):
+        owner = 2 * lax.rem(a + half - i, half) + b
+        ref = whole.at[pl.ds(pl.multiple_of(owner * block, block), block)] if kind == 0 else wo.at[owner, mine_low]
+        if i < half - 1:
+            ring[(kind, i)] = send(ref, ref, ring_send.at[0, kind, i], ring_recv.at[0, kind, i], rows=up)
+        sides.append((kind, i, send(ref, ref, ring_send.at[1, kind, i], ring_recv.at[1, kind, i], rows=beside)))
+        if kind == 1:
+            out_near.append(send(ref, ref, near_send.at[0, i], near_recv.at[0, i], seq=low))
+
+    def forward_tokens(t):
+        far[t].wait_recv()
+        near.append(
+            send(x_all.at[t, slot(top)], x_all.at[t, slot(top + 1)], tok_send.at[t, 0], tok_recv.at[t, 0], seq=low)
+        )
+
+    kept[0].wait()
+    for copy in swaps[:-1]:
+        copy.wait_recv()
+    pass_on(0, 0)
+    kept[1].wait()
+    swaps[-1].wait_recv()
+    pass_on(0, 1)
+    late = list(range(rows))
+    for i in range(1, half):
+        for kind in range(2):
+            ring[(kind, i - 1)].wait_recv()
+            pass_on(i, kind)
+        if i >= half - 2 and len(late) > 1:
+            forward_tokens(late.pop(0))
+    for t in late:
+        forward_tokens(t)
+    for kind, i, copy in sides:
+        copy.wait_recv()
+        if kind == 1:
+            owner = 2 * lax.rem(a + half - i, half) + 1 - b
+            ref = wo.at[owner, mine_low]
+            out_near.append(send(ref, ref, near_send.at[1, i], near_recv.at[1, i], seq=low))
+    kept[2].wait()
+    for copy in near + out_near:
+        copy.wait_recv()
+    for copy in swaps + far + near + list(ring.values()) + [c for _, _, c in sides] + out_near:
+        copy.wait_send()
+
+
+def open_layer(n_seq, n_rows, tokens, pieces, out_w):
+    rows, span, width = tokens.shape
+    _, local, cols = pieces.shape
+    half = n_rows // 2
+    hbm = pl.BlockSpec(memory_space=pl.ANY)
+    dma = pltpu.SemaphoreType.DMA
+    return pl.pallas_call(
+        functools.partial(opening, n_seq, n_rows),
+        out_shape=(
+            jax.ShapeDtypeStruct((rows, n_seq * span, width), BF),
+            jax.ShapeDtypeStruct((n_rows * n_seq * local, cols), BF),
+            jax.ShapeDtypeStruct((n_rows, n_seq // 2, 2) + out_w.shape, BF),
+        ),
+        in_specs=[hbm] * 3,
+        out_specs=(hbm,) * 3,
+        scratch_shapes=[
+            dma((3,)),
+            dma((n_seq,)),
+            dma((n_seq,)),
+            dma((rows, n_seq)),
+            dma((rows, n_seq)),
+            dma((2, 2, half)),
+            dma((2, 2, half)),
+            dma((2, half)),
+            dma((2, half)),
+        ],
+        compiler_params=pltpu.CompilerParams(collective_id=0, has_side_effects=True),
+        name="opening",
+    )(tokens, pieces, out_w)
+
+
+def meeting(n_seq, n_rows, *refs):
+    rows = (len(refs) - 8) // 1
+    o, (o_all, kept_sem, far_s, far_r, near_s, near_r, on_s, on_r) = refs[:rows], refs[rows:]
+    me, r = lax.axis_index("seq"), lax.axis_index("rows")
+    greet(me, r, n_seq, n_rows)
+    top = n_seq // 2
+    length = o[0].shape[1]
+    span = length // n_seq
+    low, high = flipped(me, 1), flipped(me, top)
+
+    def send(src, dst, send_sem, recv_sem, where):
+        copy = pltpu.make_async_remote_copy(
+            src_ref=src, dst_ref=dst, send_sem=send_sem, recv_sem=recv_sem,
+            device_id={"seq": where}, device_id_type=MESH,
+        )
+        copy.start()
+        return copy
+
+    def place(who, t, j, count=1):
+        return o_all.at[who, :, pl.ds(t * length + j * span, count * span)]
+
+    far, near, kept = [], [], []
+    for t in range(rows):
+        for j in range(0, n_seq, top):
+            far.append(
+                send(
+                    o[t].at[:, pl.ds((j ^ top) * span, top * span)], place(me, t, j, top),
+                    far_s.at[t, j], far_r.at[t, j], high,
+                )
+            )
+    for t in range(rows):
+        for j in range(n_seq):
+            near.append(
+                send(o[t].at[:, pl.ds((j ^ 1) * span, span)], place(me, t, j), near_s.at[t, j], near_r.at[t, j], low)
+            )
+        kept.append(pltpu.make_async_copy(o[t], place(me, t, 0, n_seq), kept_sem.at[t]))
+        kept[-1].start()
+    for t in range(rows):
+        for c, j in enumerate(range(0, n_seq, top)):
+            far[2 * t + c].wait_recv()
+            for k in range(j, j + top):
+                near.append(send(place(high, t, k), place(high, t, k ^ 1), on_s.at[t, k], on_r.at[t, k], low))
+    for copy in kept:
+        copy.wait()
+    for copy in near:
+        copy.wait_recv()
+    for copy in far + near:
+        copy.wait_send()
+
+
+def meet(n_seq, n_rows, o):
+    columns, length = o[0].shape
+    rows = len(o)
+    hbm = pl.BlockSpec(memory_space=pl.ANY)
+    dma = pltpu.SemaphoreType.DMA
+    return pl.pallas_call(
+        functools.partial(meeting, n_seq, n_rows),
+        out_shape=jax.ShapeDtypeStruct((n_seq, columns, rows * length), BF),
+        in_specs=[hbm] * rows,
+        out_specs=hbm,
+        scratch_shapes=[dma((rows,))] + [dma((rows, n_seq))] * 6,
+        compiler_params=pltpu.CompilerParams(collective_id=2, has_side_effects=True),
+        name="meeting",
+    )(*o)
+
+
+def add_rows(out, *terms):
+    rows = out.shape[0]
+    tile = min(32, rows)
+
+    @pl.loop(0, rows // tile)
+    def _(i):
+        at = pl.ds(pl.multiple_of(i * tile, tile), tile)
+        total = terms[0][at, :].astype(F32)
+        for term in terms[1:]:
+            total = total + term[at, :].astype(F32)
+        out[at, :] = total.astype(out.dtype)
+
+
+def closing(
+    n_seq, n_rows, da, dw, do, da_out, dw_out, do_out,
+    da_near, da_send, da_far, da_own, dw_near, dw_send, dw_far, dw_own, do_near, do_sum, do_next,
+    do_send, do_far, do_own, do_last, near_s, near_r, far_s, far_r, ring_s, ring_r, end_s, end_r,
+):
+    me, r = lax.axis_index("seq"), lax.axis_index("rows")
+    up, beside = greet(me, r, n_seq, n_rows)
+    a, b = lax.div(r, 2), lax.rem(r, 2)
+    half, top = n_rows // 2, n_seq // 2
+    rows = da.shape[0]
+    local = do.shape[1]
+
+    def send(src, dst, send_sem, recv_sem, **where):
+        copy = pltpu.make_async_remote_copy(
+            src_ref=src, dst_ref=dst, send_sem=send_sem, recv_sem=recv_sem,
+            device_id=where, device_id_type=MESH,
+        )
+        copy.start()
+        return copy
+
+    def owner(i, j):
+        return 2 * lax.rem(a + half - i, half) + (b if j == 0 else 1 - b)
+
+    low = flipped(me, 1)
+    high = flipped(me, top)
+    order = list(range(1, half)) + [0]
+    near_da = [
+        [send(da.at[t, k + 1], da_near.at[t, k // top], near_s.at[t, k // top], near_r.at[t, k // top], seq=low)
+         for t in range(rows)]
+        for k in (top, 0)
+    ]
+    side_dw = [
+        send(dw.at[owner(i, 1)], dw_near.at[i], ring_s.at[0, 0, i], ring_r.at[0, 0, i], rows=beside)
+        for i in order
+    ]
+    near_do = []
+    for c, k in enumerate((top, 0)):
+        whose = other(me, k + 1, n_seq)
+        for j in range(n_rows):
+            near_do.append(
+                send(do.at[j * n_seq + whose], do_near.at[c, j], near_s.at[rows + c, j], near_r.at[rows + c, j], seq=low)
+            )
+    far_da = []
+    for t in range(rows):
+        near_da[0][t].wait_recv()
+        add_rows(da_send.at[t], da.at[t, top], da_near.at[t, 1])
+        far_da.append(send(da_send.at[t], da_far.at[t], far_s.at[t], far_r.at[t], seq=high))
+
+    def ring_step(kind, n, i, near, mine, far, out, final, side):
+        side.wait_recv()
+        terms = (mine, near) if n == 0 else (mine, near, far.at[n - 1])
+        if i == 0:
+            add_rows(final, *terms)
+            return None
+        add_rows(out.at[n], *terms)
+        return send(out.at[n], far.at[n], ring_s.at[1, kind, n], ring_r.at[1, kind, n], rows=up)
+
+    ring_dw, ring_do, side_do = [], [], []
+
+    def step_dw(n):
+        i = order[n]
+        if n:
+            ring_dw[n - 1].wait_recv()
+        ring_dw.append(
+            ring_step(0, n, i, dw_near.at[i], dw.at[owner(i, 0)], dw_far, dw_send, dw_own, side_dw[n])
+        )
+
+    def step_do(n):
+        i = order[n]
+        if n:
+            ring_do[n - 1].wait_recv()
+        ring_do.append(
+            ring_step(1, n, i, do_next.at[i], do_sum.at[owner(i, 0)], do_far, do_send, do_own, side_do[n])
+        )
+
+    step_dw(0)
+    for copy in near_do:
+        copy.wait_recv()
+    for j in range(n_rows):
+        for c, k in enumerate((top, 0)):
+            add_rows(
+                do_sum.at[j, pl.ds(c * local, local)],
+                do.at[j * n_seq + other(me, k, n_seq)],
+                do_near.at[c, j],
+            )
+    for i in order:
+        side_do.append(
+            send(do_sum.at[owner(i, 1)], do_next.at[i], ring_s.at[0, 1, i], ring_r.at[0, 1, i], rows=beside)
+        )
+    for n in range(1, half):
+        step_dw(n)
+        step_do(n - 1)
+    kept = pltpu.make_async_copy(dw_own.at[pl.ds(pl.multiple_of(me * local, local), local)], dw_out.at[me], end_s.at[0])
+    kept.start()
+    ends = [
+        send(
+            dw_own.at[pl.ds(pl.multiple_of(other(me, j, n_seq) * local, local), local)],
+            dw_out.at[me], end_s.at[j], end_r.at[j], seq=other(me, j, n_seq),
+        )
+        for j in range(1, n_seq)
+    ]
+    step_do(half - 1)
+    ends.append(send(do_own.at[pl.ds(0, local)], do_last, end_s.at[n_seq], end_r.at[n_seq], seq=high))
+    for t in range(rows):
+        near_da[1][t].wait_recv()
+        add_rows(da_own.at[t], da.at[t, 0], da_near.at[t, 0])
+    for t in range(rows):
+        far_da[t].wait_recv()
+        add_rows(da_out.at[t], da_own.at[t], da_far.at[t])
+    for copy in ends:
+        copy.wait_recv()
+    add_rows(do_out, do_own.at[pl.ds(local, local)], do_last)
+    kept.wait()
+    for copy in near_da[0] + near_da[1] + side_dw + near_do + far_da + side_do + ends:
+        copy.wait_send()
+    for copy in ring_dw[:-1] + ring_do[:-1]:
+        copy.wait_send()
+
+
+def close_layer(n_seq, n_rows, da, dw, do):
+    rows, _, span, width = da.shape
+    _, block, cols = dw.shape
+    _, local, wide = do.shape
+    half = n_rows // 2
+    vmem = pl.BlockSpec(memory_space=pltpu.VMEM)
+    dma = pltpu.SemaphoreType.DMA
+    most = max(n_rows, 2)
+    return pl.pallas_call(
+        functools.partial(closing, n_seq, n_rows),
+        out_shape=(
+            jax.ShapeDtypeStruct((rows, span, width), F32),
+            jax.ShapeDtypeStruct((n_seq, local, cols), BF),
+            jax.ShapeDtypeStruct((local, wide), F32),
+        ),
+        in_specs=[vmem] * 3,
+        out_specs=(vmem,) * 3,
+        scratch_shapes=[
+            pltpu.VMEM((rows, 2, span, width), BF),
+            pltpu.VMEM((rows, span, width), BF),
+            pltpu.VMEM((rows, span, width), BF),
+            pltpu.VMEM((rows, span, width), F32),
+            pltpu.VMEM((half, block, cols), BF),
+            pltpu.VMEM((half, block, cols), BF),
+            pltpu.VMEM((half, block, cols), BF),
+            pltpu.VMEM((block, cols), BF),
+            pltpu.VMEM((2, n_rows, local, wide), BF),
+            pltpu.VMEM((n_rows, 2 * local, wide), BF),
+            pltpu.VMEM((half, 2 * local, wide), BF),
+            pltpu.VMEM((half, 2 * local, wide), BF),
+            pltpu.VMEM((half, 2 * local, wide), BF),
+            pltpu.VMEM((2 * local, wide), BF),
+            pltpu.VMEM((local, wide), BF),
+            dma((rows + 2, most)),
+            dma((rows + 2, most)),
+            dma((rows,)),
+            dma((rows,)),
+            dma((2, 2, half)),
+            dma((2, 2, half)),
+            dma((n_seq + 1,)),
+            dma((n_seq + 1,)),
+        ],
+        compiler_params=pltpu.CompilerParams(
+            collective_id=1, has_side_effects=True, vmem_limit_bytes=60 << 20
+        ),
+        name="closing",
+    )(da, dw, do)
 
 
 def head_unit(v):
@@ -300,10 +682,7 @@
     local = query_key_value_weight.shape[0]
     extra = 64
     plan = (n_seq, span, per, group, q_cols, kv_cols)
-    half = n_rows // 2
-    near = jnp.arange(n_rows, dtype=jnp.int32)
-    slot_of = 2 * ((row_at // 2 - near // 2) % half) + ((row_at % 2) ^ (near % 2))
-    device_of = 2 * ((row_at // 2 - near // 2) % half) + ((row_at % 2) ^ (near % 2))
+    rel = me ^ jnp.arange(n_seq, dtype=jnp.int32)
 
     onehot = (corpus == jnp.arange(NCORP, dtype=jnp.int32)[None, :]).astype(F32)
     counted = jnp.zeros((local, 1), BF).at[:NCORP, 0].set(jnp.sum(onehot, axis=0).astype(BF))
@@ -316,9 +695,8 @@
                 parts.append(query_key_value_weight[:, at : at + HEAD_SIZE])
         parts += [norm_gains.T, counted, jnp.zeros((local, extra - 3), BF)]
         pieces.append(jnp.concatenate(parts, axis=1))
-    mine = lax.all_to_all(jnp.stack(pieces), "seq", split_axis=0, concat_axis=0, tiled=True)
-    whole = jnp.stack(gather_rows(mine.reshape(n_seq * local, cols + extra), n_rows))
-    whole = jnp.take(whole, slot_of, axis=0).reshape(width, cols + extra)
+    x_rows, whole, w_out = open_layer(n_seq, n_rows, tokens, jnp.stack(pieces), out_weight)
+    w_out = jnp.swapaxes(w_out, 1, 2).reshape(width, -1)
     w_qkv = whole[:, :cols]
     gains = whole[:, cols : cols + 2].astype(F32).T
     counts = whole[:, cols + 2].astype(F32).reshape(n_rows, n_seq, local)[:, 0, :NCORP]
@@ -328,8 +706,6 @@
     row_scale = jnp.sum(onehot * factor[None, :], axis=1)
     qk_gain = qk_gains.astype(F32).T
 
-    x_rows = [jnp.concatenate(gather_seq(tokens[r], n_seq), axis=0) for r in range(rows)]
-    rel = me ^ jnp.arange(n_seq, dtype=jnp.int32)
     at = (rel[:, None] * span + jnp.arange(span, dtype=jnp.int32)[None, :]).reshape(length)
     pos = jnp.take(positions.reshape(rows, n_seq, span), rel, axis=1).reshape(rows, length)
     first = at[None, :] - pos
@@ -347,29 +723,18 @@
         args = (plan, me_one, qkv, cosine[r], sine[r], first[r : r + 1], qk_gain)
         o, inv = attention_forward(*args)
         kept.append((a_in, args, o, inv))
-        got = gather_seq(o, n_seq)
-        got = [
-            jnp.concatenate(
-                [got[m][:, (m ^ j) * span : ((m ^ j) + 1) * span] for j in range(n_seq)], axis=1
-            )
-            for m in range(n_seq)
-        ]
-        o_rows.append(jnp.take(jnp.stack(got), rel, axis=0).reshape(n_seq * q_cols, length))
-    o_all = jnp.concatenate(o_rows, axis=1)
-    x_all = jnp.concatenate(x_rows, axis=0).astype(F32)
-
-    out_weight = after(out_weight, w_qkv)
-    w_out = lax.all_gather(out_weight, ("rows", "seq"), axis=0, tiled=True)
+        o_rows.append(o)
+    o_all = meet(n_seq, n_rows, o_rows).reshape(n_seq * q_cols, rows * length)
+    o_all, dy_own = tie((o_all, d_output))
+    x_all = x_rows.reshape(rows * length, width).astype(F32)
+
     h_all = x_all + dot(o_all, w_out, 0, 1)
     inverse_two = inverse_rms(h_all)
     f_in = (h_all * inverse_two * gains[1]).astype(BF)
 
-    ff_local = jnp.concatenate([gate_up_weight, down_weight], axis=1)
-    ff_slots = gather_rows(after(ff_local, w_qkv), n_rows)
-    w_g = jnp.concatenate([w[:, :width] for w in ff_slots], axis=0)
-    w_u = jnp.concatenate([w[:, width : 2 * width] for w in ff_slots], axis=0)
-    w_dn = jnp.concatenate([w[:, 2 * width :] for w in ff_slots], axis=0)
-    dy_own = after(d_output, x_rows[-1])
+    w_gu = lax.all_gather(gate_up_weight, "rows", axis=0, tiled=True)
+    w_dn = lax.all_gather(down_weight, "rows", axis=0, tiled=True)
+    w_g, w_u = w_gu[:, :width], w_gu[:, width:]
     dy_all = jnp.stack(gather_seq(dy_own, n_seq), axis=1).astype(F32)
     gy = (row_scale[:, None, None, None] * dy_all).astype(BF).reshape(rows * length, width)
     gate = dot(f_in, w_g, 1, 1)
@@ -383,19 +748,18 @@
     df_part = dot(d_gate, w_g, 1, 0) + dot(d_upper, w_u, 1, 0)
     d_gain_two = jnp.sum(df_part * (h_all * inverse_two), axis=0)
     df_slots = df_part.astype(BF).reshape(rows, n_seq, span, width)
-    df = scatter_seq([df_slots[:, j] for j in range(n_seq)], n_seq).reshape(rows * span, width)
+    df_kept, df_sent = fold_seq([df_slots[:, j] for j in range(n_seq)], n_seq)
+    df_got = cross_seq(df_sent, n_seq)
     ffn_grads = jnp.concatenate(
         [dot(d_gate, f_in, 0, 0), dot(d_upper, f_in, 0, 0), dot(hidden, gy, 0, 0)], axis=1
     ).astype(BF)
-    df, ffn_grads = lax.optimization_barrier((df, ffn_grads))
-    ff_rows = gate_up_weight.shape[0]
-    ffn_sums = scatter_rows(
-        [ffn_grads[i * ff_rows : (i + 1) * ff_rows] for i in range(n_rows)], n_rows
-    )
-    y_slots = dot(after(hidden, df), w_dn, 1, 0).astype(BF).reshape(rows, n_seq, span, width)
-    y = scatter_seq([y_slots[:, j] for j in range(n_seq)], n_seq)
+    ffn_sums = lax.psum_scatter(ffn_grads, "rows", scatter_dimension=0, tiled=True)
+    y_slots = dot(hidden, w_dn, 1, 0).astype(BF)
+    y_slots = y_slots.reshape(rows, n_seq, span, width)
+    y_kept, y_sent = fold_seq([y_slots[:, j] for j in range(n_seq)], n_seq)
+    df_got, y_sent = tie((df_got, y_sent))
+    df = (df_kept + df_got.astype(F32)).reshape(rows * span, width)
     h_own = h_all.reshape(rows, n_seq, span, width)[:, 0]
-    output = (h_own + y).astype(BF)
 
     h_one = h_own.reshape(rows * span, width)
     inverse = inverse_rms(h_one)
@@ -404,36 +768,31 @@
     g_two = (row_scale[:, None, None] * d_output.astype(F32)).reshape(rows * span, width)
     d_h = g_two + inverse * (scaled - unit * jnp.mean(scaled * unit, axis=-1, keepdims=True))
     grad_att = d_h.astype(BF)
-    o_own = jnp.concatenate([o[:, :span] for o in o_rows], axis=1)
-    d_out = lax.psum_scatter(
-        dot(grad_att, o_own, 0, 1).astype(BF), ("rows", "seq"), scatter_dimension=0, tiled=True
-    ).astype(F32)
+    o_own = jnp.concatenate(
+        [o_all[:, r * length : r * length + span] for r in range(rows)], axis=1
+    )
     do_src = dot(w_out, grad_att, 0, 1).astype(BF).reshape(n_seq, q_cols, rows * span)
     do_src = jnp.take(do_src, rel, axis=0)
     do_slots = [do_src[0]] + [swap(do_src[m], "seq", n_seq, m) for m in range(1, n_seq)]
+
+    d_out = dot(grad_att, o_own, 0, 1).astype(BF)
+    do_slots[-1], y_sent = tie((do_slots[-1], y_sent))
+    y_got = cross_seq(y_sent, n_seq)
 
     d_acts, d_parts, d_heads, d_gain_one = [], [], 0.0, 0.0
     for r in range(rows):
         a_in, args, o, inv = kept[r]
         d_o = jnp.concatenate([d[:, r * span : (r + 1) * span] for d in do_slots], axis=1)
         d_act, head_sums = attention_backward(*args, o, inv, d_o)
+        if r == rows - 1:
+            d_act, y_got, ffn_sums = tie((d_act, y_got, ffn_sums))
+            output = (h_own + (y_kept + y_got.astype(F32))).astype(BF)
         d_heads = d_heads + jnp.sum(head_sums, axis=-1)
         part = dot(d_act, w_qkv, 0, 1)
         x = x_rows[r].astype(F32)
         d_gain_one = d_gain_one + jnp.sum(part * (x * inverse_rms(x)), axis=0)
-        part = part.astype(BF)
-        d_parts.append(
-            scatter_seq([part[j * span : (j + 1) * span] for j in range(n_seq)], n_seq)
-        )
+        d_parts.append(part.astype(BF).reshape(n_seq, span, width))
         d_acts.append(d_act)
-    d_a = jnp.concatenate(d_parts, axis=0)
-    x_own = tokens.astype(F32).reshape(rows * span, width)
-    inverse = inverse_rms(x_own)
-    unit = x_own * inverse
-    scaled = d_a * gains[0]
-    d_tokens = d_h + inverse * (scaled - unit * jnp.mean(scaled * unit, axis=-1, keepdims=True))
-    d_tokens = d_tokens.reshape(rows, span, width)
-
     spread = 2 * HEAD_SIZE // local
     tail = jnp.concatenate(
         [
@@ -446,11 +805,22 @@
     )
     d_w = sum(dot(kept[r][0], d_acts[r], 0, 1) for r in range(rows))
     d_w = jnp.concatenate([d_w.astype(BF), tail.astype(BF)], axis=1)
-    d_w = jnp.take(d_w.reshape(n_rows, n_seq * local, cols + extra), device_of, axis=0)
-    d_w = scatter_rows([d_w[i] for i in range(n_rows)], n_rows).astype(BF)
-    d_w = lax.all_to_all(
-        d_w.reshape(n_seq, local, cols + extra), "seq", split_axis=0, concat_axis=0, tiled=True
-    ).astype(F32)
+    d_a, d_w, d_out = close_layer(
+        n_seq,
+        n_rows,
+        jnp.stack(d_parts),
+        d_w.reshape(n_rows, n_seq * local, cols + extra),
+        d_out.reshape(n_rows * n_seq, local, -1),
+    )
+    d_a = d_a.reshape(rows * span, width)
+    d_w = d_w.astype(F32)
+    x_own = tokens.astype(F32).reshape(rows * span, width)
+    inverse = inverse_rms(x_own)
+    unit = x_own * inverse
+    scaled = d_a * gains[0]
+    d_tokens = d_h + inverse * (scaled - unit * jnp.mean(scaled * unit, axis=-1, keepdims=True))
+    d_tokens = d_tokens.reshape(rows, span, width)
+
     k_sum = [jnp.zeros((local, HEAD_SIZE), F32) for _ in range(KEY_VALUE_HEADS)]
     v_sum = [jnp.zeros((local, HEAD_SIZE), F32) for _ in range(KEY_VALUE_HEADS)]
     for t in range(n_seq):
@@ -469,8 +839,8 @@
         d_out,
         d_gains,
         d_qk_gains,
-        ffn_sums[:, : 2 * width],
-        ffn_sums[:, 2 * width :],
+        ffn_sums[:, : 2 * width].astype(F32),
+        ffn_sums[:, 2 * width :].astype(F32),
     )
 
 

time: 742 us -> 684 us (0.922)
  Pallas kernels: 45.3 us -> 289 us
  waiting for transfers between devices: 279 us -> 61.7 us
  local copies, waits for them, and re-layouts: 99.6 us -> 48.4 us
  starting transfers between devices: 47.2 us -> 7.61 us
  matrix products: 160 us -> 169 us
    pallas_call x0 -> x3, Pallas kernels: none -> 243 us  [the longest x1 114 us: open_layer(): pl.pallas_call(functools.partial(opening, n_seq, n_rows), out_shape=(jax....]
    ppermute x46 -> x12, waiting for transfers between devices: 172 us -> 61 us  [swap(): return lax.ppermute(v, axis, [(i, i ^ bit) for i in range(n)])]
    ppermute x12 -> x0, waiting for transfers between devices: 89.2 us -> none  [ring(): lax.ppermute(v, 'rows', [(r, (r + 2) % n_rows) for r in range(n_rows)])]
    unnamed x182 -> x160, local copies, waits for them, and re-layouts: 42.3 us -> 5.92 us
    ppermute x46 -> x12, starting transfers between devices: 33.2 us -> 7.49 us  [swap(): return lax.ppermute(v, axis, [(i, i ^ bit) for i in range(n)])]
    all_to_all x2 -> x0, waiting for transfers between devices: 17.5 us -> none  [the longest x1 13.3 us: on_device(): lax.all_to_all(jnp.stack(pieces), 'seq', split_axis=0, concat_axis=0, til...]
    gather x4 -> x0, local copies, waits for them, and re-layouts: 12 us -> none  [the longest x2 6.31 us: on_device(): jnp.take(jnp.stack(got), rel, axis=0).reshape(n_seq * q_cols, length)]
    add x5 -> x0, other arithmetic: 10.2 us -> none  [the longest x3 7.14 us: scatter_seq(): live = {j: live[j].astype(F32) + sent[j].astype(F32) for j in keep}]
  transfers between devices with their start and end apart: 62 -> 15, of which waited for: 30 -> 3; matrix products, arithmetic and copies ran while one was open for 30% -> 36% of each run, Pallas kernels for 6% -> 43%
where the time goes in v3:
time: 684 us; the launch traced here: 674 us
  Pallas kernels  289 us (42%)
  matrix products  169 us (25%)
  other arithmetic  82.2 us (12%)
  waiting for transfers between devices  61.7 us (9%)
  local copies, waits for them, and re-layouts  48.4 us (7%)
  between operations  15.5 us (2%)
  starting transfers between devices  7.61 us (1%)
    dot_general x18, matrix products, dot(): lax.dot_general(a, b, (((ca,), (cb,)), ((), ())), preferred_element_type=...  169 us
    pallas_call x1, Pallas kernels, open_layer(): pl.pallas_call(functools.partial(opening, n_seq, n_rows), out_shape=(jax....  114 us
    pallas_call x1, Pallas kernels, close_layer(): pl.pallas_call(functools.partial(closing, n_seq, n_rows), out_shape=(jax....  82.5 us
    ppermute x12, waiting for transfers between devices, swap(): return lax.ppermute(v, axis, [(i, i ^ bit) for i in range(n)])  61 us
    pallas_call x1, Pallas kernels, meet(): pl.pallas_call(functools.partial(meeting, n_seq, n_rows), out_shape=jax.S...  46.8 us
    pallas_call x2, Pallas kernels, attention_backward(): pl.pallas_call(functools.partial(backward_heads, plan), out_shape=(jax.Sh...  31.5 us
    pallas_call x2, Pallas kernels, attention_forward(): pl.pallas_call(functools.partial(forward_heads, plan), out_shape=(jax.Sha...  14.2 us
  transfers between devices with their start and end apart: 15, of which 3 were waited for; matrix products, arithmetic and copies ran while one was open for 36% of the time, Pallas kernels for 43%

profile of v3, /device:TPU:0, one launch (start us, length us, event | category | flops | bytes accessed | tf_op | source)
XLA Modules:
  0.0 673.7 jit_solution(809657990430714367)
XLA Ops:
  12.1 1.1 fusion.81
  13.2 1.0 fusion.82
  15.6 113.8 %opening.1 = (bf16[2,1024,2048]{2,1,0:T(8,128)(2,1)}, bf16[2048,640]{1,0:T(8,128)(2,1)}, bf16[8,2,2,64,1280]{4,3,2,1,0:T(8,128)(2,1)}) custom-call(bf16[2,256,2048]{2,1,0:T(8,128)(2,1)} %tokens.1, bf16[4,64,640]{2,1,0:T(8,128)(2,1)} %pad_maximum_fusion.5.pieces, bf16[64,1280]{1,0:T(8,128)(2,1)} %out_w.1), custom_call_target="tpu_custom_call" | custom-call | tf_op jit(solution)/shard_map/opening/pallas_call | solution.py:193
  129.4 1.2 convert_bitcast_fusion
  130.7 0.9 slice_reduce_fusion
  131.6 4.7 fusion.9
  136.4 1.0 multiply_sine_fusion
  137.9 3.2 fusion.49.x_ref
  141.1 7.1 %attention_forward.3 = (bf16[320,1024]{1,0:T(8,128)(2,1)S(1)}, f32[5,1,1024]{2,1,0:T(1,128)S(1)}) custom-call(s32[1]{0:T(128)} %bitcast.8.me_ref, bf16[576,1024]{1,0:T(8,128)(2,1)S(1)} %fusion.49.x_ref, f32[32,1024]{1,0:T(8,128)S(1)} %get-tuple-element.164.cos_ref, f32[32,1024]{1,0:T(8,128)S(1)} %get-tuple-element.134.sin_ref, ...), custom_call_target="tpu_custom_call" | custom-call | flops 1342177280 | bytes 4194304 | tf_op jit(solution)/shard_map/attention_forward/pallas_call | solution.py:601
  148.3 3.2 fusion.46.x_ref
  151.6 7.1 %attention_forward.2 = (bf16[320,1024]{1,0:T(8,128)(2,1)S(1)}, f32[5,1,1024]{2,1,0:T(1,128)S(1)}) custom-call(s32[1]{0:T(128)} %bitcast.8.me_ref, bf16[576,1024]{1,0:T(8,128)(2,1)S(1)} %fusion.46.x_ref, f32[32,1024]{1,0:T(8,128)S(1)} %get-tuple-element.165.cos_ref, f32[32,1024]{1,0:T(8,128)S(1)} %get-tuple-element.133.sin_ref, ...), custom_call_target="tpu_custom_call" | custom-call | flops 1342177280 | bytes 4194304 | tf_op jit(solution)/shard_map/attention_forward/pallas_call | solution.py:601
  159.5 46.8 %meeting.1 = bf16[4,320,2048]{2,1,0:T(8,128)(2,1)} custom-call(bf16[320,1024]{1,0:T(8,128)(2,1)} %copy-done.4, bf16[320,1024]{1,0:T(8,128)(2,1)} %copy-done.2), custom_call_target="tpu_custom_call" | custom-call | tf_op jit(solution)/shard_map/meeting/pallas_call | solution.py:273
  206.4 1.6 collective-permute-start.2
  208.0 1.4 slice_reduce_fusion.2
  209.4 5.3 copy.62
  214.9 20.6 %multiply_reduce_fusion.1 = (f32[2048]{0:T(1024)S(1)}, f32[2048,2048]{1,0:T(8,128)}) fusion(bf16[1280,2048]{1,0:T(8,128)(2,1)} %bitcast.244, bf16[2048,1280]{1,0:T(8,128)(2,1)} %bitcast.246, bf16[2,1024,2048]{2,1,0:T(8,128)(2,1)} %get-tuple-element.43), kind=kOutput, calls=%fused_computation.7 | convolution fusion | flops 10754193408 | bytes 35659776 | tf_op jit(solution)/shard_map/dot_general | solution.py:28
  235.5 18.7 %collective-permute-done.2 = bf16[2,256,2048]{2,1,0:T(8,128)(2,1)} collective-permute-done((bf16[2,256,2048]{2,1,0:T(8,128)(2,1)S(1)}, bf16[2,256,2048]{2,1,0:T(8,128)(2,1)}, u32[]{:S(2)}, u32[]{:S(2)}) %collective-permute-start.2) | collective-permute-done | bytes 2097184 | tf_op jit(solution)/shard_map/ppermute | solution.py:32
  254.5 4.8 slice.356
  259.4 9.5 %multiply_convert_fusion = bf16[2048,2048]{1,0:T(8,128)(2,1)} fusion(f32[2048,2048]{1,0:T(8,128)} %get-tuple-element.162, f32[2048]{0:T(1024)S(1)} %get-tuple-element.86, f32[2048]{0:T(1024)S(1)} %add_rsqrt_fusion), kind=kLoop, calls=%fused_computation.6 | loop fusion | flops 12582912 | bytes 25182208 | tf_op jit(solution)/shard_map/convert_element_type | solution.py:733
  268.9 6.1 pad_maximum_fusion.1
  274.9 8.1 %fusion = bf16[2048,2048]{1,0:T(8,128)(2,1)} fusion(bf16[2,4,256,2048]{3,2,1,0:T(8,128)(2,1)} %pad_maximum_fusion.1, f32[2048]{0:T(1024)S(1)} %bitcast.265), kind=kLoop, calls=%fused_computation.3 | loop fusion | flops 12582912 | bytes 16785408 | tf_op jit(solution)/shard_map/convert_element_type | solution.py:739
  283.0 12.0 %fusion.32 = f32[2048,704]{0,1:T(8,128)} fusion(bf16[2048,2048]{1,0:T(8,128)(2,1)} %multiply_convert_fusion, bf16[704,4096]{1,0:T(8,128)(2,1)} %all-gather.3.cloned.1.call-done), kind=kOutput, calls=%fused_computation.72 | convolution fusion | flops 5905580032 | bytes 17039360 | tf_op jit(solution)/shard_map/dot_general | solution.py:28
  295.0 10.1 %fusion.36 = f32[2048,704]{0,1:T(8,128)} fusion(bf16[2048,2048]{1,0:T(8,128)(2,1)} %multiply_convert_fusion, bf16[704,4096]{1,0:T(8,128)(2,1)S(1)} %copy-done.61), kind=kOutput, calls=%fused_computation.76 | convolution fusion | flops 5905580032 | bytes 17039360 | tf_op jit(solution)/shard_map/dot_general | solution.py:28
  305.1 14.0 %multiply_convert_fusion.3 = (bf16[2048,704]{0,1:T(8,128)(2,1)S(1)}, bf16[2048,704]{0,1:T(8,128)(2,1)S(1)}, bf16[2048,704]{0,1:T(8,128)(2,1)S(1)}) fusion(f32[2048,704]{0,1:T(8,128)} %fusion.32, f32[2048,704]{0,1:T(8,128)} %fusion.36, bf16[2048,2048]{1,0:T(8,128)(2,1)} %fusion, bf16[704,2048]{1,0:T(8,128)(2,1)} %all-gather.5.cloned.1.call-done), kind=kOutput, calls=%fused_computation.30 | convolution fusion | flops 5927206912 | bytes 31457280 | tf_op jit(solution)/shard_map/dot_general | solution.py:28
  319.1 10.6 %convolution_convert_fusion.2 = bf16[704,2048]{1,0:T(8,128)(2,1)S(1)} fusion(bf16[2048,704]{0,1:T(8,128)(2,1)S(1)} %get-tuple-element.94, bf16[2048,2048]{1,0:T(8,128)(2,1)} %fusion), kind=kOutput, calls=%fused_computation.66 | convolution fusion | flops 5907021824 | bytes 14155776 | tf_op jit(solution)/shard_map/dot_general | solution.py:28
  329.8 8.9 %convolution_convert_fusion.4 = bf16[704,2048]{1,0:T(8,128)(2,1)S(1)} fusion(bf16[2048,704]{0,1:T(8,128)(2,1)S(1)} %get-tuple-element.95, bf16[2048,2048]{1,0:T(8,128)(2,1)} %multiply_convert_fusion), kind=kOutput, calls=%fused_computation.68 | convolution fusion | flops 5907021824 | bytes 14155776 | tf_op jit(solution)/shard_map/dot_general | solution.py:28
  338.7 6.4 convolution_convert_fusion.3
  345.1 3.9 pad_maximum_fusion
  349.0 12.5 %fusion.30 = f32[2048,2048]{1,0:T(8,128)} fusion(bf16[2048,704]{0,1:T(8,128)(2,1)} %copy-done.66, bf16[704,4096]{1,0:T(8,128)(2,1)} %all-gather.3.cloned.1.call-done), kind=kOutput, calls=%fused_computation.70 | convolution fusion | flops 5905580032 | bytes 22544384 | tf_op jit(solution)/shard_map/dot_general | solution.py:28
  361.5 18.1 %multiply_reduce_fusion = (bf16[2048]{0:T(1024)(128)(2,1)S(1)}, bf16[2048,2048]{1,0:T(8,128)(2,1)}) fusion(f32[2048,2048]{1,0:T(8,128)} %get-tuple-element.162, f32[2048]{0:T(1024)S(1)} %add_rsqrt_fusion, f32[2048,2048]{1,0:T(8,128)} %fusion.30, bf16[2048,704]{0,1:T(8,128)(2,1)S(1)} %get-tuple-element.95, bf16[704,4096]{1,0:T(8,128)(2,1)} %all-gather.3.cloned.1.call-done), kind=kOutput, calls=%fused_computation.5 | convolution fusion | flops 5926549504 | bytes 47722496 | tf_op jit(solution)/shard_map/dot_general | solution.py:28
  379.6 2.9 slice_bitcast_fusion.4
  383.1 9.0 %convolution_convert_fusion.1 = bf16[2048,2048]{1,0:T(8,128)(2,1)S(1)} fusion(bf16[2048,704]{0,1:T(8,128)(2,1)} %copy-done.67, bf16[704,2048]{1,0:T(8,128)(2,1)S(1)} %copy-done.62), kind=kOutput, calls=%fused_computation.26 | convolution fusion | flops 5909774336 | bytes 14155776 | tf_op jit(solution)/shard_map/dot_general | solution.py:28
  392.1 1.7 slice_bitcast_fusion.6
  394.4 5.2 fusion.27
  399.6 1.6 collective-permute-start.6
  402.7 2.2 fusion.76
  405.0 2.1 fusion.26
  407.1 40.2 %collective-permute-done.6 = bf16[2,256,2048]{2,1,0:T(8,128)(2,1)S(1)} collective-permute-done((bf16[2,256,2048]{2,1,0:T(8,128)(2,1)S(1)}, bf16[2,256,2048]{2,1,0:T(8,128)(2,1)S(1)}, u32[]{:S(2)}, u32[]{:S(2)}) %collective-permute-start.6) | collective-permute-done | bytes 2097184 | tf_op jit(solution)/shard_map/ppermute | solution.py:32
  447.3 3.2 multiply_reduce_fusion.2
  450.7 3.3 convert_multiply_fusion.7
  454.0 3.0 convolution_convert_fusion.5
  458.5 1.1 collective-permute-start.9
  459.9 5.5 fusion.23
  465.5 4.7 convolution_convert_fusion
  471.7 1.5 collective-permute-start.11
  473.2 2.0 collective-permute-done.9
  476.7 15.6 %attention_backward.3 = (bf16[576,1024]{1,0:T(8,128)(2,1)S(1)}, f32[2,64,128]{2,1,0:T(8,128)S(1)}) custom-call(s32[1]{0:T(128)} %bitcast.8.me_ref, bf16[576,1024]{1,0:T(8,128)(2,1)S(1)} %copy-done.23, f32[32,1024]{1,0:T(8,128)S(1)} %copy-done.13, f32[32,1024]{1,0:T(8,128)S(1)} %copy-done.11, s32[1,1024]{1,0:T(1,128)S(1)} %copy-done.19, ...), custom_call_target="tpu_custom_call" | custom-call | flops 3355443200 | bytes 6291456 | tf_op jit(solution)/shard_map/attention_backward/pallas_call | solution.py:631
  492.5 1.2 pad_maximum_fusion.3.do_ref
  493.8 15.8 %attention_backward.2 = (bf16[576,1024]{1,0:T(8,128)(2,1)S(1)}, f32[2,64,128]{2,1,0:T(8,128)S(1)}) custom-call(s32[1]{0:T(128)} %bitcast.8.me_ref, bf16[576,1024]{1,0:T(8,128)(2,1)S(1)} %copy-done.21, f32[32,1024]{1,0:T(8,128)S(1)} %copy-done.9, f32[32,1024]{1,0:T(8,128)S(1)} %copy-done.7, s32[1,1024]{1,0:T(1,128)S(1)} %copy-done.17, f32[64,2]{1,0:T(8,128)S(1)} %bitcast.226, ...), custom_call_target="tpu_custom_call" | custom-call | flops 3355443200 | bytes 6291456 | tf_op jit(solution)/shard_map/attention_backward/pallas_call | solution.py:631
  509.6 1.0 copy-done.24
  511.1 7.4 %fusion.40 = f32[1024,2048]{1,0:T(8,128)} fusion(bf16[576,1024]{1,0:T(8,128)(2,1)S(1)} %get-tuple-element.58, bf16[2048,640]{1,0:T(8,128)(2,1)} %get-tuple-element.44), kind=kOutput, calls=%fused_computation.88 | convolution fusion | flops 2415919104 | bytes 12189696 | tf_op jit(solution)/shard_map/dot_general | solution.py:28
  518.5 7.1 %fusion.55 = f32[2048,576]{0,1:T(8,128)} fusion(bf16[576,1024]{1,0:T(8,128)(2,1)S(1)} %get-tuple-element.58, f32[2048]{0:T(1024)S(1)} %copy-done.44, f32[1024]{0:T(1024)S(1)} %copy-done.58, bf16[2,1024,2048]{2,1,0:T(8,128)(2,1)} %get-tuple-element.43), kind=kOutput, calls=%fused_computation.104 | convolution fusion | flops 2424307712 | bytes 10104832 | tf_op jit(solution)/shard_map/dot_general | solution.py:28
  525.7 7.9 %add_convert_fusion.1 = bf16[2048,576]{0,1:T(8,128)(2,1)} fusion(f32[2048,576]{0,1:T(8,128)} %fusion.55, bf16[576,1024]{1,0:T(8,128)(2,1)S(1)} %copy-done.25, f32[1024]{0:T(1024)S(1)} %copy-done.56, f32[2048]{0:T(1024)S(1)} %copy-done.44, bf16[2,1024,2048]{2,1,0:T(8,128)(2,1)} %get-tuple-element.43), kind=kOutput, calls=%fused_computation.37 | convolution fusion | flops 2426667008 | bytes 12464128 | tf_op jit(solution)/shard_map/dot_general | solution.py:28
  533.6 10.7 %fusion.6 = (f32[2048]{0:T(1024)S(1)}, f32[2048]{0:T(1024)S(1)}, bf16[1024,2048]{1,0:T(8,128)(2,1)}, bf16[1024,2048]{1,0:T(8,128)(2,1)}) fusion(f32[1024]{0:T(1024)S(1)} %copy-done.56, bf16[2,1024,2048]{2,1,0:T(8,128)(2,1)} %get-tuple-element.43, f32[1024,2048]{1,0:T(8,128)S(1)} %copy-done.65, f32[1024]{0:T(1024)S(1)} %copy-done.58, ...), kind=kOutput, calls=%fused_computation.18 | convolution fusion | flops 2436886528 | bytes 28991488 | tf_op jit(solution)/shard_map/dot_general | solution.py:28
  544.4 8.9 %concatenate.47 = bf16[2048,640]{0,1:T(8,128)(2,1)S(1)} concatenate(bf16[2048,576]{0,1:T(8,128)(2,1)} %add_convert_fusion.1, bf16[2048,1]{0,1:T(2,128)(2,1)S(1)} %add.222, bf16[2048,1]{0,1:T(2,128)(2,1)S(1)} %broadcast_in_dim.56, bf16[2048,2]{0,1:T(2,128)(2,1)S(1)} %tile.10, bf16[2048,60]{0,1:T(8,128)(2,1)S(1)} %broadcast_in_dim.57), dimensions={1} | concatenate | bytes 5242880 | tf_op jit(solution)/shard_map/concatenate | solution.py:807
  553.3 2.6 copy.74
  555.9 7.5 %pad_maximum_fusion.2.da = bf16[2,4,256,2048]{3,2,1,0:T(8,128)(2,1)} fusion(bf16[1,4,256,2048]{3,2,1,0:T(8,128)(2,1)} %bitcast.253, bf16[1,4,256,2048]{3,2,1,0:T(8,128)(2,1)} %bitcast.252), kind=kLoop, calls=%fused_computation.24 | loop fusion | flops 4194304 | bytes 16777216 | tf_op jit(solution)/shard_map/stack | solution.py:811
  563.4 82.5 %closing.1 = (f32[2,256,2048]{2,1,0:T(8,128)}, bf16[4,64,640]{2,1,0:T(8,128)(2,1)}, f32[64,1280]{1,0:T(8,128)}) custom-call(bf16[2,4,256,2048]{3,2,1,0:T(8,128)(2,1)} %pad_maximum_fusion.2.da, bf16[8,256,640]{2,1,0:T(8,128)(2,1)} %bitcast.235, bf16[32,64,1280]{2,1,0:T(8,128)(2,1)} %bitcast.250), custom_call_target="tpu_custom_call" | custom-call | tf_op jit(solution)/shard_map/closing/pallas_call | solution.py:424
  645.9 1.2 convert_element_type.243
  650.0 2.0 concatenate.49
  652.1 3.2 fusion.14
  655.3 0.9 slice_convert_fusion.1
  656.2 1.2 slice_convert_fusion
  657.5 8.4 %fusion.17 = (f32[2,256,2048]{2,1,0:T(8,128)}, bf16[2,256,2048]{2,1,0:T(8,128)(2,1)}) fusion(bf16[2,256,2048]{2,1,0:T(8,128)(2,1)S(1)} %copy-done.30, f32[2,256,2048]{2,1,0:T(8,128)} %get-tuple-element.62, f32[2,256]{1,0:T(2,128)S(1)} %broadcast_multiply_fusion, f32[2048]{0:T(1024)S(1)} %copy-done.45, f32[2,256]{1,0:T(2,128)S(1)} %copy-done.50, ...), kind=kLoop, calls=%fused_computation.41 | loop fusion | flops 23068672 | bytes 29384712 | tf_op jit(solution)/shard_map/add | solution.py:821
  (247 shorter events, 19.7 us)
Async XLA Ops:
  7.2 275.8 %all-gather.3.cloned.1.call-start = ((), (), s32[]{:S(2)}) async-start(), calls=%async_computation.1 | async-start | bytes 6488064 | tf_op jit(solution)/shard_map/all_gather | solution.py:735
  7.9 297.2 %all-gather.5.cloned.1.call-start = ((), (), s32[]{:S(2)}) async-start(), calls=%async_computation.2 | async-start | bytes 3244032 | tf_op jit(solution)/shard_map/all_gather | solution.py:736
  10.9 140.7 %copy-start.14 = (f32[2,64]{0,1:T(8,128)}, f32[2,64]{0,1:T(8,128)S(1)}, u32[]{:S(2)}) copy-start(f32[2,64]{0,1:T(8,128)S(1)} %copy.61) | copy-start | bytes 1540
  130.7 6.9 %copy-start.38 = (bf16[2048,640]{1,0:T(8,128)(2,1)S(1)}, bf16[2048,640]{1,0:T(8,128)(2,1)}, u32[]{:S(2)}) copy-start(bf16[2048,640]{1,0:T(8,128)(2,1)} %get-tuple-element.44) | copy-start | bytes 7864324
  131.6 16.7 %copy-start.43 = (f32[2048]{0:T(1024)}, f32[2048]{0:T(1024)S(1)}, u32[]{:S(2)}) copy-start(f32[2048]{0:T(1024)S(1)} %get-tuple-element.87) | copy-start | bytes 24580
  131.6 127.8 %copy-start.41 = (f32[2048]{0:T(1024)}, f32[2048]{0:T(1024)S(1)}, u32[]{:S(2)}) copy-start(f32[2048]{0:T(1024)S(1)} %get-tuple-element.86) | copy-start | bytes 24580
  131.6 6.3 copy-start.34
  136.4 15.1 %copy-start.18 = (s32[1,1024]{1,0:T(1,128)}, s32[1,1024]{1,0:T(1,128)S(1)}, u32[]{:S(2)}) copy-start(s32[1,1024]{1,0:T(1,128)S(1)} %get-tuple-element.155.first_ref) | copy-start | bytes 12292
  137.5 14.0 %copy-start.10 = (f32[32,1024]{1,0:T(8,128)}, f32[32,1024]{1,0:T(8,128)S(1)}, u32[]{:S(2)}) copy-start(f32[32,1024]{1,0:T(8,128)S(1)} %get-tuple-element.133.sin_ref) | copy-start | bytes 393220
  137.5 14.0 %copy-start.12 = (f32[32,1024]{1,0:T(8,128)}, f32[32,1024]{1,0:T(8,128)S(1)}, u32[]{:S(2)}) copy-start(f32[32,1024]{1,0:T(8,128)S(1)} %get-tuple-element.165.cos_ref) | copy-start | bytes 393220
  141.1 10.4 %copy-start.20 = (bf16[576,1024]{1,0:T(8,128)(2,1)}, bf16[576,1024]{1,0:T(8,128)(2,1)S(1)}, u32[]{:S(2)}) copy-start(bf16[576,1024]{1,0:T(8,128)(2,1)S(1)} %fusion.49.x_ref) | copy-start | bytes 3538948
  151.5 7.2 %copy-start.22 = (bf16[576,1024]{1,0:T(8,128)(2,1)}, bf16[576,1024]{1,0:T(8,128)(2,1)S(1)}, u32[]{:S(2)}) copy-start(bf16[576,1024]{1,0:T(8,128)(2,1)S(1)} %fusion.46.x_ref) | copy-start | bytes 3538948
  159.5 46.8 %copy-start.31 = (bf16[2,256,2048]{2,1,0:T(8,128)(2,1)S(1)}, bf16[2,256,2048]{2,1,0:T(8,128)(2,1)}, u32[]{:S(2)}) copy-start(bf16[2,256,2048]{2,1,0:T(8,128)(2,1)} %param.14) | copy-start | bytes 6291460
  206.4 47.9 %collective-permute-start.2 = (bf16[2,256,2048]{2,1,0:T(8,128)(2,1)S(1)}, bf16[2,256,2048]{2,1,0:T(8,128)(2,1)}, u32[]{:S(2)}, u32[]{:S(2)}) collective-permute-start(bf16[2,256,2048]{2,1,0:T(8,128)(2,1)S(1)} %copy-done.31), channel_id=1, source_target_pairs={{0,2},{1,3},{2,0},{3,1},{4,6},{5,7},{6,4},{7,5},{8,10},{9,11},{10,... | collective-permute-start | bytes 6291464 | tf_op jit(solution)/shard_map/ppermute | solution.py:32
  207.9 60.9 %collective-permute-start.1 = (bf16[2,256,2048]{2,1,0:T(8,128)(2,1)S(1)}, bf16[2,256,2048]{2,1,0:T(8,128)(2,1)}, u32[]{:S(2)}, u32[]{:S(2)}) collective-permute-start(bf16[2,256,2048]{2,1,0:T(8,128)(2,1)S(1)} %copy-done.31), channel_id=1, source_target_pairs={{0,1},{1,0},{2,3},{3,2},{4,5},{5,4},{6,7},{7,6},{8,9},{9,8},{10,11... | collective-permute-start | bytes 6291464 | tf_op jit(solution)/shard_map/ppermute | solution.py:32
  207.9 317.7 %reduce-scatter.2.cloned.1.call-start = ((), (), s32[]{:S(2)}) async-start(), calls=%async_computation.3 | async-start | bytes 9732096 | tf_op jit(solution)/shard_map/reduce_scatter | solution.py:756
  214.9 39.3 %copy-start.63 = (s32[4]{0:T(128)S(1)}, s32[4]{0:T(128)}, u32[]{:S(2)}) copy-start(s32[4]{0:T(128)} %param.17) | copy-start | bytes 52
  214.9 39.3 %copy-start.64 = (s32[2,1]{0,1:T(1,128)S(1)}, s32[2,1]{0,1:T(1,128)}, u32[]{:S(2)}) copy-start(s32[2,1]{0,1:T(1,128)} %param.16) | copy-start | bytes 28
  254.2 14.6 %collective-permute-start.3 = (bf16[2,256,2048]{2,1,0:T(8,128)(2,1)}, bf16[2,256,2048]{2,1,0:T(8,128)(2,1)S(1)}, u32[]{:S(2)}, u32[]{:S(2)}) collective-permute-start(bf16[2,256,2048]{2,1,0:T(8,128)(2,1)} %collective-permute-done.2), channel_id=1, source_target_pairs={{0,1},{1,0},{2,3},{3,2},{4,5},{5,4},{6,7},{7,6},{8,9},{9,8},{10,11... | collective-permute-start | bytes 6291464 | tf_op jit(solution)/shard_map/ppermute | solution.py:32
  283.0 12.0 %copy-start.61 = (bf16[704,4096]{1,0:T(8,128)(2,1)S(1)}, bf16[704,4096]{1,0:T(8,128)(2,1)}, u32[]{:S(2)}) copy-start(bf16[704,4096]{1,0:T(8,128)(2,1)} %all-gather.3.cloned.1.call-done) | copy-start | bytes 17301508
  319.1 10.7 %copy-start.67 = (bf16[2048,704]{0,1:T(8,128)(2,1)}, bf16[2048,704]{0,1:T(8,128)(2,1)S(1)}, u32[]{:S(2)}) copy-start(bf16[2048,704]{0,1:T(8,128)(2,1)S(1)} %get-tuple-element.94) | copy-start | bytes 8650756
  319.1 19.6 %copy-start.66 = (bf16[2048,704]{0,1:T(8,128)(2,1)}, bf16[2048,704]{0,1:T(8,128)(2,1)S(1)}, u32[]{:S(2)}) copy-start(bf16[2048,704]{0,1:T(8,128)(2,1)S(1)} %get-tuple-element.96) | copy-start | bytes 8650756
  319.1 19.5 %slice-start.4 = ((s8[8388608]{0:T(1024)(128)(4,1)}), s8[4194304]{0:T(1024)(128)(4,1)S(1)}, s32[]{:S(2)}) async-start(s8[8388608]{0:T(1024)(128)(4,1)} %bitcast.242), calls=%async_computation.8 | async-start | bytes 8388608
  329.8 8.9 %slice-start.5 = ((s8[8388608]{0:T(1024)(128)(4,1)}), s8[4194304]{0:T(1024)(128)(4,1)S(1)}, s32[]{:S(2)}) async-start(s8[8388608]{0:T(1024)(128)(4,1)} %bitcast.242), calls=%async_computation.9 | async-start | bytes 8388608
  382.5 11.9 %collective-permute-start.5 = (bf16[2,256,2048]{2,1,0:T(8,128)(2,1)S(1)}, bf16[2,256,2048]{2,1,0:T(8,128)(2,1)S(1)}, u32[]{:S(2)}, u32[]{:S(2)}) collective-permute-start(bf16[2,256,2048]{2,1,0:T(8,128)(2,1)S(1)} %get-tuple-element.102), channel_id=1, source_target_pairs={{0,1},{1,0},{2,3},{3,2},{4,5},{5,4},{6,7},{7,6},{8,9},{9,8},{10,11... | collective-permute-start | bytes 6291464 | tf_op jit(solution)/shard_map/ppermute | solution.py:32
  383.1 18.0 %slice-start = ((s8[16777216]{0:T(1024)(128)(4,1)}), s8[4194304]{0:T(1024)(128)(4,1)S(1)}, s32[]{:S(2)}) async-start(s8[16777216]{0:T(1024)(128)(4,1)} %bitcast.229), calls=%async_computation.4 | async-start | bytes 8388608
  383.1 18.0 %slice-start.1 = ((s8[16777216]{0:T(1024)(128)(4,1)}), s8[4194304]{0:T(1024)(128)(4,1)S(1)}, s32[]{:S(2)}) async-start(s8[16777216]{0:T(1024)(128)(4,1)} %bitcast.229), calls=%async_computation.5 | async-start | bytes 8388608
  383.1 18.0 %slice-start.2 = ((s8[16777216]{0:T(1024)(128)(4,1)}), s8[4194304]{0:T(1024)(128)(4,1)S(1)}, s32[]{:S(2)}) async-start(s8[16777216]{0:T(1024)(128)(4,1)} %bitcast.229), calls=%async_computation.6 | async-start | bytes 8388608
  392.1 12.8 %copy-start.35 = (bf16[2048,2048]{1,0:T(8,128)(2,1)}, bf16[2048,2048]{1,0:T(8,128)(2,1)S(1)}, u32[]{:S(2)}) copy-start(bf16[2048,2048]{1,0:T(8,128)(2,1)S(1)} %convolution_convert_fusion.1) | copy-start | bytes 25165828
  392.1 9.1 %slice-start.3 = ((s8[16777216]{0:T(1024)(128)(4,1)}), s8[4194304]{0:T(1024)(128)(4,1)S(1)}, s32[]{:S(2)}) async-start(s8[16777216]{0:T(1024)(128)(4,1)} %bitcast.229), calls=%async_computation.7 | async-start | bytes 8388608
  393.9 11.1 %collective-permute-start.7 = (bf16[2,256,2048]{2,1,0:T(8,128)(2,1)S(1)}, bf16[2,256,2048]{2,1,0:T(8,128)(2,1)S(1)}, u32[]{:S(2)}, u32[]{:S(2)}) collective-permute-start(bf16[2,256,2048]{2,1,0:T(8,128)(2,1)S(1)} %get-tuple-element.100), channel_id=1, source_target_pairs={{0,1},{1,0},{2,3},{3,2},{4,5},{5,4},{6,7},{7,6},{8,9},{9,8},{10,11... | collective-permute-start | bytes 6291464 | tf_op jit(solution)/shard_map/ppermute | solution.py:32
  394.0 7.6 %copy-start.29 = (bf16[2,256,2048]{2,1,0:T(8,128)(2,1)S(1)}, bf16[2,256,2048]{2,1,0:T(8,128)(2,1)}, u32[]{:S(2)}) copy-start(bf16[2,256,2048]{2,1,0:T(8,128)(2,1)} %tokens.1) | copy-start | bytes 6291460
  394.0 53.3 %collective-permute-start.4 = (bf16[2,256,2048]{2,1,0:T(8,128)(2,1)S(1)}, bf16[2,256,2048]{2,1,0:T(8,128)(2,1)}, u32[]{:S(2)}, u32[]{:S(2)}) collective-permute-start(bf16[2,256,2048]{2,1,0:T(8,128)(2,1)S(1)} %get-tuple-element.101), channel_id=1, source_target_pairs={{0,1},{1,0},{2,3},{3,2},{4,5},{5,4},{6,7},{7,6},{8,9},{9,8},{10,11... | collective-permute-start | bytes 6291464 | tf_op jit(solution)/shard_map/ppermute | solution.py:32
  399.6 47.7 %collective-permute-start.6 = (bf16[2,256,2048]{2,1,0:T(8,128)(2,1)S(1)}, bf16[2,256,2048]{2,1,0:T(8,128)(2,1)S(1)}, u32[]{:S(2)}, u32[]{:S(2)}) collective-permute-start(bf16[2,256,2048]{2,1,0:T(8,128)(2,1)S(1)} %fusion.27), channel_id=1, source_target_pairs={{0,2},{1,3},{2,0},{3,1},{4,6},{5,7},{6,4},{7,5},{8,10},{9,11},{10,... | collective-permute-start | bytes 6291464 | tf_op jit(solution)/shard_map/ppermute | solution.py:32
  401.6 49.1 %copy-start.46 = (f32[2,256]{1,0:T(2,128)}, f32[2,256]{1,0:T(2,128)S(1)}, u32[]{:S(2)}) copy-start(f32[2,256]{1,0:T(2,128)S(1)} %get-tuple-element.158) | copy-start | bytes 6148
  402.7 44.6 %copy-start.42 = (f32[2048]{0:T(1024)S(1)}, f32[2048]{0:T(1024)}, u32[]{:S(2)}) copy-start(f32[2048]{0:T(1024)} %copy-done.41) | copy-start | bytes 24580
  404.9 252.6 %collective-permute-start = (bf16[2,256,2048]{2,1,0:T(8,128)(2,1)}, bf16[2,256,2048]{2,1,0:T(8,128)(2,1)}, u32[]{:S(2)}, u32[]{:S(2)}) collective-permute-start(bf16[2,256,2048]{2,1,0:T(8,128)(2,1)} %get-tuple-element.99), channel_id=1, source_target_pairs={{0,1},{1,0},{2,3},{3,2},{4,5},{5,4},{6,7},{7,6},{8,9},{9,8},{10,11... | collective-permute-start | bytes 6291464 | tf_op jit(solution)/shard_map/ppermute | solution.py:32
  447.3 6.6 slice-start.6
  458.0 13.0 %collective-permute-start.10 = (bf16[320,512]{1,0:T(8,128)(2,1)S(1)}, bf16[320,512]{1,0:T(8,128)(2,1)S(1)}, u32[]{:S(2)}, u32[]{:S(2)}) collective-permute-start(bf16[320,512]{1,0:T(8,128)(2,1)S(1)} %get-tuple-element.108), channel_id=1, source_target_pairs={{0,3},{1,2},{2,1},{3,0},{4,7},{5,6},{6,5},{7,4},{8,11},{9,10},{10,... | collective-permute-start | bytes 983048 | tf_op jit(solution)/shard_map/ppermute | solution.py:32
  458.5 16.6 %collective-permute-start.9 = (bf16[320,512]{1,0:T(8,128)(2,1)S(1)}, bf16[320,512]{1,0:T(8,128)(2,1)S(1)}, u32[]{:S(2)}, u32[]{:S(2)}) collective-permute-start(bf16[320,512]{1,0:T(8,128)(2,1)S(1)} %get-tuple-element.109), channel_id=1, source_target_pairs={{0,2},{1,3},{2,0},{3,1},{4,6},{5,7},{6,4},{7,5},{8,10},{9,11},{10,... | collective-permute-start | bytes 983048 | tf_op jit(solution)/shard_map/ppermute | solution.py:32
  459.9 5.5 copy-start.37
  465.5 11.2 %copy-start.5 = (bf16[320,1024]{1,0:T(8,128)(2,1)S(1)}, bf16[320,1024]{1,0:T(8,128)(2,1)}, u32[]{:S(2)}) copy-start(bf16[320,1024]{1,0:T(8,128)(2,1)} %copy-done.4) | copy-start | bytes 1966084
  465.5 11.2 %copy-start.11 = (f32[32,1024]{1,0:T(8,128)S(1)}, f32[32,1024]{1,0:T(8,128)}, u32[]{:S(2)}) copy-start(f32[32,1024]{1,0:T(8,128)} %copy-done.10) | copy-start | bytes 393220
  465.5 11.2 %copy-start.13 = (f32[32,1024]{1,0:T(8,128)S(1)}, f32[32,1024]{1,0:T(8,128)}, u32[]{:S(2)}) copy-start(f32[32,1024]{1,0:T(8,128)} %copy-done.12) | copy-start | bytes 393220
  465.5 11.2 %copy-start.15 = (f32[2,64]{0,1:T(8,128)S(1)}, f32[2,64]{0,1:T(8,128)}, u32[]{:S(2)}) copy-start(f32[2,64]{0,1:T(8,128)} %copy-done.14) | copy-start | bytes 1540
  465.5 11.2 %copy-start.19 = (s32[1,1024]{1,0:T(1,128)S(1)}, s32[1,1024]{1,0:T(1,128)}, u32[]{:S(2)}) copy-start(s32[1,1024]{1,0:T(1,128)} %copy-done.18) | copy-start | bytes 12292
  465.5 11.2 %copy-start.23 = (bf16[576,1024]{1,0:T(8,128)(2,1)S(1)}, bf16[576,1024]{1,0:T(8,128)(2,1)}, u32[]{:S(2)}) copy-start(bf16[576,1024]{1,0:T(8,128)(2,1)} %copy-done.22) | copy-start | bytes 3538948
  470.9 5.0 collective-permute-start.8
  471.7 54.0 %collective-permute-start.11 = (bf16[2,256,2048]{2,1,0:T(8,128)(2,1)}, bf16[2,256,2048]{2,1,0:T(8,128)(2,1)}, u32[]{:S(2)}, u32[]{:S(2)}) collective-permute-start(bf16[2,256,2048]{2,1,0:T(8,128)(2,1)} %fusion.26), channel_id=1, source_target_pairs={{0,2},{1,3},{2,0},{3,1},{4,6},{5,7},{6,4},{7,5},{8,10},{9,11},{10,... | collective-permute-start | bytes 6291464 | tf_op jit(solution)/shard_map/ppermute | solution.py:32
  476.7 17.0 %copy-start.3 = (bf16[320,1024]{1,0:T(8,128)(2,1)S(1)}, bf16[320,1024]{1,0:T(8,128)(2,1)}, u32[]{:S(2)}) copy-start(bf16[320,1024]{1,0:T(8,128)(2,1)} %copy-done.2) | copy-start | bytes 1966084
  476.7 17.0 %copy-start.7 = (f32[32,1024]{1,0:T(8,128)S(1)}, f32[32,1024]{1,0:T(8,128)}, u32[]{:S(2)}) copy-start(f32[32,1024]{1,0:T(8,128)} %copy-done.6) | copy-start | bytes 393220
  476.7 17.0 %copy-start.9 = (f32[32,1024]{1,0:T(8,128)S(1)}, f32[32,1024]{1,0:T(8,128)}, u32[]{:S(2)}) copy-start(f32[32,1024]{1,0:T(8,128)} %copy-done.8) | copy-start | bytes 393220
  476.7 17.0 %copy-start.17 = (s32[1,1024]{1,0:T(1,128)S(1)}, s32[1,1024]{1,0:T(1,128)}, u32[]{:S(2)}) copy-start(s32[1,1024]{1,0:T(1,128)} %copy-done.16) | copy-start | bytes 12292
  476.7 17.0 %copy-start.21 = (bf16[576,1024]{1,0:T(8,128)(2,1)S(1)}, bf16[576,1024]{1,0:T(8,128)(2,1)}, u32[]{:S(2)}) copy-start(bf16[576,1024]{1,0:T(8,128)(2,1)} %copy-done.20) | copy-start | bytes 3538948
  511.1 7.5 %copy-start.44 = (f32[2048]{0:T(1024)S(1)}, f32[2048]{0:T(1024)}, u32[]{:S(2)}) copy-start(f32[2048]{0:T(1024)} %copy-done.43) | copy-start | bytes 24580
  511.1 7.5 %copy-start.58 = (f32[1024]{0:T(1024)S(1)}, f32[1024]{0:T(1024)}, u32[]{:S(2)}) copy-start(f32[1024]{0:T(1024)} %copy-done.57) | copy-start | bytes 12292
  518.5 7.2 %copy-start.25 = (bf16[576,1024]{1,0:T(8,128)(2,1)S(1)}, bf16[576,1024]{1,0:T(8,128)(2,1)}, u32[]{:S(2)}) copy-start(bf16[576,1024]{1,0:T(8,128)(2,1)} %copy-done.24) | copy-start | bytes 3538948
  518.5 7.2 %copy-start.56 = (f32[1024]{0:T(1024)S(1)}, f32[1024]{0:T(1024)}, u32[]{:S(2)}) copy-start(f32[1024]{0:T(1024)} %copy-done.55) | copy-start | bytes 12292
  525.7 7.9 %copy-start.39 = (bf16[2048,640]{1,0:T(8,128)(2,1)S(1)}, bf16[2048,640]{1,0:T(8,128)(2,1)}, u32[]{:S(2)}) copy-start(bf16[2048,640]{1,0:T(8,128)(2,1)} %get-tuple-element.44) | copy-start | bytes 7864324
  525.7 7.9 %copy-start.65 = (f32[1024,2048]{1,0:T(8,128)S(1)}, f32[1024,2048]{1,0:T(8,128)}, u32[]{:S(2)}) copy-start(f32[1024,2048]{1,0:T(8,128)} %fusion.40) | copy-start | bytes 25165828
  645.9 6.1 copy-start.30
  648.0 7.3 %copy-start.36 = (bf16[88,6144]{1,0:T(8,128)(2,1)S(1)}, bf16[88,6144]{1,0:T(8,128)(2,1)}, u32[]{:S(2)}) copy-start(bf16[88,6144]{1,0:T(8,128)(2,1)} %reduce-scatter.2.cloned.1.call-done) | copy-start | bytes 3244036
  657.5 8.5 %copy-start.40 = (f32[64,1280]{1,0:T(8,128)S(1)}, f32[64,1280]{1,0:T(8,128)}, u32[]{:S(2)}) copy-start(f32[64,1280]{1,0:T(8,128)} %get-tuple-element.177) | copy-start | bytes 983044
  657.5 9.2 %copy-start.1 = (s32[2,1024]{1,0:T(2,128)S(1)}, s32[2,1024]{1,0:T(2,128)}, u32[]{:S(2)}) copy-start(s32[2,1024]{1,0:T(2,128)} %param.15) | copy-start | bytes 24580
  (27 other events, 99.0 us)
Sparse Core Ops, SparseCore 0:
  10.2 138.5 all-gather.2
  208.1 55.1 all-gather.4
  349.2 151.7 reduce-scatter.1

commit v4 on v3

--- a/solution.py
+++ b/solution.py
@@ -90,8 +90,8 @@
 
 
 def opening(
-    n_seq, n_rows, tokens, pieces, out_w, x_all, whole, wo,
-    kept_sem, swap_send, swap_recv, tok_send, tok_recv, ring_send, ring_recv, near_send, near_recv,
+    n_seq, n_rows, tokens, pieces, x_all, whole,
+    kept_sem, swap_send, swap_recv, tok_send, tok_recv, ring_send, ring_recv,
 ):
     me, r = lax.axis_index("seq"), lax.axis_index("rows")
     a, b = lax.div(r, 2), lax.rem(r, 2)
@@ -101,7 +101,6 @@
     block = n_seq * local
     up, beside = greet(me, r, n_seq, n_rows)
     low, high = flipped(me, 1), flipped(me, top)
-    mine_low, mine_top = lax.rem(me, 2), lax.div(me, 2)
 
     def send(src, dst, send_sem, recv_sem, **where):
         copy = pltpu.make_async_remote_copy(
@@ -111,11 +110,13 @@
         copy.start()
         return copy
 
+    def slot(j):
+        return pl.ds(j * span, span)
+
     mine = whole.at[pl.ds(pl.multiple_of(r * block + me * local, local), local)]
     kept = [
         pltpu.make_async_copy(pieces.at[me], mine, kept_sem.at[0]),
-        pltpu.make_async_copy(out_w, wo.at[r, mine_low, mine_top], kept_sem.at[1]),
-        pltpu.make_async_copy(tokens, x_all.at[:, pl.ds(0, span)], kept_sem.at[2]),
+        pltpu.make_async_copy(tokens, x_all.at[:, slot(0)], kept_sem.at[1]),
     ]
     for copy in kept:
         copy.start()
@@ -123,11 +124,6 @@
         send(pieces.at[other(me, j, n_seq)], mine, swap_send.at[j], swap_recv.at[j], seq=other(me, j, n_seq))
         for j in range(1, n_seq)
     ]
-    swaps.append(send(out_w, wo.at[r, mine_low, mine_top], swap_send.at[0], swap_recv.at[0], seq=high))
-
-    def slot(j):
-        return pl.ds(j * span, span)
-
     far = [
         send(tokens.at[t], x_all.at[t, slot(top)], tok_send.at[t, top], tok_recv.at[t, top], seq=high)
         for t in range(rows)
@@ -136,58 +132,40 @@
         send(tokens.at[t], x_all.at[t, slot(1)], tok_send.at[t, 1], tok_recv.at[t, 1], seq=low)
         for t in range(rows)
     ]
-    ring = {}
-    sides = []
-    out_near = []
-
-    def pass_on(i, kind):
+    ring, sides = [], []
+
+    def pass_on(i):
         owner = 2 * lax.rem(a + half - i, half) + b
-        ref = whole.at[pl.ds(pl.multiple_of(owner * block, block), block)] if kind == 0 else wo.at[owner, mine_low]
+        ref = whole.at[pl.ds(pl.multiple_of(owner * block, block), block)]
         if i < half - 1:
-            ring[(kind, i)] = send(ref, ref, ring_send.at[0, kind, i], ring_recv.at[0, kind, i], rows=up)
-        sides.append((kind, i, send(ref, ref, ring_send.at[1, kind, i], ring_recv.at[1, kind, i], rows=beside)))
-        if kind == 1:
-            out_near.append(send(ref, ref, near_send.at[0, i], near_recv.at[0, i], seq=low))
-
-    def forward_tokens(t):
+            ring.append(send(ref, ref, ring_send.at[0, i], ring_recv.at[0, i], rows=up))
+        sides.append(send(ref, ref, ring_send.at[1, i], ring_recv.at[1, i], rows=beside))
+
+    kept[0].wait()
+    for copy in swaps:
+        copy.wait_recv()
+    pass_on(0)
+    for i in range(1, half):
+        ring[i - 1].wait_recv()
+        pass_on(i)
+    for t in range(rows):
         far[t].wait_recv()
         near.append(
-            send(x_all.at[t, slot(top)], x_all.at[t, slot(top + 1)], tok_send.at[t, 0], tok_recv.at[t, 0], seq=low)
+            send(
+                x_all.at[t, slot(top)], x_all.at[t, slot(top + 1)],
+                tok_send.at[t, 0], tok_recv.at[t, 0], seq=low,
+            )
         )
-
-    kept[0].wait()
-    for copy in swaps[:-1]:
+    kept[1].wait()
+    for copy in sides + near:
         copy.wait_recv()
-    pass_on(0, 0)
-    kept[1].wait()
-    swaps[-1].wait_recv()
-    pass_on(0, 1)
-    late = list(range(rows))
-    for i in range(1, half):
-        for kind in range(2):
-            ring[(kind, i - 1)].wait_recv()
-            pass_on(i, kind)
-        if i >= half - 2 and len(late) > 1:
-            forward_tokens(late.pop(0))
-    for t in late:
-        forward_tokens(t)
-    for kind, i, copy in sides:
-        copy.wait_recv()
-        if kind == 1:
-            owner = 2 * lax.rem(a + half - i, half) + 1 - b
-            ref = wo.at[owner, mine_low]
-            out_near.append(send(ref, ref, near_send.at[1, i], near_recv.at[1, i], seq=low))
-    kept[2].wait()
-    for copy in near + out_near:
-        copy.wait_recv()
-    for copy in swaps + far + near + list(ring.values()) + [c for _, _, c in sides] + out_near:
+    for copy in swaps + far + near + ring + sides:
         copy.wait_send()
 
 
-def open_layer(n_seq, n_rows, tokens, pieces, out_w):
+def open_layer(n_seq, n_rows, tokens, pieces):
     rows, span, width = tokens.shape
     _, local, cols = pieces.shape
-    half = n_rows // 2
     hbm = pl.BlockSpec(memory_space=pl.ANY)
     dma = pltpu.SemaphoreType.DMA
     return pl.pallas_call(
@@ -195,48 +173,64 @@
         out_shape=(
             jax.ShapeDtypeStruct((rows, n_seq * span, width), BF),
             jax.ShapeDtypeStruct((n_rows * n_seq * local, cols), BF),
-            jax.ShapeDtypeStruct((n_rows, n_seq // 2, 2) + out_w.shape, BF),
-        ),
-        in_specs=[hbm] * 3,
-        out_specs=(hbm,) * 3,
+        ),
+        in_specs=[hbm] * 2,
+        out_specs=(hbm,) * 2,
         scratch_shapes=[
-            dma((3,)),
+            dma((2,)),
             dma((n_seq,)),
             dma((n_seq,)),
             dma((rows, n_seq)),
             dma((rows, n_seq)),
-            dma((2, 2, half)),
-            dma((2, 2, half)),
-            dma((2, half)),
-            dma((2, half)),
+            dma((2, n_rows // 2)),
+            dma((2, n_rows // 2)),
         ],
         compiler_params=pltpu.CompilerParams(collective_id=0, has_side_effects=True),
         name="opening",
-    )(tokens, pieces, out_w)
+    )(tokens, pieces)
 
 
 def meeting(n_seq, n_rows, *refs):
-    rows = (len(refs) - 8) // 1
-    o, (o_all, kept_sem, far_s, far_r, near_s, near_r, on_s, on_r) = refs[:rows], refs[rows:]
+    rows = len(refs) - 16
+    o, (
+        out_w, o_all, wo, kept_sem, far_s, far_r, near_s, near_r, on_s, on_r,
+        pair_s, pair_r, ring_s, ring_r, side_s, side_r,
+    ) = refs[:rows], refs[rows:]
     me, r = lax.axis_index("seq"), lax.axis_index("rows")
-    greet(me, r, n_seq, n_rows)
+    up, beside = greet(me, r, n_seq, n_rows)
+    a, b = lax.div(r, 2), lax.rem(r, 2)
+    half = n_rows // 2
     top = n_seq // 2
     length = o[0].shape[1]
     span = length // n_seq
     low, high = flipped(me, 1), flipped(me, top)
 
-    def send(src, dst, send_sem, recv_sem, where):
+    def send(src, dst, send_sem, recv_sem, where, axis="seq"):
         copy = pltpu.make_async_remote_copy(
             src_ref=src, dst_ref=dst, send_sem=send_sem, recv_sem=recv_sem,
-            device_id={"seq": where}, device_id_type=MESH,
+            device_id={axis: where}, device_id_type=MESH,
         )
         copy.start()
         return copy
 
+    mine_low, mine_top = lax.rem(me, 2), lax.div(me, 2)
+    mine = wo.at[r, mine_low, mine_top]
+    own = pltpu.make_async_copy(out_w, mine, kept_sem.at[rows])
+    own.start()
+    pair = send(out_w, mine, pair_s, pair_r, high)
+
     def place(who, t, j, count=1):
         return o_all.at[who, :, pl.ds(t * length + j * span, count * span)]
 
-    far, near, kept = [], [], []
+    far, near, kept, ring, sides, lows = [], [], [], [], [], []
+
+    def pass_on(i):
+        ref = wo.at[2 * lax.rem(a + half - i, half) + b, mine_low]
+        if i < half - 1:
+            ring.append(send(ref, ref, ring_s.at[i], ring_r.at[i], up, "rows"))
+        sides.append(send(ref, ref, side_s.at[0, i], side_r.at[0, i], beside, "rows"))
+        lows.append(send(ref, ref, side_s.at[1, i], side_r.at[1, i], low))
+
     for t in range(rows):
         for j in range(0, n_seq, top):
             far.append(
@@ -252,33 +246,50 @@
             )
         kept.append(pltpu.make_async_copy(o[t], place(me, t, 0, n_seq), kept_sem.at[t]))
         kept[-1].start()
+    own.wait()
+    pair.wait_recv()
+    pass_on(0)
+    for i in range(1, half):
+        ring[i - 1].wait_recv()
+        pass_on(i)
     for t in range(rows):
         for c, j in enumerate(range(0, n_seq, top)):
             far[2 * t + c].wait_recv()
             for k in range(j, j + top):
                 near.append(send(place(high, t, k), place(high, t, k ^ 1), on_s.at[t, k], on_r.at[t, k], low))
+    for i in range(half):
+        sides[i].wait_recv()
+        ref = wo.at[2 * lax.rem(a + half - i, half) + 1 - b, mine_low]
+        lows.append(send(ref, ref, side_s.at[2, i], side_r.at[2, i], low))
     for copy in kept:
         copy.wait()
-    for copy in near:
+    for copy in near + lows:
         copy.wait_recv()
-    for copy in far + near:
+    for copy in far + near + [pair] + ring + sides + lows:
         copy.wait_send()
 
 
-def meet(n_seq, n_rows, o):
+def meet(n_seq, n_rows, o, out_w):
     columns, length = o[0].shape
     rows = len(o)
     hbm = pl.BlockSpec(memory_space=pl.ANY)
     dma = pltpu.SemaphoreType.DMA
     return pl.pallas_call(
         functools.partial(meeting, n_seq, n_rows),
-        out_shape=jax.ShapeDtypeStruct((n_seq, columns, rows * length), BF),
-        in_specs=[hbm] * rows,
-        out_specs=hbm,
-        scratch_shapes=[dma((rows,))] + [dma((rows, n_seq))] * 6,
+        out_shape=(
+            jax.ShapeDtypeStruct((n_seq, columns, rows * length), BF),
+            jax.ShapeDtypeStruct((n_rows, 2, n_seq // 2) + out_w.shape, BF),
+        ),
+        in_specs=[hbm] * (rows + 1),
+        out_specs=(hbm, hbm),
+        scratch_shapes=[dma((rows + 1,))]
+        + [dma((rows, n_seq))] * 6
+        + [dma, dma]
+        + [dma((n_rows // 2,))] * 2
+        + [dma((3, n_rows // 2))] * 2,
         compiler_params=pltpu.CompilerParams(collective_id=2, has_side_effects=True),
         name="meeting",
-    )(*o)
+    )(*o, out_w)
 
 
 def add_rows(out, *terms):
@@ -295,15 +306,19 @@
 
 
 def closing(
-    n_seq, n_rows, da, dw, do, da_out, dw_out, do_out,
-    da_near, da_send, da_far, da_own, dw_near, dw_send, dw_far, dw_own, do_near, do_sum, do_next,
-    do_send, do_far, do_own, do_last, near_s, near_r, far_s, far_r, ring_s, ring_r, end_s, end_r,
+    n_seq, n_rows, *refs
 ):
+    rows = len(refs) - 28
+    da = refs[:rows]
+    (
+        dw, do, da_out, dw_out, do_out,
+        da_near, da_send, da_far, da_own, dw_near, dw_send, dw_far, dw_own, do_near, do_sum, do_next,
+        do_send, do_far, do_own, do_last, near_s, near_r, far_s, far_r, ring_s, ring_r, end_s, end_r,
+    ) = refs[rows:]
     me, r = lax.axis_index("seq"), lax.axis_index("rows")
     up, beside = greet(me, r, n_seq, n_rows)
     a, b = lax.div(r, 2), lax.rem(r, 2)
     half, top = n_rows // 2, n_seq // 2
-    rows = da.shape[0]
     local = do.shape[1]
 
     def send(src, dst, send_sem, recv_sem, **where):
@@ -321,14 +336,26 @@
     high = flipped(me, top)
     order = list(range(1, half)) + [0]
     near_da = [
-        [send(da.at[t, k + 1], da_near.at[t, k // top], near_s.at[t, k // top], near_r.at[t, k // top], seq=low)
+        [send(da[t].at[k + 1], da_near.at[t, k // top], near_s.at[t, k // top], near_r.at[t, k // top], seq=low)
          for t in range(rows)]
         for k in (top, 0)
     ]
-    side_dw = [
-        send(dw.at[owner(i, 1)], dw_near.at[i], ring_s.at[0, 0, i], ring_r.at[0, 0, i], rows=beside)
-        for i in order
-    ]
+    side_dw, side_do = [], []
+
+    def beside_next():
+        n = len(side_dw) + len(side_do)
+        i = order[n % half]
+        if n < half:
+            side_dw.append(
+                send(dw.at[owner(i, 1)], dw_near.at[i], ring_s.at[0, 0, i], ring_r.at[0, 0, i], rows=beside)
+            )
+        elif n < 2 * half:
+            side_do.append(
+                send(do_sum.at[owner(i, 1)], do_next.at[i], ring_s.at[0, 1, i], ring_r.at[0, 1, i], rows=beside)
+            )
+
+    beside_next()
+    beside_next()
     near_do = []
     for c, k in enumerate((top, 0)):
         whose = other(me, k + 1, n_seq)
@@ -339,11 +366,12 @@
     far_da = []
     for t in range(rows):
         near_da[0][t].wait_recv()
-        add_rows(da_send.at[t], da.at[t, top], da_near.at[t, 1])
+        add_rows(da_send.at[t], da[t].at[top], da_near.at[t, 1])
         far_da.append(send(da_send.at[t], da_far.at[t], far_s.at[t], far_r.at[t], seq=high))
 
     def ring_step(kind, n, i, near, mine, far, out, final, side):
         side.wait_recv()
+        beside_next()
         terms = (mine, near) if n == 0 else (mine, near, far.at[n - 1])
         if i == 0:
             add_rows(final, *terms)
@@ -351,7 +379,7 @@
         add_rows(out.at[n], *terms)
         return send(out.at[n], far.at[n], ring_s.at[1, kind, n], ring_r.at[1, kind, n], rows=up)
 
-    ring_dw, ring_do, side_do = [], [], []
+    ring_dw, ring_do = [], []
 
     def step_dw(n):
         i = order[n]
@@ -379,13 +407,9 @@
                 do.at[j * n_seq + other(me, k, n_seq)],
                 do_near.at[c, j],
             )
-    for i in order:
-        side_do.append(
-            send(do_sum.at[owner(i, 1)], do_next.at[i], ring_s.at[0, 1, i], ring_r.at[0, 1, i], rows=beside)
-        )
     for n in range(1, half):
         step_dw(n)
-        step_do(n - 1)
+    step_do(0)
     kept = pltpu.make_async_copy(dw_own.at[pl.ds(pl.multiple_of(me * local, local), local)], dw_out.at[me], end_s.at[0])
     kept.start()
     ends = [
@@ -395,11 +419,12 @@
         )
         for j in range(1, n_seq)
     ]
-    step_do(half - 1)
+    for n in range(1, half):
+        step_do(n)
     ends.append(send(do_own.at[pl.ds(0, local)], do_last, end_s.at[n_seq], end_r.at[n_seq], seq=high))
     for t in range(rows):
         near_da[1][t].wait_recv()
-        add_rows(da_own.at[t], da.at[t, 0], da_near.at[t, 0])
+        add_rows(da_own.at[t], da[t].at[0], da_near.at[t, 0])
     for t in range(rows):
         far_da[t].wait_recv()
         add_rows(da_out.at[t], da_own.at[t], da_far.at[t])
@@ -414,7 +439,8 @@
 
 
 def close_layer(n_seq, n_rows, da, dw, do):
-    rows, _, span, width = da.shape
+    rows = len(da)
+    _, span, width = da[0].shape
     _, block, cols = dw.shape
     _, local, wide = do.shape
     half = n_rows // 2
@@ -428,7 +454,7 @@
             jax.ShapeDtypeStruct((n_seq, local, cols), BF),
             jax.ShapeDtypeStruct((local, wide), F32),
         ),
-        in_specs=[vmem] * 3,
+        in_specs=[vmem] * (rows + 2),
         out_specs=(vmem,) * 3,
         scratch_shapes=[
             pltpu.VMEM((rows, 2, span, width), BF),
@@ -459,7 +485,7 @@
             collective_id=1, has_side_effects=True, vmem_limit_bytes=60 << 20
         ),
         name="closing",
-    )(da, dw, do)
+    )(*da, dw, do)
 
 
 def head_unit(v):
@@ -695,8 +721,8 @@
                 parts.append(query_key_value_weight[:, at : at + HEAD_SIZE])
         parts += [norm_gains.T, counted, jnp.zeros((local, extra - 3), BF)]
         pieces.append(jnp.concatenate(parts, axis=1))
-    x_rows, whole, w_out = open_layer(n_seq, n_rows, tokens, jnp.stack(pieces), out_weight)
-    w_out = jnp.swapaxes(w_out, 1, 2).reshape(width, -1)
+    x_rows, whole = open_layer(n_seq, n_rows, tokens, jnp.stack(pieces))
+    x_rows, d_output = tie((x_rows, d_output))
     w_qkv = whole[:, :cols]
     gains = whole[:, cols : cols + 2].astype(F32).T
     counts = whole[:, cols + 2].astype(F32).reshape(n_rows, n_seq, local)[:, 0, :NCORP]
@@ -724,19 +750,24 @@
         o, inv = attention_forward(*args)
         kept.append((a_in, args, o, inv))
         o_rows.append(o)
-    o_all = meet(n_seq, n_rows, o_rows).reshape(n_seq * q_cols, rows * length)
-    o_all, dy_own = tie((o_all, d_output))
+    dy_far = cross_seq(d_output, n_seq)
+    o_rows[-1], dy_far = tie((o_rows[-1], dy_far))
+    o_all, w_out = meet(n_seq, n_rows, o_rows, out_weight)
+    o_all = o_all.reshape(n_seq * q_cols, rows * length)
+    w_out = jnp.swapaxes(w_out, 1, 2).reshape(width, -1)
+    dy_all = [d_output, swap(d_output, "seq", n_seq, 1), dy_far, swap(dy_far, "seq", n_seq, 1)]
+    dy_all = jnp.stack(dy_all, axis=1)
     x_all = x_rows.reshape(rows * length, width).astype(F32)
 
     h_all = x_all + dot(o_all, w_out, 0, 1)
     inverse_two = inverse_rms(h_all)
     f_in = (h_all * inverse_two * gains[1]).astype(BF)
 
-    w_gu = lax.all_gather(gate_up_weight, "rows", axis=0, tiled=True)
-    w_dn = lax.all_gather(down_weight, "rows", axis=0, tiled=True)
-    w_g, w_u = w_gu[:, :width], w_gu[:, width:]
-    dy_all = jnp.stack(gather_seq(dy_own, n_seq), axis=1).astype(F32)
-    gy = (row_scale[:, None, None, None] * dy_all).astype(BF).reshape(rows * length, width)
+    w_ff = jnp.concatenate([gate_up_weight, down_weight], axis=1)
+    w_ff = lax.all_gather(w_ff, "rows", axis=0, tiled=True)
+    w_g, w_u, w_dn = (w_ff[:, i * width : (i + 1) * width] for i in range(3))
+    gy = row_scale[:, None, None, None] * dy_all.astype(F32)
+    gy = gy.astype(BF).reshape(rows * length, width)
     gate = dot(f_in, w_g, 1, 1)
     upper = dot(f_in, w_u, 1, 1)
     sigma = jax.nn.sigmoid(gate)
@@ -745,11 +776,14 @@
     d_hidden = dot(gy, w_dn, 1, 1)
     d_upper = (d_hidden * active).astype(BF)
     d_gate = (d_hidden * upper * sigma * (1.0 + gate * (1.0 - sigma))).astype(BF)
-    df_part = dot(d_gate, w_g, 1, 0) + dot(d_upper, w_u, 1, 0)
-    d_gain_two = jnp.sum(df_part * (h_all * inverse_two), axis=0)
-    df_slots = df_part.astype(BF).reshape(rows, n_seq, span, width)
-    df_kept, df_sent = fold_seq([df_slots[:, j] for j in range(n_seq)], n_seq)
-    df_got = cross_seq(df_sent, n_seq)
+    df_rows = []
+    for r in range(rows):
+        at = slice(r * length, (r + 1) * length)
+        part = dot(d_gate[at], w_g, 1, 0) + dot(d_upper[at], w_u, 1, 0)
+        part = part.astype(BF).reshape(n_seq, span, width)
+        df_rows.append(fold_seq([part[j] for j in range(n_seq)], n_seq))
+    sent, d_gate, d_upper, hidden = tie(([v for _, v in df_rows], d_gate, d_upper, hidden))
+    df_rows = [(v[0], cross_seq(sent[r], n_seq)) for r, v in enumerate(df_rows)]
     ffn_grads = jnp.concatenate(
         [dot(d_gate, f_in, 0, 0), dot(d_upper, f_in, 0, 0), dot(hidden, gy, 0, 0)], axis=1
     ).astype(BF)
@@ -757,59 +791,62 @@
     y_slots = dot(hidden, w_dn, 1, 0).astype(BF)
     y_slots = y_slots.reshape(rows, n_seq, span, width)
     y_kept, y_sent = fold_seq([y_slots[:, j] for j in range(n_seq)], n_seq)
-    df_got, y_sent = tie((df_got, y_sent))
-    df = (df_kept + df_got.astype(F32)).reshape(rows * span, width)
     h_own = h_all.reshape(rows, n_seq, span, width)[:, 0]
 
-    h_one = h_own.reshape(rows * span, width)
-    inverse = inverse_rms(h_one)
-    unit = h_one * inverse
-    scaled = df * gains[1]
-    g_two = (row_scale[:, None, None] * d_output.astype(F32)).reshape(rows * span, width)
-    d_h = g_two + inverse * (scaled - unit * jnp.mean(scaled * unit, axis=-1, keepdims=True))
-    grad_att = d_h.astype(BF)
+    d_h, grad_att, do_rows, d_gain_two = [], [], [], 0.0
+    for r in range(rows):
+        inverse = inverse_rms(h_own[r])
+        unit = h_own[r] * inverse
+        df = df_rows[r][0] + df_rows[r][1].astype(F32)
+        d_gain_two = d_gain_two + jnp.sum(df * unit, axis=0)
+        scaled = df * gains[1]
+        g_two = row_scale[r] * d_output[r].astype(F32)
+        d_h.append(
+            g_two + inverse * (scaled - unit * jnp.mean(scaled * unit, axis=-1, keepdims=True))
+        )
+        grad_att.append(d_h[r].astype(BF))
+        do_src = dot(w_out, grad_att[r], 0, 1).astype(BF).reshape(n_seq, q_cols, span)
+        do_src = jnp.take(do_src, rel, axis=0)
+        do_slots = [do_src[0]] + [swap(do_src[m], "seq", n_seq, m) for m in range(1, n_seq)]
+        if r == rows - 1:
+            do_slots, y_sent = tie((do_slots, y_sent))
+        do_rows.append(jnp.concatenate(do_slots, axis=1))
+    y_got = cross_seq(y_sent, n_seq)
     o_own = jnp.concatenate(
         [o_all[:, r * length : r * length + span] for r in range(rows)], axis=1
     )
-    do_src = dot(w_out, grad_att, 0, 1).astype(BF).reshape(n_seq, q_cols, rows * span)
-    do_src = jnp.take(do_src, rel, axis=0)
-    do_slots = [do_src[0]] + [swap(do_src[m], "seq", n_seq, m) for m in range(1, n_seq)]
-
-    d_out = dot(grad_att, o_own, 0, 1).astype(BF)
-    do_slots[-1], y_sent = tie((do_slots[-1], y_sent))
-    y_got = cross_seq(y_sent, n_seq)
-
-    d_acts, d_parts, d_heads, d_gain_one = [], [], 0.0, 0.0
+    d_out = dot(jnp.concatenate(grad_att, axis=0), o_own, 0, 1).astype(BF)
+
+    d_acts, d_parts, d_heads = [], [], 0.0
     for r in range(rows):
         a_in, args, o, inv = kept[r]
-        d_o = jnp.concatenate([d[:, r * span : (r + 1) * span] for d in do_slots], axis=1)
-        d_act, head_sums = attention_backward(*args, o, inv, d_o)
+        d_act, head_sums = attention_backward(*args, o, inv, do_rows[r])
         if r == rows - 1:
-            d_act, y_got, ffn_sums = tie((d_act, y_got, ffn_sums))
+            d_act, y_got = tie((d_act, y_got))
             output = (h_own + (y_kept + y_got.astype(F32))).astype(BF)
         d_heads = d_heads + jnp.sum(head_sums, axis=-1)
         part = dot(d_act, w_qkv, 0, 1)
-        x = x_rows[r].astype(F32)
-        d_gain_one = d_gain_one + jnp.sum(part * (x * inverse_rms(x)), axis=0)
-        d_parts.append(part.astype(BF).reshape(n_seq, span, width))
+        part = part.astype(BF)
+        if r == rows - 1:
+            part, ffn_sums, output = tie((part, ffn_sums, output))
+        d_parts.append(part.reshape(n_seq, span, width))
         d_acts.append(d_act)
     spread = 2 * HEAD_SIZE // local
     tail = jnp.concatenate(
         [
-            d_gain_one[:, None],
             d_gain_two[:, None],
             jnp.tile(d_heads.reshape(local, spread), (width // local, 1)),
-            jnp.zeros((width, extra - 2 - spread), F32),
+            jnp.zeros((width, extra - 1 - spread), F32),
         ],
         axis=1,
     )
     d_w = sum(dot(kept[r][0], d_acts[r], 0, 1) for r in range(rows))
-    d_w = jnp.concatenate([d_w.astype(BF), tail.astype(BF)], axis=1)
+    d_w = jnp.pad(d_w, ((0, 0), (0, extra))) + jnp.pad(tail, ((0, 0), (cols, 0)))
     d_a, d_w, d_out = close_layer(
         n_seq,
         n_rows,
-        jnp.stack(d_parts),
-        d_w.reshape(n_rows, n_seq * local, cols + extra),
+        d_parts,
+        d_w.astype(BF).reshape(n_rows, n_seq * local, cols + extra),
         d_out.reshape(n_rows * n_seq, local, -1),
     )
     d_a = d_a.reshape(rows * span, width)
@@ -818,7 +855,7 @@
     inverse = inverse_rms(x_own)
     unit = x_own * inverse
     scaled = d_a * gains[0]
-    d_tokens = d_h + inverse * (scaled - unit * jnp.mean(scaled * unit, axis=-1, keepdims=True))
+    d_tokens = jnp.concatenate(d_h, axis=0) + inverse * (scaled - unit * jnp.mean(scaled * unit, axis=-1, keepdims=True))
     d_tokens = d_tokens.reshape(rows, span, width)
 
     k_sum = [jnp.zeros((local, HEAD_SIZE), F32) for _ in range(KEY_VALUE_HEADS)]
@@ -829,9 +866,11 @@
             k_sum[lead[t] + m] += d_w[t, :, a : a + HEAD_SIZE]
             v_sum[lead[t] + m] += d_w[t, :, a + kv_cols : a + kv_cols + HEAD_SIZE]
     d_qkv = jnp.concatenate([d_w[t, :, :q_cols] for t in range(n_seq)] + k_sum + v_sum, axis=1)
-    ends = jnp.sum(d_w[:, :, cols : cols + 2 + spread], axis=0)
-    d_gains = ends[:, :2].T
-    d_qk_gains = ends[:, 2:].reshape(2, HEAD_SIZE)
+    d_gain_one = jnp.sum(query_key_value_weight.astype(F32) * d_qkv, axis=1)
+    d_gain_one = d_gain_one / norm_gains[0].astype(F32)
+    ends = jnp.sum(d_w[:, :, cols : cols + 1 + spread], axis=0)
+    d_gains = jnp.stack([d_gain_one, ends[:, 0]], axis=0)
+    d_qk_gains = ends[:, 1:].reshape(2, HEAD_SIZE)
     return (
         output,
         d_tokens,

time: 684 us -> 630 us (0.921)
  Pallas kernels: 289 us -> 257 us
  local copies, waits for them, and re-layouts: 48.4 us -> 34.4 us
  waiting for transfers between devices: 61.7 us -> 51.6 us
  matrix products: 169 us -> 162 us
    pallas_call x1, Pallas kernels: 114 us -> 85.1 us  [open_layer(): pl.pallas_call(functools.partial(opening, n_seq, n_rows), out_shape=(jax....]
    concatenate x2 -> x1, local copies, waits for them, and re-layouts: 11.5 us -> 0.07 us  [on_device(): jnp.concatenate([d_gain_two[:, None], jnp.tile(d_heads.reshape(local, spr...]
    convert_element_type x2 -> x4, other arithmetic: 13.6 us -> 23.6 us  [the longest x1 8.08 us: on_device(): gy = gy.astype(BF).reshape(rows * length, width)]
    ppermute x12 -> x18, waiting for transfers between devices: 61 us -> 51.6 us  [swap(): return lax.ppermute(v, axis, [(i, i ^ bit) for i in range(n)])]
    dot_general x18 -> x21, matrix products: 169 us -> 162 us  [dot(): lax.dot_general(a, b, (((ca,), (cb,)), ((), ())), preferred_element_type=...]
    another operation x5 -> x3, other arithmetic: 14.3 us -> 7.99 us  [the longest x1 6.64 us: on_device(): dy_all = jnp.stack(dy_all, axis=1)]
  transfers between devices with their start and end apart: 15 -> 20, of which waited for: 3 -> 6; matrix products, arithmetic and copies ran while one was open for 36% -> 29% of each run, Pallas kernels for 43% -> 29%
where the time goes in v4:
time: 630 us; the launch traced here: 619 us
  Pallas kernels  257 us (41%)
  matrix products  162 us (26%)
  other arithmetic  87.9 us (14%)
  waiting for transfers between devices  51.6 us (8%)
  local copies, waits for them, and re-layouts  34.4 us (5%)
  between operations  15.6 us (2%)
  starting transfers between devices  10.4 us (2%)
    dot_general x21, matrix products, dot(): lax.dot_general(a, b, (((ca,), (cb,)), ((), ())), preferred_element_type=...  162 us
    pallas_call x1, Pallas kernels, open_layer(): pl.pallas_call(functools.partial(opening, n_seq, n_rows), out_shape=(jax....  85.1 us
    pallas_call x1, Pallas kernels, close_layer(): pl.pallas_call(functools.partial(closing, n_seq, n_rows), out_shape=(jax....  77.3 us
    ppermute x18, waiting for transfers between devices, swap(): return lax.ppermute(v, axis, [(i, i ^ bit) for i in range(n)])  51.6 us
    pallas_call x1, Pallas kernels, meet(): pl.pallas_call(functools.partial(meeting, n_seq, n_rows), out_shape=(jax....  49.7 us
    pallas_call x2, Pallas kernels, attention_backward(): pl.pallas_call(functools.partial(backward_heads, plan), out_shape=(jax.Sh...  31.1 us
    pallas_call x2, Pallas kernels, attention_forward(): pl.pallas_call(functools.partial(forward_heads, plan), out_shape=(jax.Sha...  14.2 us
  transfers between devices with their start and end apart: 20, of which 6 were waited for; matrix products, arithmetic and copies ran while one was open for 29% of the time, Pallas kernels for 29%

profile of v4, /device:TPU:0, one launch (start us, length us, event | category | flops | bytes accessed | tf_op | source)
XLA Modules:
  0.0 619.1 jit_solution(3854778246572178972)
XLA Ops:
  7.3 2.4 pad_maximum_fusion.3
  14.7 85.1 %opening.1 = (bf16[2,1024,2048]{2,1,0:T(8,128)(2,1)}, bf16[2048,640]{1,0:T(8,128)(2,1)}) custom-call(bf16[2,256,2048]{2,1,0:T(8,128)(2,1)} %tokens.1, bf16[4,64,640]{2,1,0:T(8,128)(2,1)} %pad_maximum_fusion.6.pieces), custom_call_target="tpu_custom_call" | custom-call | tf_op jit(solution)/shard_map/opening/pallas_call | solution.py:171
  101.7 1.4 slice_reduce_fusion.2
  104.7 4.4 fusion.4
  110.2 1.2 convert_bitcast_fusion
  112.5 6.2 %fusion.46.x_ref = bf16[576,1024]{1,0:T(8,128)(2,1)S(1)} fusion(bf16[2048,640]{1,0:T(8,128)(2,1)} %get-tuple-element.55, f32[1024]{0:T(1024)S(1)} %get-tuple-element.170, f32[2048]{0:T(1024)S(1)} %get-tuple-element.100, bf16[2,1024,2048]{2,1,0:T(8,128)(2,1)} %get-tuple-element.57), kind=kOutput, calls=%fused_computation.98 | convolution fusion | flops 2424897536 | bytes 8007680 | tf_op jit(solution)/shard_map/dot_general | solution.py:28
  118.8 7.1 %attention_forward.3 = (bf16[320,1024]{1,0:T(8,128)(2,1)S(1)}, f32[5,1,1024]{2,1,0:T(1,128)S(1)}) custom-call(s32[1]{0:T(128)} %bitcast.me_ref, bf16[576,1024]{1,0:T(8,128)(2,1)S(1)} %fusion.46.x_ref, f32[32,1024]{1,0:T(8,128)S(1)} %get-tuple-element.142.cos_ref, f32[32,1024]{1,0:T(8,128)S(1)} %get-tuple-element.140.sin_ref, ...), custom_call_target="tpu_custom_call" | custom-call | flops 1342177280 | bytes 4194304 | tf_op jit(solution)/shard_map/attention_forward/pallas_call | solution.py:627
  126.0 3.1 fusion.43.x_ref
  129.1 7.1 %attention_forward.2 = (bf16[320,1024]{1,0:T(8,128)(2,1)S(1)}, f32[5,1,1024]{2,1,0:T(1,128)S(1)}) custom-call(s32[1]{0:T(128)} %bitcast.me_ref, bf16[576,1024]{1,0:T(8,128)(2,1)S(1)} %fusion.43.x_ref, f32[32,1024]{1,0:T(8,128)S(1)} %get-tuple-element.143.cos_ref, f32[32,1024]{1,0:T(8,128)S(1)} %get-tuple-element.141.sin_ref, ...), custom_call_target="tpu_custom_call" | custom-call | flops 1342177280 | bytes 4194304 | tf_op jit(solution)/shard_map/attention_forward/pallas_call | solution.py:627
  137.1 11.0 %collective-permute-done = bf16[2,256,2048]{2,1,0:T(8,128)(2,1)} collective-permute-done((bf16[2,256,2048]{2,1,0:T(8,128)(2,1)S(1)}, bf16[2,256,2048]{2,1,0:T(8,128)(2,1)}, u32[]{:S(2)}, u32[]{:S(2)}) %collective-permute-start) | collective-permute-done | bytes 2097184 | tf_op jit(solution)/shard_map/ppermute | solution.py:32
  148.1 49.7 %meeting.1 = (bf16[4,320,2048]{2,1,0:T(8,128)(2,1)}, bf16[8,2,2,64,1280]{4,3,2,1,0:T(8,128)(2,1)}) custom-call(bf16[320,1024]{1,0:T(8,128)(2,1)} %copy-done.4, bf16[320,1024]{1,0:T(8,128)(2,1)} %copy-done.2, bf16[64,1280]{1,0:T(8,128)(2,1)} %refs_2_.1), custom_call_target="tpu_custom_call" | custom-call | tf_op jit(solution)/shard_map/meeting/pallas_call | solution.py:277
  197.9 3.1 copy.38
  200.9 20.6 %multiply_reduce_fusion = (f32[2048]{0:T(1024)S(1)}, f32[2048,2048]{1,0:T(8,128)}) fusion(bf16[1280,2048]{1,0:T(8,128)(2,1)} %bitcast.241, bf16[2048,1280]{1,0:T(8,128)(2,1)S(1)} %bitcast.222, bf16[2,1024,2048]{2,1,0:T(8,128)(2,1)} %get-tuple-element.57), kind=kOutput, calls=%fused_computation.7 | convolution fusion | flops 10754193408 | bytes 35659776 | tf_op jit(solution)/shard_map/dot_general | solution.py:28
  221.5 9.5 %multiply_convert_fusion = bf16[2048,2048]{1,0:T(8,128)(2,1)} fusion(f32[2048,2048]{1,0:T(8,128)} %get-tuple-element.167, f32[2048]{0:T(1024)S(1)} %get-tuple-element.99, f32[2048]{0:T(1024)S(1)} %add_rsqrt_fusion), kind=kLoop, calls=%fused_computation.6 | loop fusion | flops 12582912 | bytes 25182208 | tf_op jit(solution)/shard_map/convert_element_type | solution.py:764
  231.1 6.6 %pad_maximum_fusion.1 = bf16[2,4,256,2048]{3,2,1,0:T(8,128)(2,1)} fusion(bf16[2,1,256,2048]{3,2,1,0:T(8,128)(2,1)} %bitcast.34, bf16[2,1,256,2048]{3,2,1,0:T(8,128)(2,1)} %bitcast.33, bf16[2,1,256,2048]{3,2,1,0:T(8,128)(2,1)} %bitcast.31, bf16[2,1,256,2048]{3,2,1,0:T(8,128)(2,1)S(1)} %bitcast.221), kind=kLoop, calls=%fused_computation.19 | loop fusion | flops 12582912 | bytes 16777216 | tf_op jit(solution)/shard_map/stack | solution.py:759
  237.7 8.1 %fusion = bf16[2048,2048]{1,0:T(8,128)(2,1)} fusion(bf16[2,4,256,2048]{3,2,1,0:T(8,128)(2,1)} %pad_maximum_fusion.1, f32[2048]{0:T(1024)S(1)} %bitcast.244), kind=kLoop, calls=%fused_computation.4 | loop fusion | flops 12582912 | bytes 16785408 | tf_op jit(solution)/shard_map/convert_element_type | solution.py:770
  245.8 11.8 %fusion.26 = f32[2048,704]{0,1:T(8,128)} fusion(bf16[2048,2048]{1,0:T(8,128)(2,1)} %multiply_convert_fusion, bf16[704,6144]{1,0:T(8,128)(2,1)} %all-gather.2.cloned.1.call-done), kind=kOutput, calls=%fused_computation.62 | convolution fusion | flops 5905580032 | bytes 17039360 | tf_op jit(solution)/shard_map/dot_general | solution.py:28
  257.6 11.9 %fusion.30 = f32[2048,704]{0,1:T(8,128)} fusion(bf16[2048,2048]{1,0:T(8,128)(2,1)} %multiply_convert_fusion, bf16[704,6144]{1,0:T(8,128)(2,1)} %all-gather.2.cloned.1.call-done), kind=kOutput, calls=%fused_computation.66 | convolution fusion | flops 5905580032 | bytes 17039360 | tf_op jit(solution)/shard_map/dot_general | solution.py:28
  269.5 13.8 %multiply_convert_fusion.1 = (bf16[2048,704]{0,1:T(8,128)(2,1)}, bf16[2048,704]{0,1:T(8,128)(2,1)S(1)}, bf16[2048,704]{0,1:T(8,128)(2,1)S(1)}) fusion(f32[2048,704]{0,1:T(8,128)} %fusion.30, f32[2048,704]{0,1:T(8,128)} %fusion.26, bf16[2048,2048]{1,0:T(8,128)(2,1)S(1)} %copy-done.25, bf16[704,6144]{1,0:T(8,128)(2,1)} %all-gather.2.cloned.1.call-done), kind=kOutput, calls=%fused_computation.24 | convolution fusion | flops 5927206912 | bytes 31457280 | tf_op jit(solution)/shard_map/dot_general | solution.py:28
  283.2 7.4 %fusion.22 = f32[1024,2048]{1,0:T(8,128)S(1)} fusion(bf16[704,6144]{1,0:T(8,128)(2,1)} %all-gather.2.cloned.1.call-done, bf16[2048,704]{0,1:T(8,128)(2,1)S(1)} %get-tuple-element.75), kind=kOutput, calls=%fused_computation.58 | convolution fusion | flops 2952790016 | bytes 12713984 | tf_op jit(solution)/shard_map/dot_general | solution.py:28
  290.7 5.5 add_convert_fusion
  296.2 1.3 fusion.77
  298.0 2.0 copy-done.61
  299.9 7.6 %fusion.24 = f32[1024,2048]{1,0:T(8,128)} fusion(bf16[704,6144]{1,0:T(8,128)(2,1)} %all-gather.2.cloned.1.call-done, bf16[2048,704]{0,1:T(8,128)(2,1)S(1)} %copy-done.61), kind=kOutput, calls=%fused_computation.60 | convolution fusion | flops 2952790016 | bytes 12713984 | tf_op jit(solution)/shard_map/dot_general | solution.py:28
  307.5 8.2 %add_convert_fusion.1 = bf16[1024,2048]{1,0:T(8,128)(2,1)S(1)} fusion(f32[1024,2048]{1,0:T(8,128)} %fusion.24, bf16[704,6144]{1,0:T(8,128)(2,1)} %all-gather.2.cloned.1.call-done, bf16[2048,704]{0,1:T(8,128)(2,1)} %copy-done.62), kind=kOutput, calls=%fused_computation.21 | convolution fusion | flops 2956984320 | bytes 16908288 | tf_op jit(solution)/shard_map/dot_general | solution.py:28
  315.7 1.4 fusion.76
  317.9 1.9 collective-permute-done.5
  319.8 1.4 add_convert_fusion.3
  321.2 8.0 %convolution_convert_fusion.4 = bf16[704,2048]{1,0:T(8,128)(2,1)S(1)} fusion(bf16[2048,704]{0,1:T(8,128)(2,1)} %get-tuple-element.67, bf16[2048,2048]{1,0:T(8,128)(2,1)S(1)} %copy-done.25), kind=kOutput, calls=%fused_computation.49 | convolution fusion | flops 5907021824 | bytes 14155776 | tf_op jit(solution)/shard_map/dot_general | solution.py:28
  329.2 6.3 %convolution_convert_fusion.6 = bf16[704,2048]{1,0:T(8,128)(2,1)S(1)} fusion(bf16[2048,704]{0,1:T(8,128)(2,1)S(1)} %copy-done.61, bf16[2048,2048]{1,0:T(8,128)(2,1)S(1)} %bitcast.220), kind=kOutput, calls=%fused_computation.51 | convolution fusion | flops 5907021824 | bytes 14155776 | tf_op jit(solution)/shard_map/dot_general | solution.py:28
  335.6 6.3 %convolution_convert_fusion.5 = bf16[704,2048]{1,0:T(8,128)(2,1)S(1)} fusion(bf16[2048,704]{0,1:T(8,128)(2,1)S(1)} %copy-done.63, bf16[2048,2048]{1,0:T(8,128)(2,1)S(1)} %bitcast.220), kind=kOutput, calls=%fused_computation.50 | convolution fusion | flops 5907021824 | bytes 14155776 | tf_op jit(solution)/shard_map/dot_general | solution.py:28
  341.9 4.1 pad_maximum_fusion
  348.1 2.7 multiply_reduce_fusion.4
  350.9 2.4 fusion.75
  355.9 10.0 %convolution_convert_fusion.1 = bf16[2048,2048]{1,0:T(8,128)(2,1)S(1)} fusion(bf16[2048,704]{0,1:T(8,128)(2,1)} %get-tuple-element.67, bf16[704,6144]{1,0:T(8,128)(2,1)} %all-gather.2.cloned.1.call-done), kind=kOutput, calls=%fused_computation.23 | convolution fusion | flops 5909774336 | bytes 14155776 | tf_op jit(solution)/shard_map/dot_general | solution.py:28
  365.9 2.5 slice_bitcast_fusion.2
  368.4 2.1 copy-done.22
  371.1 8.9 %collective-permute-done.6 = bf16[256,2048]{1,0:T(8,128)(2,1)S(1)} collective-permute-done((bf16[256,2048]{1,0:T(8,128)(2,1)}, bf16[256,2048]{1,0:T(8,128)(2,1)S(1)}, u32[]{:S(2)}, u32[]{:S(2)}) %collective-permute-start.6) | collective-permute-done | bytes 1048608 | tf_op jit(solution)/shard_map/ppermute | solution.py:32
  380.0 21.9 %collective-permute-done.14 = bf16[256,2048]{1,0:T(8,128)(2,1)S(1)} collective-permute-done((bf16[256,2048]{1,0:T(8,128)(2,1)S(1)}, bf16[256,2048]{1,0:T(8,128)(2,1)S(1)}, u32[]{:S(2)}, u32[]{:S(2)}) %collective-permute-start.14) | collective-permute-done | bytes 1048608 | tf_op jit(solution)/shard_map/ppermute | solution.py:32
  402.0 3.3 multiply_reduce_fusion.2
  405.3 6.6 %fusion.73 = (bf16[256,2048]{1,0:T(8,128)(2,1)S(1)}, f32[256,2048]{1,0:T(8,128)}, bf16[256,2048]{1,0:T(8,128)(2,1)S(1)}, f32[256,2048]{1,0:T(8,128)}) fusion(f32[256]{0:T(256)S(1)} %broadcast_multiply_fusion.1, f32[2,4,256,2048]{3,2,1,0:T(8,128)S(1)} %bitcast.211, f32[2048]{0:T(1024)S(1)} %copy-done.44, bf16[256,2048]{1,0:T(8,128)(2,1)S(1)} %collective-permute-done.14, ...), kind=kLoop, calls=%fused_computation.190 | loop fusion | flops 14680064 | bytes 18886664 | tf_op jit(solution)/shard_map/convert_element_type | solution.py:807
  411.9 1.6 convolution_convert_fusion.8
  414.1 5.0 convolution_convert_fusion.7
  419.2 1.7 gather_fusion.2
  421.8 1.3 collective-permute-start.9
  424.3 5.1 convolution_convert_fusion
  429.5 4.6 fusion.18
  436.3 2.5 pad_maximum_fusion.2
  438.9 2.3 collective-permute-done.16
  441.3 15.6 %attention_backward.3 = (bf16[576,1024]{1,0:T(8,128)(2,1)S(1)}, f32[2,64,128]{2,1,0:T(8,128)S(1)}) custom-call(s32[1]{0:T(128)} %bitcast.me_ref, bf16[576,1024]{1,0:T(8,128)(2,1)S(1)} %copy-done.19, f32[32,1024]{1,0:T(8,128)S(1)} %copy-done.9, f32[32,1024]{1,0:T(8,128)S(1)} %get-tuple-element.140.sin_ref, s32[1,1024]{1,0:T(1,128)S(1)} %copy-done.15, ...), custom_call_target="tpu_custom_call" | custom-call | flops 3355443200 | bytes 6291456 | tf_op jit(solution)/shard_map/attention_backward/pallas_call | solution.py:657
  457.0 7.0 %convolution_convert_fusion.2 = bf16[1024,2048]{1,0:T(8,128)(2,1)} fusion(bf16[576,1024]{1,0:T(8,128)(2,1)S(1)} %get-tuple-element.81, bf16[2048,640]{1,0:T(8,128)(2,1)} %get-tuple-element.55), kind=kOutput, calls=%fused_computation.47 | convolution fusion | flops 2418016256 | bytes 7995392 | tf_op jit(solution)/shard_map/dot_general | solution.py:28
  464.2 15.5 %attention_backward.2 = (bf16[576,1024]{1,0:T(8,128)(2,1)S(1)}, f32[2,64,128]{2,1,0:T(8,128)S(1)}) custom-call(s32[1]{0:T(128)} %bitcast.me_ref, bf16[576,1024]{1,0:T(8,128)(2,1)S(1)} %copy-done.17, f32[32,1024]{1,0:T(8,128)S(1)} %copy-done.7, f32[32,1024]{1,0:T(8,128)S(1)} %get-tuple-element.141.sin_ref, s32[1,1024]{1,0:T(1,128)S(1)} %copy-done.13, ...), custom_call_target="tpu_custom_call" | custom-call | flops 3355443200 | bytes 6291456 | tf_op jit(solution)/shard_map/attention_backward/pallas_call | solution.py:657
  480.2 5.5 collective-permute-done.11
  485.7 4.8 fusion.58
  490.5 4.7 convolution_add_fusion
  495.3 1.9 add_convert_fusion.2
  497.2 4.4 copy.45
  501.6 6.8 %convolution_convert_fusion.3 = bf16[1024,2048]{1,0:T(8,128)(2,1)} fusion(bf16[576,1024]{1,0:T(8,128)(2,1)S(1)} %get-tuple-element.74, bf16[2048,640]{1,0:T(8,128)(2,1)} %get-tuple-element.55), kind=kOutput, calls=%fused_computation.48 | convolution fusion | flops 2418016256 | bytes 7995392 | tf_op jit(solution)/shard_map/dot_general | solution.py:28
  508.4 7.0 %fusion.16 = bf16[2,256,2048]{2,1,0:T(8,128)(2,1)} fusion(f32[2,4,256,2048]{3,2,1,0:T(8,128)} %bitcast.207, bf16[2,256,2048]{2,1,0:T(8,128)(2,1)} %collective-permute-done.11, bf16[2,256,2048]{2,1,0:T(8,128)(2,1)} %collective-permute-done.12, bf16[2,4,256,2048]{3,2,1,0:T(8,128)(2,1)} %bitcast.218), kind=kLoop, calls=%fused_computation.41 | loop fusion | flops 7340032 | bytes 12582912 | tf_op jit(solution)/shard_map/convert_element_type | solution.py:826
  515.4 1.9 slice_convert_fusion.1
  517.3 2.3 slice_convert_fusion
  519.7 77.3 %closing.1 = (f32[2,256,2048]{2,1,0:T(8,128)}, bf16[4,64,640]{2,1,0:T(8,128)(2,1)}, f32[64,1280]{1,0:T(8,128)}) custom-call(bf16[4,256,2048]{2,1,0:T(8,128)(2,1)} %bitcast.229, bf16[4,256,2048]{2,1,0:T(8,128)(2,1)} %bitcast.230, bf16[8,256,640]{2,1,0:T(8,128)(2,1)} %bitcast.213, bf16[32,64,1280]{2,1,0:T(8,128)(2,1)} %bitcast.227), custom_call_target="tpu_custom_call" | custom-call | tf_op jit(solution)/shard_map/closing/pallas_call | solution.py:450
  599.2 3.1 fusion.10
  604.2 6.6 %fusion.13 = f32[2,256,2048]{2,1,0:T(8,128)} fusion(f32[2,256,2048]{2,1,0:T(8,128)} %bitcast.212, bf16[2,256,2048]{2,1,0:T(8,128)(2,1)S(1)} %copy-done.21, f32[2,256,2048]{2,1,0:T(8,128)} %get-tuple-element.85, f32[2,256]{1,0:T(2,128)S(1)} %broadcast_multiply_fusion, f32[2048]{0:T(1024)S(1)} %copy-done.46, f32[2,256]{1,0:T(2,128)S(1)} %add_rsqrt_fusion.3), kind=kLoop, calls=%fused_computation.37 | loop fusion | flops 7340032 | bytes 14692352 | tf_op jit(solution)/shard_map/add | solution.py:858
  (261 shorter events, 28.8 us)
Async XLA Ops:
  7.2 96.1 %copy-start = (s32[2,1024]{1,0:T(2,128)S(1)}, s32[2,1024]{1,0:T(2,128)}, u32[]{:S(2)}) copy-start(s32[2,1024]{1,0:T(2,128)} %param.17) | copy-start | bytes 24580
  7.2 96.7 %copy-start.59 = (s32[2,1]{0,1:T(1,128)S(1)}, s32[2,1]{0,1:T(1,128)}, u32[]{:S(2)}) copy-start(s32[2,1]{0,1:T(1,128)} %param.18) | copy-start | bytes 28
  7.2 92.7 %copy-start.26 = (bf16[2,256,2048]{2,1,0:T(8,128)(2,1)S(1)}, bf16[2,256,2048]{2,1,0:T(8,128)(2,1)}, u32[]{:S(2)}) copy-start(bf16[2,256,2048]{2,1,0:T(8,128)(2,1)} %param.16) | copy-start | bytes 6291460
  7.2 96.7 %copy-start.58 = (s32[4]{0:T(128)S(1)}, s32[4]{0:T(128)}, u32[]{:S(2)}) copy-start(s32[4]{0:T(128)} %param.19) | copy-start | bytes 52
  7.2 238.6 %all-gather.2.cloned.1.call-start = ((), (), s32[]{:S(2)}) async-start(), calls=%async_computation.1 | async-start | bytes 9732096 | tf_op jit(solution)/shard_map/all_gather | solution.py:767
  9.7 505.7 %reduce-scatter.2.cloned.1.call-start = ((), (), s32[]{:S(2)}) async-start(), calls=%async_computation.2 | async-start | bytes 9732096 | tf_op jit(solution)/shard_map/reduce_scatter | solution.py:790
  99.9 131.2 %collective-permute-start.1 = (bf16[2,256,2048]{2,1,0:T(8,128)(2,1)S(1)}, bf16[2,256,2048]{2,1,0:T(8,128)(2,1)}, u32[]{:S(2)}, u32[]{:S(2)}) collective-permute-start(bf16[2,256,2048]{2,1,0:T(8,128)(2,1)S(1)} %copy-done.26), channel_id=1, source_target_pairs={{0,1},{1,0},{2,3},{3,2},{4,5},{5,4},{6,7},{7,6},{8,9},{9,8},{10,11... | collective-permute-start | bytes 6291464 | tf_op jit(solution)/shard_map/ppermute | solution.py:32
  100.0 48.1 %collective-permute-start = (bf16[2,256,2048]{2,1,0:T(8,128)(2,1)S(1)}, bf16[2,256,2048]{2,1,0:T(8,128)(2,1)}, u32[]{:S(2)}, u32[]{:S(2)}) collective-permute-start(bf16[2,256,2048]{2,1,0:T(8,128)(2,1)S(1)} %copy-done.26), channel_id=1, source_target_pairs={{0,2},{1,3},{2,0},{3,1},{4,6},{5,7},{6,4},{7,5},{8,10},{9,11},{10,... | collective-permute-start | bytes 6291464 | tf_op jit(solution)/shard_map/ppermute | solution.py:32
  104.6 14.2 %copy-start.14 = (s32[1,1024]{1,0:T(1,128)}, s32[1,1024]{1,0:T(1,128)S(1)}, u32[]{:S(2)}) copy-start(s32[1,1024]{1,0:T(1,128)S(1)} %get-tuple-element.160.first_ref) | copy-start | bytes 12292
  104.6 24.5 %copy-start.12 = (s32[1,1024]{1,0:T(1,128)}, s32[1,1024]{1,0:T(1,128)S(1)}, u32[]{:S(2)}) copy-start(s32[1,1024]{1,0:T(1,128)S(1)} %get-tuple-element.161.first_ref) | copy-start | bytes 12292
  109.1 9.6 %copy-start.49 = (f32[1024]{0:T(1024)}, f32[1024]{0:T(1024)S(1)}, u32[]{:S(2)}) copy-start(f32[1024]{0:T(1024)S(1)} %get-tuple-element.170) | copy-start | bytes 12292
  109.1 16.8 %copy-start.51 = (f32[1024]{0:T(1024)}, f32[1024]{0:T(1024)S(1)}, u32[]{:S(2)}) copy-start(f32[1024]{0:T(1024)S(1)} %get-tuple-element.171) | copy-start | bytes 12292
  112.3 13.6 %copy-start.45 = (f32[2048]{0:T(1024)}, f32[2048]{0:T(1024)S(1)}, u32[]{:S(2)}) copy-start(f32[2048]{0:T(1024)S(1)} %get-tuple-element.100) | copy-start | bytes 24580
  112.3 109.2 %copy-start.43 = (f32[2048]{0:T(1024)}, f32[2048]{0:T(1024)S(1)}, u32[]{:S(2)}) copy-start(f32[2048]{0:T(1024)S(1)} %get-tuple-element.99) | copy-start | bytes 24580
  112.5 16.7 %copy-start.10 = (f32[2,64]{0,1:T(8,128)}, f32[2,64]{0,1:T(8,128)S(1)}, u32[]{:S(2)}) copy-start(f32[2,64]{0,1:T(8,128)S(1)} %copy.37) | copy-start | bytes 1540
  112.5 16.6 %copy-start.6 = (f32[32,1024]{1,0:T(8,128)}, f32[32,1024]{1,0:T(8,128)S(1)}, u32[]{:S(2)}) copy-start(f32[32,1024]{1,0:T(8,128)S(1)} %get-tuple-element.143.cos_ref) | copy-start | bytes 393220
  112.5 13.4 %slice-start.4 = ((s8[8388608]{0:T(1024)(128)(4,1)}), s8[4194304]{0:T(1024)(128)(4,1)S(1)}, s32[]{:S(2)}) async-start(s8[8388608]{0:T(1024)(128)(4,1)} %bitcast.214), calls=%async_computation.7 | async-start | bytes 8388608
  112.5 13.4 %slice-start.5 = ((s8[8388608]{0:T(1024)(128)(4,1)}), s8[4194304]{0:T(1024)(128)(4,1)S(1)}, s32[]{:S(2)}) async-start(s8[8388608]{0:T(1024)(128)(4,1)} %bitcast.214), calls=%async_computation.8 | async-start | bytes 8388608
  118.8 7.1 %copy-start.18 = (bf16[576,1024]{1,0:T(8,128)(2,1)}, bf16[576,1024]{1,0:T(8,128)(2,1)S(1)}, u32[]{:S(2)}) copy-start(bf16[576,1024]{1,0:T(8,128)(2,1)S(1)} %fusion.46.x_ref) | copy-start | bytes 3538948
  118.8 7.2 %copy-start.37 = (bf16[2048,640]{1,0:T(8,128)(2,1)S(1)}, bf16[2048,640]{1,0:T(8,128)(2,1)}, u32[]{:S(2)}) copy-start(bf16[2048,640]{1,0:T(8,128)(2,1)} %get-tuple-element.55) | copy-start | bytes 7864324
  129.1 7.1 %copy-start.16 = (bf16[576,1024]{1,0:T(8,128)(2,1)}, bf16[576,1024]{1,0:T(8,128)(2,1)S(1)}, u32[]{:S(2)}) copy-start(bf16[576,1024]{1,0:T(8,128)(2,1)S(1)} %fusion.43.x_ref) | copy-start | bytes 3538948
  148.1 83.0 %collective-permute-start.2 = (bf16[2,256,2048]{2,1,0:T(8,128)(2,1)}, bf16[2,256,2048]{2,1,0:T(8,128)(2,1)}, u32[]{:S(2)}, u32[]{:S(2)}) collective-permute-start(bf16[2,256,2048]{2,1,0:T(8,128)(2,1)} %collective-permute-done), channel_id=1, source_target_pairs={{0,1},{1,0},{2,3},{3,2},{4,5},{5,4},{6,7},{7,6},{8,9},{9,8},{10,11... | collective-permute-start | bytes 6291464 | tf_op jit(solution)/shard_map/ppermute | solution.py:32
  200.9 20.6 %copy-start.30 = (bf16[8,2,2,64,1280]{4,3,2,1,0:T(8,128)(2,1)}, bf16[8,2,2,64,1280]{4,3,2,1,0:T(8,128)(2,1)S(1)}, u32[]{:S(2)}) copy-start(bf16[8,2,2,64,1280]{4,3,2,1,0:T(8,128)(2,1)S(1)} %copy.38) | copy-start | bytes 15728644
  257.6 11.9 %copy-start.25 = (bf16[2048,2048]{1,0:T(8,128)(2,1)S(1)}, bf16[2048,2048]{1,0:T(8,128)(2,1)}, u32[]{:S(2)}) copy-start(bf16[2048,2048]{1,0:T(8,128)(2,1)} %fusion) | copy-start | bytes 25165828
  283.2 7.4 %copy-start.60 = (bf16[2048,704]{0,1:T(8,128)(2,1)}, bf16[2048,704]{0,1:T(8,128)(2,1)S(1)}, u32[]{:S(2)}) copy-start(bf16[2048,704]{0,1:T(8,128)(2,1)S(1)} %get-tuple-element.75) | copy-start | bytes 8650756
  283.2 7.4 %copy-start.62 = (bf16[2048,704]{0,1:T(8,128)(2,1)}, bf16[2048,704]{0,1:T(8,128)(2,1)S(1)}, u32[]{:S(2)}) copy-start(bf16[2048,704]{0,1:T(8,128)(2,1)S(1)} %get-tuple-element.76) | copy-start | bytes 8650756
  296.2 21.3 %copy-start.28 = (bf16[1024,2048]{1,0:T(8,128)(2,1)}, bf16[1024,2048]{1,0:T(8,128)(2,1)S(1)}, u32[]{:S(2)}) copy-start(bf16[1024,2048]{1,0:T(8,128)(2,1)S(1)} %add_convert_fusion) | copy-start | bytes 12582916
  297.5 20.0 %collective-permute-start.4 = (bf16[256,2048]{1,0:T(8,128)(2,1)S(1)}, bf16[256,2048]{1,0:T(8,128)(2,1)S(1)}, u32[]{:S(2)}, u32[]{:S(2)}) collective-permute-start(bf16[256,2048]{1,0:T(8,128)(2,1)S(1)} %get-tuple-element.117), channel_id=1, source_target_pairs={{0,1},{1,0},{2,3},{3,2},{4,5},{5,4},{6,7},{7,6},{8,9},{9,8},{10,11... | collective-permute-start | bytes 3145736 | tf_op jit(solution)/shard_map/ppermute | solution.py:32
  317.1 2.7 collective-permute-start.5
  317.5 11.7 %slice-start.6 = ((s8[8388608]{0:T(1024)(128)(4,1)}), s8[4194304]{0:T(1024)(128)(4,1)S(1)}, s32[]{:S(2)}) async-start(s8[8388608]{0:T(1024)(128)(4,1)} %bitcast.219), calls=%async_computation.9 | async-start | bytes 8388608
  321.2 8.0 %slice-start.7 = ((s8[8388608]{0:T(1024)(128)(4,1)}), s8[4194304]{0:T(1024)(128)(4,1)S(1)}, s32[]{:S(2)}) async-start(s8[8388608]{0:T(1024)(128)(4,1)} %bitcast.219), calls=%async_computation.10 | async-start | bytes 8388608
  348.1 53.8 %slice-start = ((s8[16777216]{0:T(1024)(128)(4,1)}), s8[4194304]{0:T(1024)(128)(4,1)S(1)}, s32[]{:S(2)}) async-start(s8[16777216]{0:T(1024)(128)(4,1)} %bitcast.208), calls=%async_computation.3 | async-start | bytes 8388608
  353.3 17.3 %collective-permute-start.13 = (bf16[256,2048]{1,0:T(8,128)(2,1)}, bf16[256,2048]{1,0:T(8,128)(2,1)S(1)}, u32[]{:S(2)}, u32[]{:S(2)}) collective-permute-start(bf16[256,2048]{1,0:T(8,128)(2,1)} %get-tuple-element.116), channel_id=1, source_target_pairs={{0,1},{1,0},{2,3},{3,2},{4,5},{5,4},{6,7},{7,6},{8,9},{9,8},{10,11... | collective-permute-start | bytes 3145736 | tf_op jit(solution)/shard_map/ppermute | solution.py:32
  353.7 48.3 %slice-start.1 = ((s8[16777216]{0:T(1024)(128)(4,1)}), s8[4194304]{0:T(1024)(128)(4,1)S(1)}, s32[]{:S(2)}) async-start(s8[16777216]{0:T(1024)(128)(4,1)} %bitcast.208), calls=%async_computation.4 | async-start | bytes 8388608
  353.7 48.3 %slice-start.2 = ((s8[16777216]{0:T(1024)(128)(4,1)}), s8[4194304]{0:T(1024)(128)(4,1)S(1)}, s32[]{:S(2)}) async-start(s8[16777216]{0:T(1024)(128)(4,1)} %bitcast.208), calls=%async_computation.5 | async-start | bytes 8388608
  353.7 48.3 %slice-start.3 = ((s8[16777216]{0:T(1024)(128)(4,1)}), s8[4194304]{0:T(1024)(128)(4,1)S(1)}, s32[]{:S(2)}) async-start(s8[16777216]{0:T(1024)(128)(4,1)} %bitcast.208), calls=%async_computation.6 | async-start | bytes 8388608
  353.7 17.4 %collective-permute-start.3 = (bf16[256,2048]{1,0:T(8,128)(2,1)}, bf16[256,2048]{1,0:T(8,128)(2,1)S(1)}, u32[]{:S(2)}, u32[]{:S(2)}) collective-permute-start(bf16[256,2048]{1,0:T(8,128)(2,1)} %get-tuple-element.114), channel_id=1, source_target_pairs={{0,1},{1,0},{2,3},{3,2},{4,5},{5,4},{6,7},{7,6},{8,9},{9,8},{10,11... | collective-permute-start | bytes 3145736 | tf_op jit(solution)/shard_map/ppermute | solution.py:32
  353.8 26.2 %collective-permute-start.6 = (bf16[256,2048]{1,0:T(8,128)(2,1)}, bf16[256,2048]{1,0:T(8,128)(2,1)S(1)}, u32[]{:S(2)}, u32[]{:S(2)}) collective-permute-start(bf16[256,2048]{1,0:T(8,128)(2,1)} %add_convert_fusion.3), channel_id=1, source_target_pairs={{0,2},{1,3},{2,0},{3,1},{4,6},{5,7},{6,4},{7,5},{8,10},{9,11},{10,... | collective-permute-start | bytes 3145736 | tf_op jit(solution)/shard_map/ppermute | solution.py:32
  355.1 46.9 %collective-permute-start.14 = (bf16[256,2048]{1,0:T(8,128)(2,1)S(1)}, bf16[256,2048]{1,0:T(8,128)(2,1)S(1)}, u32[]{:S(2)}, u32[]{:S(2)}) collective-permute-start(bf16[256,2048]{1,0:T(8,128)(2,1)S(1)} %add_convert_fusion.4), channel_id=1, source_target_pairs={{0,2},{1,3},{2,0},{3,1},{4,6},{5,7},{6,4},{7,5},{8,10},{9,11},{10,... | collective-permute-start | bytes 3145736 | tf_op jit(solution)/shard_map/ppermute | solution.py:32
  365.9 36.1 %copy-start.44 = (f32[2048]{0:T(1024)S(1)}, f32[2048]{0:T(1024)}, u32[]{:S(2)}) copy-start(f32[2048]{0:T(1024)} %copy-done.43) | copy-start | bytes 24580
  370.6 137.9 %collective-permute-start.12 = (bf16[2,256,2048]{2,1,0:T(8,128)(2,1)}, bf16[2,256,2048]{2,1,0:T(8,128)(2,1)}, u32[]{:S(2)}, u32[]{:S(2)}) collective-permute-start(bf16[2,256,2048]{2,1,0:T(8,128)(2,1)} %get-tuple-element.110), channel_id=1, source_target_pairs={{0,1},{1,0},{2,3},{3,2},{4,5},{5,4},{6,7},{7,6},{8,9},{9,8},{10,11... | collective-permute-start | bytes 6291464 | tf_op jit(solution)/shard_map/ppermute | solution.py:32
  370.6 34.7 %copy-start.27 = (bf16[2,256,2048]{2,1,0:T(8,128)(2,1)S(1)}, bf16[2,256,2048]{2,1,0:T(8,128)(2,1)}, u32[]{:S(2)}) copy-start(bf16[2,256,2048]{2,1,0:T(8,128)(2,1)} %param.16) | copy-start | bytes 6291460
  370.6 58.9 %collective-permute-start.10 = (bf16[2,256,2048]{2,1,0:T(8,128)(2,1)}, bf16[2,256,2048]{2,1,0:T(8,128)(2,1)}, u32[]{:S(2)}, u32[]{:S(2)}) collective-permute-start(bf16[2,256,2048]{2,1,0:T(8,128)(2,1)} %get-tuple-element.111), channel_id=1, source_target_pairs={{0,1},{1,0},{2,3},{3,2},{4,5},{5,4},{6,7},{7,6},{8,9},{9,8},{10,11... | collective-permute-start | bytes 6291464 | tf_op jit(solution)/shard_map/ppermute | solution.py:32
  402.0 9.9 %slice-start.8 = ((s8[5242880]{0:T(1024)(128)(4,1)}), s8[4194304]{0:T(1024)(128)(4,1)S(1)}, s32[]{:S(2)}) async-start(s8[5242880]{0:T(1024)(128)(4,1)} %bitcast.224), calls=%async_computation.11 | async-start | bytes 8388608
  421.2 17.7 %collective-permute-start.17 = (bf16[320,256]{1,0:T(8,128)(2,1)S(1)}, bf16[320,256]{1,0:T(8,128)(2,1)S(1)}, u32[]{:S(2)}, u32[]{:S(2)}) collective-permute-start(bf16[320,256]{1,0:T(8,128)(2,1)S(1)} %get-tuple-element.133), channel_id=1, source_target_pairs={{0,3},{1,2},{2,1},{3,0},{4,7},{5,6},{6,5},{7,4},{8,11},{9,10},{10,... | collective-permute-start | bytes 491528 | tf_op jit(solution)/shard_map/ppermute | solution.py:32
  421.8 12.4 %collective-permute-start.9 = (bf16[320,256]{1,0:T(8,128)(2,1)S(1)}, bf16[320,256]{1,0:T(8,128)(2,1)S(1)}, u32[]{:S(2)}, u32[]{:S(2)}) collective-permute-start(bf16[320,256]{1,0:T(8,128)(2,1)S(1)} %get-tuple-element.136), channel_id=1, source_target_pairs={{0,3},{1,2},{2,1},{3,0},{4,7},{5,6},{6,5},{7,4},{8,11},{9,10},{10,... | collective-permute-start | bytes 491528 | tf_op jit(solution)/shard_map/ppermute | solution.py:32
  423.1 11.8 %collective-permute-start.8 = (bf16[320,256]{1,0:T(8,128)(2,1)S(1)}, bf16[320,256]{1,0:T(8,128)(2,1)S(1)}, u32[]{:S(2)}, u32[]{:S(2)}) collective-permute-start(bf16[320,256]{1,0:T(8,128)(2,1)S(1)} %get-tuple-element.137), channel_id=1, source_target_pairs={{0,2},{1,3},{2,0},{3,1},{4,6},{5,7},{6,4},{7,5},{8,10},{9,11},{10,... | collective-permute-start | bytes 491528 | tf_op jit(solution)/shard_map/ppermute | solution.py:32
  429.5 6.8 %copy-start.23 = (f32[256,2048]{1,0:T(8,128)S(1)}, f32[256,2048]{1,0:T(8,128)}, u32[]{:S(2)}) copy-start(f32[256,2048]{1,0:T(8,128)} %get-tuple-element.102) | copy-start | bytes 6291460
  429.5 6.8 %copy-start.24 = (f32[256,2048]{1,0:T(8,128)S(1)}, f32[256,2048]{1,0:T(8,128)}, u32[]{:S(2)}) copy-start(f32[256,2048]{1,0:T(8,128)} %get-tuple-element.106) | copy-start | bytes 6291460
  429.5 5.6 collective-permute-start.7
  434.1 7.0 %collective-permute-start.16 = (bf16[320,256]{1,0:T(8,128)(2,1)S(1)}, bf16[320,256]{1,0:T(8,128)(2,1)S(1)}, u32[]{:S(2)}, u32[]{:S(2)}) collective-permute-start(bf16[320,256]{1,0:T(8,128)(2,1)S(1)} %get-tuple-element.134), channel_id=1, source_target_pairs={{0,2},{1,3},{2,0},{3,1},{4,6},{5,7},{6,4},{7,5},{8,10},{9,11},{10,... | collective-permute-start | bytes 491528 | tf_op jit(solution)/shard_map/ppermute | solution.py:32
  435.0 6.2 %collective-permute-start.15 = (bf16[320,256]{1,0:T(8,128)(2,1)S(1)}, bf16[320,256]{1,0:T(8,128)(2,1)S(1)}, u32[]{:S(2)}, u32[]{:S(2)}) collective-permute-start(bf16[320,256]{1,0:T(8,128)(2,1)S(1)} %get-tuple-element.135), channel_id=1, source_target_pairs={{0,1},{1,0},{2,3},{3,2},{4,5},{5,4},{6,7},{7,6},{8,9},{9,8},{10,11... | collective-permute-start | bytes 491528 | tf_op jit(solution)/shard_map/ppermute | solution.py:32
  435.1 50.6 %collective-permute-start.11 = (bf16[2,256,2048]{2,1,0:T(8,128)(2,1)}, bf16[2,256,2048]{2,1,0:T(8,128)(2,1)}, u32[]{:S(2)}, u32[]{:S(2)}) collective-permute-start(bf16[2,256,2048]{2,1,0:T(8,128)(2,1)} %fusion.18), channel_id=1, source_target_pairs={{0,2},{1,3},{2,0},{3,1},{4,6},{5,7},{6,4},{7,5},{8,10},{9,11},{10,... | collective-permute-start | bytes 6291464 | tf_op jit(solution)/shard_map/ppermute | solution.py:32
  457.0 7.0 %copy-start.40 = (bf16[320,256]{1,0:T(8,128)(2,1)S(1)}, bf16[320,256]{1,0:T(8,128)(2,1)}, u32[]{:S(2)}) copy-start(bf16[320,256]{1,0:T(8,128)(2,1)} %copy-done.39) | copy-start | bytes 491524
  457.0 7.0 %copy-start.42 = (bf16[320,256]{1,0:T(8,128)(2,1)S(1)}, bf16[320,256]{1,0:T(8,128)(2,1)}, u32[]{:S(2)}) copy-start(bf16[320,256]{1,0:T(8,128)(2,1)} %copy-done.41) | copy-start | bytes 491524
  457.0 7.1 %copy-start.3 = (bf16[320,1024]{1,0:T(8,128)(2,1)S(1)}, bf16[320,1024]{1,0:T(8,128)(2,1)}, u32[]{:S(2)}) copy-start(bf16[320,1024]{1,0:T(8,128)(2,1)} %copy-done.2) | copy-start | bytes 1966084
  457.0 7.1 %copy-start.7 = (f32[32,1024]{1,0:T(8,128)S(1)}, f32[32,1024]{1,0:T(8,128)}, u32[]{:S(2)}) copy-start(f32[32,1024]{1,0:T(8,128)} %copy-done.6) | copy-start | bytes 393220
  457.0 7.1 %copy-start.13 = (s32[1,1024]{1,0:T(1,128)S(1)}, s32[1,1024]{1,0:T(1,128)}, u32[]{:S(2)}) copy-start(s32[1,1024]{1,0:T(1,128)} %copy-done.12) | copy-start | bytes 12292
  457.0 7.1 %copy-start.17 = (bf16[576,1024]{1,0:T(8,128)(2,1)S(1)}, bf16[576,1024]{1,0:T(8,128)(2,1)}, u32[]{:S(2)}) copy-start(bf16[576,1024]{1,0:T(8,128)(2,1)} %copy-done.16) | copy-start | bytes 3538948
  464.1 21.5 %copy-start.46 = (f32[2048]{0:T(1024)S(1)}, f32[2048]{0:T(1024)}, u32[]{:S(2)}) copy-start(f32[2048]{0:T(1024)} %copy-done.45) | copy-start | bytes 24580
  464.2 21.5 %copy-start.52 = (f32[1024]{0:T(1024)S(1)}, f32[1024]{0:T(1024)}, u32[]{:S(2)}) copy-start(f32[1024]{0:T(1024)} %copy-done.51) | copy-start | bytes 12292
  604.0 6.8 %copy-start.31 = (f32[64,1920]{1,0:T(8,128)}, f32[64,1920]{1,0:T(8,128)S(1)}, u32[]{:S(2)}) copy-start(f32[64,1920]{1,0:T(8,128)S(1)} %concatenate.61) | copy-start | bytes 1474564
  604.2 7.9 %copy-start.1 = (s32[2,1024]{1,0:T(2,128)S(1)}, s32[2,1024]{1,0:T(2,128)}, u32[]{:S(2)}) copy-start(s32[2,1024]{1,0:T(2,128)} %param.17) | copy-start | bytes 24580
  604.2 7.2 %copy-start.38 = (f32[64,1280]{1,0:T(8,128)S(1)}, f32[64,1280]{1,0:T(8,128)}, u32[]{:S(2)}) copy-start(f32[64,1280]{1,0:T(8,128)} %get-tuple-element.183) | copy-start | bytes 983044
  (30 other events, 116.8 us)
Sparse Core Ops, SparseCore 0:
  10.8 159.6 all-gather.1
  346.2 153.3 reduce-scatter.1

commit v5 on v4

--- a/solution.py
+++ b/solution.py
@@ -305,21 +305,26 @@
         out[at, :] = total.astype(out.dtype)
 
 
-def closing(
-    n_seq, n_rows, *refs
-):
-    rows = len(refs) - 28
-    da = refs[:rows]
+def closing(n_seq, n_rows, *refs):
+    rows = (len(refs) - 31) // 2
+    d_act, a_in = refs[:rows], refs[rows : 2 * rows]
     (
-        dw, do, da_out, dw_out, do_out,
-        da_near, da_send, da_far, da_own, dw_near, dw_send, dw_far, dw_own, do_near, do_sum, do_next,
-        do_send, do_far, do_own, do_last, near_s, near_r, far_s, far_r, ring_s, ring_r, end_s, end_r,
-    ) = refs[rows:]
+        w, tail, made, do, da_out, dw_out, do_out,
+        da, da_near, da_send, da_far, dw, dw_near, dw_send, dw_far, dw_own, dw_flip, do_near, do_sum, do_next,
+        do_send, do_far, do_own, do_last, near_s, near_r, far_s, far_r, ring_s, ring_r, ends,
+    ) = refs[2 * rows :]
+    end_s, end_r = ends.at[0], ends.at[1]
     me, r = lax.axis_index("seq"), lax.axis_index("rows")
     up, beside = greet(me, r, n_seq, n_rows)
     a, b = lax.div(r, 2), lax.rem(r, 2)
     half, top = n_rows // 2, n_seq // 2
     local = do.shape[1]
+    block = n_seq * local
+    if block % 128:
+        dw = made
+    cols, length = d_act[0].shape
+    span = length // n_seq
+    width = w.shape[0]
 
     def send(src, dst, send_sem, recv_sem, **where):
         copy = pltpu.make_async_remote_copy(
@@ -332,20 +337,51 @@
     def owner(i, j):
         return 2 * lax.rem(a + half - i, half) + (b if j == 0 else 1 - b)
 
+    def make_da(t, k):
+        @pl.loop(0, width // 256)
+        def _(i):
+            at = pl.ds(pl.multiple_of(i * 256, 256), 256)
+            da[t, k, at, :] = mm(w[at, :cols], d_act[t][:, k * span : (k + 1) * span]).astype(BF)
+
+    def make_dw(who):
+        if block % 128:
+            return
+        here = pl.ds(pl.multiple_of(who * block, block), block)
+        third = cols // 3
+
+        @pl.loop(0, 3)
+        def _(i):
+            at = pl.ds(pl.multiple_of(i * third, third), third)
+            total = mm(d_act[0][at, :], a_in[0][:, here])
+            for t in range(1, rows):
+                total = total + mm(d_act[t][at, :], a_in[t][:, here])
+            dw[who, at, :] = total.astype(BF)
+
+        dw[who, cols:, :] = tail[:, here].astype(BF)
+
     low = flipped(me, 1)
     high = flipped(me, top)
     order = list(range(1, half)) + [0]
-    near_da = [
-        [send(da[t].at[k + 1], da_near.at[t, k // top], near_s.at[t, k // top], near_r.at[t, k // top], seq=low)
-         for t in range(rows)]
-        for k in (top, 0)
-    ]
+
+    def send_near(t, k):
+        return send(
+            da.at[t, k + 1], da_near.at[t, k // top], near_s.at[t, k // top], near_r.at[t, k // top], seq=low
+        )
+
+    near_do = []
+    for c, k in enumerate((top, 0)):
+        whose = other(me, k + 1, n_seq)
+        for j in range(n_rows):
+            near_do.append(
+                send(do.at[j * n_seq + whose], do_near.at[c, j], near_s.at[rows + c, j], near_r.at[rows + c, j], seq=low)
+            )
     side_dw, side_do = [], []
 
     def beside_next():
         n = len(side_dw) + len(side_do)
         i = order[n % half]
         if n < half:
+            make_dw(owner(i, 1))
             side_dw.append(
                 send(dw.at[owner(i, 1)], dw_near.at[i], ring_s.at[0, 0, i], ring_r.at[0, 0, i], rows=beside)
             )
@@ -354,20 +390,21 @@
                 send(do_sum.at[owner(i, 1)], do_next.at[i], ring_s.at[0, 1, i], ring_r.at[0, 1, i], rows=beside)
             )
 
+    far_da = []
+    near_da = [[], []]
+    make_da(0, top + 1)
+    near_da[0].append(send_near(0, top))
     beside_next()
-    beside_next()
-    near_do = []
-    for c, k in enumerate((top, 0)):
-        whose = other(me, k + 1, n_seq)
-        for j in range(n_rows):
-            near_do.append(
-                send(do.at[j * n_seq + whose], do_near.at[c, j], near_s.at[rows + c, j], near_r.at[rows + c, j], seq=low)
-            )
-    far_da = []
     for t in range(rows):
+        if t:
+            make_da(t, top + 1)
+            near_da[0].append(send_near(t, top))
+        make_da(t, top)
         near_da[0][t].wait_recv()
-        add_rows(da_send.at[t], da[t].at[top], da_near.at[t, 1])
+        add_rows(da_send.at[t], da.at[t, top], da_near.at[t, 1])
         far_da.append(send(da_send.at[t], da_far.at[t], far_s.at[t], far_r.at[t], seq=high))
+        if t == 0:
+            beside_next()
 
     def ring_step(kind, n, i, near, mine, far, out, final, side):
         side.wait_recv()
@@ -379,10 +416,12 @@
         add_rows(out.at[n], *terms)
         return send(out.at[n], far.at[n], ring_s.at[1, kind, n], ring_r.at[1, kind, n], rows=up)
 
+    beside_next()
     ring_dw, ring_do = [], []
 
     def step_dw(n):
         i = order[n]
+        make_dw(owner(i, 0))
         if n:
             ring_dw[n - 1].wait_recv()
         ring_dw.append(
@@ -397,7 +436,6 @@
             ring_step(1, n, i, do_next.at[i], do_sum.at[owner(i, 0)], do_far, do_send, do_own, side_do[n])
         )
 
-    step_dw(0)
     for copy in near_do:
         copy.wait_recv()
     for j in range(n_rows):
@@ -407,46 +445,63 @@
                 do.at[j * n_seq + other(me, k, n_seq)],
                 do_near.at[c, j],
             )
+    step_dw(0)
+    for t in range(rows):
+        make_da(t, 1)
+        near_da[1].append(send_near(t, 0))
+        make_da(t, 0)
     for n in range(1, half):
         step_dw(n)
+    for i in range(0, cols + tail.shape[0], 128):
+        dw_flip[:, i : i + 128] = flip(dw_own[i : i + 128, :])
     step_do(0)
-    kept = pltpu.make_async_copy(dw_own.at[pl.ds(pl.multiple_of(me * local, local), local)], dw_out.at[me], end_s.at[0])
+    kept = pltpu.make_async_copy(dw_flip.at[pl.ds(pl.multiple_of(me * local, local), local)], dw_out.at[me], end_s.at[0])
     kept.start()
-    ends = [
+    parts = [
         send(
-            dw_own.at[pl.ds(pl.multiple_of(other(me, j, n_seq) * local, local), local)],
+            dw_flip.at[pl.ds(pl.multiple_of(other(me, j, n_seq) * local, local), local)],
             dw_out.at[me], end_s.at[j], end_r.at[j], seq=other(me, j, n_seq),
         )
         for j in range(1, n_seq)
     ]
     for n in range(1, half):
         step_do(n)
-    ends.append(send(do_own.at[pl.ds(0, local)], do_last, end_s.at[n_seq], end_r.at[n_seq], seq=high))
+    parts.append(send(do_own.at[pl.ds(0, local)], do_last, end_s.at[n_seq], end_r.at[n_seq], seq=high))
     for t in range(rows):
         near_da[1][t].wait_recv()
-        add_rows(da_own.at[t], da[t].at[0], da_near.at[t, 0])
-    for t in range(rows):
         far_da[t].wait_recv()
-        add_rows(da_out.at[t], da_own.at[t], da_far.at[t])
-    for copy in ends:
+
+        @pl.loop(0, width // 256)
+        def _(i):
+            at = pl.ds(pl.multiple_of(i * 256, 256), 256)
+            total = da[t, 0, at, :].astype(F32) + da_near[t, 0, at, :].astype(F32)
+            da_out[t, :, at] = (total + da_far[t, at, :].astype(F32)).T
+
+    for copy in parts:
         copy.wait_recv()
     add_rows(do_out, do_own.at[pl.ds(local, local)], do_last)
     kept.wait()
-    for copy in near_da[0] + near_da[1] + side_dw + near_do + far_da + side_do + ends:
+    for copy in near_da[0] + near_da[1] + side_dw + near_do + far_da + side_do + parts:
         copy.wait_send()
     for copy in ring_dw[:-1] + ring_do[:-1]:
         copy.wait_send()
 
 
-def close_layer(n_seq, n_rows, da, dw, do):
-    rows = len(da)
-    _, span, width = da[0].shape
-    _, block, cols = dw.shape
+def close_layer(n_seq, n_rows, d_act, a_in, w, tail, do):
+    rows = len(d_act)
+    width, cols = w.shape
+    span = d_act[0].shape[1] // n_seq
     _, local, wide = do.shape
+    block = n_seq * local
     half = n_rows // 2
     vmem = pl.BlockSpec(memory_space=pltpu.VMEM)
     dma = pltpu.SemaphoreType.DMA
     most = max(n_rows, 2)
+    made = jnp.zeros((8, 128), BF)
+    if block % 128:
+        made = sum(dot(g, x, 1, 0) for g, x in zip(d_act, a_in)).astype(BF)
+        made = jnp.concatenate([made, tail.astype(BF)], axis=0).reshape(cols, n_rows, block)
+        made = jnp.swapaxes(made, 0, 1)
     return pl.pallas_call(
         functools.partial(closing, n_seq, n_rows),
         out_shape=(
@@ -454,16 +509,18 @@
             jax.ShapeDtypeStruct((n_seq, local, cols), BF),
             jax.ShapeDtypeStruct((local, wide), F32),
         ),
-        in_specs=[vmem] * (rows + 2),
+        in_specs=[vmem] * (2 * rows + 4),
         out_specs=(vmem,) * 3,
         scratch_shapes=[
-            pltpu.VMEM((rows, 2, span, width), BF),
-            pltpu.VMEM((rows, span, width), BF),
-            pltpu.VMEM((rows, span, width), BF),
-            pltpu.VMEM((rows, span, width), F32),
-            pltpu.VMEM((half, block, cols), BF),
-            pltpu.VMEM((half, block, cols), BF),
-            pltpu.VMEM((half, block, cols), BF),
+            pltpu.VMEM((rows, n_seq, width, span), BF),
+            pltpu.VMEM((rows, 2, width, span), BF),
+            pltpu.VMEM((rows, width, span), BF),
+            pltpu.VMEM((rows, width, span), BF),
+            pltpu.VMEM((8, 128) if block % 128 else (n_rows, cols, block), BF),
+            pltpu.VMEM((half, cols, block), BF),
+            pltpu.VMEM((half, cols, block), BF),
+            pltpu.VMEM((half, cols, block), BF),
+            pltpu.VMEM((cols, block), BF),
             pltpu.VMEM((block, cols), BF),
             pltpu.VMEM((2, n_rows, local, wide), BF),
             pltpu.VMEM((n_rows, 2 * local, wide), BF),
@@ -478,14 +535,13 @@
             dma((rows,)),
             dma((2, 2, half)),
             dma((2, 2, half)),
-            dma((n_seq + 1,)),
-            dma((n_seq + 1,)),
+            dma((2, n_seq + 1)),
         ],
         compiler_params=pltpu.CompilerParams(
-            collective_id=1, has_side_effects=True, vmem_limit_bytes=60 << 20
+            collective_id=1, has_side_effects=True, vmem_limit_bytes=62 << 20
         ),
         name="closing",
-    )(*da, dw, do)
+    )(*d_act, *a_in, w, tail, made, do)
 
 
 def head_unit(v):
@@ -808,29 +864,24 @@
         do_src = dot(w_out, grad_att[r], 0, 1).astype(BF).reshape(n_seq, q_cols, span)
         do_src = jnp.take(do_src, rel, axis=0)
         do_slots = [do_src[0]] + [swap(do_src[m], "seq", n_seq, m) for m in range(1, n_seq)]
-        if r == rows - 1:
-            do_slots, y_sent = tie((do_slots, y_sent))
-        do_rows.append(jnp.concatenate(do_slots, axis=1))
+        do_rows.append(do_slots)
+    do_rows, y_sent = tie((do_rows, y_sent))
+    do_rows = [jnp.concatenate(slots, axis=1) for slots in do_rows]
     y_got = cross_seq(y_sent, n_seq)
     o_own = jnp.concatenate(
         [o_all[:, r * length : r * length + span] for r in range(rows)], axis=1
     )
     d_out = dot(jnp.concatenate(grad_att, axis=0), o_own, 0, 1).astype(BF)
 
-    d_acts, d_parts, d_heads = [], [], 0.0
+    d_acts, d_heads = [], 0.0
     for r in range(rows):
-        a_in, args, o, inv = kept[r]
+        _, args, o, inv = kept[r]
         d_act, head_sums = attention_backward(*args, o, inv, do_rows[r])
-        if r == rows - 1:
-            d_act, y_got = tie((d_act, y_got))
-            output = (h_own + (y_kept + y_got.astype(F32))).astype(BF)
         d_heads = d_heads + jnp.sum(head_sums, axis=-1)
-        part = dot(d_act, w_qkv, 0, 1)
-        part = part.astype(BF)
-        if r == rows - 1:
-            part, ffn_sums, output = tie((part, ffn_sums, output))
-        d_parts.append(part.reshape(n_seq, span, width))
         d_acts.append(d_act)
+    d_acts[-1], y_got = tie((d_acts[-1], y_got))
+    output = (h_own + (y_kept + y_got.astype(F32))).astype(BF)
+    d_acts[-1], ffn_sums, output = tie((d_acts[-1], ffn_sums, output))
     spread = 2 * HEAD_SIZE // local
     tail = jnp.concatenate(
         [
@@ -840,13 +891,13 @@
         ],
         axis=1,
     )
-    d_w = sum(dot(kept[r][0], d_acts[r], 0, 1) for r in range(rows))
-    d_w = jnp.pad(d_w, ((0, 0), (0, extra))) + jnp.pad(tail, ((0, 0), (cols, 0)))
     d_a, d_w, d_out = close_layer(
         n_seq,
         n_rows,
-        d_parts,
-        d_w.astype(BF).reshape(n_rows, n_seq * local, cols + extra),
+        d_acts,
+        [k[0] for k in kept],
+        whole,
+        tail.T,
         d_out.reshape(n_rows * n_seq, local, -1),
     )
     d_a = d_a.reshape(rows * span, width)

time: 630 us -> 606 us (0.962); the launches traced: 619 us -> 603 us
  matrix products: 162 us -> 134 us
  waiting for transfers between devices: 51.6 us -> 63 us
  local copies, waits for them, and re-layouts: 34.4 us -> 27 us
    dot_general x21 -> x17, matrix products: 162 us -> 134 us  [dot(): lax.dot_general(a, b, (((ca,), (cb,)), ((), ())), preferred_element_type=...]
    pallas_call x1, Pallas kernels: 85.1 us -> 74.2 us  [open_layer(): pl.pallas_call(functools.partial(opening, n_seq, n_rows), out_shape=(jax....]
    reduce_scatter x1, waiting for transfers between devices: 0.01 us -> 9.06 us  [on_device(): lax.psum_scatter(ffn_grads, 'rows', scatter_dimension=0, tiled=True)]
    pallas_call x1, Pallas kernels: 77.3 us -> 85.6 us  [close_layer(): pl.pallas_call(functools.partial(closing, n_seq, n_rows), out_shape=(jax....]
    pallas_call x1, Pallas kernels: 49.7 us -> 56.4 us  [meet(): pl.pallas_call(functools.partial(meeting, n_seq, n_rows), out_shape=(jax....]
  transfers between devices with their start and end apart: 20 -> 20, of which waited for: 6 -> 9; matrix products, arithmetic and copies ran while one was open for 29% -> 24% of each run, Pallas kernels for 29% -> 29%
where the time goes in v5:
time: 606 us; the launch traced here: 603 us
  Pallas kernels  262 us (43%)
  matrix products  134 us (22%)
  other arithmetic  86.8 us (14%)
  waiting for transfers between devices  63 us (10%)
  local copies, waits for them, and re-layouts  27 us (4%)
  between operations  15.6 us (3%)
  starting transfers between devices  14.4 us (2%)
    dot_general x17, matrix products, dot(): lax.dot_general(a, b, (((ca,), (cb,)), ((), ())), preferred_element_type=...  134 us
    pallas_call x1, Pallas kernels, close_layer(): pl.pallas_call(functools.partial(closing, n_seq, n_rows), out_shape=(jax....  85.6 us
    pallas_call x1, Pallas kernels, open_layer(): pl.pallas_call(functools.partial(opening, n_seq, n_rows), out_shape=(jax....  74.2 us
    pallas_call x1, Pallas kernels, meet(): pl.pallas_call(functools.partial(meeting, n_seq, n_rows), out_shape=(jax....  56.4 us
    ppermute x18, waiting for transfers between devices, swap(): return lax.ppermute(v, axis, [(i, i ^ bit) for i in range(n)])  53.9 us
    pallas_call x2, Pallas kernels, attention_backward(): pl.pallas_call(functools.partial(backward_heads, plan), out_shape=(jax.Sh...  31.4 us
    pallas_call x2, Pallas kernels, attention_forward(): pl.pallas_call(functools.partial(forward_heads, plan), out_shape=(jax.Sha...  14.8 us
    ppermute x18, starting transfers between devices, swap(): return lax.ppermute(v, axis, [(i, i ^ bit) for i in range(n)])  14.3 us
  transfers between devices with their start and end apart: 20, of which 9 were waited for; matrix products, arithmetic and copies ran while one was open for 24% of the time, Pallas kernels for 29%

profile of v5, /device:TPU:0, one launch (start us, length us, event | category | flops | bytes accessed | tf_op | source)
XLA Modules:
  0.0 602.8 jit_solution(12083526053149447825)
XLA Ops:
  7.3 2.3 pad_maximum_fusion.3
  11.5 74.2 %opening.1 = (bf16[2,1024,2048]{2,1,0:T(8,128)(2,1)}, bf16[2048,640]{1,0:T(8,128)(2,1)}) custom-call(bf16[2,256,2048]{2,1,0:T(8,128)(2,1)} %tokens.1, bf16[4,64,640]{2,1,0:T(8,128)(2,1)} %pad_maximum_fusion.6.pieces), custom_call_target="tpu_custom_call" | custom-call | tf_op jit(solution)/shard_map/opening/pallas_call | solution.py:171
  85.8 4.6 collective-permute-start.1
  92.1 1.5 slice_reduce_fusion.2
  94.6 1.3 convert_bitcast_fusion
  96.8 4.8 fusion.4
  102.7 2.2 fusion.6
  105.0 3.1 fusion.44.x_ref
  108.3 7.1 %attention_forward.3 = (bf16[320,1024]{1,0:T(8,128)(2,1)S(1)}, f32[5,1,1024]{2,1,0:T(1,128)S(1)}) custom-call(s32[1]{0:T(128)} %bitcast.me_ref, bf16[576,1024]{1,0:T(8,128)(2,1)S(1)} %fusion.44.x_ref, f32[32,1024]{1,0:T(8,128)S(1)} %get-tuple-element.152.cos_ref, f32[32,1024]{1,0:T(8,128)S(1)} %get-tuple-element.150.sin_ref, ...), custom_call_target="tpu_custom_call" | custom-call | flops 1342177280 | bytes 4194304 | tf_op jit(solution)/shard_map/attention_forward/pallas_call | solution.py:683
  115.4 3.1 fusion.41.x_ref
  118.5 7.7 %attention_forward.2 = (bf16[320,1024]{1,0:T(8,128)(2,1)S(1)}, f32[5,1,1024]{2,1,0:T(1,128)S(1)}) custom-call(s32[1]{0:T(128)} %bitcast.me_ref, bf16[576,1024]{1,0:T(8,128)(2,1)S(1)} %fusion.41.x_ref, f32[32,1024]{1,0:T(8,128)S(1)} %get-tuple-element.153.cos_ref, f32[32,1024]{1,0:T(8,128)S(1)} %get-tuple-element.151.sin_ref, ...), custom_call_target="tpu_custom_call" | custom-call | flops 1342177280 | bytes 4194304 | tf_op jit(solution)/shard_map/attention_forward/pallas_call | solution.py:683
  127.1 11.0 %collective-permute-done = bf16[2,256,2048]{2,1,0:T(8,128)(2,1)} collective-permute-done((bf16[2,256,2048]{2,1,0:T(8,128)(2,1)S(1)}, bf16[2,256,2048]{2,1,0:T(8,128)(2,1)}, u32[]{:S(2)}, u32[]{:S(2)}) %collective-permute-start) | collective-permute-done | bytes 2097184 | tf_op jit(solution)/shard_map/ppermute | solution.py:32
  138.1 56.4 %meeting.1 = (bf16[4,320,2048]{2,1,0:T(8,128)(2,1)}, bf16[8,2,2,64,1280]{4,3,2,1,0:T(8,128)(2,1)}) custom-call(bf16[320,1024]{1,0:T(8,128)(2,1)} %copy-done.4, bf16[320,1024]{1,0:T(8,128)(2,1)} %copy-done.6, bf16[64,1280]{1,0:T(8,128)(2,1)} %refs_2_.1), custom_call_target="tpu_custom_call" | custom-call | tf_op jit(solution)/shard_map/meeting/pallas_call | solution.py:277
  194.5 3.1 copy.36
  197.6 20.7 %multiply_reduce_fusion = (f32[2048]{0:T(1024)S(1)}, f32[2048,2048]{1,0:T(8,128)}) fusion(bf16[1280,2048]{1,0:T(8,128)(2,1)} %bitcast.231, bf16[2048,1280]{1,0:T(8,128)(2,1)S(1)} %bitcast.215, bf16[2,1024,2048]{2,1,0:T(8,128)(2,1)} %get-tuple-element.61), kind=kOutput, calls=%fused_computation.7 | convolution fusion | flops 10754193408 | bytes 35659776 | tf_op jit(solution)/shard_map/dot_general | solution.py:28
  218.3 9.4 %multiply_convert_fusion = bf16[2048,2048]{1,0:T(8,128)(2,1)} fusion(f32[2048,2048]{1,0:T(8,128)} %get-tuple-element.177, f32[2048]{0:T(1024)S(1)} %get-tuple-element.107, f32[2048]{0:T(1024)S(1)} %add_rsqrt_fusion), kind=kLoop, calls=%fused_computation.6 | loop fusion | flops 12582912 | bytes 25182208 | tf_op jit(solution)/shard_map/convert_element_type | solution.py:820
  227.8 6.6 %pad_maximum_fusion.1 = bf16[2,4,256,2048]{3,2,1,0:T(8,128)(2,1)} fusion(bf16[2,1,256,2048]{3,2,1,0:T(8,128)(2,1)} %bitcast.34, bf16[2,1,256,2048]{3,2,1,0:T(8,128)(2,1)} %bitcast.33, bf16[2,1,256,2048]{3,2,1,0:T(8,128)(2,1)} %bitcast.31, bf16[2,1,256,2048]{3,2,1,0:T(8,128)(2,1)S(1)} %bitcast.213), kind=kLoop, calls=%fused_computation.19 | loop fusion | flops 12582912 | bytes 16777216 | tf_op jit(solution)/shard_map/stack | solution.py:815
  234.4 8.1 %fusion = bf16[2048,2048]{1,0:T(8,128)(2,1)} fusion(bf16[2,4,256,2048]{3,2,1,0:T(8,128)(2,1)} %pad_maximum_fusion.1, f32[2048]{0:T(1024)S(1)} %bitcast.234), kind=kLoop, calls=%fused_computation.4 | loop fusion | flops 12582912 | bytes 16785408 | tf_op jit(solution)/shard_map/convert_element_type | solution.py:826
  242.5 11.9 %fusion.30 = f32[2048,704]{0,1:T(8,128)} fusion(bf16[2048,2048]{1,0:T(8,128)(2,1)} %multiply_convert_fusion, bf16[704,6144]{1,0:T(8,128)(2,1)} %all-gather.2.cloned.1.call-done), kind=kOutput, calls=%fused_computation.62 | convolution fusion | flops 5905580032 | bytes 17039360 | tf_op jit(solution)/shard_map/dot_general | solution.py:28
  254.4 11.9 %fusion.34 = f32[2048,704]{0,1:T(8,128)} fusion(bf16[2048,2048]{1,0:T(8,128)(2,1)} %multiply_convert_fusion, bf16[704,6144]{1,0:T(8,128)(2,1)} %all-gather.2.cloned.1.call-done), kind=kOutput, calls=%fused_computation.66 | convolution fusion | flops 5905580032 | bytes 17039360 | tf_op jit(solution)/shard_map/dot_general | solution.py:28
  266.3 13.9 %multiply_convert_fusion.1 = (bf16[2048,704]{0,1:T(8,128)(2,1)}, bf16[2048,704]{0,1:T(8,128)(2,1)S(1)}, bf16[2048,704]{0,1:T(8,128)(2,1)}) fusion(f32[2048,704]{0,1:T(8,128)} %fusion.34, f32[2048,704]{0,1:T(8,128)} %fusion.30, bf16[2048,2048]{1,0:T(8,128)(2,1)S(1)} %bitcast.210, bf16[704,6144]{1,0:T(8,128)(2,1)} %all-gather.2.cloned.1.call-done), kind=kOutput, calls=%fused_computation.24 | convolution fusion | flops 5927206912 | bytes 31457280 | tf_op jit(solution)/shard_map/dot_general | solution.py:28
  280.2 5.3 fusion.26
  285.6 6.0 add_convert_fusion
  291.6 1.5 fusion.69
  293.5 8.0 %fusion.28 = f32[1024,2048]{1,0:T(8,128)} fusion(bf16[704,6144]{1,0:T(8,128)(2,1)} %all-gather.2.cloned.1.call-done, bf16[2048,704]{0,1:T(8,128)(2,1)S(1)} %get-tuple-element.80), kind=kOutput, calls=%fused_computation.60 | convolution fusion | flops 2952790016 | bytes 12713984 | tf_op jit(solution)/shard_map/dot_general | solution.py:28
  301.5 6.9 %add_convert_fusion.1 = bf16[1024,2048]{1,0:T(8,128)(2,1)S(1)} fusion(f32[1024,2048]{1,0:T(8,128)} %fusion.28, bf16[704,6144]{1,0:T(8,128)(2,1)} %all-gather.2.cloned.1.call-done, bf16[2048,704]{0,1:T(8,128)(2,1)S(1)} %copy-done.61), kind=kOutput, calls=%fused_computation.21 | convolution fusion | flops 2956984320 | bytes 16908288 | tf_op jit(solution)/shard_map/dot_general | solution.py:28
  308.4 1.5 fusion.70
  309.9 1.4 add_convert_fusion.2
  311.3 1.3 collective-permute-done.4
  312.6 1.4 add_convert_fusion.3
  314.0 8.2 %convolution_convert_fusion.2 = bf16[704,2048]{1,0:T(8,128)(2,1)S(1)} fusion(bf16[2048,704]{0,1:T(8,128)(2,1)} %get-tuple-element.72, bf16[2048,2048]{1,0:T(8,128)(2,1)S(1)} %bitcast.210), kind=kOutput, calls=%fused_computation.46 | convolution fusion | flops 5907021824 | bytes 14155776 | tf_op jit(solution)/shard_map/dot_general | solution.py:28
  322.2 6.4 %convolution_convert_fusion.4 = bf16[704,2048]{1,0:T(8,128)(2,1)S(1)} fusion(bf16[2048,704]{0,1:T(8,128)(2,1)S(1)} %get-tuple-element.80, bf16[2048,2048]{1,0:T(8,128)(2,1)S(1)} %bitcast.212), kind=kOutput, calls=%fused_computation.48 | convolution fusion | flops 5907021824 | bytes 14155776 | tf_op jit(solution)/shard_map/dot_general | solution.py:28
  328.6 6.4 %convolution_convert_fusion.3 = bf16[704,2048]{1,0:T(8,128)(2,1)S(1)} fusion(bf16[2048,704]{0,1:T(8,128)(2,1)S(1)} %copy-done.62, bf16[2048,2048]{1,0:T(8,128)(2,1)S(1)} %bitcast.212), kind=kOutput, calls=%fused_computation.47 | convolution fusion | flops 5907021824 | bytes 14155776 | tf_op jit(solution)/shard_map/dot_general | solution.py:28
  335.0 3.9 pad_maximum_fusion
  341.0 2.6 multiply_reduce_fusion.4
  344.2 1.5 collective-permute-start.6
  346.3 10.5 %convolution_convert_fusion.1 = bf16[2048,2048]{1,0:T(8,128)(2,1)S(1)} fusion(bf16[2048,704]{0,1:T(8,128)(2,1)} %get-tuple-element.72, bf16[704,6144]{1,0:T(8,128)(2,1)} %all-gather.2.cloned.1.call-done), kind=kOutput, calls=%fused_computation.23 | convolution fusion | flops 5909774336 | bytes 14155776 | tf_op jit(solution)/shard_map/dot_general | solution.py:28
  356.7 2.5 slice_bitcast_fusion.1
  359.2 2.2 copy-done.31
  361.4 9.0 %collective-permute-done.6 = bf16[256,2048]{1,0:T(8,128)(2,1)S(1)} collective-permute-done((bf16[256,2048]{1,0:T(8,128)(2,1)}, bf16[256,2048]{1,0:T(8,128)(2,1)S(1)}, u32[]{:S(2)}, u32[]{:S(2)}) %collective-permute-start.6) | collective-permute-done | bytes 1048608 | tf_op jit(solution)/shard_map/ppermute | solution.py:32
  370.4 21.7 %collective-permute-done.11 = bf16[256,2048]{1,0:T(8,128)(2,1)S(1)} collective-permute-done((bf16[256,2048]{1,0:T(8,128)(2,1)}, bf16[256,2048]{1,0:T(8,128)(2,1)S(1)}, u32[]{:S(2)}, u32[]{:S(2)}) %collective-permute-start.11) | collective-permute-done | bytes 1048608 | tf_op jit(solution)/shard_map/ppermute | solution.py:32
  392.2 3.2 multiply_reduce_fusion.2
  395.4 6.2 %fusion.66 = (bf16[256,2048]{1,0:T(8,128)(2,1)}, f32[256,2048]{1,0:T(8,128)S(1)}, bf16[256,2048]{1,0:T(8,128)(2,1)S(1)}, f32[256,2048]{1,0:T(8,128)}) fusion(f32[256]{0:T(256)S(1)} %broadcast_multiply_fusion.1, f32[2,4,256,2048]{3,2,1,0:T(8,128)S(1)} %bitcast.204, f32[2048]{0:T(1024)S(1)} %copy-done.50, bf16[256,2048]{1,0:T(8,128)(2,1)S(1)} %collective-permute-done.11, ...), kind=kLoop, calls=%fused_computation.183 | loop fusion | flops 14680064 | bytes 18886664 | tf_op jit(solution)/shard_map/convert_element_type | solution.py:863
  401.6 1.6 convolution_convert_fusion.6
  403.8 5.3 convolution_convert_fusion.5
  409.0 1.7 gather_fusion.2
  413.0 1.1 collective-permute-start.9
  414.0 3.5 collective-permute-done.14
  417.5 1.3 collective-permute-start.8
  418.9 4.6 fusion.18
  424.6 3.4 collective-permute-done.8
  428.8 1.4 fusion.68
  430.3 2.4 pad_maximum_fusion.2
  432.7 4.7 convolution_convert_fusion
  437.6 15.8 %attention_backward.2 = (bf16[576,1024]{1,0:T(8,128)(2,1)S(1)}, f32[2,64,128]{2,1,0:T(8,128)S(1)}) custom-call(s32[1]{0:T(128)} %bitcast.me_ref, bf16[576,1024]{1,0:T(8,128)(2,1)S(1)} %copy-done.25, f32[32,1024]{1,0:T(8,128)S(1)} %copy-done.15, f32[32,1024]{1,0:T(8,128)S(1)} %copy-done.13, s32[1,1024]{1,0:T(1,128)S(1)} %copy-done.21, f32[64,2]{1,0:T(8,128)S(1)} %bitcast.197, ...), custom_call_target="tpu_custom_call" | custom-call | flops 3355443200 | bytes 6291456 | tf_op jit(solution)/shard_map/attention_backward/pallas_call | solution.py:713
  454.6 15.6 %attention_backward.3 = (bf16[576,1024]{1,0:T(8,128)(2,1)S(1)}, f32[2,64,128]{2,1,0:T(8,128)S(1)}) custom-call(s32[1]{0:T(128)} %bitcast.me_ref, bf16[576,1024]{1,0:T(8,128)(2,1)S(1)} %copy-done.23, f32[32,1024]{1,0:T(8,128)S(1)} %copy-done.11, f32[32,1024]{1,0:T(8,128)S(1)} %copy-done.9, s32[1,1024]{1,0:T(1,128)S(1)} %copy-done.19, f32[64,2]{1,0:T(8,128)S(1)} %bitcast.198, ...), custom_call_target="tpu_custom_call" | custom-call | flops 3355443200 | bytes 6291456 | tf_op jit(solution)/shard_map/attention_backward/pallas_call | solution.py:713
  472.6 3.4 collective-permute-done.16
  475.9 7.1 %fusion.16 = bf16[2,256,2048]{2,1,0:T(8,128)(2,1)} fusion(f32[2,4,256,2048]{3,2,1,0:T(8,128)} %bitcast.200, bf16[2,256,2048]{2,1,0:T(8,128)(2,1)} %collective-permute-done.16, bf16[2,256,2048]{2,1,0:T(8,128)(2,1)} %collective-permute-done.17, bf16[2,4,256,2048]{3,2,1,0:T(8,128)(2,1)} %bitcast.208), kind=kLoop, calls=%fused_computation.40 | loop fusion | flops 7340032 | bytes 12582912 | tf_op jit(solution)/shard_map/convert_element_type | solution.py:883
  483.0 9.1 %reduce-scatter.2.cloned.1.call-done = bf16[88,6144]{1,0:T(8,128)(2,1)} async-done(((bf16[704,6144]{1,0:T(8,128)(2,1)}), bf16[88,6144]{1,0:T(8,128)(2,1)}) %reduce-scatter.2.cloned.1.call-update) | async-done | bytes 1081360 | tf_op jit(solution)/shard_map/reduce_scatter | solution.py:846
  492.7 85.6 %closing.1 = (f32[2,256,2048]{2,1,0:T(8,128)}, bf16[4,64,640]{2,1,0:T(8,128)(2,1)}, f32[64,1280]{1,0:T(8,128)}) custom-call(bf16[576,1024]{1,0:T(8,128)(2,1)} %copy-done.3, bf16[576,1024]{1,0:T(8,128)(2,1)} %copy-done.2, bf16[1024,2048]{1,0:T(8,128)(2,1)} %copy-done.29, bf16[1024,2048]{1,0:T(8,128)(2,1)} %copy-done.30, ...), custom_call_target="tpu_custom_call" | custom-call | tf_op jit(solution)/shard_map/closing/pallas_call | solution.py:505
  578.3 1.2 convert_element_type.262
  581.5 1.2 slice_convert_fusion
  582.7 3.1 fusion.10
  587.7 6.7 %fusion.13 = f32[2,256,2048]{2,1,0:T(8,128)} fusion(f32[2,256,2048]{2,1,0:T(8,128)} %bitcast.205, bf16[2,256,2048]{2,1,0:T(8,128)(2,1)S(1)} %copy-done.28, f32[2,256,2048]{2,1,0:T(8,128)} %get-tuple-element.93, f32[2,256]{1,0:T(2,128)S(1)} %broadcast_multiply_fusion, f32[2048]{0:T(1024)S(1)} %copy-done.48, f32[2,256]{1,0:T(2,128)S(1)} %add_rsqrt_fusion.3), kind=kLoop, calls=%fused_computation.36 | loop fusion | flops 7340032 | bytes 14692352 | tf_op jit(solution)/shard_map/add | solution.py:909
  (255 shorter events, 25.6 us)
Async XLA Ops:
  7.2 86.8 %copy-start = (s32[2,1024]{1,0:T(2,128)S(1)}, s32[2,1024]{1,0:T(2,128)}, u32[]{:S(2)}) copy-start(s32[2,1024]{1,0:T(2,128)} %param.17) | copy-start | bytes 24580
  7.2 235.3 %all-gather.2.cloned.1.call-start = ((), (), s32[]{:S(2)}) async-start(), calls=%async_computation.1 | async-start | bytes 9732096 | tf_op jit(solution)/shard_map/all_gather | solution.py:823
  9.6 76.1 %copy-start.33 = (bf16[2,256,2048]{2,1,0:T(8,128)(2,1)S(1)}, bf16[2,256,2048]{2,1,0:T(8,128)(2,1)}, u32[]{:S(2)}) copy-start(bf16[2,256,2048]{2,1,0:T(8,128)(2,1)} %param.16) | copy-start | bytes 6291460
  9.6 82.4 %copy-start.53 = (bf16[2,64]{1,0:T(2,128)(2,1)S(1)}, bf16[2,64]{1,0:T(2,128)(2,1)}, u32[]{:S(2)}) copy-start(bf16[2,64]{1,0:T(2,128)(2,1)} %param.23) | copy-start | bytes 772
  9.6 84.1 %copy-start.59 = (s32[4]{0:T(128)S(1)}, s32[4]{0:T(128)}, u32[]{:S(2)}) copy-start(s32[4]{0:T(128)} %param.19) | copy-start | bytes 52
  9.6 482.5 %reduce-scatter.2.cloned.1.call-start = ((), (), s32[]{:S(2)}) async-start(), calls=%async_computation.2 | async-start | bytes 9732096 | tf_op jit(solution)/shard_map/reduce_scatter | solution.py:846
  85.8 142.0 %collective-permute-start.1 = (bf16[2,256,2048]{2,1,0:T(8,128)(2,1)S(1)}, bf16[2,256,2048]{2,1,0:T(8,128)(2,1)}, u32[]{:S(2)}, u32[]{:S(2)}) collective-permute-start(bf16[2,256,2048]{2,1,0:T(8,128)(2,1)S(1)} %copy-done.33), channel_id=1, source_target_pairs={{0,1},{1,0},{2,3},{3,2},{4,5},{5,4},{6,7},{7,6},{8,9},{9,8},{10,11... | collective-permute-start | bytes 6291464 | tf_op jit(solution)/shard_map/ppermute | solution.py:32
  90.4 47.7 %collective-permute-start = (bf16[2,256,2048]{2,1,0:T(8,128)(2,1)S(1)}, bf16[2,256,2048]{2,1,0:T(8,128)(2,1)}, u32[]{:S(2)}, u32[]{:S(2)}) collective-permute-start(bf16[2,256,2048]{2,1,0:T(8,128)(2,1)S(1)} %copy-done.33), channel_id=1, source_target_pairs={{0,2},{1,3},{2,0},{3,1},{4,6},{5,7},{6,4},{7,5},{8,10},{9,11},{10,... | collective-permute-start | bytes 6291464 | tf_op jit(solution)/shard_map/ppermute | solution.py:32
  92.1 26.4 %copy-start.16 = (f32[2,64]{0,1:T(8,128)}, f32[2,64]{0,1:T(8,128)S(1)}, u32[]{:S(2)}) copy-start(f32[2,64]{0,1:T(8,128)S(1)} %copy.35) | copy-start | bytes 1540
  93.9 7.7 %copy-start.51 = (f32[2]{0:T(128)}, f32[2]{0:T(128)S(1)}, u32[]{:S(2)}) copy-start(f32[2]{0:T(128)S(1)} %select_reduce_fusion) | copy-start | bytes 28
  96.8 5.9 copy-start.47
  96.8 121.5 %copy-start.49 = (f32[2048]{0:T(1024)}, f32[2048]{0:T(1024)S(1)}, u32[]{:S(2)}) copy-start(f32[2048]{0:T(1024)S(1)} %get-tuple-element.107) | copy-start | bytes 24580
  96.8 5.9 copy-start.26
  102.7 5.4 copy-start.8
  102.7 15.8 %copy-start.12 = (f32[32,1024]{1,0:T(8,128)}, f32[32,1024]{1,0:T(8,128)S(1)}, u32[]{:S(2)}) copy-start(f32[32,1024]{1,0:T(8,128)S(1)} %get-tuple-element.151.sin_ref) | copy-start | bytes 393220
  104.9 10.5 %copy-start.30 = (bf16[1024,2048]{1,0:T(8,128)(2,1)}, bf16[1024,2048]{1,0:T(8,128)(2,1)S(1)}, u32[]{:S(2)}) copy-start(bf16[1024,2048]{1,0:T(8,128)(2,1)S(1)} %get-tuple-element.119.refs_3_) | copy-start | bytes 12582916
  105.0 13.6 %copy-start.20 = (s32[1,1024]{1,0:T(1,128)}, s32[1,1024]{1,0:T(1,128)S(1)}, u32[]{:S(2)}) copy-start(s32[1,1024]{1,0:T(1,128)S(1)} %get-tuple-element.171.first_ref) | copy-start | bytes 12292
  105.0 13.5 %copy-start.14 = (f32[32,1024]{1,0:T(8,128)}, f32[32,1024]{1,0:T(8,128)S(1)}, u32[]{:S(2)}) copy-start(f32[32,1024]{1,0:T(8,128)S(1)} %get-tuple-element.153.cos_ref) | copy-start | bytes 393220
  108.1 10.4 %copy-start.22 = (bf16[576,1024]{1,0:T(8,128)(2,1)}, bf16[576,1024]{1,0:T(8,128)(2,1)S(1)}, u32[]{:S(2)}) copy-start(bf16[576,1024]{1,0:T(8,128)(2,1)S(1)} %fusion.44.x_ref) | copy-start | bytes 3538948
  118.5 7.7 %copy-start.24 = (bf16[576,1024]{1,0:T(8,128)(2,1)}, bf16[576,1024]{1,0:T(8,128)(2,1)S(1)}, u32[]{:S(2)}) copy-start(bf16[576,1024]{1,0:T(8,128)(2,1)S(1)} %fusion.41.x_ref) | copy-start | bytes 3538948
  138.1 89.7 %collective-permute-start.2 = (bf16[2,256,2048]{2,1,0:T(8,128)(2,1)}, bf16[2,256,2048]{2,1,0:T(8,128)(2,1)}, u32[]{:S(2)}, u32[]{:S(2)}) collective-permute-start(bf16[2,256,2048]{2,1,0:T(8,128)(2,1)} %collective-permute-done), channel_id=1, source_target_pairs={{0,1},{1,0},{2,3},{3,2},{4,5},{5,4},{6,7},{7,6},{8,9},{9,8},{10,11... | collective-permute-start | bytes 6291464 | tf_op jit(solution)/shard_map/ppermute | solution.py:32
  197.6 20.7 %copy-start.37 = (bf16[8,2,2,64,1280]{4,3,2,1,0:T(8,128)(2,1)}, bf16[8,2,2,64,1280]{4,3,2,1,0:T(8,128)(2,1)S(1)}, u32[]{:S(2)}) copy-start(bf16[8,2,2,64,1280]{4,3,2,1,0:T(8,128)(2,1)S(1)} %copy.36) | copy-start | bytes 15728644
  242.5 23.8 %slice-start.4 = ((s8[8388608]{0:T(1024)(128)(4,1)}), s8[4194304]{0:T(1024)(128)(4,1)S(1)}, s32[]{:S(2)}) async-start(s8[8388608]{0:T(1024)(128)(4,1)} %bitcast.209), calls=%async_computation.7 | async-start | bytes 8388608
  254.4 11.9 %slice-start.5 = ((s8[8388608]{0:T(1024)(128)(4,1)}), s8[4194304]{0:T(1024)(128)(4,1)S(1)}, s32[]{:S(2)}) async-start(s8[8388608]{0:T(1024)(128)(4,1)} %bitcast.209), calls=%async_computation.8 | async-start | bytes 8388608
  291.6 18.3 %copy-start.35 = (bf16[1024,2048]{1,0:T(8,128)(2,1)}, bf16[1024,2048]{1,0:T(8,128)(2,1)S(1)}, u32[]{:S(2)}) copy-start(bf16[1024,2048]{1,0:T(8,128)(2,1)S(1)} %add_convert_fusion) | copy-start | bytes 12582916
  293.1 8.4 %copy-start.61 = (bf16[2048,704]{0,1:T(8,128)(2,1)S(1)}, bf16[2048,704]{0,1:T(8,128)(2,1)}, u32[]{:S(2)}) copy-start(bf16[2048,704]{0,1:T(8,128)(2,1)} %get-tuple-element.81) | copy-start | bytes 8650756
  293.1 16.8 %collective-permute-start.5 = (bf16[256,2048]{1,0:T(8,128)(2,1)S(1)}, bf16[256,2048]{1,0:T(8,128)(2,1)S(1)}, u32[]{:S(2)}, u32[]{:S(2)}) collective-permute-start(bf16[256,2048]{1,0:T(8,128)(2,1)S(1)} %get-tuple-element.125), channel_id=1, source_target_pairs={{0,1},{1,0},{2,3},{3,2},{4,5},{5,4},{6,7},{7,6},{8,9},{9,8},{10,11... | collective-permute-start | bytes 3145736 | tf_op jit(solution)/shard_map/ppermute | solution.py:32
  309.9 2.7 collective-permute-start.4
  309.9 12.2 %slice-start.6 = ((s8[8388608]{0:T(1024)(128)(4,1)}), s8[4194304]{0:T(1024)(128)(4,1)S(1)}, s32[]{:S(2)}) async-start(s8[8388608]{0:T(1024)(128)(4,1)} %bitcast.211), calls=%async_computation.9 | async-start | bytes 8388608
  314.0 8.2 %slice-start.7 = ((s8[8388608]{0:T(1024)(128)(4,1)}), s8[4194304]{0:T(1024)(128)(4,1)S(1)}, s32[]{:S(2)}) async-start(s8[8388608]{0:T(1024)(128)(4,1)} %bitcast.211), calls=%async_computation.10 | async-start | bytes 8388608
  322.2 6.4 %copy-start.62 = (bf16[2048,704]{0,1:T(8,128)(2,1)S(1)}, bf16[2048,704]{0,1:T(8,128)(2,1)}, u32[]{:S(2)}) copy-start(bf16[2048,704]{0,1:T(8,128)(2,1)} %get-tuple-element.81) | copy-start | bytes 8650756
  343.6 17.8 %collective-permute-start.10 = (bf16[256,2048]{1,0:T(8,128)(2,1)}, bf16[256,2048]{1,0:T(8,128)(2,1)S(1)}, u32[]{:S(2)}, u32[]{:S(2)}) collective-permute-start(bf16[256,2048]{1,0:T(8,128)(2,1)} %get-tuple-element.124), channel_id=1, source_target_pairs={{0,1},{1,0},{2,3},{3,2},{4,5},{5,4},{6,7},{7,6},{8,9},{9,8},{10,11... | collective-permute-start | bytes 3145736 | tf_op jit(solution)/shard_map/ppermute | solution.py:32
  343.8 48.3 %slice-start = ((s8[16777216]{0:T(1024)(128)(4,1)}), s8[4194304]{0:T(1024)(128)(4,1)S(1)}, s32[]{:S(2)}) async-start(s8[16777216]{0:T(1024)(128)(4,1)} %bitcast.201), calls=%async_computation.3 | async-start | bytes 8388608
  343.8 48.3 %slice-start.1 = ((s8[16777216]{0:T(1024)(128)(4,1)}), s8[4194304]{0:T(1024)(128)(4,1)S(1)}, s32[]{:S(2)}) async-start(s8[16777216]{0:T(1024)(128)(4,1)} %bitcast.201), calls=%async_computation.4 | async-start | bytes 8388608
  343.8 48.3 %slice-start.2 = ((s8[16777216]{0:T(1024)(128)(4,1)}), s8[4194304]{0:T(1024)(128)(4,1)S(1)}, s32[]{:S(2)}) async-start(s8[16777216]{0:T(1024)(128)(4,1)} %bitcast.201), calls=%async_computation.5 | async-start | bytes 8388608
  343.8 48.3 %slice-start.3 = ((s8[16777216]{0:T(1024)(128)(4,1)}), s8[4194304]{0:T(1024)(128)(4,1)S(1)}, s32[]{:S(2)}) async-start(s8[16777216]{0:T(1024)(128)(4,1)} %bitcast.201), calls=%async_computation.6 | async-start | bytes 8388608
  343.8 17.6 %collective-permute-start.3 = (bf16[256,2048]{1,0:T(8,128)(2,1)}, bf16[256,2048]{1,0:T(8,128)(2,1)S(1)}, u32[]{:S(2)}, u32[]{:S(2)}) collective-permute-start(bf16[256,2048]{1,0:T(8,128)(2,1)} %get-tuple-element.126), channel_id=1, source_target_pairs={{0,1},{1,0},{2,3},{3,2},{4,5},{5,4},{6,7},{7,6},{8,9},{9,8},{10,11... | collective-permute-start | bytes 3145736 | tf_op jit(solution)/shard_map/ppermute | solution.py:32
  344.2 26.2 %collective-permute-start.6 = (bf16[256,2048]{1,0:T(8,128)(2,1)}, bf16[256,2048]{1,0:T(8,128)(2,1)S(1)}, u32[]{:S(2)}, u32[]{:S(2)}) collective-permute-start(bf16[256,2048]{1,0:T(8,128)(2,1)} %add_convert_fusion.3), channel_id=1, source_target_pairs={{0,2},{1,3},{2,0},{3,1},{4,6},{5,7},{6,4},{7,5},{8,10},{9,11},{10,... | collective-permute-start | bytes 3145736 | tf_op jit(solution)/shard_map/ppermute | solution.py:32
  345.7 46.4 %collective-permute-start.11 = (bf16[256,2048]{1,0:T(8,128)(2,1)}, bf16[256,2048]{1,0:T(8,128)(2,1)S(1)}, u32[]{:S(2)}, u32[]{:S(2)}) collective-permute-start(bf16[256,2048]{1,0:T(8,128)(2,1)} %add_convert_fusion.2), channel_id=1, source_target_pairs={{0,2},{1,3},{2,0},{3,1},{4,6},{5,7},{6,4},{7,5},{8,10},{9,11},{10,... | collective-permute-start | bytes 3145736 | tf_op jit(solution)/shard_map/ppermute | solution.py:32
  356.7 35.4 %copy-start.50 = (f32[2048]{0:T(1024)S(1)}, f32[2048]{0:T(1024)}, u32[]{:S(2)}) copy-start(f32[2048]{0:T(1024)} %copy-done.49) | copy-start | bytes 24580
  361.4 34.0 %copy-start.34 = (bf16[2,256,2048]{2,1,0:T(8,128)(2,1)S(1)}, bf16[2,256,2048]{2,1,0:T(8,128)(2,1)}, u32[]{:S(2)}) copy-start(bf16[2,256,2048]{2,1,0:T(8,128)(2,1)} %param.16) | copy-start | bytes 6291460
  361.4 57.5 %collective-permute-start.15 = (bf16[2,256,2048]{2,1,0:T(8,128)(2,1)}, bf16[2,256,2048]{2,1,0:T(8,128)(2,1)}, u32[]{:S(2)}, u32[]{:S(2)}) collective-permute-start(bf16[2,256,2048]{2,1,0:T(8,128)(2,1)} %get-tuple-element.121), channel_id=1, source_target_pairs={{0,1},{1,0},{2,3},{3,2},{4,5},{5,4},{6,7},{7,6},{8,9},{9,8},{10,11... | collective-permute-start | bytes 6291464 | tf_op jit(solution)/shard_map/ppermute | solution.py:32
  392.1 9.4 %slice-start.8 = ((s8[5242880]{0:T(1024)(128)(4,1)}), s8[4194304]{0:T(1024)(128)(4,1)S(1)}, s32[]{:S(2)}) async-start(s8[5242880]{0:T(1024)(128)(4,1)} %bitcast.217), calls=%async_computation.11 | async-start | bytes 8388608
  395.4 6.2 %slice-start.9 = ((s8[5242880]{0:T(1024)(128)(4,1)}), s8[1048576]{0:T(1024)(128)(4,1)S(1)}, s32[]{:S(2)}) async-start(s8[5242880]{0:T(1024)(128)(4,1)} %bitcast.217), calls=%async_computation.12 | async-start | bytes 2097152
  403.8 6.9 %copy-start.58 = (pred[4]{0:T(512)(128)(4,1)S(1)}, pred[4]{0:T(512)(128)(4,1)}, u32[]{:S(2)}) copy-start(pred[4]{0:T(512)(128)(4,1)} %copy-done.57) | copy-start | bytes 16
  411.0 6.6 %collective-permute-start.14 = (bf16[320,256]{1,0:T(8,128)(2,1)S(1)}, bf16[320,256]{1,0:T(8,128)(2,1)S(1)}, u32[]{:S(2)}, u32[]{:S(2)}) collective-permute-start(bf16[320,256]{1,0:T(8,128)(2,1)S(1)} %get-tuple-element.142), channel_id=1, source_target_pairs={{0,3},{1,2},{2,1},{3,0},{4,7},{5,6},{6,5},{7,4},{8,11},{9,10},{10,... | collective-permute-start | bytes 491528 | tf_op jit(solution)/shard_map/ppermute | solution.py:32
  411.5 12.0 %collective-permute-start.13 = (bf16[320,256]{1,0:T(8,128)(2,1)S(1)}, bf16[320,256]{1,0:T(8,128)(2,1)S(1)}, u32[]{:S(2)}, u32[]{:S(2)}) collective-permute-start(bf16[320,256]{1,0:T(8,128)(2,1)S(1)} %get-tuple-element.143), channel_id=1, source_target_pairs={{0,2},{1,3},{2,0},{3,1},{4,6},{5,7},{6,4},{7,5},{8,10},{9,11},{10,... | collective-permute-start | bytes 491528 | tf_op jit(solution)/shard_map/ppermute | solution.py:32
  412.5 11.4 %collective-permute-start.12 = (bf16[320,256]{1,0:T(8,128)(2,1)S(1)}, bf16[320,256]{1,0:T(8,128)(2,1)S(1)}, u32[]{:S(2)}, u32[]{:S(2)}) collective-permute-start(bf16[320,256]{1,0:T(8,128)(2,1)S(1)} %get-tuple-element.144), channel_id=1, source_target_pairs={{0,1},{1,0},{2,3},{3,2},{4,5},{5,4},{6,7},{7,6},{8,9},{9,8},{10,11... | collective-permute-start | bytes 491528 | tf_op jit(solution)/shard_map/ppermute | solution.py:32
  413.0 11.6 %collective-permute-start.9 = (bf16[320,256]{1,0:T(8,128)(2,1)S(1)}, bf16[320,256]{1,0:T(8,128)(2,1)S(1)}, u32[]{:S(2)}, u32[]{:S(2)}) collective-permute-start(bf16[320,256]{1,0:T(8,128)(2,1)S(1)} %get-tuple-element.146), channel_id=1, source_target_pairs={{0,3},{1,2},{2,1},{3,0},{4,7},{5,6},{6,5},{7,4},{8,11},{9,10},{10,... | collective-permute-start | bytes 491528 | tf_op jit(solution)/shard_map/ppermute | solution.py:32
  417.5 10.4 %collective-permute-start.8 = (bf16[320,256]{1,0:T(8,128)(2,1)S(1)}, bf16[320,256]{1,0:T(8,128)(2,1)S(1)}, u32[]{:S(2)}, u32[]{:S(2)}) collective-permute-start(bf16[320,256]{1,0:T(8,128)(2,1)S(1)} %get-tuple-element.147), channel_id=1, source_target_pairs={{0,2},{1,3},{2,0},{3,1},{4,6},{5,7},{6,4},{7,5},{8,10},{9,11},{10,... | collective-permute-start | bytes 491528 | tf_op jit(solution)/shard_map/ppermute | solution.py:32
  418.9 9.1 %collective-permute-start.7 = (bf16[320,256]{1,0:T(8,128)(2,1)S(1)}, bf16[320,256]{1,0:T(8,128)(2,1)S(1)}, u32[]{:S(2)}, u32[]{:S(2)}) collective-permute-start(bf16[320,256]{1,0:T(8,128)(2,1)S(1)} %get-tuple-element.148), channel_id=1, source_target_pairs={{0,1},{1,0},{2,3},{3,2},{4,5},{5,4},{6,7},{7,6},{8,9},{9,8},{10,11... | collective-permute-start | bytes 491528 | tf_op jit(solution)/shard_map/ppermute | solution.py:32
  423.5 6.8 %copy-start.32 = (f32[256,2048]{1,0:T(8,128)S(1)}, f32[256,2048]{1,0:T(8,128)}, u32[]{:S(2)}) copy-start(f32[256,2048]{1,0:T(8,128)} %get-tuple-element.114) | copy-start | bytes 6291460
  423.5 52.5 %collective-permute-start.17 = (bf16[2,256,2048]{2,1,0:T(8,128)(2,1)}, bf16[2,256,2048]{2,1,0:T(8,128)(2,1)}, u32[]{:S(2)}, u32[]{:S(2)}) collective-permute-start(bf16[2,256,2048]{2,1,0:T(8,128)(2,1)} %get-tuple-element.120), channel_id=1, source_target_pairs={{0,1},{1,0},{2,3},{3,2},{4,5},{5,4},{6,7},{7,6},{8,9},{9,8},{10,11... | collective-permute-start | bytes 6291464 | tf_op jit(solution)/shard_map/ppermute | solution.py:32
  428.0 48.0 %collective-permute-start.16 = (bf16[2,256,2048]{2,1,0:T(8,128)(2,1)}, bf16[2,256,2048]{2,1,0:T(8,128)(2,1)}, u32[]{:S(2)}, u32[]{:S(2)}) collective-permute-start(bf16[2,256,2048]{2,1,0:T(8,128)(2,1)} %fusion.18), channel_id=1, source_target_pairs={{0,2},{1,3},{2,0},{3,1},{4,6},{5,7},{6,4},{7,5},{8,10},{9,11},{10,... | collective-permute-start | bytes 6291464 | tf_op jit(solution)/shard_map/ppermute | solution.py:32
  437.5 17.1 %copy-start.5 = (bf16[320,1024]{1,0:T(8,128)(2,1)S(1)}, bf16[320,1024]{1,0:T(8,128)(2,1)}, u32[]{:S(2)}) copy-start(bf16[320,1024]{1,0:T(8,128)(2,1)} %copy-done.4) | copy-start | bytes 1966084
  437.6 17.0 %copy-start.9 = (f32[32,1024]{1,0:T(8,128)S(1)}, f32[32,1024]{1,0:T(8,128)}, u32[]{:S(2)}) copy-start(f32[32,1024]{1,0:T(8,128)} %copy-done.8) | copy-start | bytes 393220
  437.6 17.0 %copy-start.11 = (f32[32,1024]{1,0:T(8,128)S(1)}, f32[32,1024]{1,0:T(8,128)}, u32[]{:S(2)}) copy-start(f32[32,1024]{1,0:T(8,128)} %copy-done.10) | copy-start | bytes 393220
  437.6 17.0 %copy-start.19 = (s32[1,1024]{1,0:T(1,128)S(1)}, s32[1,1024]{1,0:T(1,128)}, u32[]{:S(2)}) copy-start(s32[1,1024]{1,0:T(1,128)} %copy-done.18) | copy-start | bytes 12292
  437.6 17.0 %copy-start.23 = (bf16[576,1024]{1,0:T(8,128)(2,1)S(1)}, bf16[576,1024]{1,0:T(8,128)(2,1)}, u32[]{:S(2)}) copy-start(bf16[576,1024]{1,0:T(8,128)(2,1)} %copy-done.22) | copy-start | bytes 3538948
  582.7 4.8 copy-start.41
  582.7 5.0 copy-start.55
  587.5 6.9 %copy-start.39 = (f32[64,1920]{1,0:T(8,128)}, f32[64,1920]{1,0:T(8,128)S(1)}, u32[]{:S(2)}) copy-start(f32[64,1920]{1,0:T(8,128)S(1)} %concatenate.61) | copy-start | bytes 1474564
  587.7 7.3 %copy-start.46 = (f32[64,1280]{1,0:T(8,128)S(1)}, f32[64,1280]{1,0:T(8,128)}, u32[]{:S(2)}) copy-start(f32[64,1280]{1,0:T(8,128)} %get-tuple-element.193) | copy-start | bytes 983044
  587.7 8.0 %copy-start.1 = (s32[2,1024]{1,0:T(2,128)S(1)}, s32[2,1024]{1,0:T(2,128)}, u32[]{:S(2)}) copy-start(s32[2,1024]{1,0:T(2,128)} %param.17) | copy-start | bytes 24580
  (29 other events, 85.0 us)
Sparse Core Ops, SparseCore 0:
  10.8 156.7 all-gather.1
  339.0 153.0 reduce-scatter.1

commit v6 on v5

--- a/solution.py
+++ b/solution.py
@@ -368,13 +368,6 @@
             da.at[t, k + 1], da_near.at[t, k // top], near_s.at[t, k // top], near_r.at[t, k // top], seq=low
         )
 
-    near_do = []
-    for c, k in enumerate((top, 0)):
-        whose = other(me, k + 1, n_seq)
-        for j in range(n_rows):
-            near_do.append(
-                send(do.at[j * n_seq + whose], do_near.at[c, j], near_s.at[rows + c, j], near_r.at[rows + c, j], seq=low)
-            )
     side_dw, side_do = [], []
 
     def beside_next():
@@ -390,34 +383,19 @@
                 send(do_sum.at[owner(i, 1)], do_next.at[i], ring_s.at[0, 1, i], ring_r.at[0, 1, i], rows=beside)
             )
 
-    far_da = []
-    near_da = [[], []]
-    make_da(0, top + 1)
-    near_da[0].append(send_near(0, top))
-    beside_next()
-    for t in range(rows):
-        if t:
-            make_da(t, top + 1)
-            near_da[0].append(send_near(t, top))
-        make_da(t, top)
-        near_da[0][t].wait_recv()
-        add_rows(da_send.at[t], da.at[t, top], da_near.at[t, 1])
-        far_da.append(send(da_send.at[t], da_far.at[t], far_s.at[t], far_r.at[t], seq=high))
-        if t == 0:
-            beside_next()
+    ring_dw, ring_do, summed = [], [], []
 
     def ring_step(kind, n, i, near, mine, far, out, final, side):
         side.wait_recv()
-        beside_next()
         terms = (mine, near) if n == 0 else (mine, near, far.at[n - 1])
         if i == 0:
             add_rows(final, *terms)
             return None
         add_rows(out.at[n], *terms)
-        return send(out.at[n], far.at[n], ring_s.at[1, kind, n], ring_r.at[1, kind, n], rows=up)
-
-    beside_next()
-    ring_dw, ring_do = [], []
+        copy = send(out.at[n], far.at[n], ring_s.at[1, kind, n], ring_r.at[1, kind, n], rows=up)
+        if summed:
+            beside_next()
+        return copy
 
     def step_dw(n):
         i = order[n]
@@ -435,6 +413,46 @@
         ring_do.append(
             ring_step(1, n, i, do_next.at[i], do_sum.at[owner(i, 0)], do_far, do_send, do_own, side_do[n])
         )
+
+    far_da = []
+    near_da = [[], []]
+    make_da(0, top + 1)
+    near_da[0].append(send_near(0, top))
+    beside_next()
+    near_do = []
+    for c, k in enumerate((top, 0)):
+        whose = other(me, k + 1, n_seq)
+        for j in range(n_rows):
+            near_do.append(
+                send(do.at[j * n_seq + whose], do_near.at[c, j], near_s.at[rows + c, j], near_r.at[rows + c, j], seq=low)
+            )
+    for t in range(rows):
+        if t:
+            make_da(t, top + 1)
+            near_da[0].append(send_near(t, top))
+            if len(side_dw) < half:
+                beside_next()
+        make_da(t, top)
+        near_da[0][t].wait_recv()
+        add_rows(da_send.at[t], da.at[t, top], da_near.at[t, 1])
+        far_da.append(send(da_send.at[t], da_far.at[t], far_s.at[t], far_r.at[t], seq=high))
+        if t == 0:
+            beside_next()
+            step_dw(0)
+    while len(side_dw) < half:
+        beside_next()
+    unfinished = list(range(rows))
+
+    def finish():
+        t = unfinished.pop(0)
+        near_da[1][t].wait_recv()
+        far_da[t].wait_recv()
+
+        @pl.loop(0, width // 256)
+        def _(i):
+            at = pl.ds(pl.multiple_of(i * 256, 256), 256)
+            total = da[t, 0, at, :].astype(F32) + da_near[t, 0, at, :].astype(F32)
+            da_out[t, :, at] = (total + da_far[t, at, :].astype(F32)).T
 
     for copy in near_do:
         copy.wait_recv()
@@ -445,16 +463,20 @@
                 do.at[j * n_seq + other(me, k, n_seq)],
                 do_near.at[c, j],
             )
-    step_dw(0)
+    summed.append(True)
+    beside_next()
+    beside_next()
+    step_dw(1)
     for t in range(rows):
         make_da(t, 1)
         near_da[1].append(send_near(t, 0))
         make_da(t, 0)
-    for n in range(1, half):
+    for n in range(2, half):
+        if n == half - 1:
+            step_do(0)
         step_dw(n)
     for i in range(0, cols + tail.shape[0], 128):
         dw_flip[:, i : i + 128] = flip(dw_own[i : i + 128, :])
-    step_do(0)
     kept = pltpu.make_async_copy(dw_flip.at[pl.ds(pl.multiple_of(me * local, local), local)], dw_out.at[me], end_s.at[0])
     kept.start()
     parts = [
@@ -464,19 +486,14 @@
         )
         for j in range(1, n_seq)
     ]
+    finish()
     for n in range(1, half):
+        if n == half - 1 and len(unfinished) == 1:
+            finish()
         step_do(n)
     parts.append(send(do_own.at[pl.ds(0, local)], do_last, end_s.at[n_seq], end_r.at[n_seq], seq=high))
-    for t in range(rows):
-        near_da[1][t].wait_recv()
-        far_da[t].wait_recv()
-
-        @pl.loop(0, width // 256)
-        def _(i):
-            at = pl.ds(pl.multiple_of(i * 256, 256), 256)
-            total = da[t, 0, at, :].astype(F32) + da_near[t, 0, at, :].astype(F32)
-            da_out[t, :, at] = (total + da_far[t, at, :].astype(F32)).T
-
+    while unfinished:
+        finish()
     for copy in parts:
         copy.wait_recv()
     add_rows(do_out, do_own.at[pl.ds(local, local)], do_last)
@@ -806,24 +823,28 @@
         o, inv = attention_forward(*args)
         kept.append((a_in, args, o, inv))
         o_rows.append(o)
-    dy_far = cross_seq(d_output, n_seq)
-    o_rows[-1], dy_far = tie((o_rows[-1], dy_far))
+    dy_far = [cross_seq(d_output[0], n_seq)]
+    o_rows[-1], dy_far[0] = tie((o_rows[-1], dy_far[0]))
+    w_ff = jnp.concatenate([gate_up_weight, down_weight], axis=1)
+    w_ff = lax.all_gather(w_ff, "rows", axis=0, tiled=True)
     o_all, w_out = meet(n_seq, n_rows, o_rows, out_weight)
+    o_all, w_ff, later = tie((o_all, w_ff, d_output[1:]))
     o_all = o_all.reshape(n_seq * q_cols, rows * length)
     w_out = jnp.swapaxes(w_out, 1, 2).reshape(width, -1)
-    dy_all = [d_output, swap(d_output, "seq", n_seq, 1), dy_far, swap(dy_far, "seq", n_seq, 1)]
-    dy_all = jnp.stack(dy_all, axis=1)
+    dy_far += [cross_seq(later[r - 1], n_seq) for r in range(1, rows)]
+    gy = []
+    for r in range(rows):
+        near = swap(d_output[r], "seq", n_seq, 1)
+        for v in (d_output[r], near, dy_far[r], swap(dy_far[r], "seq", n_seq, 1)):
+            gy.append((row_scale[r] * v.astype(F32)).astype(BF))
+    gy = jnp.concatenate(gy, axis=0)
     x_all = x_rows.reshape(rows * length, width).astype(F32)
 
     h_all = x_all + dot(o_all, w_out, 0, 1)
     inverse_two = inverse_rms(h_all)
     f_in = (h_all * inverse_two * gains[1]).astype(BF)
 
-    w_ff = jnp.concatenate([gate_up_weight, down_weight], axis=1)
-    w_ff = lax.all_gather(w_ff, "rows", axis=0, tiled=True)
     w_g, w_u, w_dn = (w_ff[:, i * width : (i + 1) * width] for i in range(3))
-    gy = row_scale[:, None, None, None] * dy_all.astype(F32)
-    gy = gy.astype(BF).reshape(rows * length, width)
     gate = dot(f_in, w_g, 1, 1)
     upper = dot(f_in, w_u, 1, 1)
     sigma = jax.nn.sigmoid(gate)
@@ -838,8 +859,7 @@
         part = dot(d_gate[at], w_g, 1, 0) + dot(d_upper[at], w_u, 1, 0)
         part = part.astype(BF).reshape(n_seq, span, width)
         df_rows.append(fold_seq([part[j] for j in range(n_seq)], n_seq))
-    sent, d_gate, d_upper, hidden = tie(([v for _, v in df_rows], d_gate, d_upper, hidden))
-    df_rows = [(v[0], cross_seq(sent[r], n_seq)) for r, v in enumerate(df_rows)]
+    df_rows = [(v, cross_seq(w, n_seq)) for v, w in df_rows]
     ffn_grads = jnp.concatenate(
         [dot(d_gate, f_in, 0, 0), dot(d_upper, f_in, 0, 0), dot(hidden, gy, 0, 0)], axis=1
     ).astype(BF)
@@ -853,7 +873,10 @@
     for r in range(rows):
         inverse = inverse_rms(h_own[r])
         unit = h_own[r] * inverse
-        df = df_rows[r][0] + df_rows[r][1].astype(F32)
+        got = df_rows[r][1]
+        if r:
+            do_rows[-1][0], got = tie((do_rows[-1][0], got))
+        df = df_rows[r][0] + got.astype(F32)
         d_gain_two = d_gain_two + jnp.sum(df * unit, axis=0)
         scaled = df * gains[1]
         g_two = row_scale[r] * d_output[r].astype(F32)

time: 606 us -> 588 us (0.970)
  waiting for transfers between devices: 63 us -> 36.9 us
  other arithmetic: 86.8 us -> 99.4 us
  matrix products: 134 us -> 126 us
  local copies, waits for them, and re-layouts: 27 us -> 34 us
    unnamed x5 -> x11, other arithmetic: 0.07 us -> 18 us
    ppermute x18 -> x21, waiting for transfers between devices: 53.9 us -> 36.9 us  [swap(): return lax.ppermute(v, axis, [(i, i ^ bit) for i in range(n)])]
    reduce_scatter x1, waiting for transfers between devices: 9.06 us -> 0.01 us  [on_device(): lax.psum_scatter(ffn_grads, 'rows', scatter_dimension=0, tiled=True)]
    convert_element_type x1 -> x0, other arithmetic: 8.14 us -> none  [on_device(): gy = gy.astype(BF).reshape(rows * length, width)]
    dot_general x17, matrix products: 134 us -> 126 us  [dot(): lax.dot_general(a, b, (((ca,), (cb,)), ((), ())), preferred_element_type=...]
    another operation x1 -> x0, other arithmetic: 6.6 us -> none  [on_device(): dy_all = jnp.stack(dy_all, axis=1)]
    ppermute x18 -> x21, starting transfers between devices: 14.3 us -> 15.3 us  [swap(): return lax.ppermute(v, axis, [(i, i ^ bit) for i in range(n)])]
  transfers between devices with their start and end apart: 20 -> 23, of which waited for: 9 -> 6; matrix products, arithmetic and copies ran while one was open for 24% -> 32% of each run, Pallas kernels for 29% -> 30%
where the time goes in v6:
time: 588 us; the launch traced here: 584 us
  Pallas kernels  257 us (44%)
  matrix products  126 us (21%)
  other arithmetic  99.4 us (17%)
  waiting for transfers between devices  36.9 us (6%)
  local copies, waits for them, and re-layouts  34 us (6%)
  between operations  15.5 us (3%)
  starting transfers between devices  15.4 us (3%)
    dot_general x17, matrix products, dot(): lax.dot_general(a, b, (((ca,), (cb,)), ((), ())), preferred_element_type=...  126 us
    pallas_call x1, Pallas kernels, close_layer(): pl.pallas_call(functools.partial(closing, n_seq, n_rows), out_shape=(jax....  81.1 us
    pallas_call x1, Pallas kernels, open_layer(): pl.pallas_call(functools.partial(opening, n_seq, n_rows), out_shape=(jax....  74.1 us
    pallas_call x1, Pallas kernels, meet(): pl.pallas_call(functools.partial(meeting, n_seq, n_rows), out_shape=(jax....  55.9 us
    ppermute x21, waiting for transfers between devices, swap(): return lax.ppermute(v, axis, [(i, i ^ bit) for i in range(n)])  36.9 us
    pallas_call x2, Pallas kernels, attention_backward(): pl.pallas_call(functools.partial(backward_heads, plan), out_shape=(jax.Sh...  31.2 us
    unnamed x11, other arithmetic  18 us
    ppermute x21, starting transfers between devices, swap(): return lax.ppermute(v, axis, [(i, i ^ bit) for i in range(n)])  15.3 us
  transfers between devices with their start and end apart: 23, of which 6 were waited for; matrix products, arithmetic and copies ran while one was open for 32% of the time, Pallas kernels for 30%

profile of v6, /device:TPU:0, one launch (start us, length us, event | category | flops | bytes accessed | tf_op | source)
XLA Modules:
  0.0 584.3 jit_solution(2713173351978775270)
XLA Ops:
  7.3 2.3 pad_maximum_fusion.2
  11.5 74.1 %opening.1 = (bf16[2,1024,2048]{2,1,0:T(8,128)(2,1)}, bf16[2048,640]{1,0:T(8,128)(2,1)}) custom-call(bf16[2,256,2048]{2,1,0:T(8,128)(2,1)} %tokens.1, bf16[4,64,640]{2,1,0:T(8,128)(2,1)} %pad_maximum_fusion.5.pieces), custom_call_target="tpu_custom_call" | custom-call | tf_op jit(solution)/shard_map/opening/pallas_call | solution.py:171
  85.7 1.6 slice_bitcast_fusion.28
  87.3 4.6 collective-permute-start.1
  93.7 1.4 slice_reduce_fusion.2
  98.1 4.8 fusion.3
  104.1 2.2 fusion.5
  106.3 3.1 fusion.45.x_ref
  109.4 7.1 %attention_forward.3 = (bf16[320,1024]{1,0:T(8,128)(2,1)S(1)}, f32[5,1,1024]{2,1,0:T(1,128)S(1)}) custom-call(s32[1]{0:T(128)} %bitcast.me_ref, bf16[576,1024]{1,0:T(8,128)(2,1)S(1)} %fusion.45.x_ref, f32[32,1024]{1,0:T(8,128)S(1)} %get-tuple-element.150.cos_ref, f32[32,1024]{1,0:T(8,128)S(1)} %get-tuple-element.148.sin_ref, ...), custom_call_target="tpu_custom_call" | custom-call | flops 1342177280 | bytes 4194304 | tf_op jit(solution)/shard_map/attention_forward/pallas_call | solution.py:700
  116.5 3.1 fusion.42.x_ref
  120.4 7.4 %attention_forward.2 = (bf16[320,1024]{1,0:T(8,128)(2,1)S(1)}, f32[5,1,1024]{2,1,0:T(1,128)S(1)}) custom-call(s32[1]{0:T(128)} %bitcast.me_ref, bf16[576,1024]{1,0:T(8,128)(2,1)S(1)} %fusion.42.x_ref, f32[32,1024]{1,0:T(8,128)S(1)} %get-tuple-element.151.cos_ref, f32[32,1024]{1,0:T(8,128)S(1)} %get-tuple-element.149.sin_ref, ...), custom_call_target="tpu_custom_call" | custom-call | flops 1342177280 | bytes 4194304 | tf_op jit(solution)/shard_map/attention_forward/pallas_call | solution.py:700
  128.9 1.9 fusion.55
  132.3 3.1 fusion.56
  135.4 3.1 fusion.57
  138.5 55.9 %meeting.1 = (bf16[4,320,2048]{2,1,0:T(8,128)(2,1)}, bf16[8,2,2,64,1280]{4,3,2,1,0:T(8,128)(2,1)}) custom-call(bf16[320,1024]{1,0:T(8,128)(2,1)} %copy-done.4, bf16[320,1024]{1,0:T(8,128)(2,1)} %copy-done.6, bf16[64,1280]{1,0:T(8,128)(2,1)} %refs_2_.1), custom_call_target="tpu_custom_call" | custom-call | tf_op jit(solution)/shard_map/meeting/pallas_call | solution.py:277
  194.4 5.4 copy.35
  199.8 3.1 fusion.58
  202.9 1.8 fusion.59
  204.7 3.1 fusion.60
  207.8 1.6 collective-permute-start.4
  209.3 20.2 %multiply_reduce_fusion = (f32[2048]{0:T(1024)S(1)}, f32[2048,2048]{1,0:T(8,128)}) fusion(bf16[1280,2048]{1,0:T(8,128)(2,1)} %bitcast.224, bf16[2048,1280]{1,0:T(8,128)(2,1)} %bitcast.205, bf16[2,1024,2048]{2,1,0:T(8,128)(2,1)} %get-tuple-element.61), kind=kOutput, calls=%fused_computation.5 | convolution fusion | flops 10754193408 | bytes 35659776 | tf_op jit(solution)/shard_map/dot_general | solution.py:28
  229.6 7.1 %multiply_convert_fusion = bf16[2048,2048]{1,0:T(8,128)(2,1)S(1)} fusion(f32[2048,2048]{1,0:T(8,128)} %get-tuple-element.173, f32[2048]{0:T(1024)S(1)} %get-tuple-element.104, f32[2048]{0:T(1024)S(1)} %add_rsqrt_fusion), kind=kLoop, calls=%fused_computation.4 | loop fusion | flops 12582912 | bytes 25182208 | tf_op jit(solution)/shard_map/convert_element_type | solution.py:845
  237.9 8.4 %fusion.29 = f32[2048,704]{0,1:T(8,128)} fusion(bf16[2048,2048]{1,0:T(8,128)(2,1)S(1)} %multiply_convert_fusion, bf16[704,6144]{1,0:T(8,128)(2,1)S(1)} %copy-done.57), kind=kOutput, calls=%fused_computation.59 | convolution fusion | flops 5905580032 | bytes 17039360 | tf_op jit(solution)/shard_map/dot_general | solution.py:28
  246.5 8.0 %fusion.33 = f32[2048,704]{0,1:T(8,128)} fusion(bf16[2048,2048]{1,0:T(8,128)(2,1)S(1)} %multiply_convert_fusion, bf16[704,6144]{1,0:T(8,128)(2,1)S(1)} %copy-done.57), kind=kOutput, calls=%fused_computation.63 | convolution fusion | flops 5905580032 | bytes 17039360 | tf_op jit(solution)/shard_map/dot_general | solution.py:28
  254.4 1.8 multiply_reduce_fusion.6
  256.2 1.9 fusion.61
  258.1 1.8 fusion.62
  260.0 15.5 %multiply_convert_fusion.1 = (bf16[2048,704]{0,1:T(8,128)(2,1)}, bf16[2048,704]{0,1:T(8,128)(2,1)S(1)}, bf16[2048,704]{0,1:T(8,128)(2,1)}) fusion(f32[2048,704]{0,1:T(8,128)} %fusion.33, f32[2048,704]{0,1:T(8,128)} %fusion.29, bf16[2048,2048]{1,0:T(8,128)(2,1)} %fusion.62, bf16[704,6144]{1,0:T(8,128)(2,1)} %all-gather.2.cloned.1.call-done), kind=kOutput, calls=%fused_computation.21 | convolution fusion | flops 5927206912 | bytes 31457280 | tf_op jit(solution)/shard_map/dot_general | solution.py:28
  275.5 10.4 %convolution_convert_fusion.2 = bf16[704,2048]{1,0:T(8,128)(2,1)S(1)} fusion(bf16[2048,704]{0,1:T(8,128)(2,1)} %get-tuple-element.110, bf16[2048,2048]{1,0:T(8,128)(2,1)} %fusion.62), kind=kOutput, calls=%fused_computation.43 | convolution fusion | flops 5907021824 | bytes 14155776 | tf_op jit(solution)/shard_map/dot_general | solution.py:28
  286.0 6.5 %convolution_convert_fusion.4 = bf16[704,2048]{1,0:T(8,128)(2,1)S(1)} fusion(bf16[2048,704]{0,1:T(8,128)(2,1)S(1)} %get-tuple-element.111, bf16[2048,2048]{1,0:T(8,128)(2,1)S(1)} %multiply_convert_fusion), kind=kOutput, calls=%fused_computation.45 | convolution fusion | flops 5907021824 | bytes 14155776 | tf_op jit(solution)/shard_map/dot_general | solution.py:28
  292.5 6.4 %convolution_convert_fusion.3 = bf16[704,2048]{1,0:T(8,128)(2,1)S(1)} fusion(bf16[2048,704]{0,1:T(8,128)(2,1)S(1)} %copy-done.62, bf16[2048,2048]{1,0:T(8,128)(2,1)S(1)} %multiply_convert_fusion), kind=kOutput, calls=%fused_computation.44 | convolution fusion | flops 5907021824 | bytes 14155776 | tf_op jit(solution)/shard_map/dot_general | solution.py:28
  299.0 3.9 pad_maximum_fusion
  303.0 7.7 %fusion.25 = f32[1024,2048]{1,0:T(8,128)} fusion(bf16[704,6144]{1,0:T(8,128)(2,1)} %all-gather.2.cloned.1.call-done, bf16[2048,704]{0,1:T(8,128)(2,1)S(1)} %get-tuple-element.111), kind=kOutput, calls=%fused_computation.55 | convolution fusion | flops 2952790016 | bytes 12713984 | tf_op jit(solution)/shard_map/dot_general | solution.py:28
  310.6 6.9 %add_convert_fusion = bf16[1024,2048]{1,0:T(8,128)(2,1)S(1)} fusion(f32[1024,2048]{1,0:T(8,128)} %fusion.25, bf16[704,6144]{1,0:T(8,128)(2,1)} %all-gather.2.cloned.1.call-done, bf16[2048,704]{0,1:T(8,128)(2,1)S(1)} %copy-done.63), kind=kOutput, calls=%fused_computation.17 | convolution fusion | flops 2956984320 | bytes 16908288 | tf_op jit(solution)/shard_map/dot_general | solution.py:28
  319.1 2.1 copy-done.61
  321.2 5.9 %fusion.27 = f32[1024,2048]{1,0:T(8,128)} fusion(bf16[704,6144]{1,0:T(8,128)(2,1)S(1)} %bitcast.231, bf16[2048,704]{0,1:T(8,128)(2,1)S(1)} %copy-done.61), kind=kOutput, calls=%fused_computation.57 | convolution fusion | flops 2952790016 | bytes 12713984 | tf_op jit(solution)/shard_map/dot_general | solution.py:28
  327.1 6.0 %add_convert_fusion.1 = bf16[1024,2048]{1,0:T(8,128)(2,1)S(1)} fusion(f32[1024,2048]{1,0:T(8,128)} %fusion.27, bf16[704,6144]{1,0:T(8,128)(2,1)S(1)} %bitcast.231, bf16[2048,704]{0,1:T(8,128)(2,1)S(1)} %copy-done.63), kind=kOutput, calls=%fused_computation.18 | convolution fusion | flops 2956984320 | bytes 16908288 | tf_op jit(solution)/shard_map/dot_general | solution.py:28
  335.0 9.3 %convolution_convert_fusion.1 = bf16[2048,2048]{1,0:T(8,128)(2,1)S(1)} fusion(bf16[2048,704]{0,1:T(8,128)(2,1)S(1)} %copy-done.64, bf16[704,6144]{1,0:T(8,128)(2,1)} %all-gather.2.cloned.1.call-done), kind=kOutput, calls=%fused_computation.20 | convolution fusion | flops 5909774336 | bytes 14155776 | tf_op jit(solution)/shard_map/dot_general | solution.py:28
  345.2 2.7 slice_bitcast_fusion.1
  351.2 19.6 %collective-permute-done.8 = bf16[256,2048]{1,0:T(8,128)(2,1)S(1)} collective-permute-done((bf16[256,2048]{1,0:T(8,128)(2,1)S(1)}, bf16[256,2048]{1,0:T(8,128)(2,1)S(1)}, u32[]{:S(2)}, u32[]{:S(2)}) %collective-permute-start.8) | collective-permute-done | bytes 1048608 | tf_op jit(solution)/shard_map/ppermute | solution.py:32
  370.8 3.5 multiply_reduce_fusion.2
  374.3 4.8 fusion.76
  379.2 2.4 convolution_convert_fusion.6
  381.7 2.7 gather_fusion.1
  386.3 6.4 %collective-permute-done.10 = bf16[256,2048]{1,0:T(8,128)(2,1)} collective-permute-done((bf16[256,2048]{1,0:T(8,128)(2,1)}, bf16[256,2048]{1,0:T(8,128)(2,1)}, u32[]{:S(2)}, u32[]{:S(2)}) %collective-permute-start.10) | collective-permute-done | bytes 1048608 | tf_op jit(solution)/shard_map/ppermute | solution.py:32
  392.7 3.5 multiply_reduce_fusion.1
  396.2 5.2 fusion.75
  401.5 1.6 convolution_convert_fusion.5
  407.8 2.8 collective-permute-done.17
  410.6 4.6 fusion.17
  415.7 1.9 collective-permute-done.13
  417.7 2.9 collective-permute-done.12
  421.9 1.4 fusion.77
  423.3 2.5 pad_maximum_fusion.1
  425.9 4.9 convolution_convert_fusion
  430.9 15.6 %attention_backward.2 = (bf16[576,1024]{1,0:T(8,128)(2,1)S(1)}, f32[2,64,128]{2,1,0:T(8,128)S(1)}) custom-call(s32[1]{0:T(128)} %bitcast.me_ref, bf16[576,1024]{1,0:T(8,128)(2,1)S(1)} %copy-done.25, f32[32,1024]{1,0:T(8,128)S(1)} %copy-done.15, f32[32,1024]{1,0:T(8,128)S(1)} %copy-done.13, s32[1,1024]{1,0:T(1,128)S(1)} %copy-done.21, f32[64,2]{1,0:T(8,128)S(1)} %bitcast.192, ...), custom_call_target="tpu_custom_call" | custom-call | flops 3355443200 | bytes 6291456 | tf_op jit(solution)/shard_map/attention_backward/pallas_call | solution.py:730
  447.8 15.6 %attention_backward.3 = (bf16[576,1024]{1,0:T(8,128)(2,1)S(1)}, f32[2,64,128]{2,1,0:T(8,128)S(1)}) custom-call(s32[1]{0:T(128)} %bitcast.me_ref, bf16[576,1024]{1,0:T(8,128)(2,1)S(1)} %copy-done.23, f32[32,1024]{1,0:T(8,128)S(1)} %copy-done.11, f32[32,1024]{1,0:T(8,128)S(1)} %copy-done.9, s32[1,1024]{1,0:T(1,128)S(1)} %copy-done.19, f32[64,2]{1,0:T(8,128)S(1)} %bitcast.193, ...), custom_call_target="tpu_custom_call" | custom-call | flops 3355443200 | bytes 6291456 | tf_op jit(solution)/shard_map/attention_backward/pallas_call | solution.py:730
  465.8 3.2 collective-permute-done.19
  468.9 7.0 %fusion.15 = bf16[2,256,2048]{2,1,0:T(8,128)(2,1)} fusion(f32[2,4,256,2048]{3,2,1,0:T(8,128)} %bitcast.199, bf16[2,256,2048]{2,1,0:T(8,128)(2,1)} %collective-permute-done.19, bf16[2,256,2048]{2,1,0:T(8,128)(2,1)} %collective-permute-done.20, bf16[2,4,256,2048]{3,2,1,0:T(8,128)(2,1)} %bitcast.203), kind=kLoop, calls=%fused_computation.37 | loop fusion | flops 7340032 | bytes 12582912 | tf_op jit(solution)/shard_map/convert_element_type | solution.py:906
  475.9 1.9 slice_convert_fusion.1
  477.8 2.3 slice_convert_fusion
  480.8 81.1 %closing.1 = (f32[2,256,2048]{2,1,0:T(8,128)}, bf16[4,64,640]{2,1,0:T(8,128)(2,1)}, f32[64,1280]{1,0:T(8,128)}) custom-call(bf16[576,1024]{1,0:T(8,128)(2,1)} %copy-done.3, bf16[576,1024]{1,0:T(8,128)(2,1)} %copy-done.2, bf16[1024,2048]{1,0:T(8,128)(2,1)} %copy-done.31, bf16[1024,2048]{1,0:T(8,128)(2,1)} %copy-done.32, ...), custom_call_target="tpu_custom_call" | custom-call | tf_op jit(solution)/shard_map/closing/pallas_call | solution.py:522
  564.2 3.1 fusion.9
  569.2 6.7 %fusion.12 = f32[2,256,2048]{2,1,0:T(8,128)} fusion(f32[2,256,2048]{2,1,0:T(8,128)} %bitcast.200, bf16[2,256,2048]{2,1,0:T(8,128)(2,1)S(1)} %copy-done.28, f32[2,256,2048]{2,1,0:T(8,128)} %get-tuple-element.93, f32[2,256]{1,0:T(2,128)S(1)} %broadcast_multiply_fusion, f32[2048]{0:T(1024)S(1)} %copy-done.49, f32[2,256]{1,0:T(2,128)S(1)} %add_rsqrt_fusion.3), kind=kLoop, calls=%fused_computation.33 | loop fusion | flops 7340032 | bytes 14692352 | tf_op jit(solution)/shard_map/add | solution.py:932
  (266 shorter events, 38.2 us)
Async XLA Ops:
  7.2 88.1 %copy-start = (s32[2,1024]{1,0:T(2,128)S(1)}, s32[2,1024]{1,0:T(2,128)}, u32[]{:S(2)}) copy-start(s32[2,1024]{1,0:T(2,128)} %param.17) | copy-start | bytes 24580
  7.2 200.6 %all-gather.2.cloned.1.call-start = ((), (), s32[]{:S(2)}) async-start(), calls=%async_computation.1 | async-start | bytes 9732096 | tf_op jit(solution)/shard_map/all_gather | solution.py:829
  9.6 76.0 %copy-start.29 = (bf16[2,256,2048]{2,1,0:T(8,128)(2,1)S(1)}, bf16[2,256,2048]{2,1,0:T(8,128)(2,1)}, u32[]{:S(2)}) copy-start(bf16[2,256,2048]{2,1,0:T(8,128)(2,1)} %param.16) | copy-start | bytes 6291460
  9.6 466.3 %reduce-scatter.2.cloned.1.call-start = ((), (), s32[]{:S(2)}) async-start(), calls=%async_computation.2 | async-start | bytes 9732096 | tf_op jit(solution)/shard_map/reduce_scatter | solution.py:866
  85.6 8.0 %copy-start.53 = (bf16[2,64]{1,0:T(2,128)(2,1)S(1)}, bf16[2,64]{1,0:T(2,128)(2,1)}, u32[]{:S(2)}) copy-start(bf16[2,64]{1,0:T(2,128)(2,1)} %param.23) | copy-start | bytes 772
  87.3 45.0 %collective-permute-start.1 = (bf16[256,2048]{1,0:T(8,128)(2,1)}, bf16[256,2048]{1,0:T(8,128)(2,1)}, u32[]{:S(2)}, u32[]{:S(2)}) collective-permute-start(bf16[256,2048]{1,0:T(8,128)(2,1)} %get-tuple-element.125), channel_id=1, source_target_pairs={{0,1},{1,0},{2,3},{3,2},{4,5},{5,4},{6,7},{7,6},{8,9},{9,8},{10,11... | collective-permute-start | bytes 3145736 | tf_op jit(solution)/shard_map/ppermute | solution.py:32
  91.9 38.9 %collective-permute-start = (bf16[256,2048]{1,0:T(8,128)(2,1)}, bf16[256,2048]{1,0:T(8,128)(2,1)}, u32[]{:S(2)}, u32[]{:S(2)}) collective-permute-start(bf16[256,2048]{1,0:T(8,128)(2,1)} %get-tuple-element.125), channel_id=1, source_target_pairs={{0,2},{1,3},{2,0},{3,1},{4,6},{5,7},{6,4},{7,5},{8,10},{9,11},{10,... | collective-permute-start | bytes 3145736 | tf_op jit(solution)/shard_map/ppermute | solution.py:32
  92.8 111.9 %collective-permute-start.3 = (bf16[256,2048]{1,0:T(8,128)(2,1)}, bf16[256,2048]{1,0:T(8,128)(2,1)}, u32[]{:S(2)}, u32[]{:S(2)}) collective-permute-start(bf16[256,2048]{1,0:T(8,128)(2,1)} %get-tuple-element.123), channel_id=1, source_target_pairs={{0,1},{1,0},{2,3},{3,2},{4,5},{5,4},{6,7},{7,6},{8,9},{9,8},{10,11... | collective-permute-start | bytes 3145736 | tf_op jit(solution)/shard_map/ppermute | solution.py:32
  93.7 26.7 %copy-start.16 = (f32[2,64]{0,1:T(8,128)}, f32[2,64]{0,1:T(8,128)S(1)}, u32[]{:S(2)}) copy-start(f32[2,64]{0,1:T(8,128)S(1)} %copy.34) | copy-start | bytes 1540
  98.1 6.0 %copy-start.48 = (f32[2048]{0:T(1024)}, f32[2048]{0:T(1024)S(1)}, u32[]{:S(2)}) copy-start(f32[2048]{0:T(1024)S(1)} %get-tuple-element.105) | copy-start | bytes 24580
  98.1 11.3 %copy-start.18 = (s32[1,1024]{1,0:T(1,128)}, s32[1,1024]{1,0:T(1,128)S(1)}, u32[]{:S(2)}) copy-start(s32[1,1024]{1,0:T(1,128)S(1)} %get-tuple-element.168.first_ref) | copy-start | bytes 12292
  98.1 22.3 %copy-start.20 = (s32[1,1024]{1,0:T(1,128)}, s32[1,1024]{1,0:T(1,128)S(1)}, u32[]{:S(2)}) copy-start(s32[1,1024]{1,0:T(1,128)S(1)} %get-tuple-element.169.first_ref) | copy-start | bytes 12292
  98.1 5.9 %copy-start.26 = (bf16[2,1024,2048]{2,1,0:T(8,128)(2,1)S(1)}, bf16[2,1024,2048]{2,1,0:T(8,128)(2,1)}, u32[]{:S(2)}) copy-start(bf16[2,1024,2048]{2,1,0:T(8,128)(2,1)} %get-tuple-element.61) | copy-start | bytes 25165828
  103.9 5.4 copy-start.8
  104.0 16.5 %copy-start.12 = (f32[32,1024]{1,0:T(8,128)}, f32[32,1024]{1,0:T(8,128)S(1)}, u32[]{:S(2)}) copy-start(f32[32,1024]{1,0:T(8,128)S(1)} %get-tuple-element.149.sin_ref) | copy-start | bytes 393220
  104.0 5.4 copy-start.10
  104.0 16.4 %copy-start.14 = (f32[32,1024]{1,0:T(8,128)}, f32[32,1024]{1,0:T(8,128)S(1)}, u32[]{:S(2)}) copy-start(f32[32,1024]{1,0:T(8,128)S(1)} %get-tuple-element.151.cos_ref) | copy-start | bytes 393220
  106.2 10.3 %copy-start.32 = (bf16[1024,2048]{1,0:T(8,128)(2,1)}, bf16[1024,2048]{1,0:T(8,128)(2,1)S(1)}, u32[]{:S(2)}) copy-start(bf16[1024,2048]{1,0:T(8,128)(2,1)S(1)} %get-tuple-element.114.refs_3_) | copy-start | bytes 12582916
  109.3 10.3 %copy-start.22 = (bf16[576,1024]{1,0:T(8,128)(2,1)}, bf16[576,1024]{1,0:T(8,128)(2,1)S(1)}, u32[]{:S(2)}) copy-start(bf16[576,1024]{1,0:T(8,128)(2,1)S(1)} %fusion.45.x_ref) | copy-start | bytes 3538948
  109.3 7.2 %copy-start.58 = (s32[4]{0:T(128)S(1)}, s32[4]{0:T(128)}, u32[]{:S(2)}) copy-start(s32[4]{0:T(128)} %param.19) | copy-start | bytes 52
  119.6 9.3 %copy-start.24 = (bf16[576,1024]{1,0:T(8,128)(2,1)}, bf16[576,1024]{1,0:T(8,128)(2,1)S(1)}, u32[]{:S(2)}) copy-start(bf16[576,1024]{1,0:T(8,128)(2,1)S(1)} %fusion.42.x_ref) | copy-start | bytes 3538948
  119.6 8.2 %copy-start.27 = (bf16[2,256,2048]{2,1,0:T(8,128)(2,1)S(1)}, bf16[2,256,2048]{2,1,0:T(8,128)(2,1)}, u32[]{:S(2)}) copy-start(bf16[2,256,2048]{2,1,0:T(8,128)(2,1)} %tokens.1) | copy-start | bytes 6291460
  127.8 7.5 %copy-start.6 = (bf16[320,1024]{1,0:T(8,128)(2,1)}, bf16[320,1024]{1,0:T(8,128)(2,1)S(1)}, u32[]{:S(2)}) copy-start(bf16[320,1024]{1,0:T(8,128)(2,1)S(1)} %get-tuple-element.66.refs_1_.o_ref) | copy-start | bytes 1966084
  130.8 69.0 %collective-permute-start.2 = (bf16[256,2048]{1,0:T(8,128)(2,1)}, bf16[256,2048]{1,0:T(8,128)(2,1)}, u32[]{:S(2)}, u32[]{:S(2)}) collective-permute-start(bf16[256,2048]{1,0:T(8,128)(2,1)} %collective-permute-done), channel_id=1, source_target_pairs={{0,1},{1,0},{2,3},{3,2},{4,5},{5,4},{6,7},{7,6},{8,9},{9,8},{10,11... | collective-permute-start | bytes 3145736 | tf_op jit(solution)/shard_map/ppermute | solution.py:32
  207.8 38.5 %collective-permute-start.4 = (bf16[256,2048]{1,0:T(8,128)(2,1)S(1)}, bf16[256,2048]{1,0:T(8,128)(2,1)S(1)}, u32[]{:S(2)}, u32[]{:S(2)}) collective-permute-start(bf16[256,2048]{1,0:T(8,128)(2,1)S(1)} %bitcast.213), channel_id=1, source_target_pairs={{0,2},{1,3},{2,0},{3,1},{4,6},{5,7},{6,4},{7,5},{8,10},{9,11},{10,... | collective-permute-start | bytes 3145736 | tf_op jit(solution)/shard_map/ppermute | solution.py:32
  229.6 8.3 %copy-start.57 = (bf16[704,6144]{1,0:T(8,128)(2,1)S(1)}, bf16[704,6144]{1,0:T(8,128)(2,1)}, u32[]{:S(2)}) copy-start(bf16[704,6144]{1,0:T(8,128)(2,1)} %all-gather.2.cloned.1.call-done) | copy-start | bytes 25952260
  246.3 11.8 %collective-permute-start.5 = (bf16[256,2048]{1,0:T(8,128)(2,1)S(1)}, bf16[256,2048]{1,0:T(8,128)(2,1)S(1)}, u32[]{:S(2)}, u32[]{:S(2)}) collective-permute-start(bf16[256,2048]{1,0:T(8,128)(2,1)S(1)} %collective-permute-done.4), channel_id=1, source_target_pairs={{0,1},{1,0},{2,3},{3,2},{4,5},{5,4},{6,7},{7,6},{8,9},{9,8},{10,11... | collective-permute-start | bytes 3145736 | tf_op jit(solution)/shard_map/ppermute | solution.py:32
  275.5 27.4 %copy-start.60 = (bf16[2048,704]{0,1:T(8,128)(2,1)}, bf16[2048,704]{0,1:T(8,128)(2,1)S(1)}, u32[]{:S(2)}) copy-start(bf16[2048,704]{0,1:T(8,128)(2,1)S(1)} %get-tuple-element.111) | copy-start | bytes 8650756
  286.0 6.6 %copy-start.62 = (bf16[2048,704]{0,1:T(8,128)(2,1)S(1)}, bf16[2048,704]{0,1:T(8,128)(2,1)}, u32[]{:S(2)}) copy-start(bf16[2048,704]{0,1:T(8,128)(2,1)} %get-tuple-element.112) | copy-start | bytes 8650756
  302.9 7.7 %copy-start.63 = (bf16[2048,704]{0,1:T(8,128)(2,1)S(1)}, bf16[2048,704]{0,1:T(8,128)(2,1)}, u32[]{:S(2)}) copy-start(bf16[2048,704]{0,1:T(8,128)(2,1)} %get-tuple-element.112) | copy-start | bytes 8650756
  302.9 16.1 %slice-start.4 = ((s8[8650752]{0:T(1024)(128)(4,1)}), s8[4194304]{0:T(1024)(128)(4,1)S(1)}, s32[]{:S(2)}) async-start(s8[8650752]{0:T(1024)(128)(4,1)} %bitcast.230), calls=%async_computation.7 | async-start | bytes 8388608
  303.0 16.1 %slice-start.5 = ((s8[8650752]{0:T(1024)(128)(4,1)}), s8[4194304]{0:T(1024)(128)(4,1)S(1)}, s32[]{:S(2)}) async-start(s8[8650752]{0:T(1024)(128)(4,1)} %bitcast.230), calls=%async_computation.8 | async-start | bytes 8388608
  310.6 8.5 %slice-start.6 = ((s8[8650752]{0:T(1024)(128)(4,1)}), s8[262144]{0:T(1024)(128)(4,1)S(1)}, s32[]{:S(2)}) async-start(s8[8650752]{0:T(1024)(128)(4,1)} %bitcast.230), calls=%async_computation.9 | async-start | bytes 524288
  317.5 32.0 %copy-start.36 = (bf16[1024,2048]{1,0:T(8,128)(2,1)}, bf16[1024,2048]{1,0:T(8,128)(2,1)S(1)}, u32[]{:S(2)}) copy-start(bf16[1024,2048]{1,0:T(8,128)(2,1)S(1)} %add_convert_fusion) | copy-start | bytes 12582916
  318.7 30.9 %collective-permute-start.9 = (bf16[256,2048]{1,0:T(8,128)(2,1)S(1)}, bf16[256,2048]{1,0:T(8,128)(2,1)S(1)}, u32[]{:S(2)}, u32[]{:S(2)}) collective-permute-start(bf16[256,2048]{1,0:T(8,128)(2,1)S(1)} %get-tuple-element.120), channel_id=1, source_target_pairs={{0,1},{1,0},{2,3},{3,2},{4,5},{5,4},{6,7},{7,6},{8,9},{9,8},{10,11... | collective-permute-start | bytes 3145736 | tf_op jit(solution)/shard_map/ppermute | solution.py:32
  333.4 17.8 %collective-permute-start.6 = (bf16[256,2048]{1,0:T(8,128)(2,1)S(1)}, bf16[256,2048]{1,0:T(8,128)(2,1)S(1)}, u32[]{:S(2)}, u32[]{:S(2)}) collective-permute-start(bf16[256,2048]{1,0:T(8,128)(2,1)S(1)} %get-tuple-element.121), channel_id=1, source_target_pairs={{0,1},{1,0},{2,3},{3,2},{4,5},{5,4},{6,7},{7,6},{8,9},{9,8},{10,11... | collective-permute-start | bytes 3145736 | tf_op jit(solution)/shard_map/ppermute | solution.py:32
  333.7 10.6 %collective-permute-start.7 = (bf16[256,2048]{1,0:T(8,128)(2,1)S(1)}, bf16[256,2048]{1,0:T(8,128)(2,1)S(1)}, u32[]{:S(2)}, u32[]{:S(2)}) collective-permute-start(bf16[256,2048]{1,0:T(8,128)(2,1)S(1)} %get-tuple-element.122), channel_id=1, source_target_pairs={{0,1},{1,0},{2,3},{3,2},{4,5},{5,4},{6,7},{7,6},{8,9},{9,8},{10,11... | collective-permute-start | bytes 3145736 | tf_op jit(solution)/shard_map/ppermute | solution.py:32
  344.8 26.1 %collective-permute-start.8 = (bf16[256,2048]{1,0:T(8,128)(2,1)S(1)}, bf16[256,2048]{1,0:T(8,128)(2,1)S(1)}, u32[]{:S(2)}, u32[]{:S(2)}) collective-permute-start(bf16[256,2048]{1,0:T(8,128)(2,1)S(1)} %add_convert_fusion.3), channel_id=1, source_target_pairs={{0,2},{1,3},{2,0},{3,1},{4,6},{5,7},{6,4},{7,5},{8,10},{9,11},{10,... | collective-permute-start | bytes 3145736 | tf_op jit(solution)/shard_map/ppermute | solution.py:32
  349.1 57.4 %collective-permute-start.18 = (bf16[2,256,2048]{2,1,0:T(8,128)(2,1)}, bf16[2,256,2048]{2,1,0:T(8,128)(2,1)}, u32[]{:S(2)}, u32[]{:S(2)}) collective-permute-start(bf16[2,256,2048]{2,1,0:T(8,128)(2,1)} %get-tuple-element.116), channel_id=1, source_target_pairs={{0,1},{1,0},{2,3},{3,2},{4,5},{5,4},{6,7},{7,6},{8,9},{9,8},{10,11... | collective-permute-start | bytes 6291464 | tf_op jit(solution)/shard_map/ppermute | solution.py:32
  349.1 43.6 %collective-permute-start.14 = (bf16[256,2048]{1,0:T(8,128)(2,1)}, bf16[256,2048]{1,0:T(8,128)(2,1)S(1)}, u32[]{:S(2)}, u32[]{:S(2)}) collective-permute-start(bf16[256,2048]{1,0:T(8,128)(2,1)} %get-tuple-element.119), channel_id=1, source_target_pairs={{0,1},{1,0},{2,3},{3,2},{4,5},{5,4},{6,7},{7,6},{8,9},{9,8},{10,11... | collective-permute-start | bytes 3145736 | tf_op jit(solution)/shard_map/ppermute | solution.py:32
  351.0 23.4 %copy-start.30 = (bf16[2,256,2048]{2,1,0:T(8,128)(2,1)S(1)}, bf16[2,256,2048]{2,1,0:T(8,128)(2,1)}, u32[]{:S(2)}) copy-start(bf16[2,256,2048]{2,1,0:T(8,128)(2,1)} %param.16) | copy-start | bytes 6291460
  351.0 41.8 %collective-permute-start.10 = (bf16[256,2048]{1,0:T(8,128)(2,1)}, bf16[256,2048]{1,0:T(8,128)(2,1)}, u32[]{:S(2)}, u32[]{:S(2)}) collective-permute-start(bf16[256,2048]{1,0:T(8,128)(2,1)} %add_convert_fusion.2), channel_id=1, source_target_pairs={{0,2},{1,3},{2,0},{3,1},{4,6},{5,7},{6,4},{7,5},{8,10},{9,11},{10,... | collective-permute-start | bytes 3145736 | tf_op jit(solution)/shard_map/ppermute | solution.py:32
  370.8 8.4 %slice-start = ((s8[5242880]{0:T(1024)(128)(4,1)}), s8[4194304]{0:T(1024)(128)(4,1)S(1)}, s32[]{:S(2)}) async-start(s8[5242880]{0:T(1024)(128)(4,1)} %bitcast.206), calls=%async_computation.3 | async-start | bytes 8388608
  392.7 8.8 %slice-start.2 = ((s8[5242880]{0:T(1024)(128)(4,1)}), s8[4194304]{0:T(1024)(128)(4,1)S(1)}, s32[]{:S(2)}) async-start(s8[5242880]{0:T(1024)(128)(4,1)} %bitcast.209), calls=%async_computation.5 | async-start | bytes 8388608
  396.2 5.3 slice-start.3
  404.2 6.5 %collective-permute-start.17 = (bf16[320,256]{1,0:T(8,128)(2,1)S(1)}, bf16[320,256]{1,0:T(8,128)(2,1)S(1)}, u32[]{:S(2)}, u32[]{:S(2)}) collective-permute-start(bf16[320,256]{1,0:T(8,128)(2,1)S(1)} %get-tuple-element.140), channel_id=1, source_target_pairs={{0,3},{1,2},{2,1},{3,0},{4,7},{5,6},{6,5},{7,4},{8,11},{9,10},{10,... | collective-permute-start | bytes 491528 | tf_op jit(solution)/shard_map/ppermute | solution.py:32
  404.3 10.9 %collective-permute-start.16 = (bf16[320,256]{1,0:T(8,128)(2,1)S(1)}, bf16[320,256]{1,0:T(8,128)(2,1)S(1)}, u32[]{:S(2)}, u32[]{:S(2)}) collective-permute-start(bf16[320,256]{1,0:T(8,128)(2,1)S(1)} %get-tuple-element.141), channel_id=1, source_target_pairs={{0,2},{1,3},{2,0},{3,1},{4,6},{5,7},{6,4},{7,5},{8,10},{9,11},{10,... | collective-permute-start | bytes 491528 | tf_op jit(solution)/shard_map/ppermute | solution.py:32
  405.3 10.4 %collective-permute-start.15 = (bf16[320,256]{1,0:T(8,128)(2,1)S(1)}, bf16[320,256]{1,0:T(8,128)(2,1)S(1)}, u32[]{:S(2)}, u32[]{:S(2)}) collective-permute-start(bf16[320,256]{1,0:T(8,128)(2,1)S(1)} %get-tuple-element.142), channel_id=1, source_target_pairs={{0,1},{1,0},{2,3},{3,2},{4,5},{5,4},{6,7},{7,6},{8,9},{9,8},{10,11... | collective-permute-start | bytes 491528 | tf_op jit(solution)/shard_map/ppermute | solution.py:32
  406.2 11.5 %collective-permute-start.13 = (bf16[320,256]{1,0:T(8,128)(2,1)S(1)}, bf16[320,256]{1,0:T(8,128)(2,1)S(1)}, u32[]{:S(2)}, u32[]{:S(2)}) collective-permute-start(bf16[320,256]{1,0:T(8,128)(2,1)S(1)} %copy-done.47), channel_id=1, source_target_pairs={{0,3},{1,2},{2,1},{3,0},{4,7},{5,6},{6,5},{7,4},{8,11},{9,10},{10,... | collective-permute-start | bytes 491528 | tf_op jit(solution)/shard_map/ppermute | solution.py:32
  406.5 14.0 %collective-permute-start.12 = (bf16[320,256]{1,0:T(8,128)(2,1)S(1)}, bf16[320,256]{1,0:T(8,128)(2,1)S(1)}, u32[]{:S(2)}, u32[]{:S(2)}) collective-permute-start(bf16[320,256]{1,0:T(8,128)(2,1)S(1)} %copy-done.46), channel_id=1, source_target_pairs={{0,2},{1,3},{2,0},{3,1},{4,6},{5,7},{6,4},{7,5},{8,10},{9,11},{10,... | collective-permute-start | bytes 491528 | tf_op jit(solution)/shard_map/ppermute | solution.py:32
  410.6 9.9 %collective-permute-start.11 = (bf16[320,256]{1,0:T(8,128)(2,1)S(1)}, bf16[320,256]{1,0:T(8,128)(2,1)S(1)}, u32[]{:S(2)}, u32[]{:S(2)}) collective-permute-start(bf16[320,256]{1,0:T(8,128)(2,1)S(1)} %get-tuple-element.146), channel_id=1, source_target_pairs={{0,1},{1,0},{2,3},{3,2},{4,5},{5,4},{6,7},{7,6},{8,9},{9,8},{10,11... | collective-permute-start | bytes 491528 | tf_op jit(solution)/shard_map/ppermute | solution.py:32
  410.6 12.6 %copy-start.35 = (f32[256,2048]{1,0:T(8,128)S(1)}, f32[256,2048]{1,0:T(8,128)}, u32[]{:S(2)}) copy-start(f32[256,2048]{1,0:T(8,128)} %get-tuple-element.107) | copy-start | bytes 6291460
  415.2 8.1 %copy-start.34 = (f32[256,2048]{1,0:T(8,128)S(1)}, f32[256,2048]{1,0:T(8,128)}, u32[]{:S(2)}) copy-start(f32[256,2048]{1,0:T(8,128)} %get-tuple-element.109) | copy-start | bytes 6291460
  415.2 53.7 %collective-permute-start.20 = (bf16[2,256,2048]{2,1,0:T(8,128)(2,1)}, bf16[2,256,2048]{2,1,0:T(8,128)(2,1)}, u32[]{:S(2)}, u32[]{:S(2)}) collective-permute-start(bf16[2,256,2048]{2,1,0:T(8,128)(2,1)} %get-tuple-element.115), channel_id=1, source_target_pairs={{0,1},{1,0},{2,3},{3,2},{4,5},{5,4},{6,7},{7,6},{8,9},{9,8},{10,11... | collective-permute-start | bytes 6291464 | tf_op jit(solution)/shard_map/ppermute | solution.py:32
  420.5 48.4 %collective-permute-start.19 = (bf16[2,256,2048]{2,1,0:T(8,128)(2,1)}, bf16[2,256,2048]{2,1,0:T(8,128)(2,1)}, u32[]{:S(2)}, u32[]{:S(2)}) collective-permute-start(bf16[2,256,2048]{2,1,0:T(8,128)(2,1)} %fusion.17), channel_id=1, source_target_pairs={{0,2},{1,3},{2,0},{3,1},{4,6},{5,7},{6,4},{7,5},{8,10},{9,11},{10,... | collective-permute-start | bytes 6291464 | tf_op jit(solution)/shard_map/ppermute | solution.py:32
  430.9 16.9 %copy-start.5 = (bf16[320,1024]{1,0:T(8,128)(2,1)S(1)}, bf16[320,1024]{1,0:T(8,128)(2,1)}, u32[]{:S(2)}) copy-start(bf16[320,1024]{1,0:T(8,128)(2,1)} %copy-done.4) | copy-start | bytes 1966084
  430.9 16.9 %copy-start.9 = (f32[32,1024]{1,0:T(8,128)S(1)}, f32[32,1024]{1,0:T(8,128)}, u32[]{:S(2)}) copy-start(f32[32,1024]{1,0:T(8,128)} %copy-done.8) | copy-start | bytes 393220
  430.9 16.9 %copy-start.11 = (f32[32,1024]{1,0:T(8,128)S(1)}, f32[32,1024]{1,0:T(8,128)}, u32[]{:S(2)}) copy-start(f32[32,1024]{1,0:T(8,128)} %copy-done.10) | copy-start | bytes 393220
  430.9 16.9 %copy-start.19 = (s32[1,1024]{1,0:T(1,128)S(1)}, s32[1,1024]{1,0:T(1,128)}, u32[]{:S(2)}) copy-start(s32[1,1024]{1,0:T(1,128)} %copy-done.18) | copy-start | bytes 12292
  430.9 16.9 %copy-start.23 = (bf16[576,1024]{1,0:T(8,128)(2,1)S(1)}, bf16[576,1024]{1,0:T(8,128)(2,1)}, u32[]{:S(2)}) copy-start(bf16[576,1024]{1,0:T(8,128)(2,1)} %copy-done.22) | copy-start | bytes 3538948
  447.8 17.1 %copy-start.54 = (f32[64]{0:T(128)S(1)}, f32[64]{0:T(128)}, u32[]{:S(2)}) copy-start(f32[64]{0:T(128)} %pad.13.clone) | copy-start | bytes 772
  569.0 6.9 %copy-start.38 = (f32[64,1920]{1,0:T(8,128)}, f32[64,1920]{1,0:T(8,128)S(1)}, u32[]{:S(2)}) copy-start(f32[64,1920]{1,0:T(8,128)S(1)} %concatenate.65) | copy-start | bytes 1474564
  569.2 7.3 %copy-start.45 = (f32[64,1280]{1,0:T(8,128)S(1)}, f32[64,1280]{1,0:T(8,128)}, u32[]{:S(2)}) copy-start(f32[64,1280]{1,0:T(8,128)} %get-tuple-element.189) | copy-start | bytes 983044
  569.2 8.0 %copy-start.1 = (s32[2,1024]{1,0:T(2,128)S(1)}, s32[2,1024]{1,0:T(2,128)}, u32[]{:S(2)}) copy-start(s32[2,1024]{1,0:T(2,128)} %param.17) | copy-start | bytes 24580
  (31 other events, 100.4 us)
Sparse Core Ops, SparseCore 0:
  10.8 156.6 all-gather.1
  303.0 152.1 reduce-scatter.1

commit v7 on v6

--- a/solution.py
+++ b/solution.py
@@ -213,8 +213,7 @@
         copy.start()
         return copy
 
-    mine_low, mine_top = lax.rem(me, 2), lax.div(me, 2)
-    mine = wo.at[r, mine_low, mine_top]
+    mine = wo.at[r, me]
     own = pltpu.make_async_copy(out_w, mine, kept_sem.at[rows])
     own.start()
     pair = send(out_w, mine, pair_s, pair_r, high)
@@ -225,11 +224,12 @@
     far, near, kept, ring, sides, lows = [], [], [], [], [], []
 
     def pass_on(i):
-        ref = wo.at[2 * lax.rem(a + half - i, half) + b, mine_low]
-        if i < half - 1:
-            ring.append(send(ref, ref, ring_s.at[i], ring_r.at[i], up, "rows"))
-        sides.append(send(ref, ref, side_s.at[0, i], side_r.at[0, i], beside, "rows"))
-        lows.append(send(ref, ref, side_s.at[1, i], side_r.at[1, i], low))
+        for u, who in enumerate((me, high)):
+            ref = wo.at[2 * lax.rem(a + half - i, half) + b, who]
+            if i < half - 1:
+                ring.append(send(ref, ref, ring_s.at[u, i], ring_r.at[u, i], up, "rows"))
+            sides.append(send(ref, ref, side_s.at[u, 0, i], side_r.at[u, 0, i], beside, "rows"))
+            lows.append(send(ref, ref, side_s.at[u, 1, i], side_r.at[u, 1, i], low))
 
     for t in range(rows):
         for j in range(0, n_seq, top):
@@ -250,7 +250,8 @@
     pair.wait_recv()
     pass_on(0)
     for i in range(1, half):
-        ring[i - 1].wait_recv()
+        for copy in ring[2 * i - 2 : 2 * i]:
+            copy.wait_recv()
         pass_on(i)
     for t in range(rows):
         for c, j in enumerate(range(0, n_seq, top)):
@@ -258,9 +259,10 @@
             for k in range(j, j + top):
                 near.append(send(place(high, t, k), place(high, t, k ^ 1), on_s.at[t, k], on_r.at[t, k], low))
     for i in range(half):
-        sides[i].wait_recv()
-        ref = wo.at[2 * lax.rem(a + half - i, half) + 1 - b, mine_low]
-        lows.append(send(ref, ref, side_s.at[2, i], side_r.at[2, i], low))
+        for u, who in enumerate((me, high)):
+            sides[2 * i + u].wait_recv()
+            ref = wo.at[2 * lax.rem(a + half - i, half) + 1 - b, who]
+            lows.append(send(ref, ref, side_s.at[u, 2, i], side_r.at[u, 2, i], low))
     for copy in kept:
         copy.wait()
     for copy in near + lows:
@@ -278,15 +280,15 @@
         functools.partial(meeting, n_seq, n_rows),
         out_shape=(
             jax.ShapeDtypeStruct((n_seq, columns, rows * length), BF),
-            jax.ShapeDtypeStruct((n_rows, 2, n_seq // 2) + out_w.shape, BF),
+            jax.ShapeDtypeStruct((n_rows, n_seq) + out_w.shape, BF),
         ),
         in_specs=[hbm] * (rows + 1),
         out_specs=(hbm, hbm),
         scratch_shapes=[dma((rows + 1,))]
         + [dma((rows, n_seq))] * 6
         + [dma, dma]
-        + [dma((n_rows // 2,))] * 2
-        + [dma((3, n_rows // 2))] * 2,
+        + [dma((2, n_rows // 2))] * 2
+        + [dma((2, 3, n_rows // 2))] * 2,
         compiler_params=pltpu.CompilerParams(collective_id=2, has_side_effects=True),
         name="meeting",
     )(*o, out_w)
@@ -830,7 +832,7 @@
     o_all, w_out = meet(n_seq, n_rows, o_rows, out_weight)
     o_all, w_ff, later = tie((o_all, w_ff, d_output[1:]))
     o_all = o_all.reshape(n_seq * q_cols, rows * length)
-    w_out = jnp.swapaxes(w_out, 1, 2).reshape(width, -1)
+    w_out = w_out.reshape(width, -1)
     dy_far += [cross_seq(later[r - 1], n_seq) for r in range(1, rows)]
     gy = []
     for r in range(rows):
@@ -859,12 +861,17 @@
         part = dot(d_gate[at], w_g, 1, 0) + dot(d_upper[at], w_u, 1, 0)
         part = part.astype(BF).reshape(n_seq, span, width)
         df_rows.append(fold_seq([part[j] for j in range(n_seq)], n_seq))
-    df_rows = [(v, cross_seq(w, n_seq)) for v, w in df_rows]
+    first_sent, hidden_again = tie((df_rows[0][1], hidden))
+    crossed = [cross_seq(first_sent, n_seq)]
+    for r in range(1, rows):
+        crossed[-1], sent = tie((crossed[-1], df_rows[r][1]))
+        crossed.append(cross_seq(sent, n_seq))
+    df_rows = [(v, w) for (v, _), w in zip(df_rows, crossed)]
     ffn_grads = jnp.concatenate(
         [dot(d_gate, f_in, 0, 0), dot(d_upper, f_in, 0, 0), dot(hidden, gy, 0, 0)], axis=1
     ).astype(BF)
     ffn_sums = lax.psum_scatter(ffn_grads, "rows", scatter_dimension=0, tiled=True)
-    y_slots = dot(hidden, w_dn, 1, 0).astype(BF)
+    y_slots = dot(hidden_again, w_dn, 1, 0).astype(BF)
     y_slots = y_slots.reshape(rows, n_seq, span, width)
     y_kept, y_sent = fold_seq([y_slots[:, j] for j in range(n_seq)], n_seq)
     h_own = h_all.reshape(rows, n_seq, span, width)[:, 0]
@@ -891,17 +898,17 @@
     do_rows, y_sent = tie((do_rows, y_sent))
     do_rows = [jnp.concatenate(slots, axis=1) for slots in do_rows]
     y_got = cross_seq(y_sent, n_seq)
-    o_own = jnp.concatenate(
-        [o_all[:, r * length : r * length + span] for r in range(rows)], axis=1
-    )
-    d_out = dot(jnp.concatenate(grad_att, axis=0), o_own, 0, 1).astype(BF)
-
     d_acts, d_heads = [], 0.0
     for r in range(rows):
         _, args, o, inv = kept[r]
         d_act, head_sums = attention_backward(*args, o, inv, do_rows[r])
         d_heads = d_heads + jnp.sum(head_sums, axis=-1)
         d_acts.append(d_act)
+    d_acts[-1], grad_all = tie((d_acts[-1], jnp.concatenate(grad_att, axis=0)))
+    o_own = jnp.concatenate(
+        [o_all[:, r * length : r * length + span] for r in range(rows)], axis=1
+    )
+    d_out = dot(grad_all, o_own, 0, 1).astype(BF)
     d_acts[-1], y_got = tie((d_acts[-1], y_got))
     output = (h_own + (y_kept + y_got.astype(F32))).astype(BF)
     d_acts[-1], ffn_sums, output = tie((d_acts[-1], ffn_sums, output))

time: 588 us -> 581 us (0.988)
  waiting for transfers between devices: 36.9 us -> 25 us
    ppermute x21, waiting for transfers between devices: 36.9 us -> 25 us  [swap(): return lax.ppermute(v, axis, [(i, i ^ bit) for i in range(n)])]
    unnamed x11 -> x10, other arithmetic: 18 us -> 17.9 us
  transfers between devices with their start and end apart: 23 -> 23, of which waited for: 6 -> 4; matrix products, arithmetic and copies ran while one was open for 32% -> 32% of each run, Pallas kernels for 30% -> 31%
where the time goes in v7:
time: 581 us; the launch traced here: 577 us
  Pallas kernels  257 us (44%)
  matrix products  128 us (22%)
  other arithmetic  104 us (18%)
  local copies, waits for them, and re-layouts  30.6 us (5%)
  waiting for transfers between devices  25 us (4%)
  starting transfers between devices  16.4 us (3%)
  between operations  15.4 us (3%)
    dot_general x17, matrix products, dot(): lax.dot_general(a, b, (((ca,), (cb,)), ((), ())), preferred_element_type=...  128 us
    pallas_call x1, Pallas kernels, close_layer(): pl.pallas_call(functools.partial(closing, n_seq, n_rows), out_shape=(jax....  81.3 us
    pallas_call x1, Pallas kernels, open_layer(): pl.pallas_call(functools.partial(opening, n_seq, n_rows), out_shape=(jax....  74.1 us
    pallas_call x1, Pallas kernels, meet(): pl.pallas_call(functools.partial(meeting, n_seq, n_rows), out_shape=(jax....  55.5 us
    pallas_call x2, Pallas kernels, attention_backward(): pl.pallas_call(functools.partial(backward_heads, plan), out_shape=(jax.Sh...  31.7 us
    ppermute x21, waiting for transfers between devices, swap(): return lax.ppermute(v, axis, [(i, i ^ bit) for i in range(n)])  25 us
    unnamed x10, other arithmetic  17.9 us
    ppermute x21, starting transfers between devices, swap(): return lax.ppermute(v, axis, [(i, i ^ bit) for i in range(n)])  16.4 us
  transfers between devices with their start and end apart: 23, of which 4 were waited for; matrix products, arithmetic and copies ran while one was open for 32% of the time, Pallas kernels for 31%

profile of v7, /device:TPU:0, one launch (start us, length us, event | category | flops | bytes accessed | tf_op | source)
XLA Modules:
  0.0 576.8 jit_solution(2497585906314421908)
XLA Ops:
  7.3 2.3 pad_maximum_fusion.3
  11.5 74.1 %opening.1 = (bf16[2,1024,2048]{2,1,0:T(8,128)(2,1)}, bf16[2048,640]{1,0:T(8,128)(2,1)}) custom-call(bf16[2,256,2048]{2,1,0:T(8,128)(2,1)} %tokens.1, bf16[4,64,640]{2,1,0:T(8,128)(2,1)} %pad_maximum_fusion.6.pieces), custom_call_target="tpu_custom_call" | custom-call | tf_op jit(solution)/shard_map/opening/pallas_call | solution.py:171
  85.7 1.6 slice_bitcast_fusion.28
  87.3 4.6 collective-permute-start.1
  93.7 1.4 slice_reduce_fusion.2
  98.4 4.9 fusion.3
  104.4 2.2 fusion.5
  106.6 3.0 fusion.42.x_ref
  109.7 7.1 %attention_forward.3 = (bf16[320,1024]{1,0:T(8,128)(2,1)S(1)}, f32[5,1,1024]{2,1,0:T(1,128)S(1)}) custom-call(s32[1]{0:T(128)} %bitcast.me_ref, bf16[576,1024]{1,0:T(8,128)(2,1)S(1)} %fusion.42.x_ref, f32[32,1024]{1,0:T(8,128)S(1)} %get-tuple-element.162.cos_ref, f32[32,1024]{1,0:T(8,128)S(1)} %get-tuple-element.160.sin_ref, ...), custom_call_target="tpu_custom_call" | custom-call | flops 1342177280 | bytes 4194304 | tf_op jit(solution)/shard_map/attention_forward/pallas_call | solution.py:702
  116.8 3.1 fusion.39.x_ref
  120.0 7.6 %attention_forward.2 = (bf16[320,1024]{1,0:T(8,128)(2,1)S(1)}, f32[5,1,1024]{2,1,0:T(1,128)S(1)}) custom-call(s32[1]{0:T(128)} %bitcast.me_ref, bf16[576,1024]{1,0:T(8,128)(2,1)S(1)} %fusion.39.x_ref, f32[32,1024]{1,0:T(8,128)S(1)} %get-tuple-element.163.cos_ref, f32[32,1024]{1,0:T(8,128)S(1)} %get-tuple-element.161.sin_ref, ...), custom_call_target="tpu_custom_call" | custom-call | flops 1342177280 | bytes 4194304 | tf_op jit(solution)/shard_map/attention_forward/pallas_call | solution.py:702
  129.4 1.9 fusion.52
  132.8 3.0 fusion.53
  135.8 3.1 fusion.54
  138.9 55.5 %meeting.1 = (bf16[4,320,2048]{2,1,0:T(8,128)(2,1)}, bf16[8,4,64,1280]{3,2,1,0:T(8,128)(2,1)}) custom-call(bf16[320,1024]{1,0:T(8,128)(2,1)} %copy-done.4, bf16[320,1024]{1,0:T(8,128)(2,1)} %copy-done.6, bf16[64,1280]{1,0:T(8,128)(2,1)} %refs_2_.1), custom_call_target="tpu_custom_call" | custom-call | tf_op jit(solution)/shard_map/meeting/pallas_call | solution.py:279
  194.4 3.1 fusion.55
  197.5 1.8 fusion.56
  199.4 3.1 fusion.57
  202.4 1.6 collective-permute-start.4
  204.1 20.2 %multiply_reduce_fusion = (f32[2048]{0:T(1024)S(1)}, f32[2048,2048]{1,0:T(8,128)}) fusion(bf16[1280,2048]{1,0:T(8,128)(2,1)} %bitcast.216, bf16[2048,1280]{1,0:T(8,128)(2,1)} %bitcast.222, bf16[2,1024,2048]{2,1,0:T(8,128)(2,1)} %get-tuple-element.67), kind=kOutput, calls=%fused_computation.5 | convolution fusion | flops 10754193408 | bytes 35659776 | tf_op jit(solution)/shard_map/dot_general | solution.py:28
  224.3 7.1 %multiply_convert_fusion = bf16[2048,2048]{1,0:T(8,128)(2,1)S(1)} fusion(f32[2048,2048]{1,0:T(8,128)} %get-tuple-element.185, f32[2048]{0:T(1024)S(1)} %get-tuple-element.116, f32[2048]{0:T(1024)S(1)} %add_rsqrt_fusion), kind=kLoop, calls=%fused_computation.4 | loop fusion | flops 12582912 | bytes 25182208 | tf_op jit(solution)/shard_map/convert_element_type | solution.py:847
  232.6 8.1 %fusion.29 = f32[2048,704]{0,1:T(8,128)} fusion(bf16[2048,2048]{1,0:T(8,128)(2,1)S(1)} %multiply_convert_fusion, bf16[704,6144]{1,0:T(8,128)(2,1)S(1)} %copy-done.56), kind=kOutput, calls=%fused_computation.59 | convolution fusion | flops 5905580032 | bytes 17039360 | tf_op jit(solution)/shard_map/dot_general | solution.py:28
  240.9 8.0 %fusion.33 = f32[2048,704]{0,1:T(8,128)} fusion(bf16[2048,2048]{1,0:T(8,128)(2,1)S(1)} %multiply_convert_fusion, bf16[704,6144]{1,0:T(8,128)(2,1)S(1)} %copy-done.56), kind=kOutput, calls=%fused_computation.63 | convolution fusion | flops 5905580032 | bytes 17039360 | tf_op jit(solution)/shard_map/dot_general | solution.py:28
  248.9 1.8 multiply_reduce_fusion.6
  250.7 1.8 fusion.58
  252.5 1.8 fusion.59
  254.3 15.6 %multiply_convert_fusion.1 = (bf16[2048,704]{0,1:T(8,128)(2,1)}, bf16[2048,704]{0,1:T(8,128)(2,1)S(1)}, bf16[2048,704]{0,1:T(8,128)(2,1)}) fusion(f32[2048,704]{0,1:T(8,128)} %fusion.33, f32[2048,704]{0,1:T(8,128)} %fusion.29, bf16[2048,2048]{1,0:T(8,128)(2,1)} %fusion.59, bf16[704,6144]{1,0:T(8,128)(2,1)} %all-gather.2.cloned.1.call-done), kind=kOutput, calls=%fused_computation.21 | convolution fusion | flops 5927206912 | bytes 31457280 | tf_op jit(solution)/shard_map/dot_general | solution.py:28
  269.9 10.4 %convolution_convert_fusion.2 = bf16[704,2048]{1,0:T(8,128)(2,1)S(1)} fusion(bf16[2048,704]{0,1:T(8,128)(2,1)} %get-tuple-element.84, bf16[2048,2048]{1,0:T(8,128)(2,1)} %fusion.59), kind=kOutput, calls=%fused_computation.43 | convolution fusion | flops 5907021824 | bytes 14155776 | tf_op jit(solution)/shard_map/dot_general | solution.py:28
  280.4 6.8 %convolution_convert_fusion.4 = bf16[704,2048]{1,0:T(8,128)(2,1)S(1)} fusion(bf16[2048,704]{0,1:T(8,128)(2,1)S(1)} %get-tuple-element.123, bf16[2048,2048]{1,0:T(8,128)(2,1)S(1)} %multiply_convert_fusion), kind=kOutput, calls=%fused_computation.45 | convolution fusion | flops 5907021824 | bytes 14155776 | tf_op jit(solution)/shard_map/dot_general | solution.py:28
  287.2 6.4 %convolution_convert_fusion.3 = bf16[704,2048]{1,0:T(8,128)(2,1)S(1)} fusion(bf16[2048,704]{0,1:T(8,128)(2,1)S(1)} %copy-done.61, bf16[2048,2048]{1,0:T(8,128)(2,1)S(1)} %multiply_convert_fusion), kind=kOutput, calls=%fused_computation.44 | convolution fusion | flops 5907021824 | bytes 14155776 | tf_op jit(solution)/shard_map/dot_general | solution.py:28
  293.7 3.8 pad_maximum_fusion
  297.5 2.4 fusion.74
  299.9 5.4 fusion.27
  305.4 5.5 add_convert_fusion.1
  312.8 7.6 %fusion.25 = f32[1024,2048]{1,0:T(8,128)} fusion(bf16[704,6144]{1,0:T(8,128)(2,1)} %all-gather.2.cloned.1.call-done, bf16[2048,704]{0,1:T(8,128)(2,1)S(1)} %copy-done.60), kind=kOutput, calls=%fused_computation.55 | convolution fusion | flops 2952790016 | bytes 12713984 | tf_op jit(solution)/shard_map/dot_general | solution.py:28
  320.4 7.1 %add_convert_fusion = bf16[1024,2048]{1,0:T(8,128)(2,1)S(1)} fusion(f32[1024,2048]{1,0:T(8,128)} %fusion.25, bf16[704,6144]{1,0:T(8,128)(2,1)} %all-gather.2.cloned.1.call-done, bf16[2048,704]{0,1:T(8,128)(2,1)S(1)} %copy-done.62), kind=kOutput, calls=%fused_computation.17 | convolution fusion | flops 2956984320 | bytes 16908288 | tf_op jit(solution)/shard_map/dot_general | solution.py:28
  331.2 8.8 %convolution_convert_fusion.1 = bf16[2048,2048]{1,0:T(8,128)(2,1)S(1)} fusion(bf16[2048,704]{0,1:T(8,128)(2,1)S(1)} %copy-done.63, bf16[704,6144]{1,0:T(8,128)(2,1)} %all-gather.2.cloned.1.call-done), kind=kOutput, calls=%fused_computation.20 | convolution fusion | flops 5909774336 | bytes 14155776 | tf_op jit(solution)/shard_map/dot_general | solution.py:28
  340.5 2.7 slice_bitcast_fusion.1
  343.2 1.6 copy-done.33
  344.9 1.4 add_convert_fusion.2
  346.3 19.2 %collective-permute-done.8 = bf16[256,2048]{1,0:T(8,128)(2,1)S(1)} collective-permute-done((bf16[256,2048]{1,0:T(8,128)(2,1)S(1)}, bf16[256,2048]{1,0:T(8,128)(2,1)S(1)}, u32[]{:S(2)}, u32[]{:S(2)}) %collective-permute-start.8) | collective-permute-done | bytes 1048608 | tf_op jit(solution)/shard_map/ppermute | solution.py:32
  365.9 3.5 multiply_reduce_fusion.2
  369.4 4.9 fusion.73
  374.3 2.4 convolution_convert_fusion.6
  376.7 2.7 gather_fusion.1
  383.3 4.6 fusion.17
  387.9 4.0 collective-permute-done.10
  391.9 2.8 multiply_reduce_fusion.1
  394.7 4.8 fusion.72
  399.6 2.4 convolution_convert_fusion.5
  402.0 1.9 gather_fusion.2
  406.1 4.5 pad_maximum_fusion.1
  412.2 2.5 collective-permute-start.19
  414.7 1.6 pad_maximum_fusion.2
  416.5 16.0 %attention_backward.2 = (bf16[576,1024]{1,0:T(8,128)(2,1)S(1)}, f32[2,64,128]{2,1,0:T(8,128)S(1)}) custom-call(s32[1]{0:T(128)} %bitcast.me_ref, bf16[576,1024]{1,0:T(8,128)(2,1)S(1)} %copy-done.25, f32[32,1024]{1,0:T(8,128)S(1)} %copy-done.15, f32[32,1024]{1,0:T(8,128)S(1)} %copy-done.13, s32[1,1024]{1,0:T(1,128)S(1)} %copy-done.21, f32[64,2]{1,0:T(8,128)S(1)} %bitcast.192, ...), custom_call_target="tpu_custom_call" | custom-call | flops 3355443200 | bytes 6291456 | tf_op jit(solution)/shard_map/attention_backward/pallas_call | solution.py:732
  434.9 15.6 %attention_backward.3 = (bf16[576,1024]{1,0:T(8,128)(2,1)S(1)}, f32[2,64,128]{2,1,0:T(8,128)S(1)}) custom-call(s32[1]{0:T(128)} %bitcast.me_ref, bf16[576,1024]{1,0:T(8,128)(2,1)S(1)} %copy-done.23, f32[32,1024]{1,0:T(8,128)S(1)} %copy-done.11, f32[32,1024]{1,0:T(8,128)S(1)} %copy-done.9, s32[1,1024]{1,0:T(1,128)S(1)} %copy-done.19, f32[64,2]{1,0:T(8,128)S(1)} %bitcast.193, ...), custom_call_target="tpu_custom_call" | custom-call | flops 3355443200 | bytes 6291456 | tf_op jit(solution)/shard_map/attention_backward/pallas_call | solution.py:732
  452.0 1.6 maximum_bitcast_fusion.refs_5_
  453.6 6.9 %convolution_convert_fusion = bf16[2048,1280]{1,0:T(8,128)(2,1)} fusion(bf16[512,2048]{1,0:T(8,128)(2,1)} %pad_maximum_fusion.2, bf16[1280,256]{1,0:T(8,128)(2,1)S(1)} %copy-done.46, bf16[1280,256]{1,0:T(8,128)(2,1)S(1)} %copy-done.45), kind=kOutput, calls=%fused_computation.19 | convolution fusion | flops 2689597440 | bytes 8650752 | tf_op jit(solution)/shard_map/dot_general | solution.py:28
  461.3 7.0 %fusion.15 = bf16[2,256,2048]{2,1,0:T(8,128)(2,1)} fusion(f32[2,4,256,2048]{3,2,1,0:T(8,128)} %bitcast.199, bf16[2,256,2048]{2,1,0:T(8,128)(2,1)} %collective-permute-done.19, bf16[2,256,2048]{2,1,0:T(8,128)(2,1)} %collective-permute-done.20, bf16[2,4,256,2048]{3,2,1,0:T(8,128)(2,1)} %bitcast.203), kind=kLoop, calls=%fused_computation.37 | loop fusion | flops 7340032 | bytes 12582912 | tf_op jit(solution)/shard_map/convert_element_type | solution.py:913
  468.3 1.9 slice_convert_fusion.1
  470.2 2.3 slice_convert_fusion
  473.1 81.3 %closing.1 = (f32[2,256,2048]{2,1,0:T(8,128)}, bf16[4,64,640]{2,1,0:T(8,128)(2,1)}, f32[64,1280]{1,0:T(8,128)}) custom-call(bf16[576,1024]{1,0:T(8,128)(2,1)} %copy-done.3, bf16[576,1024]{1,0:T(8,128)(2,1)} %copy-done.2, bf16[1024,2048]{1,0:T(8,128)(2,1)} %copy-done.31, bf16[1024,2048]{1,0:T(8,128)(2,1)} %copy-done.32, ...), custom_call_target="tpu_custom_call" | custom-call | tf_op jit(solution)/shard_map/closing/pallas_call | solution.py:524
  556.7 3.1 fusion.9
  561.8 6.7 %fusion.12 = f32[2,256,2048]{2,1,0:T(8,128)} fusion(f32[2,256,2048]{2,1,0:T(8,128)} %bitcast.200, bf16[2,256,2048]{2,1,0:T(8,128)(2,1)S(1)} %copy-done.28, f32[2,256,2048]{2,1,0:T(8,128)} %get-tuple-element.105, f32[2,256]{1,0:T(2,128)S(1)} %broadcast_multiply_fusion, f32[2048]{0:T(1024)S(1)} %copy-done.49, f32[2,256]{1,0:T(2,128)S(1)} %copy-done.50), kind=kLoop, calls=%fused_computation.33 | loop fusion | flops 7340032 | bytes 14692352 | tf_op jit(solution)/shard_map/add | solution.py:939
  (257 shorter events, 37.4 us)
Async XLA Ops:
  7.2 88.1 %copy-start = (s32[2,1024]{1,0:T(2,128)S(1)}, s32[2,1024]{1,0:T(2,128)}, u32[]{:S(2)}) copy-start(s32[2,1024]{1,0:T(2,128)} %param.17) | copy-start | bytes 24580
  7.2 195.2 %all-gather.2.cloned.1.call-start = ((), (), s32[]{:S(2)}) async-start(), calls=%async_computation.1 | async-start | bytes 9732096 | tf_op jit(solution)/shard_map/all_gather | solution.py:831
  9.6 76.0 %copy-start.29 = (bf16[2,256,2048]{2,1,0:T(8,128)(2,1)S(1)}, bf16[2,256,2048]{2,1,0:T(8,128)(2,1)}, u32[]{:S(2)}) copy-start(bf16[2,256,2048]{2,1,0:T(8,128)(2,1)} %param.16) | copy-start | bytes 6291460
  9.6 458.7 %reduce-scatter.2.cloned.1.call-start = ((), (), s32[]{:S(2)}) async-start(), calls=%async_computation.2 | async-start | bytes 9732096 | tf_op jit(solution)/shard_map/reduce_scatter | solution.py:873
  85.6 8.0 %copy-start.53 = (bf16[2,64]{1,0:T(2,128)(2,1)S(1)}, bf16[2,64]{1,0:T(2,128)(2,1)}, u32[]{:S(2)}) copy-start(bf16[2,64]{1,0:T(2,128)(2,1)} %param.23) | copy-start | bytes 772
  85.7 10.3 %copy-start.57 = (s32[4]{0:T(128)S(1)}, s32[4]{0:T(128)}, u32[]{:S(2)}) copy-start(s32[4]{0:T(128)} %param.19) | copy-start | bytes 52
  87.3 45.4 %collective-permute-start.1 = (bf16[256,2048]{1,0:T(8,128)(2,1)}, bf16[256,2048]{1,0:T(8,128)(2,1)}, u32[]{:S(2)}, u32[]{:S(2)}) collective-permute-start(bf16[256,2048]{1,0:T(8,128)(2,1)} %get-tuple-element.137), channel_id=1, source_target_pairs={{0,1},{1,0},{2,3},{3,2},{4,5},{5,4},{6,7},{7,6},{8,9},{9,8},{10,11... | collective-permute-start | bytes 3145736 | tf_op jit(solution)/shard_map/ppermute | solution.py:32
  91.9 39.3 %collective-permute-start = (bf16[256,2048]{1,0:T(8,128)(2,1)}, bf16[256,2048]{1,0:T(8,128)(2,1)}, u32[]{:S(2)}, u32[]{:S(2)}) collective-permute-start(bf16[256,2048]{1,0:T(8,128)(2,1)} %get-tuple-element.137), channel_id=1, source_target_pairs={{0,2},{1,3},{2,0},{3,1},{4,6},{5,7},{6,4},{7,5},{8,10},{9,11},{10,... | collective-permute-start | bytes 3145736 | tf_op jit(solution)/shard_map/ppermute | solution.py:32
  92.8 106.5 %collective-permute-start.3 = (bf16[256,2048]{1,0:T(8,128)(2,1)}, bf16[256,2048]{1,0:T(8,128)(2,1)}, u32[]{:S(2)}, u32[]{:S(2)}) collective-permute-start(bf16[256,2048]{1,0:T(8,128)(2,1)} %get-tuple-element.135), channel_id=1, source_target_pairs={{0,1},{1,0},{2,3},{3,2},{4,5},{5,4},{6,7},{7,6},{8,9},{9,8},{10,11... | collective-permute-start | bytes 3145736 | tf_op jit(solution)/shard_map/ppermute | solution.py:32
  93.7 26.2 %copy-start.16 = (f32[2,64]{0,1:T(8,128)}, f32[2,64]{0,1:T(8,128)S(1)}, u32[]{:S(2)}) copy-start(f32[2,64]{0,1:T(8,128)S(1)} %copy.33) | copy-start | bytes 1540
  98.3 6.1 %copy-start.48 = (f32[2048]{0:T(1024)}, f32[2048]{0:T(1024)S(1)}, u32[]{:S(2)}) copy-start(f32[2048]{0:T(1024)S(1)} %get-tuple-element.117) | copy-start | bytes 24580
  98.3 11.3 %copy-start.18 = (s32[1,1024]{1,0:T(1,128)}, s32[1,1024]{1,0:T(1,128)S(1)}, u32[]{:S(2)}) copy-start(s32[1,1024]{1,0:T(1,128)S(1)} %get-tuple-element.180.first_ref) | copy-start | bytes 12292
  98.3 21.6 %copy-start.20 = (s32[1,1024]{1,0:T(1,128)}, s32[1,1024]{1,0:T(1,128)S(1)}, u32[]{:S(2)}) copy-start(s32[1,1024]{1,0:T(1,128)S(1)} %get-tuple-element.181.first_ref) | copy-start | bytes 12292
  98.3 6.0 %copy-start.26 = (bf16[2,1024,2048]{2,1,0:T(8,128)(2,1)S(1)}, bf16[2,1024,2048]{2,1,0:T(8,128)(2,1)}, u32[]{:S(2)}) copy-start(bf16[2,1024,2048]{2,1,0:T(8,128)(2,1)} %get-tuple-element.67) | copy-start | bytes 25165828
  104.3 15.7 %copy-start.12 = (f32[32,1024]{1,0:T(8,128)}, f32[32,1024]{1,0:T(8,128)S(1)}, u32[]{:S(2)}) copy-start(f32[32,1024]{1,0:T(8,128)S(1)} %get-tuple-element.161.sin_ref) | copy-start | bytes 393220
  104.3 15.6 %copy-start.14 = (f32[32,1024]{1,0:T(8,128)}, f32[32,1024]{1,0:T(8,128)S(1)}, u32[]{:S(2)}) copy-start(f32[32,1024]{1,0:T(8,128)S(1)} %get-tuple-element.163.cos_ref) | copy-start | bytes 393220
  106.6 10.3 %copy-start.32 = (bf16[1024,2048]{1,0:T(8,128)(2,1)}, bf16[1024,2048]{1,0:T(8,128)(2,1)S(1)}, u32[]{:S(2)}) copy-start(bf16[1024,2048]{1,0:T(8,128)(2,1)S(1)} %get-tuple-element.126.refs_3_) | copy-start | bytes 12582916
  109.7 10.2 %copy-start.22 = (bf16[576,1024]{1,0:T(8,128)(2,1)}, bf16[576,1024]{1,0:T(8,128)(2,1)S(1)}, u32[]{:S(2)}) copy-start(bf16[576,1024]{1,0:T(8,128)(2,1)S(1)} %fusion.42.x_ref) | copy-start | bytes 3538948
  119.9 8.9 %copy-start.24 = (bf16[576,1024]{1,0:T(8,128)(2,1)}, bf16[576,1024]{1,0:T(8,128)(2,1)S(1)}, u32[]{:S(2)}) copy-start(bf16[576,1024]{1,0:T(8,128)(2,1)S(1)} %fusion.39.x_ref) | copy-start | bytes 3538948
  119.9 8.4 %copy-start.27 = (bf16[2,256,2048]{2,1,0:T(8,128)(2,1)S(1)}, bf16[2,256,2048]{2,1,0:T(8,128)(2,1)}, u32[]{:S(2)}) copy-start(bf16[2,256,2048]{2,1,0:T(8,128)(2,1)} %tokens.1) | copy-start | bytes 6291460
  127.6 8.2 %copy-start.6 = (bf16[320,1024]{1,0:T(8,128)(2,1)}, bf16[320,1024]{1,0:T(8,128)(2,1)S(1)}, u32[]{:S(2)}) copy-start(bf16[320,1024]{1,0:T(8,128)(2,1)S(1)} %get-tuple-element.72.refs_1_.o_ref) | copy-start | bytes 1966084
  131.3 63.1 %collective-permute-start.2 = (bf16[256,2048]{1,0:T(8,128)(2,1)}, bf16[256,2048]{1,0:T(8,128)(2,1)}, u32[]{:S(2)}, u32[]{:S(2)}) collective-permute-start(bf16[256,2048]{1,0:T(8,128)(2,1)} %collective-permute-done), channel_id=1, source_target_pairs={{0,1},{1,0},{2,3},{3,2},{4,5},{5,4},{6,7},{7,6},{8,9},{9,8},{10,11... | collective-permute-start | bytes 3145736 | tf_op jit(solution)/shard_map/ppermute | solution.py:32
  202.4 38.3 %collective-permute-start.4 = (bf16[256,2048]{1,0:T(8,128)(2,1)S(1)}, bf16[256,2048]{1,0:T(8,128)(2,1)S(1)}, u32[]{:S(2)}, u32[]{:S(2)}) collective-permute-start(bf16[256,2048]{1,0:T(8,128)(2,1)S(1)} %bitcast.205), channel_id=1, source_target_pairs={{0,2},{1,3},{2,0},{3,1},{4,6},{5,7},{6,4},{7,5},{8,10},{9,11},{10,... | collective-permute-start | bytes 3145736 | tf_op jit(solution)/shard_map/ppermute | solution.py:32
  224.3 8.3 %copy-start.56 = (bf16[704,6144]{1,0:T(8,128)(2,1)S(1)}, bf16[704,6144]{1,0:T(8,128)(2,1)}, u32[]{:S(2)}) copy-start(bf16[704,6144]{1,0:T(8,128)(2,1)} %all-gather.2.cloned.1.call-done) | copy-start | bytes 25952260
  240.7 11.8 %collective-permute-start.5 = (bf16[256,2048]{1,0:T(8,128)(2,1)S(1)}, bf16[256,2048]{1,0:T(8,128)(2,1)S(1)}, u32[]{:S(2)}, u32[]{:S(2)}) collective-permute-start(bf16[256,2048]{1,0:T(8,128)(2,1)S(1)} %collective-permute-done.4), channel_id=1, source_target_pairs={{0,1},{1,0},{2,3},{3,2},{4,5},{5,4},{6,7},{7,6},{8,9},{9,8},{10,11... | collective-permute-start | bytes 3145736 | tf_op jit(solution)/shard_map/ppermute | solution.py:32
  269.9 30.0 %copy-start.59 = (bf16[2048,704]{0,1:T(8,128)(2,1)}, bf16[2048,704]{0,1:T(8,128)(2,1)S(1)}, u32[]{:S(2)}) copy-start(bf16[2048,704]{0,1:T(8,128)(2,1)S(1)} %get-tuple-element.123) | copy-start | bytes 8650756
  280.3 6.9 %copy-start.61 = (bf16[2048,704]{0,1:T(8,128)(2,1)S(1)}, bf16[2048,704]{0,1:T(8,128)(2,1)}, u32[]{:S(2)}) copy-start(bf16[2048,704]{0,1:T(8,128)(2,1)} %get-tuple-element.124) | copy-start | bytes 8650756
  311.2 18.4 %collective-permute-start.7 = (bf16[256,2048]{1,0:T(8,128)(2,1)S(1)}, bf16[256,2048]{1,0:T(8,128)(2,1)S(1)}, u32[]{:S(2)}, u32[]{:S(2)}) collective-permute-start(bf16[256,2048]{1,0:T(8,128)(2,1)S(1)} %get-tuple-element.134), channel_id=1, source_target_pairs={{0,1},{1,0},{2,3},{3,2},{4,5},{5,4},{6,7},{7,6},{8,9},{9,8},{10,11... | collective-permute-start | bytes 3145736 | tf_op jit(solution)/shard_map/ppermute | solution.py:32
  327.5 17.4 %copy-start.35 = (bf16[1024,2048]{1,0:T(8,128)(2,1)}, bf16[1024,2048]{1,0:T(8,128)(2,1)S(1)}, u32[]{:S(2)}) copy-start(bf16[1024,2048]{1,0:T(8,128)(2,1)S(1)} %add_convert_fusion) | copy-start | bytes 12582916
  328.7 63.1 %collective-permute-start.14 = (bf16[256,2048]{1,0:T(8,128)(2,1)}, bf16[256,2048]{1,0:T(8,128)(2,1)S(1)}, u32[]{:S(2)}, u32[]{:S(2)}) collective-permute-start(bf16[256,2048]{1,0:T(8,128)(2,1)} %get-tuple-element.131), channel_id=1, source_target_pairs={{0,1},{1,0},{2,3},{3,2},{4,5},{5,4},{6,7},{7,6},{8,9},{9,8},{10,11... | collective-permute-start | bytes 3145736 | tf_op jit(solution)/shard_map/ppermute | solution.py:32
  329.1 15.8 %collective-permute-start.9 = (bf16[256,2048]{1,0:T(8,128)(2,1)S(1)}, bf16[256,2048]{1,0:T(8,128)(2,1)S(1)}, u32[]{:S(2)}, u32[]{:S(2)}) collective-permute-start(bf16[256,2048]{1,0:T(8,128)(2,1)S(1)} %get-tuple-element.132), channel_id=1, source_target_pairs={{0,1},{1,0},{2,3},{3,2},{4,5},{5,4},{6,7},{7,6},{8,9},{9,8},{10,11... | collective-permute-start | bytes 3145736 | tf_op jit(solution)/shard_map/ppermute | solution.py:32
  329.3 36.6 %collective-permute-start.6 = (bf16[256,2048]{1,0:T(8,128)(2,1)S(1)}, bf16[256,2048]{1,0:T(8,128)(2,1)S(1)}, u32[]{:S(2)}, u32[]{:S(2)}) collective-permute-start(bf16[256,2048]{1,0:T(8,128)(2,1)S(1)} %get-tuple-element.133), channel_id=1, source_target_pairs={{0,1},{1,0},{2,3},{3,2},{4,5},{5,4},{6,7},{7,6},{8,9},{9,8},{10,11... | collective-permute-start | bytes 3145736 | tf_op jit(solution)/shard_map/ppermute | solution.py:32
  340.0 25.4 %collective-permute-start.8 = (bf16[256,2048]{1,0:T(8,128)(2,1)S(1)}, bf16[256,2048]{1,0:T(8,128)(2,1)S(1)}, u32[]{:S(2)}, u32[]{:S(2)}) collective-permute-start(bf16[256,2048]{1,0:T(8,128)(2,1)S(1)} %add_convert_fusion.3), channel_id=1, source_target_pairs={{0,2},{1,3},{2,0},{3,1},{4,6},{5,7},{6,4},{7,5},{8,10},{9,11},{10,... | collective-permute-start | bytes 3145736 | tf_op jit(solution)/shard_map/ppermute | solution.py:32
  344.7 38.3 %collective-permute-start.18 = (bf16[2,256,2048]{2,1,0:T(8,128)(2,1)}, bf16[2,256,2048]{2,1,0:T(8,128)(2,1)}, u32[]{:S(2)}, u32[]{:S(2)}) collective-permute-start(bf16[2,256,2048]{2,1,0:T(8,128)(2,1)} %get-tuple-element.128), channel_id=1, source_target_pairs={{0,1},{1,0},{2,3},{3,2},{4,5},{5,4},{6,7},{7,6},{8,9},{9,8},{10,11... | collective-permute-start | bytes 6291464 | tf_op jit(solution)/shard_map/ppermute | solution.py:32
  346.3 23.1 %copy-start.30 = (bf16[2,256,2048]{2,1,0:T(8,128)(2,1)S(1)}, bf16[2,256,2048]{2,1,0:T(8,128)(2,1)}, u32[]{:S(2)}) copy-start(bf16[2,256,2048]{2,1,0:T(8,128)(2,1)} %param.16) | copy-start | bytes 6291460
  365.5 26.4 %collective-permute-start.10 = (bf16[256,2048]{1,0:T(8,128)(2,1)}, bf16[256,2048]{1,0:T(8,128)(2,1)}, u32[]{:S(2)}, u32[]{:S(2)}) collective-permute-start(bf16[256,2048]{1,0:T(8,128)(2,1)} %add_convert_fusion.2), channel_id=1, source_target_pairs={{0,2},{1,3},{2,0},{3,1},{4,6},{5,7},{6,4},{7,5},{8,10},{9,11},{10,... | collective-permute-start | bytes 3145736 | tf_op jit(solution)/shard_map/ppermute | solution.py:32
  365.9 8.4 %slice-start = ((s8[5242880]{0:T(1024)(128)(4,1)}), s8[4194304]{0:T(1024)(128)(4,1)S(1)}, s32[]{:S(2)}) async-start(s8[5242880]{0:T(1024)(128)(4,1)} %bitcast.223), calls=%async_computation.3 | async-start | bytes 8388608
  381.4 23.4 %collective-permute-start.13 = (bf16[320,256]{1,0:T(8,128)(2,1)}, bf16[320,256]{1,0:T(8,128)(2,1)S(1)}, u32[]{:S(2)}, u32[]{:S(2)}) collective-permute-start(bf16[320,256]{1,0:T(8,128)(2,1)} %get-tuple-element.156), channel_id=1, source_target_pairs={{0,3},{1,2},{2,1},{3,0},{4,7},{5,6},{6,5},{7,4},{8,11},{9,10},{10,... | collective-permute-start | bytes 491528 | tf_op jit(solution)/shard_map/ppermute | solution.py:32
  381.8 29.4 %collective-permute-start.12 = (bf16[320,256]{1,0:T(8,128)(2,1)}, bf16[320,256]{1,0:T(8,128)(2,1)}, u32[]{:S(2)}, u32[]{:S(2)}) collective-permute-start(bf16[320,256]{1,0:T(8,128)(2,1)} %get-tuple-element.157), channel_id=1, source_target_pairs={{0,2},{1,3},{2,0},{3,1},{4,6},{5,7},{6,4},{7,5},{8,10},{9,11},{10,... | collective-permute-start | bytes 491528 | tf_op jit(solution)/shard_map/ppermute | solution.py:32
  383.1 8.8 %copy-start.36 = (bf16[1024,2048]{1,0:T(8,128)(2,1)S(1)}, bf16[1024,2048]{1,0:T(8,128)(2,1)}, u32[]{:S(2)}) copy-start(bf16[1024,2048]{1,0:T(8,128)(2,1)} %copy-done.35) | copy-start | bytes 12582916
  383.1 28.2 %collective-permute-start.11 = (bf16[320,256]{1,0:T(8,128)(2,1)}, bf16[320,256]{1,0:T(8,128)(2,1)}, u32[]{:S(2)}, u32[]{:S(2)}) collective-permute-start(bf16[320,256]{1,0:T(8,128)(2,1)} %get-tuple-element.158), channel_id=1, source_target_pairs={{0,1},{1,0},{2,3},{3,2},{4,5},{5,4},{6,7},{7,6},{8,9},{9,8},{10,11... | collective-permute-start | bytes 491528 | tf_op jit(solution)/shard_map/ppermute | solution.py:32
  383.3 16.2 %slice-start.2 = ((s8[5242880]{0:T(1024)(128)(4,1)}), s8[4194304]{0:T(1024)(128)(4,1)S(1)}, s32[]{:S(2)}) async-start(s8[5242880]{0:T(1024)(128)(4,1)} %bitcast.226), calls=%async_computation.5 | async-start | bytes 8388608
  391.9 7.7 %slice-start.3 = ((s8[5242880]{0:T(1024)(128)(4,1)}), s8[1048576]{0:T(1024)(128)(4,1)S(1)}, s32[]{:S(2)}) async-start(s8[5242880]{0:T(1024)(128)(4,1)} %bitcast.226), calls=%async_computation.6 | async-start | bytes 2097152
  404.2 7.1 %collective-permute-start.17 = (bf16[320,256]{1,0:T(8,128)(2,1)S(1)}, bf16[320,256]{1,0:T(8,128)(2,1)S(1)}, u32[]{:S(2)}, u32[]{:S(2)}) collective-permute-start(bf16[320,256]{1,0:T(8,128)(2,1)S(1)} %get-tuple-element.152), channel_id=1, source_target_pairs={{0,3},{1,2},{2,1},{3,0},{4,7},{5,6},{6,5},{7,4},{8,11},{9,10},{10,... | collective-permute-start | bytes 491528 | tf_op jit(solution)/shard_map/ppermute | solution.py:32
  404.2 8.0 %collective-permute-start.16 = (bf16[320,256]{1,0:T(8,128)(2,1)S(1)}, bf16[320,256]{1,0:T(8,128)(2,1)S(1)}, u32[]{:S(2)}, u32[]{:S(2)}) collective-permute-start(bf16[320,256]{1,0:T(8,128)(2,1)S(1)} %get-tuple-element.153), channel_id=1, source_target_pairs={{0,2},{1,3},{2,0},{3,1},{4,6},{5,7},{6,4},{7,5},{8,10},{9,11},{10,... | collective-permute-start | bytes 491528 | tf_op jit(solution)/shard_map/ppermute | solution.py:32
  404.7 7.5 %collective-permute-start.15 = (bf16[320,256]{1,0:T(8,128)(2,1)S(1)}, bf16[320,256]{1,0:T(8,128)(2,1)S(1)}, u32[]{:S(2)}, u32[]{:S(2)}) collective-permute-start(bf16[320,256]{1,0:T(8,128)(2,1)S(1)} %get-tuple-element.154), channel_id=1, source_target_pairs={{0,1},{1,0},{2,3},{3,2},{4,5},{5,4},{6,7},{7,6},{8,9},{9,8},{10,11... | collective-permute-start | bytes 491528 | tf_op jit(solution)/shard_map/ppermute | solution.py:32
  406.1 8.6 %copy-start.39 = (bf16[256,2048]{1,0:T(8,128)(2,1)S(1)}, bf16[256,2048]{1,0:T(8,128)(2,1)}, u32[]{:S(2)}) copy-start(bf16[256,2048]{1,0:T(8,128)(2,1)} %copy-done.38) | copy-start | bytes 3145732
  406.1 8.6 %copy-start.41 = (bf16[256,2048]{1,0:T(8,128)(2,1)S(1)}, bf16[256,2048]{1,0:T(8,128)(2,1)}, u32[]{:S(2)}) copy-start(bf16[256,2048]{1,0:T(8,128)(2,1)} %copy-done.40) | copy-start | bytes 3145732
  410.6 5.8 %copy-start.15 = (f32[32,1024]{1,0:T(8,128)S(1)}, f32[32,1024]{1,0:T(8,128)}, u32[]{:S(2)}) copy-start(f32[32,1024]{1,0:T(8,128)} %copy-done.14) | copy-start | bytes 393220
  410.6 5.8 %copy-start.17 = (f32[2,64]{0,1:T(8,128)S(1)}, f32[2,64]{0,1:T(8,128)}, u32[]{:S(2)}) copy-start(f32[2,64]{0,1:T(8,128)} %copy-done.16) | copy-start | bytes 1540
  410.6 5.8 %copy-start.21 = (s32[1,1024]{1,0:T(1,128)S(1)}, s32[1,1024]{1,0:T(1,128)}, u32[]{:S(2)}) copy-start(s32[1,1024]{1,0:T(1,128)} %copy-done.20) | copy-start | bytes 12292
  410.6 5.8 %copy-start.25 = (bf16[576,1024]{1,0:T(8,128)(2,1)S(1)}, bf16[576,1024]{1,0:T(8,128)(2,1)}, u32[]{:S(2)}) copy-start(bf16[576,1024]{1,0:T(8,128)(2,1)} %copy-done.24) | copy-start | bytes 3538948
  411.2 50.1 %collective-permute-start.20 = (bf16[2,256,2048]{2,1,0:T(8,128)(2,1)}, bf16[2,256,2048]{2,1,0:T(8,128)(2,1)}, u32[]{:S(2)}, u32[]{:S(2)}) collective-permute-start(bf16[2,256,2048]{2,1,0:T(8,128)(2,1)} %get-tuple-element.127), channel_id=1, source_target_pairs={{0,1},{1,0},{2,3},{3,2},{4,5},{5,4},{6,7},{7,6},{8,9},{9,8},{10,11... | collective-permute-start | bytes 6291464 | tf_op jit(solution)/shard_map/ppermute | solution.py:32
  412.2 49.1 %collective-permute-start.19 = (bf16[2,256,2048]{2,1,0:T(8,128)(2,1)}, bf16[2,256,2048]{2,1,0:T(8,128)(2,1)}, u32[]{:S(2)}, u32[]{:S(2)}) collective-permute-start(bf16[2,256,2048]{2,1,0:T(8,128)(2,1)} %fusion.17), channel_id=1, source_target_pairs={{0,2},{1,3},{2,0},{3,1},{4,6},{5,7},{6,4},{7,5},{8,10},{9,11},{10,... | collective-permute-start | bytes 6291464 | tf_op jit(solution)/shard_map/ppermute | solution.py:32
  416.4 18.4 %copy-start.5 = (bf16[320,1024]{1,0:T(8,128)(2,1)S(1)}, bf16[320,1024]{1,0:T(8,128)(2,1)}, u32[]{:S(2)}) copy-start(bf16[320,1024]{1,0:T(8,128)(2,1)} %copy-done.4) | copy-start | bytes 1966084
  416.4 18.4 %copy-start.9 = (f32[32,1024]{1,0:T(8,128)S(1)}, f32[32,1024]{1,0:T(8,128)}, u32[]{:S(2)}) copy-start(f32[32,1024]{1,0:T(8,128)} %copy-done.8) | copy-start | bytes 393220
  416.4 18.4 %copy-start.11 = (f32[32,1024]{1,0:T(8,128)S(1)}, f32[32,1024]{1,0:T(8,128)}, u32[]{:S(2)}) copy-start(f32[32,1024]{1,0:T(8,128)} %copy-done.10) | copy-start | bytes 393220
  416.5 18.4 %copy-start.19 = (s32[1,1024]{1,0:T(1,128)S(1)}, s32[1,1024]{1,0:T(1,128)}, u32[]{:S(2)}) copy-start(s32[1,1024]{1,0:T(1,128)} %copy-done.18) | copy-start | bytes 12292
  416.5 18.4 %copy-start.23 = (bf16[576,1024]{1,0:T(8,128)(2,1)S(1)}, bf16[576,1024]{1,0:T(8,128)(2,1)}, u32[]{:S(2)}) copy-start(bf16[576,1024]{1,0:T(8,128)(2,1)} %copy-done.22) | copy-start | bytes 3538948
  434.8 18.7 %copy-start.45 = (bf16[1280,256]{1,0:T(8,128)(2,1)S(1)}, bf16[1280,256]{1,0:T(8,128)(2,1)}, u32[]{:S(2)}) copy-start(bf16[1280,256]{1,0:T(8,128)(2,1)} %get-tuple-element.129) | copy-start | bytes 1966084
  434.8 18.7 %copy-start.46 = (bf16[1280,256]{1,0:T(8,128)(2,1)S(1)}, bf16[1280,256]{1,0:T(8,128)(2,1)}, u32[]{:S(2)}) copy-start(bf16[1280,256]{1,0:T(8,128)(2,1)} %get-tuple-element.130) | copy-start | bytes 1966084
  561.6 6.9 %copy-start.42 = (f32[64,1920]{1,0:T(8,128)}, f32[64,1920]{1,0:T(8,128)S(1)}, u32[]{:S(2)}) copy-start(f32[64,1920]{1,0:T(8,128)S(1)} %concatenate.65) | copy-start | bytes 1474564
  561.7 7.3 %copy-start.47 = (f32[64,1280]{1,0:T(8,128)S(1)}, f32[64,1280]{1,0:T(8,128)}, u32[]{:S(2)}) copy-start(f32[64,1280]{1,0:T(8,128)} %get-tuple-element.201) | copy-start | bytes 983044
  561.7 8.0 %copy-start.1 = (s32[2,1024]{1,0:T(2,128)S(1)}, s32[2,1024]{1,0:T(2,128)}, u32[]{:S(2)}) copy-start(s32[2,1024]{1,0:T(2,128)} %param.17) | copy-start | bytes 24580
  (27 other events, 92.8 us)
Sparse Core Ops, SparseCore 0:
  10.8 156.6 all-gather.1
  297.6 152.1 reduce-scatter.1

commit v8 on v7

--- a/solution.py
+++ b/solution.py
@@ -861,8 +861,8 @@
         part = dot(d_gate[at], w_g, 1, 0) + dot(d_upper[at], w_u, 1, 0)
         part = part.astype(BF).reshape(n_seq, span, width)
         df_rows.append(fold_seq([part[j] for j in range(n_seq)], n_seq))
-    first_sent, hidden_again = tie((df_rows[0][1], hidden))
-    crossed = [cross_seq(first_sent, n_seq)]
+    crossed = [cross_seq(df_rows[0][1], n_seq)]
+    crossed[0], hidden_again = tie((crossed[0], hidden))
     for r in range(1, rows):
         crossed[-1], sent = tie((crossed[-1], df_rows[r][1]))
         crossed.append(cross_seq(sent, n_seq))

time: 581 us -> 575 us (0.990)
    unnamed x10 -> x11, other arithmetic: 17.9 us -> 18 us
  transfers between devices with their start and end apart: 23 -> 23, of which waited for: 4 -> 3; matrix products, arithmetic and copies ran while one was open for 32% -> 33% of each run, Pallas kernels for 31% -> 31%
where the time goes in v8:
time: 575 us; the launch traced here: 572 us
  Pallas kernels  257 us (45%)
  matrix products  129 us (22%)
  other arithmetic  104 us (18%)
  local copies, waits for them, and re-layouts  27.8 us (5%)
  waiting for transfers between devices  23.8 us (4%)
  between operations  15.4 us (3%)
  starting transfers between devices  14.7 us (3%)
    dot_general x17, matrix products, dot(): lax.dot_general(a, b, (((ca,), (cb,)), ((), ())), preferred_element_type=...  129 us
    pallas_call x1, Pallas kernels, close_layer(): pl.pallas_call(functools.partial(closing, n_seq, n_rows), out_shape=(jax....  80.8 us
    pallas_call x1, Pallas kernels, open_layer(): pl.pallas_call(functools.partial(opening, n_seq, n_rows), out_shape=(jax....  74.1 us
    pallas_call x1, Pallas kernels, meet(): pl.pallas_call(functools.partial(meeting, n_seq, n_rows), out_shape=(jax....  55.8 us
    pallas_call x2, Pallas kernels, attention_backward(): pl.pallas_call(functools.partial(backward_heads, plan), out_shape=(jax.Sh...  31.4 us
    ppermute x21, waiting for transfers between devices, swap(): return lax.ppermute(v, axis, [(i, i ^ bit) for i in range(n)])  23.8 us
    unnamed x11, other arithmetic  18 us
    ppermute x21, starting transfers between devices, swap(): return lax.ppermute(v, axis, [(i, i ^ bit) for i in range(n)])  14.6 us
  transfers between devices with their start and end apart: 23, of which 3 were waited for; matrix products, arithmetic and copies ran while one was open for 33% of the time, Pallas kernels for 31%

profile of v8, /device:TPU:0, one launch (start us, length us, event | category | flops | bytes accessed | tf_op | source)
XLA Modules:
  0.0 571.5 jit_solution(10262493710777917791)
XLA Ops:
  7.3 2.3 pad_maximum_fusion.3
  11.5 74.1 %opening.1 = (bf16[2,1024,2048]{2,1,0:T(8,128)(2,1)}, bf16[2048,640]{1,0:T(8,128)(2,1)}) custom-call(bf16[2,256,2048]{2,1,0:T(8,128)(2,1)} %tokens.1, bf16[4,64,640]{2,1,0:T(8,128)(2,1)} %pad_maximum_fusion.6.pieces), custom_call_target="tpu_custom_call" | custom-call | tf_op jit(solution)/shard_map/opening/pallas_call | solution.py:171
  85.7 1.6 slice_bitcast_fusion.28
  87.3 4.6 collective-permute-start.1
  93.7 1.4 slice_reduce_fusion.2
  96.1 1.2 convert_bitcast_fusion
  98.3 4.8 fusion.3
  104.2 2.2 fusion.5
  106.4 3.0 fusion.42.x_ref
  109.6 7.1 %attention_forward.3 = (bf16[320,1024]{1,0:T(8,128)(2,1)S(1)}, f32[5,1,1024]{2,1,0:T(1,128)S(1)}) custom-call(s32[1]{0:T(128)} %bitcast.me_ref, bf16[576,1024]{1,0:T(8,128)(2,1)S(1)} %fusion.42.x_ref, f32[32,1024]{1,0:T(8,128)S(1)} %get-tuple-element.162.cos_ref, f32[32,1024]{1,0:T(8,128)S(1)} %get-tuple-element.160.sin_ref, ...), custom_call_target="tpu_custom_call" | custom-call | flops 1342177280 | bytes 4194304 | tf_op jit(solution)/shard_map/attention_forward/pallas_call | solution.py:702
  116.7 3.1 fusion.39.x_ref
  119.8 7.4 %attention_forward.2 = (bf16[320,1024]{1,0:T(8,128)(2,1)S(1)}, f32[5,1,1024]{2,1,0:T(1,128)S(1)}) custom-call(s32[1]{0:T(128)} %bitcast.me_ref, bf16[576,1024]{1,0:T(8,128)(2,1)S(1)} %fusion.39.x_ref, f32[32,1024]{1,0:T(8,128)S(1)} %get-tuple-element.163.cos_ref, f32[32,1024]{1,0:T(8,128)S(1)} %get-tuple-element.161.sin_ref, ...), custom_call_target="tpu_custom_call" | custom-call | flops 1342177280 | bytes 4194304 | tf_op jit(solution)/shard_map/attention_forward/pallas_call | solution.py:702
  129.0 1.9 fusion.52
  132.4 3.1 fusion.53
  135.5 3.1 fusion.54
  138.6 55.8 %meeting.1 = (bf16[4,320,2048]{2,1,0:T(8,128)(2,1)}, bf16[8,4,64,1280]{3,2,1,0:T(8,128)(2,1)}) custom-call(bf16[320,1024]{1,0:T(8,128)(2,1)} %copy-done.4, bf16[320,1024]{1,0:T(8,128)(2,1)} %copy-done.6, bf16[64,1280]{1,0:T(8,128)(2,1)} %refs_2_.1), custom_call_target="tpu_custom_call" | custom-call | tf_op jit(solution)/shard_map/meeting/pallas_call | solution.py:279
  194.4 3.1 fusion.55
  197.5 1.8 fusion.56
  199.3 3.1 fusion.57
  202.4 1.6 collective-permute-start.4
  204.0 20.2 %multiply_reduce_fusion = (f32[2048]{0:T(1024)S(1)}, f32[2048,2048]{1,0:T(8,128)}) fusion(bf16[1280,2048]{1,0:T(8,128)(2,1)} %bitcast.216, bf16[2048,1280]{1,0:T(8,128)(2,1)} %bitcast.224, bf16[2,1024,2048]{2,1,0:T(8,128)(2,1)} %get-tuple-element.67), kind=kOutput, calls=%fused_computation.5 | convolution fusion | flops 10754193408 | bytes 35659776 | tf_op jit(solution)/shard_map/dot_general | solution.py:28
  224.2 7.1 %multiply_convert_fusion = bf16[2048,2048]{1,0:T(8,128)(2,1)S(1)} fusion(f32[2048,2048]{1,0:T(8,128)} %get-tuple-element.185, f32[2048]{0:T(1024)S(1)} %get-tuple-element.116, f32[2048]{0:T(1024)S(1)} %add_rsqrt_fusion), kind=kLoop, calls=%fused_computation.4 | loop fusion | flops 12582912 | bytes 25182208 | tf_op jit(solution)/shard_map/convert_element_type | solution.py:847
  232.5 8.4 %fusion.29 = f32[2048,704]{0,1:T(8,128)} fusion(bf16[2048,2048]{1,0:T(8,128)(2,1)S(1)} %multiply_convert_fusion, bf16[704,6144]{1,0:T(8,128)(2,1)S(1)} %copy-done.56), kind=kOutput, calls=%fused_computation.59 | convolution fusion | flops 5905580032 | bytes 17039360 | tf_op jit(solution)/shard_map/dot_general | solution.py:28
  241.2 8.0 %fusion.33 = f32[2048,704]{0,1:T(8,128)} fusion(bf16[2048,2048]{1,0:T(8,128)(2,1)S(1)} %multiply_convert_fusion, bf16[704,6144]{1,0:T(8,128)(2,1)S(1)} %copy-done.56), kind=kOutput, calls=%fused_computation.63 | convolution fusion | flops 5905580032 | bytes 17039360 | tf_op jit(solution)/shard_map/dot_general | solution.py:28
  249.1 1.8 multiply_reduce_fusion.6
  250.9 1.9 fusion.58
  252.8 1.8 fusion.59
  254.7 15.6 %multiply_convert_fusion.1 = (bf16[2048,704]{0,1:T(8,128)(2,1)}, bf16[2048,704]{0,1:T(8,128)(2,1)S(1)}, bf16[2048,704]{0,1:T(8,128)(2,1)}) fusion(f32[2048,704]{0,1:T(8,128)} %fusion.33, f32[2048,704]{0,1:T(8,128)} %fusion.29, bf16[2048,2048]{1,0:T(8,128)(2,1)} %fusion.59, bf16[704,6144]{1,0:T(8,128)(2,1)} %all-gather.2.cloned.1.call-done), kind=kOutput, calls=%fused_computation.21 | convolution fusion | flops 5927206912 | bytes 31457280 | tf_op jit(solution)/shard_map/dot_general | solution.py:28
  270.3 9.4 %convolution_convert_fusion.2 = bf16[704,2048]{1,0:T(8,128)(2,1)S(1)} fusion(bf16[2048,704]{0,1:T(8,128)(2,1)} %get-tuple-element.84, bf16[2048,2048]{1,0:T(8,128)(2,1)} %fusion.59), kind=kOutput, calls=%fused_computation.43 | convolution fusion | flops 5907021824 | bytes 14155776 | tf_op jit(solution)/shard_map/dot_general | solution.py:28
  279.7 6.6 %convolution_convert_fusion.4 = bf16[704,2048]{1,0:T(8,128)(2,1)S(1)} fusion(bf16[2048,704]{0,1:T(8,128)(2,1)S(1)} %get-tuple-element.123, bf16[2048,2048]{1,0:T(8,128)(2,1)S(1)} %multiply_convert_fusion), kind=kOutput, calls=%fused_computation.45 | convolution fusion | flops 5907021824 | bytes 14155776 | tf_op jit(solution)/shard_map/dot_general | solution.py:28
  286.4 6.4 %convolution_convert_fusion.3 = bf16[704,2048]{1,0:T(8,128)(2,1)S(1)} fusion(bf16[2048,704]{0,1:T(8,128)(2,1)S(1)} %copy-done.59, bf16[2048,2048]{1,0:T(8,128)(2,1)S(1)} %multiply_convert_fusion), kind=kOutput, calls=%fused_computation.44 | convolution fusion | flops 5907021824 | bytes 14155776 | tf_op jit(solution)/shard_map/dot_general | solution.py:28
  292.8 3.9 pad_maximum_fusion
  296.8 7.7 %fusion.27 = f32[1024,2048]{1,0:T(8,128)} fusion(bf16[704,6144]{1,0:T(8,128)(2,1)} %all-gather.2.cloned.1.call-done, bf16[2048,704]{0,1:T(8,128)(2,1)S(1)} %get-tuple-element.123), kind=kOutput, calls=%fused_computation.57 | convolution fusion | flops 2952790016 | bytes 12713984 | tf_op jit(solution)/shard_map/dot_general | solution.py:28
  304.4 6.9 %add_convert_fusion.1 = bf16[1024,2048]{1,0:T(8,128)(2,1)S(1)} fusion(f32[1024,2048]{1,0:T(8,128)} %fusion.27, bf16[704,6144]{1,0:T(8,128)(2,1)} %all-gather.2.cloned.1.call-done, bf16[2048,704]{0,1:T(8,128)(2,1)S(1)} %copy-done.60), kind=kOutput, calls=%fused_computation.18 | convolution fusion | flops 2956984320 | bytes 16908288 | tf_op jit(solution)/shard_map/dot_general | solution.py:28
  311.9 5.9 %fusion.25 = f32[1024,2048]{1,0:T(8,128)} fusion(bf16[704,6144]{1,0:T(8,128)(2,1)S(1)} %bitcast.223, bf16[2048,704]{0,1:T(8,128)(2,1)S(1)} %get-tuple-element.123), kind=kOutput, calls=%fused_computation.55 | convolution fusion | flops 2952790016 | bytes 12713984 | tf_op jit(solution)/shard_map/dot_general | solution.py:28
  317.8 6.2 %add_convert_fusion = bf16[1024,2048]{1,0:T(8,128)(2,1)S(1)} fusion(f32[1024,2048]{1,0:T(8,128)} %fusion.25, bf16[704,6144]{1,0:T(8,128)(2,1)S(1)} %bitcast.223, bf16[2048,704]{0,1:T(8,128)(2,1)S(1)} %copy-done.60), kind=kOutput, calls=%fused_computation.17 | convolution fusion | flops 2956984320 | bytes 16908288 | tf_op jit(solution)/shard_map/dot_general | solution.py:28
  324.0 1.3 fusion.75
  326.8 2.5 fusion.74
  329.3 1.3 add_convert_fusion.2
  330.6 21.0 %collective-permute-done.8 = bf16[256,2048]{1,0:T(8,128)(2,1)S(1)} collective-permute-done((bf16[256,2048]{1,0:T(8,128)(2,1)S(1)}, bf16[256,2048]{1,0:T(8,128)(2,1)S(1)}, u32[]{:S(2)}, u32[]{:S(2)}) %collective-permute-start.8) | collective-permute-done | bytes 1048608 | tf_op jit(solution)/shard_map/ppermute | solution.py:32
  352.0 3.5 multiply_reduce_fusion.2
  355.5 4.9 fusion.73
  360.4 2.4 convolution_convert_fusion.6
  362.9 2.7 gather_fusion.1
  366.7 9.7 %convolution_convert_fusion.1 = bf16[2048,2048]{1,0:T(8,128)(2,1)S(1)} fusion(bf16[2048,704]{0,1:T(8,128)(2,1)} %get-tuple-element.84, bf16[704,6144]{1,0:T(8,128)(2,1)} %all-gather.2.cloned.1.call-done), kind=kOutput, calls=%fused_computation.20 | convolution fusion | flops 5909774336 | bytes 14155776 | tf_op jit(solution)/shard_map/dot_general | solution.py:28
  379.1 2.3 slice_bitcast_fusion.1
  383.1 2.9 multiply_reduce_fusion.1
  386.1 5.0 fusion.72
  391.1 2.5 convolution_convert_fusion.5
  393.6 1.9 gather_fusion.2
  396.8 4.3 pad_maximum_fusion.1
  402.7 4.6 fusion.17
  409.2 1.6 pad_maximum_fusion.2
  410.9 15.6 %attention_backward.2 = (bf16[576,1024]{1,0:T(8,128)(2,1)S(1)}, f32[2,64,128]{2,1,0:T(8,128)S(1)}) custom-call(s32[1]{0:T(128)} %bitcast.me_ref, bf16[576,1024]{1,0:T(8,128)(2,1)S(1)} %copy-done.25, f32[32,1024]{1,0:T(8,128)S(1)} %copy-done.15, f32[32,1024]{1,0:T(8,128)S(1)} %copy-done.13, s32[1,1024]{1,0:T(1,128)S(1)} %copy-done.21, f32[64,2]{1,0:T(8,128)S(1)} %bitcast.192, ...), custom_call_target="tpu_custom_call" | custom-call | flops 3355443200 | bytes 6291456 | tf_op jit(solution)/shard_map/attention_backward/pallas_call | solution.py:732
  428.9 15.8 %attention_backward.3 = (bf16[576,1024]{1,0:T(8,128)(2,1)S(1)}, f32[2,64,128]{2,1,0:T(8,128)S(1)}) custom-call(s32[1]{0:T(128)} %bitcast.me_ref, bf16[576,1024]{1,0:T(8,128)(2,1)S(1)} %copy-done.23, f32[32,1024]{1,0:T(8,128)S(1)} %copy-done.11, f32[32,1024]{1,0:T(8,128)S(1)} %copy-done.9, s32[1,1024]{1,0:T(1,128)S(1)} %copy-done.19, f32[64,2]{1,0:T(8,128)S(1)} %bitcast.193, ...), custom_call_target="tpu_custom_call" | custom-call | flops 3355443200 | bytes 6291456 | tf_op jit(solution)/shard_map/attention_backward/pallas_call | solution.py:732
  446.1 1.6 maximum_bitcast_fusion.refs_5_
  447.7 6.8 %convolution_convert_fusion = bf16[2048,1280]{1,0:T(8,128)(2,1)} fusion(bf16[512,2048]{1,0:T(8,128)(2,1)} %pad_maximum_fusion.2, bf16[1280,256]{1,0:T(8,128)(2,1)S(1)} %copy-done.46, bf16[1280,256]{1,0:T(8,128)(2,1)S(1)} %copy-done.45), kind=kOutput, calls=%fused_computation.19 | convolution fusion | flops 2689597440 | bytes 8650752 | tf_op jit(solution)/shard_map/dot_general | solution.py:28
  454.6 1.9 collective-permute-done.19
  456.5 7.0 %fusion.15 = bf16[2,256,2048]{2,1,0:T(8,128)(2,1)} fusion(f32[2,4,256,2048]{3,2,1,0:T(8,128)} %bitcast.199, bf16[2,256,2048]{2,1,0:T(8,128)(2,1)} %collective-permute-done.19, bf16[2,256,2048]{2,1,0:T(8,128)(2,1)} %collective-permute-done.20, bf16[2,4,256,2048]{3,2,1,0:T(8,128)(2,1)} %bitcast.203), kind=kLoop, calls=%fused_computation.37 | loop fusion | flops 7340032 | bytes 12582912 | tf_op jit(solution)/shard_map/convert_element_type | solution.py:913
  463.5 1.9 slice_convert_fusion.1
  465.4 2.3 slice_convert_fusion
  468.3 80.8 %closing.1 = (f32[2,256,2048]{2,1,0:T(8,128)}, bf16[4,64,640]{2,1,0:T(8,128)(2,1)}, f32[64,1280]{1,0:T(8,128)}) custom-call(bf16[576,1024]{1,0:T(8,128)(2,1)} %copy-done.3, bf16[576,1024]{1,0:T(8,128)(2,1)} %copy-done.2, bf16[1024,2048]{1,0:T(8,128)(2,1)} %copy-done.31, bf16[1024,2048]{1,0:T(8,128)(2,1)} %copy-done.32, ...), custom_call_target="tpu_custom_call" | custom-call | tf_op jit(solution)/shard_map/closing/pallas_call | solution.py:524
  551.4 3.1 fusion.9
  556.5 6.7 %fusion.12 = f32[2,256,2048]{2,1,0:T(8,128)} fusion(f32[2,256,2048]{2,1,0:T(8,128)} %bitcast.200, bf16[2,256,2048]{2,1,0:T(8,128)(2,1)S(1)} %copy-done.28, f32[2,256,2048]{2,1,0:T(8,128)} %get-tuple-element.105, f32[2,256]{1,0:T(2,128)S(1)} %broadcast_multiply_fusion, f32[2048]{0:T(1024)S(1)} %copy-done.49, f32[2,256]{1,0:T(2,128)S(1)} %copy-done.50), kind=kLoop, calls=%fused_computation.33 | loop fusion | flops 7340032 | bytes 14692352 | tf_op jit(solution)/shard_map/add | solution.py:939
  (258 shorter events, 33.8 us)
Async XLA Ops:
  7.2 88.1 %copy-start = (s32[2,1024]{1,0:T(2,128)S(1)}, s32[2,1024]{1,0:T(2,128)}, u32[]{:S(2)}) copy-start(s32[2,1024]{1,0:T(2,128)} %param.17) | copy-start | bytes 24580
  7.2 195.2 %all-gather.2.cloned.1.call-start = ((), (), s32[]{:S(2)}) async-start(), calls=%async_computation.1 | async-start | bytes 9732096 | tf_op jit(solution)/shard_map/all_gather | solution.py:831
  9.6 76.0 %copy-start.29 = (bf16[2,256,2048]{2,1,0:T(8,128)(2,1)S(1)}, bf16[2,256,2048]{2,1,0:T(8,128)(2,1)}, u32[]{:S(2)}) copy-start(bf16[2,256,2048]{2,1,0:T(8,128)(2,1)} %param.16) | copy-start | bytes 6291460
  9.6 453.8 %reduce-scatter.2.cloned.1.call-start = ((), (), s32[]{:S(2)}) async-start(), calls=%async_computation.2 | async-start | bytes 9732096 | tf_op jit(solution)/shard_map/reduce_scatter | solution.py:873
  85.6 7.9 %copy-start.53 = (bf16[2,64]{1,0:T(2,128)(2,1)S(1)}, bf16[2,64]{1,0:T(2,128)(2,1)}, u32[]{:S(2)}) copy-start(bf16[2,64]{1,0:T(2,128)(2,1)} %param.23) | copy-start | bytes 772
  85.7 10.2 %copy-start.57 = (s32[4]{0:T(128)S(1)}, s32[4]{0:T(128)}, u32[]{:S(2)}) copy-start(s32[4]{0:T(128)} %param.19) | copy-start | bytes 52
  87.3 45.1 %collective-permute-start.1 = (bf16[256,2048]{1,0:T(8,128)(2,1)}, bf16[256,2048]{1,0:T(8,128)(2,1)}, u32[]{:S(2)}, u32[]{:S(2)}) collective-permute-start(bf16[256,2048]{1,0:T(8,128)(2,1)} %get-tuple-element.137), channel_id=1, source_target_pairs={{0,1},{1,0},{2,3},{3,2},{4,5},{5,4},{6,7},{7,6},{8,9},{9,8},{10,11... | collective-permute-start | bytes 3145736 | tf_op jit(solution)/shard_map/ppermute | solution.py:32
  91.9 38.9 %collective-permute-start = (bf16[256,2048]{1,0:T(8,128)(2,1)}, bf16[256,2048]{1,0:T(8,128)(2,1)}, u32[]{:S(2)}, u32[]{:S(2)}) collective-permute-start(bf16[256,2048]{1,0:T(8,128)(2,1)} %get-tuple-element.137), channel_id=1, source_target_pairs={{0,2},{1,3},{2,0},{3,1},{4,6},{5,7},{6,4},{7,5},{8,10},{9,11},{10,... | collective-permute-start | bytes 3145736 | tf_op jit(solution)/shard_map/ppermute | solution.py:32
  92.8 106.6 %collective-permute-start.3 = (bf16[256,2048]{1,0:T(8,128)(2,1)}, bf16[256,2048]{1,0:T(8,128)(2,1)}, u32[]{:S(2)}, u32[]{:S(2)}) collective-permute-start(bf16[256,2048]{1,0:T(8,128)(2,1)} %get-tuple-element.135), channel_id=1, source_target_pairs={{0,1},{1,0},{2,3},{3,2},{4,5},{5,4},{6,7},{7,6},{8,9},{9,8},{10,11... | collective-permute-start | bytes 3145736 | tf_op jit(solution)/shard_map/ppermute | solution.py:32
  93.7 26.1 %copy-start.16 = (f32[2,64]{0,1:T(8,128)}, f32[2,64]{0,1:T(8,128)S(1)}, u32[]{:S(2)}) copy-start(f32[2,64]{0,1:T(8,128)S(1)} %copy.33) | copy-start | bytes 1540
  98.2 6.0 %copy-start.48 = (f32[2048]{0:T(1024)}, f32[2048]{0:T(1024)S(1)}, u32[]{:S(2)}) copy-start(f32[2048]{0:T(1024)S(1)} %get-tuple-element.117) | copy-start | bytes 24580
  98.3 11.3 %copy-start.18 = (s32[1,1024]{1,0:T(1,128)}, s32[1,1024]{1,0:T(1,128)S(1)}, u32[]{:S(2)}) copy-start(s32[1,1024]{1,0:T(1,128)S(1)} %get-tuple-element.180.first_ref) | copy-start | bytes 12292
  98.3 21.5 %copy-start.20 = (s32[1,1024]{1,0:T(1,128)}, s32[1,1024]{1,0:T(1,128)S(1)}, u32[]{:S(2)}) copy-start(s32[1,1024]{1,0:T(1,128)S(1)} %get-tuple-element.181.first_ref) | copy-start | bytes 12292
  98.3 5.9 %copy-start.26 = (bf16[2,1024,2048]{2,1,0:T(8,128)(2,1)S(1)}, bf16[2,1024,2048]{2,1,0:T(8,128)(2,1)}, u32[]{:S(2)}) copy-start(bf16[2,1024,2048]{2,1,0:T(8,128)(2,1)} %get-tuple-element.67) | copy-start | bytes 25165828
  104.1 5.4 copy-start.8
  104.1 15.7 %copy-start.12 = (f32[32,1024]{1,0:T(8,128)}, f32[32,1024]{1,0:T(8,128)S(1)}, u32[]{:S(2)}) copy-start(f32[32,1024]{1,0:T(8,128)S(1)} %get-tuple-element.161.sin_ref) | copy-start | bytes 393220
  104.2 5.4 copy-start.10
  104.2 15.6 %copy-start.14 = (f32[32,1024]{1,0:T(8,128)}, f32[32,1024]{1,0:T(8,128)S(1)}, u32[]{:S(2)}) copy-start(f32[32,1024]{1,0:T(8,128)S(1)} %get-tuple-element.163.cos_ref) | copy-start | bytes 393220
  106.4 10.3 %copy-start.32 = (bf16[1024,2048]{1,0:T(8,128)(2,1)}, bf16[1024,2048]{1,0:T(8,128)(2,1)S(1)}, u32[]{:S(2)}) copy-start(bf16[1024,2048]{1,0:T(8,128)(2,1)S(1)} %get-tuple-element.126.refs_3_) | copy-start | bytes 12582916
  109.5 10.2 %copy-start.22 = (bf16[576,1024]{1,0:T(8,128)(2,1)}, bf16[576,1024]{1,0:T(8,128)(2,1)S(1)}, u32[]{:S(2)}) copy-start(bf16[576,1024]{1,0:T(8,128)(2,1)S(1)} %fusion.42.x_ref) | copy-start | bytes 3538948
  119.8 8.6 %copy-start.24 = (bf16[576,1024]{1,0:T(8,128)(2,1)}, bf16[576,1024]{1,0:T(8,128)(2,1)S(1)}, u32[]{:S(2)}) copy-start(bf16[576,1024]{1,0:T(8,128)(2,1)S(1)} %fusion.39.x_ref) | copy-start | bytes 3538948
  119.8 8.1 %copy-start.27 = (bf16[2,256,2048]{2,1,0:T(8,128)(2,1)S(1)}, bf16[2,256,2048]{2,1,0:T(8,128)(2,1)}, u32[]{:S(2)}) copy-start(bf16[2,256,2048]{2,1,0:T(8,128)(2,1)} %tokens.1) | copy-start | bytes 6291460
  127.2 8.3 %copy-start.6 = (bf16[320,1024]{1,0:T(8,128)(2,1)}, bf16[320,1024]{1,0:T(8,128)(2,1)S(1)}, u32[]{:S(2)}) copy-start(bf16[320,1024]{1,0:T(8,128)(2,1)S(1)} %get-tuple-element.72.refs_1_.o_ref) | copy-start | bytes 1966084
  130.8 63.6 %collective-permute-start.2 = (bf16[256,2048]{1,0:T(8,128)(2,1)}, bf16[256,2048]{1,0:T(8,128)(2,1)}, u32[]{:S(2)}, u32[]{:S(2)}) collective-permute-start(bf16[256,2048]{1,0:T(8,128)(2,1)} %collective-permute-done), channel_id=1, source_target_pairs={{0,1},{1,0},{2,3},{3,2},{4,5},{5,4},{6,7},{7,6},{8,9},{9,8},{10,11... | collective-permute-start | bytes 3145736 | tf_op jit(solution)/shard_map/ppermute | solution.py:32
  202.4 38.6 %collective-permute-start.4 = (bf16[256,2048]{1,0:T(8,128)(2,1)S(1)}, bf16[256,2048]{1,0:T(8,128)(2,1)S(1)}, u32[]{:S(2)}, u32[]{:S(2)}) collective-permute-start(bf16[256,2048]{1,0:T(8,128)(2,1)S(1)} %bitcast.205), channel_id=1, source_target_pairs={{0,2},{1,3},{2,0},{3,1},{4,6},{5,7},{6,4},{7,5},{8,10},{9,11},{10,... | collective-permute-start | bytes 3145736 | tf_op jit(solution)/shard_map/ppermute | solution.py:32
  224.2 8.3 %copy-start.56 = (bf16[704,6144]{1,0:T(8,128)(2,1)S(1)}, bf16[704,6144]{1,0:T(8,128)(2,1)}, u32[]{:S(2)}) copy-start(bf16[704,6144]{1,0:T(8,128)(2,1)} %all-gather.2.cloned.1.call-done) | copy-start | bytes 25952260
  241.0 11.9 %collective-permute-start.5 = (bf16[256,2048]{1,0:T(8,128)(2,1)S(1)}, bf16[256,2048]{1,0:T(8,128)(2,1)S(1)}, u32[]{:S(2)}, u32[]{:S(2)}) collective-permute-start(bf16[256,2048]{1,0:T(8,128)(2,1)S(1)} %collective-permute-done.4), channel_id=1, source_target_pairs={{0,1},{1,0},{2,3},{3,2},{4,5},{5,4},{6,7},{7,6},{8,9},{9,8},{10,11... | collective-permute-start | bytes 3145736 | tf_op jit(solution)/shard_map/ppermute | solution.py:32
  279.7 6.6 %copy-start.59 = (bf16[2048,704]{0,1:T(8,128)(2,1)S(1)}, bf16[2048,704]{0,1:T(8,128)(2,1)}, u32[]{:S(2)}) copy-start(bf16[2048,704]{0,1:T(8,128)(2,1)} %get-tuple-element.124) | copy-start | bytes 8650756
  296.7 7.7 %copy-start.60 = (bf16[2048,704]{0,1:T(8,128)(2,1)S(1)}, bf16[2048,704]{0,1:T(8,128)(2,1)}, u32[]{:S(2)}) copy-start(bf16[2048,704]{0,1:T(8,128)(2,1)} %get-tuple-element.124) | copy-start | bytes 8650756
  296.8 15.2 %slice-start = ((s8[8650752]{0:T(1024)(128)(4,1)}), s8[4194304]{0:T(1024)(128)(4,1)S(1)}, s32[]{:S(2)}) async-start(s8[8650752]{0:T(1024)(128)(4,1)} %bitcast.222), calls=%async_computation.3 | async-start | bytes 8388608
  296.8 15.2 %slice-start.1 = ((s8[8650752]{0:T(1024)(128)(4,1)}), s8[4194304]{0:T(1024)(128)(4,1)S(1)}, s32[]{:S(2)}) async-start(s8[8650752]{0:T(1024)(128)(4,1)} %bitcast.222), calls=%async_computation.4 | async-start | bytes 8388608
  304.4 7.5 %slice-start.2 = ((s8[8650752]{0:T(1024)(128)(4,1)}), s8[262144]{0:T(1024)(128)(4,1)S(1)}, s32[]{:S(2)}) async-start(s8[8650752]{0:T(1024)(128)(4,1)} %bitcast.222), calls=%async_computation.5 | async-start | bytes 524288
  311.5 14.3 %collective-permute-start.7 = (bf16[256,2048]{1,0:T(8,128)(2,1)S(1)}, bf16[256,2048]{1,0:T(8,128)(2,1)S(1)}, u32[]{:S(2)}, u32[]{:S(2)}) collective-permute-start(bf16[256,2048]{1,0:T(8,128)(2,1)S(1)} %get-tuple-element.134), channel_id=1, source_target_pairs={{0,1},{1,0},{2,3},{3,2},{4,5},{5,4},{6,7},{7,6},{8,9},{9,8},{10,11... | collective-permute-start | bytes 3145736 | tf_op jit(solution)/shard_map/ppermute | solution.py:32
  324.0 5.3 copy-start.35
  325.3 3.9 collective-permute-start.9
  325.6 26.5 %collective-permute-start.6 = (bf16[256,2048]{1,0:T(8,128)(2,1)S(1)}, bf16[256,2048]{1,0:T(8,128)(2,1)S(1)}, u32[]{:S(2)}, u32[]{:S(2)}) collective-permute-start(bf16[256,2048]{1,0:T(8,128)(2,1)S(1)} %get-tuple-element.133), channel_id=1, source_target_pairs={{0,1},{1,0},{2,3},{3,2},{4,5},{5,4},{6,7},{7,6},{8,9},{9,8},{10,11... | collective-permute-start | bytes 3145736 | tf_op jit(solution)/shard_map/ppermute | solution.py:32
  326.3 25.3 %collective-permute-start.8 = (bf16[256,2048]{1,0:T(8,128)(2,1)S(1)}, bf16[256,2048]{1,0:T(8,128)(2,1)S(1)}, u32[]{:S(2)}, u32[]{:S(2)}) collective-permute-start(bf16[256,2048]{1,0:T(8,128)(2,1)S(1)} %add_convert_fusion.3), channel_id=1, source_target_pairs={{0,2},{1,3},{2,0},{3,1},{4,6},{5,7},{6,4},{7,5},{8,10},{9,11},{10,... | collective-permute-start | bytes 3145736 | tf_op jit(solution)/shard_map/ppermute | solution.py:32
  329.3 52.6 %collective-permute-start.14 = (bf16[256,2048]{1,0:T(8,128)(2,1)}, bf16[256,2048]{1,0:T(8,128)(2,1)S(1)}, u32[]{:S(2)}, u32[]{:S(2)}) collective-permute-start(bf16[256,2048]{1,0:T(8,128)(2,1)} %get-tuple-element.131), channel_id=1, source_target_pairs={{0,1},{1,0},{2,3},{3,2},{4,5},{5,4},{6,7},{7,6},{8,9},{9,8},{10,11... | collective-permute-start | bytes 3145736 | tf_op jit(solution)/shard_map/ppermute | solution.py:32
  330.6 24.9 %copy-start.30 = (bf16[2,256,2048]{2,1,0:T(8,128)(2,1)S(1)}, bf16[2,256,2048]{2,1,0:T(8,128)(2,1)}, u32[]{:S(2)}) copy-start(bf16[2,256,2048]{2,1,0:T(8,128)(2,1)} %param.16) | copy-start | bytes 6291460
  351.6 30.1 %collective-permute-start.10 = (bf16[256,2048]{1,0:T(8,128)(2,1)}, bf16[256,2048]{1,0:T(8,128)(2,1)}, u32[]{:S(2)}, u32[]{:S(2)}) collective-permute-start(bf16[256,2048]{1,0:T(8,128)(2,1)} %add_convert_fusion.2), channel_id=1, source_target_pairs={{0,2},{1,3},{2,0},{3,1},{4,6},{5,7},{6,4},{7,5},{8,10},{9,11},{10,... | collective-permute-start | bytes 3145736 | tf_op jit(solution)/shard_map/ppermute | solution.py:32
  352.0 8.4 %slice-start.3 = ((s8[5242880]{0:T(1024)(128)(4,1)}), s8[4194304]{0:T(1024)(128)(4,1)S(1)}, s32[]{:S(2)}) async-start(s8[5242880]{0:T(1024)(128)(4,1)} %bitcast.225), calls=%async_computation.6 | async-start | bytes 8388608
  376.4 5.3 copy-start.33
  377.3 24.5 %collective-permute-start.13 = (bf16[320,256]{1,0:T(8,128)(2,1)}, bf16[320,256]{1,0:T(8,128)(2,1)S(1)}, u32[]{:S(2)}, u32[]{:S(2)}) collective-permute-start(bf16[320,256]{1,0:T(8,128)(2,1)} %get-tuple-element.156), channel_id=1, source_target_pairs={{0,3},{1,2},{2,1},{3,0},{4,7},{5,6},{6,5},{7,4},{8,11},{9,10},{10,... | collective-permute-start | bytes 491528 | tf_op jit(solution)/shard_map/ppermute | solution.py:32
  377.7 29.6 %collective-permute-start.12 = (bf16[320,256]{1,0:T(8,128)(2,1)}, bf16[320,256]{1,0:T(8,128)(2,1)}, u32[]{:S(2)}, u32[]{:S(2)}) collective-permute-start(bf16[320,256]{1,0:T(8,128)(2,1)} %get-tuple-element.157), channel_id=1, source_target_pairs={{0,2},{1,3},{2,0},{3,1},{4,6},{5,7},{6,4},{7,5},{8,10},{9,11},{10,... | collective-permute-start | bytes 491528 | tf_op jit(solution)/shard_map/ppermute | solution.py:32
  378.9 28.8 %collective-permute-start.11 = (bf16[320,256]{1,0:T(8,128)(2,1)}, bf16[320,256]{1,0:T(8,128)(2,1)}, u32[]{:S(2)}, u32[]{:S(2)}) collective-permute-start(bf16[320,256]{1,0:T(8,128)(2,1)} %get-tuple-element.158), channel_id=1, source_target_pairs={{0,1},{1,0},{2,3},{3,2},{4,5},{5,4},{6,7},{7,6},{8,9},{9,8},{10,11... | collective-permute-start | bytes 491528 | tf_op jit(solution)/shard_map/ppermute | solution.py:32
  381.7 20.8 %collective-permute-start.18 = (bf16[2,256,2048]{2,1,0:T(8,128)(2,1)}, bf16[2,256,2048]{2,1,0:T(8,128)(2,1)}, u32[]{:S(2)}, u32[]{:S(2)}) collective-permute-start(bf16[2,256,2048]{2,1,0:T(8,128)(2,1)} %get-tuple-element.128), channel_id=1, source_target_pairs={{0,1},{1,0},{2,3},{3,2},{4,5},{5,4},{6,7},{7,6},{8,9},{9,8},{10,11... | collective-permute-start | bytes 6291464 | tf_op jit(solution)/shard_map/ppermute | solution.py:32
  383.1 8.0 %slice-start.5 = ((s8[5242880]{0:T(1024)(128)(4,1)}), s8[4194304]{0:T(1024)(128)(4,1)S(1)}, s32[]{:S(2)}) async-start(s8[5242880]{0:T(1024)(128)(4,1)} %bitcast.228), calls=%async_computation.8 | async-start | bytes 8388608
  395.7 12.0 %collective-permute-start.17 = (bf16[320,256]{1,0:T(8,128)(2,1)S(1)}, bf16[320,256]{1,0:T(8,128)(2,1)S(1)}, u32[]{:S(2)}, u32[]{:S(2)}) collective-permute-start(bf16[320,256]{1,0:T(8,128)(2,1)S(1)} %get-tuple-element.152), channel_id=1, source_target_pairs={{0,3},{1,2},{2,1},{3,0},{4,7},{5,6},{6,5},{7,4},{8,11},{9,10},{10,... | collective-permute-start | bytes 491528 | tf_op jit(solution)/shard_map/ppermute | solution.py:32
  401.8 6.9 %collective-permute-start.16 = (bf16[320,256]{1,0:T(8,128)(2,1)S(1)}, bf16[320,256]{1,0:T(8,128)(2,1)S(1)}, u32[]{:S(2)}, u32[]{:S(2)}) collective-permute-start(bf16[320,256]{1,0:T(8,128)(2,1)S(1)} %get-tuple-element.153), channel_id=1, source_target_pairs={{0,2},{1,3},{2,0},{3,1},{4,6},{5,7},{6,4},{7,5},{8,10},{9,11},{10,... | collective-permute-start | bytes 491528 | tf_op jit(solution)/shard_map/ppermute | solution.py:32
  402.5 6.7 %copy-start.39 = (bf16[256,2048]{1,0:T(8,128)(2,1)S(1)}, bf16[256,2048]{1,0:T(8,128)(2,1)}, u32[]{:S(2)}) copy-start(bf16[256,2048]{1,0:T(8,128)(2,1)} %copy-done.38) | copy-start | bytes 3145732
  402.5 6.7 %copy-start.41 = (bf16[256,2048]{1,0:T(8,128)(2,1)S(1)}, bf16[256,2048]{1,0:T(8,128)(2,1)}, u32[]{:S(2)}) copy-start(bf16[256,2048]{1,0:T(8,128)(2,1)} %copy-done.40) | copy-start | bytes 3145732
  402.5 6.2 %collective-permute-start.15 = (bf16[320,256]{1,0:T(8,128)(2,1)S(1)}, bf16[320,256]{1,0:T(8,128)(2,1)S(1)}, u32[]{:S(2)}, u32[]{:S(2)}) collective-permute-start(bf16[320,256]{1,0:T(8,128)(2,1)S(1)} %get-tuple-element.154), channel_id=1, source_target_pairs={{0,1},{1,0},{2,3},{3,2},{4,5},{5,4},{6,7},{7,6},{8,9},{9,8},{10,11... | collective-permute-start | bytes 491528 | tf_op jit(solution)/shard_map/ppermute | solution.py:32
  407.3 49.1 %collective-permute-start.20 = (bf16[2,256,2048]{2,1,0:T(8,128)(2,1)}, bf16[2,256,2048]{2,1,0:T(8,128)(2,1)}, u32[]{:S(2)}, u32[]{:S(2)}) collective-permute-start(bf16[2,256,2048]{2,1,0:T(8,128)(2,1)} %get-tuple-element.127), channel_id=1, source_target_pairs={{0,1},{1,0},{2,3},{3,2},{4,5},{5,4},{6,7},{7,6},{8,9},{9,8},{10,11... | collective-permute-start | bytes 6291464 | tf_op jit(solution)/shard_map/ppermute | solution.py:32
  408.7 47.8 %collective-permute-start.19 = (bf16[2,256,2048]{2,1,0:T(8,128)(2,1)}, bf16[2,256,2048]{2,1,0:T(8,128)(2,1)}, u32[]{:S(2)}, u32[]{:S(2)}) collective-permute-start(bf16[2,256,2048]{2,1,0:T(8,128)(2,1)} %fusion.17), channel_id=1, source_target_pairs={{0,2},{1,3},{2,0},{3,1},{4,6},{5,7},{6,4},{7,5},{8,10},{9,11},{10,... | collective-permute-start | bytes 6291464 | tf_op jit(solution)/shard_map/ppermute | solution.py:32
  410.9 18.0 %copy-start.5 = (bf16[320,1024]{1,0:T(8,128)(2,1)S(1)}, bf16[320,1024]{1,0:T(8,128)(2,1)}, u32[]{:S(2)}) copy-start(bf16[320,1024]{1,0:T(8,128)(2,1)} %copy-done.4) | copy-start | bytes 1966084
  410.9 17.9 %copy-start.9 = (f32[32,1024]{1,0:T(8,128)S(1)}, f32[32,1024]{1,0:T(8,128)}, u32[]{:S(2)}) copy-start(f32[32,1024]{1,0:T(8,128)} %copy-done.8) | copy-start | bytes 393220
  410.9 17.9 %copy-start.11 = (f32[32,1024]{1,0:T(8,128)S(1)}, f32[32,1024]{1,0:T(8,128)}, u32[]{:S(2)}) copy-start(f32[32,1024]{1,0:T(8,128)} %copy-done.10) | copy-start | bytes 393220
  410.9 17.9 %copy-start.19 = (s32[1,1024]{1,0:T(1,128)S(1)}, s32[1,1024]{1,0:T(1,128)}, u32[]{:S(2)}) copy-start(s32[1,1024]{1,0:T(1,128)} %copy-done.18) | copy-start | bytes 12292
  410.9 17.9 %copy-start.23 = (bf16[576,1024]{1,0:T(8,128)(2,1)S(1)}, bf16[576,1024]{1,0:T(8,128)(2,1)}, u32[]{:S(2)}) copy-start(bf16[576,1024]{1,0:T(8,128)(2,1)} %copy-done.22) | copy-start | bytes 3538948
  428.9 18.8 %copy-start.45 = (bf16[1280,256]{1,0:T(8,128)(2,1)S(1)}, bf16[1280,256]{1,0:T(8,128)(2,1)}, u32[]{:S(2)}) copy-start(bf16[1280,256]{1,0:T(8,128)(2,1)} %get-tuple-element.129) | copy-start | bytes 1966084
  428.9 18.8 %copy-start.46 = (bf16[1280,256]{1,0:T(8,128)(2,1)S(1)}, bf16[1280,256]{1,0:T(8,128)(2,1)}, u32[]{:S(2)}) copy-start(bf16[1280,256]{1,0:T(8,128)(2,1)} %get-tuple-element.130) | copy-start | bytes 1966084
  556.3 6.9 %copy-start.42 = (f32[64,1920]{1,0:T(8,128)}, f32[64,1920]{1,0:T(8,128)S(1)}, u32[]{:S(2)}) copy-start(f32[64,1920]{1,0:T(8,128)S(1)} %concatenate.65) | copy-start | bytes 1474564
  556.4 7.3 %copy-start.47 = (f32[64,1280]{1,0:T(8,128)S(1)}, f32[64,1280]{1,0:T(8,128)}, u32[]{:S(2)}) copy-start(f32[64,1280]{1,0:T(8,128)} %get-tuple-element.201) | copy-start | bytes 983044
  556.4 8.0 %copy-start.1 = (s32[2,1024]{1,0:T(2,128)S(1)}, s32[2,1024]{1,0:T(2,128)}, u32[]{:S(2)}) copy-start(s32[2,1024]{1,0:T(2,128)} %param.17) | copy-start | bytes 24580
  (27 other events, 84.2 us)
Sparse Core Ops, SparseCore 0:
  10.8 156.6 all-gather.1
  296.9 152.1 reduce-scatter.1

commit v9 on v8

--- a/solution.py
+++ b/solution.py
@@ -834,17 +834,18 @@
     o_all = o_all.reshape(n_seq * q_cols, rows * length)
     w_out = w_out.reshape(width, -1)
     dy_far += [cross_seq(later[r - 1], n_seq) for r in range(1, rows)]
+    x_all = x_rows.reshape(rows * length, width).astype(F32)
+
+    h_all = x_all + dot(o_all, w_out, 0, 1)
+    inverse_two = inverse_rms(h_all)
+    f_in = (h_all * inverse_two * gains[1]).astype(BF)
+    f_in, dy_far[-1] = tie((f_in, dy_far[-1]))
     gy = []
     for r in range(rows):
         near = swap(d_output[r], "seq", n_seq, 1)
         for v in (d_output[r], near, dy_far[r], swap(dy_far[r], "seq", n_seq, 1)):
             gy.append((row_scale[r] * v.astype(F32)).astype(BF))
     gy = jnp.concatenate(gy, axis=0)
-    x_all = x_rows.reshape(rows * length, width).astype(F32)
-
-    h_all = x_all + dot(o_all, w_out, 0, 1)
-    inverse_two = inverse_rms(h_all)
-    f_in = (h_all * inverse_two * gains[1]).astype(BF)
 
     w_g, w_u, w_dn = (w_ff[:, i * width : (i + 1) * width] for i in range(3))
     gate = dot(f_in, w_g, 1, 1)

time: 575 us -> 574 us (level)
    unnamed x139 -> x151, local copies, waits for them, and re-layouts: 6.3 us -> 11.9 us
    unnamed x11 -> x13, other arithmetic: 18 us -> 14 us
  transfers between devices with their start and end apart: 23 -> 23, of which waited for: 3 -> 3; matrix products, arithmetic and copies ran while one was open for 33% -> 31% of each run, Pallas kernels for 31% -> 31%
where the time goes in v9:
time: 574 us; the launch traced here: 570 us
  Pallas kernels  256 us (45%)
  matrix products  127 us (22%)
  other arithmetic  100 us (17%)
  local copies, waits for them, and re-layouts  33.3 us (6%)
  waiting for transfers between devices  23.8 us (4%)
  between operations  15.6 us (3%)
  starting transfers between devices  14.7 us (3%)
    dot_general x17, matrix products, dot(): lax.dot_general(a, b, (((ca,), (cb,)), ((), ())), preferred_element_type=...  127 us
    pallas_call x1, Pallas kernels, close_layer(): pl.pallas_call(functools.partial(closing, n_seq, n_rows), out_shape=(jax....  81 us
    pallas_call x1, Pallas kernels, open_layer(): pl.pallas_call(functools.partial(opening, n_seq, n_rows), out_shape=(jax....  74.1 us
    pallas_call x1, Pallas kernels, meet(): pl.pallas_call(functools.partial(meeting, n_seq, n_rows), out_shape=(jax....  55.5 us
    pallas_call x2, Pallas kernels, attention_backward(): pl.pallas_call(functools.partial(backward_heads, plan), out_shape=(jax.Sh...  31.4 us
    ppermute x21, waiting for transfers between devices, swap(): return lax.ppermute(v, axis, [(i, i ^ bit) for i in range(n)])  23.7 us
    ppermute x21, starting transfers between devices, swap(): return lax.ppermute(v, axis, [(i, i ^ bit) for i in range(n)])  14.6 us
    pallas_call x2, Pallas kernels, attention_forward(): pl.pallas_call(functools.partial(forward_heads, plan), out_shape=(jax.Sha...  14.5 us
  transfers between devices with their start and end apart: 23, of which 3 were waited for; matrix products, arithmetic and copies ran while one was open for 31% of the time, Pallas kernels for 31%

profile of v9, /device:TPU:0, one launch (start us, length us, event | category | flops | bytes accessed | tf_op | source)
XLA Modules:
  0.0 570.4 jit_solution(11375084430448658146)
XLA Ops:
  7.3 2.3 pad_maximum_fusion.3
  11.5 74.1 %opening.1 = (bf16[2,1024,2048]{2,1,0:T(8,128)(2,1)}, bf16[2048,640]{1,0:T(8,128)(2,1)}) custom-call(bf16[2,256,2048]{2,1,0:T(8,128)(2,1)} %tokens.1, bf16[4,64,640]{2,1,0:T(8,128)(2,1)} %pad_maximum_fusion.6.pieces), custom_call_target="tpu_custom_call" | custom-call | tf_op jit(solution)/shard_map/opening/pallas_call | solution.py:171
  85.7 1.6 slice_bitcast_fusion.28
  87.3 4.6 collective-permute-start.1
  93.7 1.4 slice_reduce_fusion.2
  96.1 1.2 convert_bitcast_fusion
  98.3 4.8 fusion.3
  104.3 2.2 fusion.5
  106.5 3.0 fusion.42.x_ref
  109.6 7.1 %attention_forward.3 = (bf16[320,1024]{1,0:T(8,128)(2,1)S(1)}, f32[5,1,1024]{2,1,0:T(1,128)S(1)}) custom-call(s32[1]{0:T(128)} %bitcast.me_ref, bf16[576,1024]{1,0:T(8,128)(2,1)S(1)} %fusion.42.x_ref, f32[32,1024]{1,0:T(8,128)S(1)} %get-tuple-element.166.cos_ref, f32[32,1024]{1,0:T(8,128)S(1)} %get-tuple-element.164.sin_ref, ...), custom_call_target="tpu_custom_call" | custom-call | flops 1342177280 | bytes 4194304 | tf_op jit(solution)/shard_map/attention_forward/pallas_call | solution.py:702
  116.7 3.1 fusion.39.x_ref
  119.9 7.4 %attention_forward.2 = (bf16[320,1024]{1,0:T(8,128)(2,1)S(1)}, f32[5,1,1024]{2,1,0:T(1,128)S(1)}) custom-call(s32[1]{0:T(128)} %bitcast.me_ref, bf16[576,1024]{1,0:T(8,128)(2,1)S(1)} %fusion.39.x_ref, f32[32,1024]{1,0:T(8,128)S(1)} %get-tuple-element.167.cos_ref, f32[32,1024]{1,0:T(8,128)S(1)} %get-tuple-element.165.sin_ref, ...), custom_call_target="tpu_custom_call" | custom-call | flops 1342177280 | bytes 4194304 | tf_op jit(solution)/shard_map/attention_forward/pallas_call | solution.py:702
  131.4 2.1 fusion.53
  133.5 2.1 fusion.54
  135.6 3.3 copy-done.50
  138.9 55.5 %meeting.1 = (bf16[4,320,2048]{2,1,0:T(8,128)(2,1)}, bf16[8,4,64,1280]{3,2,1,0:T(8,128)(2,1)}) custom-call(bf16[320,1024]{1,0:T(8,128)(2,1)} %copy-done.4, bf16[320,1024]{1,0:T(8,128)(2,1)} %copy-done.6, bf16[64,1280]{1,0:T(8,128)(2,1)} %refs_2_.1), custom_call_target="tpu_custom_call" | custom-call | tf_op jit(solution)/shard_map/meeting/pallas_call | solution.py:279
  194.4 3.1 fusion.55
  197.5 1.9 fusion.56
  199.4 3.0 fusion.57
  202.4 1.6 collective-permute-start.4
  204.0 20.1 %multiply_reduce_fusion = (f32[2048]{0:T(1024)S(1)}, f32[2048,2048]{1,0:T(8,128)}) fusion(bf16[1280,2048]{1,0:T(8,128)(2,1)} %bitcast.216, bf16[2048,1280]{1,0:T(8,128)(2,1)} %bitcast.228, bf16[2,1024,2048]{2,1,0:T(8,128)(2,1)} %get-tuple-element.69), kind=kOutput, calls=%fused_computation.5 | convolution fusion | flops 10754193408 | bytes 35659776 | tf_op jit(solution)/shard_map/dot_general | solution.py:28
  224.1 2.0 multiply_reduce_fusion.6
  226.1 7.7 %multiply_convert_fusion = bf16[2048,2048]{1,0:T(8,128)(2,1)S(1)} fusion(f32[2048,2048]{1,0:T(8,128)} %get-tuple-element.189, f32[2048]{0:T(1024)S(1)} %get-tuple-element.120, f32[2048]{0:T(1024)S(1)} %add_rsqrt_fusion), kind=kLoop, calls=%fused_computation.4 | loop fusion | flops 12582912 | bytes 25182208 | tf_op jit(solution)/shard_map/convert_element_type | solution.py:841
  234.1 8.4 %fusion.29 = f32[2048,704]{0,1:T(8,128)} fusion(bf16[2048,2048]{1,0:T(8,128)(2,1)S(1)} %multiply_convert_fusion, bf16[704,6144]{1,0:T(8,128)(2,1)S(1)} %bitcast.225), kind=kOutput, calls=%fused_computation.59 | convolution fusion | flops 5905580032 | bytes 17039360 | tf_op jit(solution)/shard_map/dot_general | solution.py:28
  244.3 3.3 copy-done.51
  247.6 7.9 %fusion.19 = f32[2048,704]{0,1:T(8,128)} fusion(bf16[2048,2048]{1,0:T(8,128)(2,1)S(1)} %fusion.59, bf16[704,6144]{1,0:T(8,128)(2,1)S(1)} %bitcast.225), kind=kOutput, calls=%fused_computation.49 | convolution fusion | flops 5905580032 | bytes 17039360 | tf_op jit(solution)/shard_map/dot_general | solution.py:28
  255.5 13.6 %multiply_convert_fusion.1 = (bf16[2048,704]{0,1:T(8,128)(2,1)}, bf16[2048,704]{0,1:T(8,128)(2,1)S(1)}, bf16[2048,704]{0,1:T(8,128)(2,1)}) fusion(f32[2048,704]{0,1:T(8,128)} %fusion.29, f32[2048,704]{0,1:T(8,128)} %fusion.19, bf16[2048,2048]{1,0:T(8,128)(2,1)S(1)} %multiply_convert_fusion, bf16[704,6144]{1,0:T(8,128)(2,1)} %all-gather.2.cloned.1.call-done), kind=kOutput, calls=%fused_computation.21 | convolution fusion | flops 5927206912 | bytes 31457280 | tf_op jit(solution)/shard_map/dot_general | solution.py:28
  269.2 9.4 %convolution_convert_fusion.2 = bf16[704,2048]{1,0:T(8,128)(2,1)S(1)} fusion(bf16[2048,704]{0,1:T(8,128)(2,1)} %get-tuple-element.88, bf16[2048,2048]{1,0:T(8,128)(2,1)} %copy-done.51), kind=kOutput, calls=%fused_computation.43 | convolution fusion | flops 5907021824 | bytes 14155776 | tf_op jit(solution)/shard_map/dot_general | solution.py:28
  278.6 6.6 %convolution_convert_fusion.4 = bf16[704,2048]{1,0:T(8,128)(2,1)S(1)} fusion(bf16[2048,704]{0,1:T(8,128)(2,1)S(1)} %get-tuple-element.127, bf16[2048,2048]{1,0:T(8,128)(2,1)S(1)} %multiply_convert_fusion), kind=kOutput, calls=%fused_computation.45 | convolution fusion | flops 5907021824 | bytes 14155776 | tf_op jit(solution)/shard_map/dot_general | solution.py:28
  285.2 6.4 %convolution_convert_fusion.3 = bf16[704,2048]{1,0:T(8,128)(2,1)S(1)} fusion(bf16[2048,704]{0,1:T(8,128)(2,1)S(1)} %copy-done.60, bf16[2048,2048]{1,0:T(8,128)(2,1)S(1)} %multiply_convert_fusion), kind=kOutput, calls=%fused_computation.44 | convolution fusion | flops 5907021824 | bytes 14155776 | tf_op jit(solution)/shard_map/dot_general | solution.py:28
  291.7 3.9 pad_maximum_fusion
  295.6 7.7 %fusion.27 = f32[1024,2048]{1,0:T(8,128)} fusion(bf16[704,6144]{1,0:T(8,128)(2,1)} %all-gather.2.cloned.1.call-done, bf16[2048,704]{0,1:T(8,128)(2,1)S(1)} %get-tuple-element.127), kind=kOutput, calls=%fused_computation.57 | convolution fusion | flops 2952790016 | bytes 12713984 | tf_op jit(solution)/shard_map/dot_general | solution.py:28
  303.3 6.9 %add_convert_fusion.1 = bf16[1024,2048]{1,0:T(8,128)(2,1)S(1)} fusion(f32[1024,2048]{1,0:T(8,128)} %fusion.27, bf16[704,6144]{1,0:T(8,128)(2,1)} %all-gather.2.cloned.1.call-done, bf16[2048,704]{0,1:T(8,128)(2,1)S(1)} %copy-done.61), kind=kOutput, calls=%fused_computation.18 | convolution fusion | flops 2956984320 | bytes 16908288 | tf_op jit(solution)/shard_map/dot_general | solution.py:28
  310.8 5.7 %fusion.25 = f32[1024,2048]{1,0:T(8,128)} fusion(bf16[704,6144]{1,0:T(8,128)(2,1)S(1)} %bitcast.227, bf16[2048,704]{0,1:T(8,128)(2,1)S(1)} %get-tuple-element.127), kind=kOutput, calls=%fused_computation.55 | convolution fusion | flops 2952790016 | bytes 12713984 | tf_op jit(solution)/shard_map/dot_general | solution.py:28
  316.6 6.2 %add_convert_fusion = bf16[1024,2048]{1,0:T(8,128)(2,1)S(1)} fusion(f32[1024,2048]{1,0:T(8,128)} %fusion.25, bf16[704,6144]{1,0:T(8,128)(2,1)S(1)} %bitcast.227, bf16[2048,704]{0,1:T(8,128)(2,1)S(1)} %copy-done.61), kind=kOutput, calls=%fused_computation.17 | convolution fusion | flops 2956984320 | bytes 16908288 | tf_op jit(solution)/shard_map/dot_general | solution.py:28
  322.8 1.3 fusion.75
  325.6 2.5 fusion.74
  328.1 1.4 add_convert_fusion.2
  329.5 20.9 %collective-permute-done.8 = bf16[256,2048]{1,0:T(8,128)(2,1)S(1)} collective-permute-done((bf16[256,2048]{1,0:T(8,128)(2,1)S(1)}, bf16[256,2048]{1,0:T(8,128)(2,1)S(1)}, u32[]{:S(2)}, u32[]{:S(2)}) %collective-permute-start.8) | collective-permute-done | bytes 1048608 | tf_op jit(solution)/shard_map/ppermute | solution.py:32
  350.8 3.5 multiply_reduce_fusion.2
  354.3 4.9 fusion.73
  359.2 2.4 convolution_convert_fusion.6
  361.7 2.6 gather_fusion.1
  365.5 9.7 %convolution_convert_fusion.1 = bf16[2048,2048]{1,0:T(8,128)(2,1)S(1)} fusion(bf16[2048,704]{0,1:T(8,128)(2,1)} %get-tuple-element.88, bf16[704,6144]{1,0:T(8,128)(2,1)} %all-gather.2.cloned.1.call-done), kind=kOutput, calls=%fused_computation.20 | convolution fusion | flops 5909774336 | bytes 14155776 | tf_op jit(solution)/shard_map/dot_general | solution.py:28
  377.9 2.3 slice_bitcast_fusion.1
  380.6 1.3 copy-done.36
  381.9 2.9 multiply_reduce_fusion.1
  384.9 5.0 fusion.72
  389.9 2.5 convolution_convert_fusion.5
  392.4 1.9 gather_fusion.2
  395.6 4.3 pad_maximum_fusion.1
  401.4 4.6 fusion.17
  407.9 1.6 pad_maximum_fusion.2
  409.6 15.6 %attention_backward.2 = (bf16[576,1024]{1,0:T(8,128)(2,1)S(1)}, f32[2,64,128]{2,1,0:T(8,128)S(1)}) custom-call(s32[1]{0:T(128)} %bitcast.me_ref, bf16[576,1024]{1,0:T(8,128)(2,1)S(1)} %copy-done.25, f32[32,1024]{1,0:T(8,128)S(1)} %copy-done.15, f32[32,1024]{1,0:T(8,128)S(1)} %copy-done.13, s32[1,1024]{1,0:T(1,128)S(1)} %copy-done.21, f32[64,2]{1,0:T(8,128)S(1)} %bitcast.192, ...), custom_call_target="tpu_custom_call" | custom-call | flops 3355443200 | bytes 6291456 | tf_op jit(solution)/shard_map/attention_backward/pallas_call | solution.py:732
  427.6 15.8 %attention_backward.3 = (bf16[576,1024]{1,0:T(8,128)(2,1)S(1)}, f32[2,64,128]{2,1,0:T(8,128)S(1)}) custom-call(s32[1]{0:T(128)} %bitcast.me_ref, bf16[576,1024]{1,0:T(8,128)(2,1)S(1)} %copy-done.23, f32[32,1024]{1,0:T(8,128)S(1)} %copy-done.11, f32[32,1024]{1,0:T(8,128)S(1)} %copy-done.9, s32[1,1024]{1,0:T(1,128)S(1)} %copy-done.19, f32[64,2]{1,0:T(8,128)S(1)} %bitcast.193, ...), custom_call_target="tpu_custom_call" | custom-call | flops 3355443200 | bytes 6291456 | tf_op jit(solution)/shard_map/attention_backward/pallas_call | solution.py:732
  444.8 1.6 maximum_bitcast_fusion.refs_5_
  446.4 6.8 %convolution_convert_fusion = bf16[2048,1280]{1,0:T(8,128)(2,1)} fusion(bf16[512,2048]{1,0:T(8,128)(2,1)} %pad_maximum_fusion.2, bf16[1280,256]{1,0:T(8,128)(2,1)S(1)} %copy-done.46, bf16[1280,256]{1,0:T(8,128)(2,1)S(1)} %copy-done.45), kind=kOutput, calls=%fused_computation.19 | convolution fusion | flops 2689597440 | bytes 8650752 | tf_op jit(solution)/shard_map/dot_general | solution.py:28
  453.2 1.9 collective-permute-done.19
  455.1 7.0 %fusion.15 = bf16[2,256,2048]{2,1,0:T(8,128)(2,1)} fusion(f32[2,4,256,2048]{3,2,1,0:T(8,128)} %bitcast.199, bf16[2,256,2048]{2,1,0:T(8,128)(2,1)} %collective-permute-done.19, bf16[2,256,2048]{2,1,0:T(8,128)(2,1)} %collective-permute-done.20, bf16[2,4,256,2048]{3,2,1,0:T(8,128)(2,1)} %bitcast.203), kind=kLoop, calls=%fused_computation.37 | loop fusion | flops 7340032 | bytes 12582912 | tf_op jit(solution)/shard_map/convert_element_type | solution.py:914
  462.1 1.9 slice_convert_fusion.1
  464.1 2.3 slice_convert_fusion
  467.0 81.0 %closing.1 = (f32[2,256,2048]{2,1,0:T(8,128)}, bf16[4,64,640]{2,1,0:T(8,128)(2,1)}, f32[64,1280]{1,0:T(8,128)}) custom-call(bf16[576,1024]{1,0:T(8,128)(2,1)} %copy-done.3, bf16[576,1024]{1,0:T(8,128)(2,1)} %copy-done.2, bf16[1024,2048]{1,0:T(8,128)(2,1)} %copy-done.31, bf16[1024,2048]{1,0:T(8,128)(2,1)} %copy-done.32, ...), custom_call_target="tpu_custom_call" | custom-call | tf_op jit(solution)/shard_map/closing/pallas_call | solution.py:524
  550.3 3.1 fusion.9
  555.3 6.7 %fusion.12 = f32[2,256,2048]{2,1,0:T(8,128)} fusion(f32[2,256,2048]{2,1,0:T(8,128)} %bitcast.200, bf16[2,256,2048]{2,1,0:T(8,128)(2,1)S(1)} %copy-done.28, f32[2,256,2048]{2,1,0:T(8,128)} %get-tuple-element.109, f32[2,256]{1,0:T(2,128)S(1)} %broadcast_multiply_fusion, f32[2048]{0:T(1024)S(1)} %copy-done.49, f32[2,256]{1,0:T(2,128)S(1)} %copy-done.52), kind=kLoop, calls=%fused_computation.33 | loop fusion | flops 7340032 | bytes 14692352 | tf_op jit(solution)/shard_map/add | solution.py:940
  (272 shorter events, 34.0 us)
Async XLA Ops:
  7.2 88.1 %copy-start = (s32[2,1024]{1,0:T(2,128)S(1)}, s32[2,1024]{1,0:T(2,128)}, u32[]{:S(2)}) copy-start(s32[2,1024]{1,0:T(2,128)} %param.17) | copy-start | bytes 24580
  7.2 195.2 %all-gather.2.cloned.1.call-start = ((), (), s32[]{:S(2)}) async-start(), calls=%async_computation.1 | async-start | bytes 9732096 | tf_op jit(solution)/shard_map/all_gather | solution.py:831
  9.6 76.0 %copy-start.29 = (bf16[2,256,2048]{2,1,0:T(8,128)(2,1)S(1)}, bf16[2,256,2048]{2,1,0:T(8,128)(2,1)}, u32[]{:S(2)}) copy-start(bf16[2,256,2048]{2,1,0:T(8,128)(2,1)} %param.16) | copy-start | bytes 6291460
  9.6 452.5 %reduce-scatter.2.cloned.1.call-start = ((), (), s32[]{:S(2)}) async-start(), calls=%async_computation.2 | async-start | bytes 9732096 | tf_op jit(solution)/shard_map/reduce_scatter | solution.py:874
  85.6 8.0 %copy-start.55 = (bf16[2,64]{1,0:T(2,128)(2,1)S(1)}, bf16[2,64]{1,0:T(2,128)(2,1)}, u32[]{:S(2)}) copy-start(bf16[2,64]{1,0:T(2,128)(2,1)} %param.23) | copy-start | bytes 772
  85.7 10.2 %copy-start.58 = (s32[4]{0:T(128)S(1)}, s32[4]{0:T(128)}, u32[]{:S(2)}) copy-start(s32[4]{0:T(128)} %param.19) | copy-start | bytes 52
  87.3 44.1 %collective-permute-start.1 = (bf16[256,2048]{1,0:T(8,128)(2,1)}, bf16[256,2048]{1,0:T(8,128)(2,1)}, u32[]{:S(2)}, u32[]{:S(2)}) collective-permute-start(bf16[256,2048]{1,0:T(8,128)(2,1)} %get-tuple-element.141), channel_id=1, source_target_pairs={{0,1},{1,0},{2,3},{3,2},{4,5},{5,4},{6,7},{7,6},{8,9},{9,8},{10,11... | collective-permute-start | bytes 3145736 | tf_op jit(solution)/shard_map/ppermute | solution.py:32
  91.9 37.9 %collective-permute-start = (bf16[256,2048]{1,0:T(8,128)(2,1)}, bf16[256,2048]{1,0:T(8,128)(2,1)}, u32[]{:S(2)}, u32[]{:S(2)}) collective-permute-start(bf16[256,2048]{1,0:T(8,128)(2,1)} %get-tuple-element.141), channel_id=1, source_target_pairs={{0,2},{1,3},{2,0},{3,1},{4,6},{5,7},{6,4},{7,5},{8,10},{9,11},{10,... | collective-permute-start | bytes 3145736 | tf_op jit(solution)/shard_map/ppermute | solution.py:32
  92.8 106.6 %collective-permute-start.3 = (bf16[256,2048]{1,0:T(8,128)(2,1)}, bf16[256,2048]{1,0:T(8,128)(2,1)}, u32[]{:S(2)}, u32[]{:S(2)}) collective-permute-start(bf16[256,2048]{1,0:T(8,128)(2,1)} %get-tuple-element.139), channel_id=1, source_target_pairs={{0,1},{1,0},{2,3},{3,2},{4,5},{5,4},{6,7},{7,6},{8,9},{9,8},{10,11... | collective-permute-start | bytes 3145736 | tf_op jit(solution)/shard_map/ppermute | solution.py:32
  93.7 26.1 %copy-start.16 = (f32[2,64]{0,1:T(8,128)}, f32[2,64]{0,1:T(8,128)S(1)}, u32[]{:S(2)}) copy-start(f32[2,64]{0,1:T(8,128)S(1)} %copy.33) | copy-start | bytes 1540
  98.3 6.0 %copy-start.48 = (f32[2048]{0:T(1024)}, f32[2048]{0:T(1024)S(1)}, u32[]{:S(2)}) copy-start(f32[2048]{0:T(1024)S(1)} %get-tuple-element.121) | copy-start | bytes 24580
  98.3 11.3 %copy-start.18 = (s32[1,1024]{1,0:T(1,128)}, s32[1,1024]{1,0:T(1,128)S(1)}, u32[]{:S(2)}) copy-start(s32[1,1024]{1,0:T(1,128)S(1)} %get-tuple-element.184.first_ref) | copy-start | bytes 12292
  98.3 21.5 %copy-start.20 = (s32[1,1024]{1,0:T(1,128)}, s32[1,1024]{1,0:T(1,128)S(1)}, u32[]{:S(2)}) copy-start(s32[1,1024]{1,0:T(1,128)S(1)} %get-tuple-element.185.first_ref) | copy-start | bytes 12292
  98.3 5.9 %copy-start.26 = (bf16[2,1024,2048]{2,1,0:T(8,128)(2,1)S(1)}, bf16[2,1024,2048]{2,1,0:T(8,128)(2,1)}, u32[]{:S(2)}) copy-start(bf16[2,1024,2048]{2,1,0:T(8,128)(2,1)} %get-tuple-element.69) | copy-start | bytes 25165828
  104.2 15.7 %copy-start.12 = (f32[32,1024]{1,0:T(8,128)}, f32[32,1024]{1,0:T(8,128)S(1)}, u32[]{:S(2)}) copy-start(f32[32,1024]{1,0:T(8,128)S(1)} %get-tuple-element.165.sin_ref) | copy-start | bytes 393220
  104.2 15.6 %copy-start.14 = (f32[32,1024]{1,0:T(8,128)}, f32[32,1024]{1,0:T(8,128)S(1)}, u32[]{:S(2)}) copy-start(f32[32,1024]{1,0:T(8,128)S(1)} %get-tuple-element.167.cos_ref) | copy-start | bytes 393220
  106.5 10.3 %copy-start.32 = (bf16[1024,2048]{1,0:T(8,128)(2,1)}, bf16[1024,2048]{1,0:T(8,128)(2,1)S(1)}, u32[]{:S(2)}) copy-start(bf16[1024,2048]{1,0:T(8,128)(2,1)S(1)} %get-tuple-element.130.refs_3_) | copy-start | bytes 12582916
  109.6 10.2 %copy-start.22 = (bf16[576,1024]{1,0:T(8,128)(2,1)}, bf16[576,1024]{1,0:T(8,128)(2,1)S(1)}, u32[]{:S(2)}) copy-start(bf16[576,1024]{1,0:T(8,128)(2,1)S(1)} %fusion.42.x_ref) | copy-start | bytes 3538948
  119.8 8.6 %copy-start.24 = (bf16[576,1024]{1,0:T(8,128)(2,1)}, bf16[576,1024]{1,0:T(8,128)(2,1)S(1)}, u32[]{:S(2)}) copy-start(bf16[576,1024]{1,0:T(8,128)(2,1)S(1)} %fusion.39.x_ref) | copy-start | bytes 3538948
  119.8 8.1 %copy-start.27 = (bf16[2,256,2048]{2,1,0:T(8,128)(2,1)S(1)}, bf16[2,256,2048]{2,1,0:T(8,128)(2,1)}, u32[]{:S(2)}) copy-start(bf16[2,256,2048]{2,1,0:T(8,128)(2,1)} %tokens.1) | copy-start | bytes 6291460
  127.2 6.3 %copy-start.6 = (bf16[320,1024]{1,0:T(8,128)(2,1)}, bf16[320,1024]{1,0:T(8,128)(2,1)S(1)}, u32[]{:S(2)}) copy-start(bf16[320,1024]{1,0:T(8,128)(2,1)S(1)} %get-tuple-element.74.refs_1_.o_ref) | copy-start | bytes 1966084
  129.9 64.5 %collective-permute-start.2 = (bf16[256,2048]{1,0:T(8,128)(2,1)}, bf16[256,2048]{1,0:T(8,128)(2,1)}, u32[]{:S(2)}, u32[]{:S(2)}) collective-permute-start(bf16[256,2048]{1,0:T(8,128)(2,1)} %collective-permute-done), channel_id=1, source_target_pairs={{0,1},{1,0},{2,3},{3,2},{4,5},{5,4},{6,7},{7,6},{8,9},{9,8},{10,11... | collective-permute-start | bytes 3145736 | tf_op jit(solution)/shard_map/ppermute | solution.py:32
  202.4 31.4 %collective-permute-start.4 = (bf16[256,2048]{1,0:T(8,128)(2,1)S(1)}, bf16[256,2048]{1,0:T(8,128)(2,1)S(1)}, u32[]{:S(2)}, u32[]{:S(2)}) collective-permute-start(bf16[256,2048]{1,0:T(8,128)(2,1)S(1)} %bitcast.205), channel_id=1, source_target_pairs={{0,2},{1,3},{2,0},{3,1},{4,6},{5,7},{6,4},{7,5},{8,10},{9,11},{10,... | collective-permute-start | bytes 3145736 | tf_op jit(solution)/shard_map/ppermute | solution.py:32
  224.1 10.0 %slice-start.2 = ((s8[8650752]{0:T(1024)(128)(4,1)}), s8[4194304]{0:T(1024)(128)(4,1)S(1)}, s32[]{:S(2)}) async-start(s8[8650752]{0:T(1024)(128)(4,1)} %bitcast.224), calls=%async_computation.5 | async-start | bytes 8388608
  226.1 8.0 %slice-start.3 = ((s8[8650752]{0:T(1024)(128)(4,1)}), s8[4194304]{0:T(1024)(128)(4,1)S(1)}, s32[]{:S(2)}) async-start(s8[8650752]{0:T(1024)(128)(4,1)} %bitcast.224), calls=%async_computation.6 | async-start | bytes 8388608
  226.1 8.0 %slice-start.4 = ((s8[8650752]{0:T(1024)(128)(4,1)}), s8[262144]{0:T(1024)(128)(4,1)S(1)}, s32[]{:S(2)}) async-start(s8[8650752]{0:T(1024)(128)(4,1)} %bitcast.224), calls=%async_computation.7 | async-start | bytes 524288
  226.1 16.4 %slice-start = ((s8[8388608]{0:T(1024)(128)(4,1)}), s8[4194304]{0:T(1024)(128)(4,1)S(1)}, s32[]{:S(2)}) async-start(s8[8388608]{0:T(1024)(128)(4,1)} %bitcast.218), calls=%async_computation.3 | async-start | bytes 8388608
  233.8 8.7 %slice-start.1 = ((s8[8388608]{0:T(1024)(128)(4,1)}), s8[4194304]{0:T(1024)(128)(4,1)S(1)}, s32[]{:S(2)}) async-start(s8[8388608]{0:T(1024)(128)(4,1)} %bitcast.218), calls=%async_computation.4 | async-start | bytes 8388608
  233.8 9.6 %collective-permute-start.5 = (bf16[256,2048]{1,0:T(8,128)(2,1)S(1)}, bf16[256,2048]{1,0:T(8,128)(2,1)S(1)}, u32[]{:S(2)}, u32[]{:S(2)}) collective-permute-start(bf16[256,2048]{1,0:T(8,128)(2,1)S(1)} %collective-permute-done.4), channel_id=1, source_target_pairs={{0,1},{1,0},{2,3},{3,2},{4,5},{5,4},{6,7},{7,6},{8,9},{9,8},{10,11... | collective-permute-start | bytes 3145736 | tf_op jit(solution)/shard_map/ppermute | solution.py:32
  278.6 6.6 %copy-start.60 = (bf16[2048,704]{0,1:T(8,128)(2,1)S(1)}, bf16[2048,704]{0,1:T(8,128)(2,1)}, u32[]{:S(2)}) copy-start(bf16[2048,704]{0,1:T(8,128)(2,1)} %get-tuple-element.128) | copy-start | bytes 8650756
  295.6 7.7 %copy-start.61 = (bf16[2048,704]{0,1:T(8,128)(2,1)S(1)}, bf16[2048,704]{0,1:T(8,128)(2,1)}, u32[]{:S(2)}) copy-start(bf16[2048,704]{0,1:T(8,128)(2,1)} %get-tuple-element.128) | copy-start | bytes 8650756
  295.6 15.2 %slice-start.5 = ((s8[8650752]{0:T(1024)(128)(4,1)}), s8[4194304]{0:T(1024)(128)(4,1)S(1)}, s32[]{:S(2)}) async-start(s8[8650752]{0:T(1024)(128)(4,1)} %bitcast.226), calls=%async_computation.8 | async-start | bytes 8388608
  295.6 15.2 %slice-start.6 = ((s8[8650752]{0:T(1024)(128)(4,1)}), s8[4194304]{0:T(1024)(128)(4,1)S(1)}, s32[]{:S(2)}) async-start(s8[8650752]{0:T(1024)(128)(4,1)} %bitcast.226), calls=%async_computation.9 | async-start | bytes 8388608
  303.3 7.5 %slice-start.7 = ((s8[8650752]{0:T(1024)(128)(4,1)}), s8[262144]{0:T(1024)(128)(4,1)S(1)}, s32[]{:S(2)}) async-start(s8[8650752]{0:T(1024)(128)(4,1)} %bitcast.226), calls=%async_computation.10 | async-start | bytes 524288
  310.4 14.2 %collective-permute-start.7 = (bf16[256,2048]{1,0:T(8,128)(2,1)S(1)}, bf16[256,2048]{1,0:T(8,128)(2,1)S(1)}, u32[]{:S(2)}, u32[]{:S(2)}) collective-permute-start(bf16[256,2048]{1,0:T(8,128)(2,1)S(1)} %get-tuple-element.138), channel_id=1, source_target_pairs={{0,1},{1,0},{2,3},{3,2},{4,5},{5,4},{6,7},{7,6},{8,9},{9,8},{10,11... | collective-permute-start | bytes 3145736 | tf_op jit(solution)/shard_map/ppermute | solution.py:32
  324.1 4.0 collective-permute-start.9
  324.3 26.5 %collective-permute-start.6 = (bf16[256,2048]{1,0:T(8,128)(2,1)S(1)}, bf16[256,2048]{1,0:T(8,128)(2,1)S(1)}, u32[]{:S(2)}, u32[]{:S(2)}) collective-permute-start(bf16[256,2048]{1,0:T(8,128)(2,1)S(1)} %get-tuple-element.137), channel_id=1, source_target_pairs={{0,1},{1,0},{2,3},{3,2},{4,5},{5,4},{6,7},{7,6},{8,9},{9,8},{10,11... | collective-permute-start | bytes 3145736 | tf_op jit(solution)/shard_map/ppermute | solution.py:32
  325.0 25.3 %collective-permute-start.8 = (bf16[256,2048]{1,0:T(8,128)(2,1)S(1)}, bf16[256,2048]{1,0:T(8,128)(2,1)S(1)}, u32[]{:S(2)}, u32[]{:S(2)}) collective-permute-start(bf16[256,2048]{1,0:T(8,128)(2,1)S(1)} %add_convert_fusion.3), channel_id=1, source_target_pairs={{0,2},{1,3},{2,0},{3,1},{4,6},{5,7},{6,4},{7,5},{8,10},{9,11},{10,... | collective-permute-start | bytes 3145736 | tf_op jit(solution)/shard_map/ppermute | solution.py:32
  328.1 52.6 %collective-permute-start.14 = (bf16[256,2048]{1,0:T(8,128)(2,1)}, bf16[256,2048]{1,0:T(8,128)(2,1)S(1)}, u32[]{:S(2)}, u32[]{:S(2)}) collective-permute-start(bf16[256,2048]{1,0:T(8,128)(2,1)} %get-tuple-element.135), channel_id=1, source_target_pairs={{0,1},{1,0},{2,3},{3,2},{4,5},{5,4},{6,7},{7,6},{8,9},{9,8},{10,11... | collective-permute-start | bytes 3145736 | tf_op jit(solution)/shard_map/ppermute | solution.py:32
  329.4 24.8 %copy-start.30 = (bf16[2,256,2048]{2,1,0:T(8,128)(2,1)S(1)}, bf16[2,256,2048]{2,1,0:T(8,128)(2,1)}, u32[]{:S(2)}) copy-start(bf16[2,256,2048]{2,1,0:T(8,128)(2,1)} %param.16) | copy-start | bytes 6291460
  350.3 30.2 %collective-permute-start.10 = (bf16[256,2048]{1,0:T(8,128)(2,1)}, bf16[256,2048]{1,0:T(8,128)(2,1)}, u32[]{:S(2)}, u32[]{:S(2)}) collective-permute-start(bf16[256,2048]{1,0:T(8,128)(2,1)} %add_convert_fusion.2), channel_id=1, source_target_pairs={{0,2},{1,3},{2,0},{3,1},{4,6},{5,7},{6,4},{7,5},{8,10},{9,11},{10,... | collective-permute-start | bytes 3145736 | tf_op jit(solution)/shard_map/ppermute | solution.py:32
  350.8 8.4 %slice-start.8 = ((s8[5242880]{0:T(1024)(128)(4,1)}), s8[4194304]{0:T(1024)(128)(4,1)S(1)}, s32[]{:S(2)}) async-start(s8[5242880]{0:T(1024)(128)(4,1)} %bitcast.229), calls=%async_computation.11 | async-start | bytes 8388608
  376.0 24.4 %collective-permute-start.13 = (bf16[320,256]{1,0:T(8,128)(2,1)}, bf16[320,256]{1,0:T(8,128)(2,1)S(1)}, u32[]{:S(2)}, u32[]{:S(2)}) collective-permute-start(bf16[320,256]{1,0:T(8,128)(2,1)} %get-tuple-element.160), channel_id=1, source_target_pairs={{0,3},{1,2},{2,1},{3,0},{4,7},{5,6},{6,5},{7,4},{8,11},{9,10},{10,... | collective-permute-start | bytes 491528 | tf_op jit(solution)/shard_map/ppermute | solution.py:32
  376.4 29.7 %collective-permute-start.12 = (bf16[320,256]{1,0:T(8,128)(2,1)}, bf16[320,256]{1,0:T(8,128)(2,1)}, u32[]{:S(2)}, u32[]{:S(2)}) collective-permute-start(bf16[320,256]{1,0:T(8,128)(2,1)} %get-tuple-element.161), channel_id=1, source_target_pairs={{0,2},{1,3},{2,0},{3,1},{4,6},{5,7},{6,4},{7,5},{8,10},{9,11},{10,... | collective-permute-start | bytes 491528 | tf_op jit(solution)/shard_map/ppermute | solution.py:32
  377.7 28.8 %collective-permute-start.11 = (bf16[320,256]{1,0:T(8,128)(2,1)}, bf16[320,256]{1,0:T(8,128)(2,1)}, u32[]{:S(2)}, u32[]{:S(2)}) collective-permute-start(bf16[320,256]{1,0:T(8,128)(2,1)} %get-tuple-element.162), channel_id=1, source_target_pairs={{0,1},{1,0},{2,3},{3,2},{4,5},{5,4},{6,7},{7,6},{8,9},{9,8},{10,11... | collective-permute-start | bytes 491528 | tf_op jit(solution)/shard_map/ppermute | solution.py:32
  380.5 20.7 %collective-permute-start.18 = (bf16[2,256,2048]{2,1,0:T(8,128)(2,1)}, bf16[2,256,2048]{2,1,0:T(8,128)(2,1)}, u32[]{:S(2)}, u32[]{:S(2)}) collective-permute-start(bf16[2,256,2048]{2,1,0:T(8,128)(2,1)} %get-tuple-element.132), channel_id=1, source_target_pairs={{0,1},{1,0},{2,3},{3,2},{4,5},{5,4},{6,7},{7,6},{8,9},{9,8},{10,11... | collective-permute-start | bytes 6291464 | tf_op jit(solution)/shard_map/ppermute | solution.py:32
  381.9 8.0 %slice-start.10 = ((s8[5242880]{0:T(1024)(128)(4,1)}), s8[4194304]{0:T(1024)(128)(4,1)S(1)}, s32[]{:S(2)}) async-start(s8[5242880]{0:T(1024)(128)(4,1)} %bitcast.232), calls=%async_computation.13 | async-start | bytes 8388608
  394.5 11.9 %collective-permute-start.17 = (bf16[320,256]{1,0:T(8,128)(2,1)S(1)}, bf16[320,256]{1,0:T(8,128)(2,1)S(1)}, u32[]{:S(2)}, u32[]{:S(2)}) collective-permute-start(bf16[320,256]{1,0:T(8,128)(2,1)S(1)} %get-tuple-element.156), channel_id=1, source_target_pairs={{0,3},{1,2},{2,1},{3,0},{4,7},{5,6},{6,5},{7,4},{8,11},{9,10},{10,... | collective-permute-start | bytes 491528 | tf_op jit(solution)/shard_map/ppermute | solution.py:32
  400.5 6.9 %collective-permute-start.16 = (bf16[320,256]{1,0:T(8,128)(2,1)S(1)}, bf16[320,256]{1,0:T(8,128)(2,1)S(1)}, u32[]{:S(2)}, u32[]{:S(2)}) collective-permute-start(bf16[320,256]{1,0:T(8,128)(2,1)S(1)} %get-tuple-element.157), channel_id=1, source_target_pairs={{0,2},{1,3},{2,0},{3,1},{4,6},{5,7},{6,4},{7,5},{8,10},{9,11},{10,... | collective-permute-start | bytes 491528 | tf_op jit(solution)/shard_map/ppermute | solution.py:32
  401.2 6.7 %copy-start.39 = (bf16[256,2048]{1,0:T(8,128)(2,1)S(1)}, bf16[256,2048]{1,0:T(8,128)(2,1)}, u32[]{:S(2)}) copy-start(bf16[256,2048]{1,0:T(8,128)(2,1)} %copy-done.38) | copy-start | bytes 3145732
  401.2 6.7 %copy-start.41 = (bf16[256,2048]{1,0:T(8,128)(2,1)S(1)}, bf16[256,2048]{1,0:T(8,128)(2,1)}, u32[]{:S(2)}) copy-start(bf16[256,2048]{1,0:T(8,128)(2,1)} %copy-done.40) | copy-start | bytes 3145732
  401.2 6.2 %collective-permute-start.15 = (bf16[320,256]{1,0:T(8,128)(2,1)S(1)}, bf16[320,256]{1,0:T(8,128)(2,1)S(1)}, u32[]{:S(2)}, u32[]{:S(2)}) collective-permute-start(bf16[320,256]{1,0:T(8,128)(2,1)S(1)} %get-tuple-element.158), channel_id=1, source_target_pairs={{0,1},{1,0},{2,3},{3,2},{4,5},{5,4},{6,7},{7,6},{8,9},{9,8},{10,11... | collective-permute-start | bytes 491528 | tf_op jit(solution)/shard_map/ppermute | solution.py:32
  406.1 49.1 %collective-permute-start.20 = (bf16[2,256,2048]{2,1,0:T(8,128)(2,1)}, bf16[2,256,2048]{2,1,0:T(8,128)(2,1)}, u32[]{:S(2)}, u32[]{:S(2)}) collective-permute-start(bf16[2,256,2048]{2,1,0:T(8,128)(2,1)} %get-tuple-element.131), channel_id=1, source_target_pairs={{0,1},{1,0},{2,3},{3,2},{4,5},{5,4},{6,7},{7,6},{8,9},{9,8},{10,11... | collective-permute-start | bytes 6291464 | tf_op jit(solution)/shard_map/ppermute | solution.py:32
  407.4 47.8 %collective-permute-start.19 = (bf16[2,256,2048]{2,1,0:T(8,128)(2,1)}, bf16[2,256,2048]{2,1,0:T(8,128)(2,1)}, u32[]{:S(2)}, u32[]{:S(2)}) collective-permute-start(bf16[2,256,2048]{2,1,0:T(8,128)(2,1)} %fusion.17), channel_id=1, source_target_pairs={{0,2},{1,3},{2,0},{3,1},{4,6},{5,7},{6,4},{7,5},{8,10},{9,11},{10,... | collective-permute-start | bytes 6291464 | tf_op jit(solution)/shard_map/ppermute | solution.py:32
  409.6 17.9 %copy-start.5 = (bf16[320,1024]{1,0:T(8,128)(2,1)S(1)}, bf16[320,1024]{1,0:T(8,128)(2,1)}, u32[]{:S(2)}) copy-start(bf16[320,1024]{1,0:T(8,128)(2,1)} %copy-done.4) | copy-start | bytes 1966084
  409.6 17.9 %copy-start.9 = (f32[32,1024]{1,0:T(8,128)S(1)}, f32[32,1024]{1,0:T(8,128)}, u32[]{:S(2)}) copy-start(f32[32,1024]{1,0:T(8,128)} %copy-done.8) | copy-start | bytes 393220
  409.6 17.9 %copy-start.11 = (f32[32,1024]{1,0:T(8,128)S(1)}, f32[32,1024]{1,0:T(8,128)}, u32[]{:S(2)}) copy-start(f32[32,1024]{1,0:T(8,128)} %copy-done.10) | copy-start | bytes 393220
  409.6 17.9 %copy-start.19 = (s32[1,1024]{1,0:T(1,128)S(1)}, s32[1,1024]{1,0:T(1,128)}, u32[]{:S(2)}) copy-start(s32[1,1024]{1,0:T(1,128)} %copy-done.18) | copy-start | bytes 12292
  409.6 17.9 %copy-start.23 = (bf16[576,1024]{1,0:T(8,128)(2,1)S(1)}, bf16[576,1024]{1,0:T(8,128)(2,1)}, u32[]{:S(2)}) copy-start(bf16[576,1024]{1,0:T(8,128)(2,1)} %copy-done.22) | copy-start | bytes 3538948
  427.6 18.8 %copy-start.45 = (bf16[1280,256]{1,0:T(8,128)(2,1)S(1)}, bf16[1280,256]{1,0:T(8,128)(2,1)}, u32[]{:S(2)}) copy-start(bf16[1280,256]{1,0:T(8,128)(2,1)} %get-tuple-element.133) | copy-start | bytes 1966084
  427.6 18.8 %copy-start.46 = (bf16[1280,256]{1,0:T(8,128)(2,1)S(1)}, bf16[1280,256]{1,0:T(8,128)(2,1)}, u32[]{:S(2)}) copy-start(bf16[1280,256]{1,0:T(8,128)(2,1)} %get-tuple-element.134) | copy-start | bytes 1966084
  555.1 6.9 %copy-start.42 = (f32[64,1920]{1,0:T(8,128)}, f32[64,1920]{1,0:T(8,128)S(1)}, u32[]{:S(2)}) copy-start(f32[64,1920]{1,0:T(8,128)S(1)} %concatenate.65) | copy-start | bytes 1474564
  555.3 7.3 %copy-start.47 = (f32[64,1280]{1,0:T(8,128)S(1)}, f32[64,1280]{1,0:T(8,128)}, u32[]{:S(2)}) copy-start(f32[64,1280]{1,0:T(8,128)} %get-tuple-element.205) | copy-start | bytes 983044
  555.3 8.0 %copy-start.1 = (s32[2,1024]{1,0:T(2,128)S(1)}, s32[2,1024]{1,0:T(2,128)}, u32[]{:S(2)}) copy-start(s32[2,1024]{1,0:T(2,128)} %param.17) | copy-start | bytes 24580
  (33 other events, 111.8 us)
Sparse Core Ops, SparseCore 0:
  10.8 156.6 all-gather.1
  295.7 152.2 reduce-scatter.1
